TPU v7x, 32 devices: a whole 2x2x4 slice. The times are simulated.
32 devices in a mesh: groups: 2 (over y), expert: 4 (over z), dp: 4 (over x, core), rep: 1.
Axes of the slice: x: 2, y: 2, z: 4, core: 2. Of those that a mesh axis runs over, the one named last changes fastest.
Arguments:
- tokens: bfloat16 [4096, 1024], P(('groups', 'expert', 'dp')), parts along dimension 0, may hold values from -6 to 6
- routes: int32 [4096, 6], P(('groups', 'expert', 'dp')), parts along dimension 0, may hold values from 0 to 11, all different within a row; in each aligned block of 64 rows (0 to 63, 64 to 127, ...) at most 32 rows name the same one
- gate_weight: bfloat16 [8, 1024, 768], P('expert', ('dp', 'rep')), may hold values from -0.1875 to 0.1875
- up_weight: bfloat16 [8, 1024, 768], P('expert', ('dp', 'rep')), may hold values from -0.1875 to 0.1875
- down_weight: bfloat16 [8, 1024, 768], P('expert', ('dp', 'rep')), may hold values from -0.21875 to 0.21875
- router: bfloat16 [1024, 12], replicated, may hold values from -0.1875 to 0.1875
- const_vec: bfloat16 [2, 1024], replicated, may hold values from -6 to 6
- const_gate: bfloat16 [1024, 2], replicated, may hold values from -0.1875 to 0.1875
- grad_out: bfloat16 [4096, 1024], P(('groups', 'expert', 'dp')), parts along dimension 0, may hold values from -6 to 6
Outputs:
- mixed: bfloat16 [4096, 1024], P(('groups', 'expert', 'dp')), parts along dimension 0
- grad_tokens: bfloat16 [4096, 1024], P(('groups', 'expert', 'dp')), parts along dimension 0
- grad_gate: bfloat16 [16, 1024, 768], P(('groups', 'expert'), ('dp', 'rep')), parts along dimension 0
- grad_up: bfloat16 [16, 1024, 768], P(('groups', 'expert'), ('dp', 'rep')), parts along dimension 0
- grad_down: bfloat16 [16, 1024, 768], P(('groups', 'expert'), ('dp', 'rep')), parts along dimension 0
- grad_router: float32 [2048, 12], P('groups'), parts along dimension 0
- grad_const_vec: float32 [4, 1024], P('groups'), parts along dimension 0
- grad_const_gate: float32 [2048, 2], P('groups'), parts along dimension 0
There are 2 independent parts, one for each index of `groups`. A program takes and returns all parts, laid end to end along the dimension named above; an argument that names none is the same for every part. Nothing has to cross between parts.
Inputs may be any that keep to these rules, and one draw needn't show every extreme that they name: `routes`: in each aligned block of 64 rows, no id is named by more than 32 rows. A row names 6 different ids.
All inputs are finite; a program needn't handle non-finite values.
Results may differ from a plain program's by a relative error of at most 0.012.
Values may be sent and summed in bfloat16 or wider, within the bound.
No kernel may reach another device: no remote copies, remote signals or barrier semaphores. Data moves between devices by JAX's collectives and lax.ppermute only.
A program may use at most 64 MiB of HBM per device.

v0:
```python
import jax
import jax.numpy as jnp
from jax import lax
from jax.sharding import PartitionSpec as P

ROWS_CONTRACT = (((0,), (0,)), ((), ()))
LAST_CONTRACT = (((1,), (1,)), ((), ()))


def silu_slope(argument):
    logistic = jax.nn.sigmoid(argument)
    return logistic * (1.0 + argument * (1.0 - logistic))


def expert_forward(token_rows, w_gate, w_up, w_down):
    pre_gate = jnp.dot(token_rows, w_gate, preferred_element_type=jnp.float32)
    pre_up = jnp.dot(token_rows, w_up, preferred_element_type=jnp.float32)
    hidden = (jax.nn.silu(pre_gate) * pre_up).astype(jnp.bfloat16)
    output_rows = lax.dot_general(hidden, w_down, LAST_CONTRACT, preferred_element_type=jnp.float32)
    return (output_rows.astype(jnp.bfloat16), hidden, pre_gate, pre_up)


def expert_backward(pre_gate, pre_up, upstream, w_gate, w_up, w_down):
    d_hidden = jnp.dot(upstream, w_down, preferred_element_type=jnp.float32)
    d_gate = (d_hidden * pre_up * silu_slope(pre_gate)).astype(jnp.bfloat16)
    d_up = (d_hidden * jax.nn.silu(pre_gate)).astype(jnp.bfloat16)
    back_rows = lax.dot_general(d_gate, w_gate, LAST_CONTRACT, preferred_element_type=jnp.float32)
    back_rows = back_rows + lax.dot_general(
        d_up, w_up, LAST_CONTRACT, preferred_element_type=jnp.float32
    )
    return (back_rows.astype(jnp.bfloat16), d_gate, d_up)


def block_terms(token_rows, hidden, upstream, d_gate, d_up):
    term_gate = lax.dot_general(
        token_rows, d_gate, ROWS_CONTRACT, preferred_element_type=jnp.float32
    )
    term_up = lax.dot_general(token_rows, d_up, ROWS_CONTRACT, preferred_element_type=jnp.float32)
    term_down = lax.dot_general(upstream, hidden, ROWS_CONTRACT, preferred_element_type=jnp.float32)
    return (term_gate, term_up, term_down)


def token_trip(buffer):
    return lax.all_to_all(buffer, ("expert", "dp"), split_axis=0, concat_axis=0, tiled=True)


def on_device(
    tokens, routes, gate_weight, up_weight, down_weight, router, const_vec, const_gate, grad_out
):
    shard_rows, top_count = routes.shape
    row_count = shard_rows // lax.axis_size("rep")
    first_row = lax.axis_index("rep") * row_count
    tokens = lax.dynamic_slice_in_dim(tokens, first_row, row_count, 0)
    routes = lax.dynamic_slice_in_dim(routes, first_row, row_count, 0)
    grad_out = lax.dynamic_slice_in_dim(grad_out, first_row, row_count, 0)
    model_width = tokens.shape[1]
    id_count = router.shape[1]
    const_count = const_vec.shape[0]
    expert_count = id_count - 2 - const_count
    half_rows = row_count // 2
    capacity = (half_rows * top_count + id_count - 1) // id_count
    target_count = lax.axis_size("expert") * lax.axis_size("dp")
    slot_count = target_count * capacity
    stored_experts, stored_rows, hidden_width = gate_weight.shape
    spread = lax.axis_size("dp") * lax.axis_size("rep")
    id_range = lax.broadcasted_iota(jnp.int32, (1, 1, id_count), 2)
    picks = routes[:, :, None] == id_range
    named = jnp.sum(picks.astype(jnp.float32), axis=1)
    row_index = lax.broadcasted_iota(jnp.int32, (row_count, row_count), 0)
    column_index = lax.broadcasted_iota(jnp.int32, (row_count, row_count), 1)
    before = (
        (column_index < row_index) & (column_index // half_rows == row_index // half_rows)
    ).astype(jnp.float32)
    earlier = jnp.dot(before, named, precision=lax.Precision.HIGHEST)
    slot = jnp.sum(jnp.where(picks, earlier[:, None, :], 0.0), axis=2).astype(jnp.int32)
    member = lax.broadcasted_iota(jnp.int32, (row_count, top_count), 0) // half_rows
    routed = routes < expert_count
    target = jnp.where(routed, (2 * routes + member) * capacity + slot, slot_count)
    slot_range = lax.broadcasted_iota(jnp.int32, (slot_count, 1), 0)
    pair_range = lax.broadcasted_iota(jnp.int32, (1, row_count * top_count), 1)
    hits = slot_range == target.reshape(1, -1)
    owner = jnp.sum(jnp.where(hits, pair_range, 0), axis=1)
    filled = jnp.any(hits, axis=1)
    owner_token = owner // top_count
    target_safe = jnp.where(routed, target, 0)
    logits = jnp.dot(tokens, router, preferred_element_type=jnp.float32)
    chosen = jnp.sum(jnp.where(picks, jax.nn.sigmoid(logits)[:, None, :], 0.0), axis=2)
    gates = chosen.astype(jnp.bfloat16)
    gates_float = gates.astype(jnp.float32)
    slot_gate = jnp.where(filled, gates.reshape(-1)[owner], jnp.zeros((), jnp.bfloat16)).astype(
        jnp.float32
    )
    repeat = spread // stored_experts
    fetched = (
        lax.all_to_all(
            jnp.repeat(gate_weight, repeat, axis=0),
            ("dp", "rep"),
            split_axis=0,
            concat_axis=1,
            tiled=True,
        ),
        lax.all_to_all(
            jnp.repeat(up_weight, repeat, axis=0),
            ("dp", "rep"),
            split_axis=0,
            concat_axis=1,
            tiled=True,
        ),
        lax.all_to_all(
            jnp.repeat(down_weight, repeat, axis=0),
            ("dp", "rep"),
            split_axis=0,
            concat_axis=1,
            tiled=True,
        ),
    )
    w_gate = fetched[0].reshape(model_width, hidden_width)
    w_up = fetched[1].reshape(model_width, hidden_width)
    w_down = fetched[2].reshape(model_width, hidden_width)
    send_rows = jnp.where(filled[:, None], tokens[owner_token], jnp.zeros((), jnp.bfloat16))
    arrived = token_trip(send_rows.reshape(target_count, capacity, model_width)).reshape(
        slot_count, model_width
    )
    output_rows, hidden, pre_gate, pre_up = expert_forward(arrived, w_gate, w_up, w_down)
    returned = token_trip(output_rows.reshape(target_count, capacity, model_width)).reshape(
        slot_count, model_width
    )
    picked_out = returned[target_safe].astype(jnp.float32)
    mixed_sum = jnp.sum(
        jnp.where(routed[:, :, None], gates_float[:, :, None] * picked_out, 0.0), axis=1
    )
    cotangent_all = grad_out.astype(jnp.float32)
    routed_grad = jnp.sum(
        jnp.where(routed[:, :, None], picked_out * cotangent_all[:, None, :], 0.0), axis=2
    )
    upstream_send = (slot_gate[:, None] * grad_out[owner_token].astype(jnp.float32)).astype(
        jnp.bfloat16
    )
    upstream = token_trip(upstream_send.reshape(target_count, capacity, model_width)).reshape(
        slot_count, model_width
    )
    back_rows, d_gate, d_up = expert_backward(pre_gate, pre_up, upstream, w_gate, w_up, w_down)
    terms = block_terms(arrived, hidden, upstream, d_gate, d_up)
    sent_terms = tuple(
        (term.astype(jnp.bfloat16).reshape(spread, stored_rows, hidden_width) for term in terms)
    )
    gathered_terms = (
        lax.all_to_all(sent_terms[0], ("dp", "rep"), split_axis=0, concat_axis=0, tiled=True),
        lax.all_to_all(sent_terms[1], ("dp", "rep"), split_axis=0, concat_axis=0, tiled=True),
        lax.all_to_all(sent_terms[2], ("dp", "rep"), split_axis=0, concat_axis=0, tiled=True),
    )
    copies = spread // stored_experts
    grad_gate, grad_up, grad_down = (
        jnp.sum(
            arrived_term.reshape(stored_experts, copies, stored_rows, hidden_width),
            axis=1,
            dtype=jnp.float32,
        ).astype(jnp.bfloat16)
        for arrived_term in gathered_terms
    )
    returned_back = token_trip(back_rows.reshape(target_count, capacity, model_width)).reshape(
        slot_count, model_width
    )
    back_sum = jnp.sum(
        jnp.where(routed[:, :, None], returned_back[target_safe].astype(jnp.float32), 0.0), axis=1
    )
    is_copy = routes == expert_count + 1
    const_ids = expert_count + 2 + lax.broadcasted_iota(jnp.int32, (1, 1, const_count), 2)
    is_const = routes[:, :, None] == const_ids
    copy_weight = jnp.sum(jnp.where(is_copy, gates_float, 0.0), axis=1)
    const_weight = jnp.sum(jnp.where(is_const, gates_float[:, :, None], 0.0), axis=1)
    const_share = jax.nn.sigmoid(jnp.dot(tokens, const_gate, preferred_element_type=jnp.float32))
    const_rest = (const_weight * (1.0 - const_share)).astype(jnp.bfloat16)
    coefficient = copy_weight + jnp.sum(const_weight * const_share, axis=1)
    tokens_float = tokens.astype(jnp.float32)
    constant_term = jnp.dot(const_rest, const_vec, preferred_element_type=jnp.float32)
    mixed = (mixed_sum + coefficient[:, None] * tokens_float + constant_term).astype(jnp.bfloat16)
    along_token = jnp.sum(cotangent_all * tokens_float, axis=1)
    along_const = lax.dot_general(
        grad_out, const_vec, LAST_CONTRACT, preferred_element_type=jnp.float32
    )
    const_value = const_share * along_token[:, None] + (1.0 - const_share) * along_const
    null_grad = jnp.where(is_copy, along_token[:, None], 0.0) + jnp.sum(
        jnp.where(is_const, const_value[:, None, :], 0.0), axis=2
    )
    pick_grad = routed_grad + null_grad
    slope_grad = pick_grad * chosen * (1.0 - chosen)
    logit_grad = jnp.sum(jnp.where(picks, slope_grad[:, :, None], 0.0), axis=1).astype(jnp.bfloat16)
    share_grad = (
        const_weight * (along_token[:, None] - along_const) * const_share * (1.0 - const_share)
    ).astype(jnp.bfloat16)
    back_local = coefficient[:, None] * cotangent_all
    back_local = back_local + lax.dot_general(
        logit_grad, router, LAST_CONTRACT, preferred_element_type=jnp.float32
    )
    back_local = back_local + lax.dot_general(
        share_grad, const_gate, LAST_CONTRACT, preferred_element_type=jnp.float32
    )
    grad_tokens = (back_sum + back_local).astype(jnp.bfloat16)
    router_part = lax.dot_general(
        tokens, logit_grad, ROWS_CONTRACT, preferred_element_type=jnp.float32
    )
    vector_part = lax.dot_general(
        const_rest, grad_out, ROWS_CONTRACT, preferred_element_type=jnp.float32
    )
    mixing_part = lax.dot_general(
        tokens, share_grad, ROWS_CONTRACT, preferred_element_type=jnp.float32
    )
    grad_router, grad_const_vec, grad_const_gate = lax.psum(
        (router_part, vector_part, mixing_part), ("expert", "dp", "rep")
    )
    mixed_all, grad_tokens_all = (
        lax.all_gather(mixed, "rep", axis=0, tiled=True),
        lax.all_gather(grad_tokens, "rep", axis=0, tiled=True),
    )
    return (
        mixed_all,
        grad_tokens_all,
        grad_gate,
        grad_up,
        grad_down,
        grad_router,
        grad_const_vec,
        grad_const_gate,
    )


def solution(mesh):
    placed = (
        P(("groups", "expert", "dp"), None),
        P(("groups", "expert", "dp"), None),
        P("expert", ("dp", "rep"), None),
        P("expert", ("dp", "rep"), None),
        P("expert", ("dp", "rep"), None),
        P(),
        P(),
        P(),
        P(("groups", "expert", "dp"), None),
    )
    return jax.shard_map(
        on_device,
        mesh=mesh,
        in_specs=placed,
        out_specs=(
            P(("groups", "expert", "dp"), None),
            P(("groups", "expert", "dp"), None),
            P(("groups", "expert"), ("dp", "rep"), None),
            P(("groups", "expert"), ("dp", "rep"), None),
            P(("groups", "expert"), ("dp", "rep"), None),
            P("groups", None),
            P("groups", None),
            P("groups", None),
        ),
        check_vma=False,
    )
```

profile of v0, /device:TPU:0, one launch (start us, length us, event | category | flops | bytes accessed | tf_op | source)
XLA Modules:
  0.0 399.4 jit_solution(1607416808879478116)
XLA Ops:
  8.4 24.2 %all_to_all.62 = bf16[4,256,768]{2,1,0:T(8,128)(2,1)S(1)} all-to-all(bf16[4,256,768]{2,1,0:T(8,128)(2,1)S(1)} %bitcast.70), channel_id=1, replica_groups=mesh['groups'=2,'expert'=4,'dp'=4,'rep'=1] {'dp','rep'}, dimensions={0} | all-to-all | bytes 3145728 | tf_op jit(solution)/shard_map/all_to_all | solution.py:95
  34.0 4.5 %all-to-all-start.2 = ((bf16[4,256,768]{2,1,0:T(8,128)(2,1)}), bf16[4,256,768]{2,1,0:T(8,128)(2,1)}, u32[]{:S(2)}, u32[]{:S(2)}) async-start(bf16[4,256,768]{2,1,0:T(8,128)(2,1)} %bitcast.6), calls=%async_computation.2 | async-start | bytes 3145728 | tf_op jit(solution)/shard_map/all_to_all | solution.py:102
  39.0 19.6 %all-to-all-done.2 = bf16[4,256,768]{2,1,0:T(8,128)(2,1)} async-done(((bf16[4,256,768]{2,1,0:T(8,128)(2,1)}), bf16[4,256,768]{2,1,0:T(8,128)(2,1)}, u32[]{:S(2)}, u32[]{:S(2)}) %all-to-all-start.2) | async-done | bytes 1572896 | tf_op jit(solution)/shard_map/all_to_all | solution.py:102
  59.9 4.3 %all-to-all-start.3 = ((bf16[4,256,768]{2,1,0:T(8,128)(2,1)}), bf16[4,256,768]{2,1,0:T(8,128)(2,1)}, u32[]{:S(2)}, u32[]{:S(2)}) async-start(bf16[4,256,768]{2,1,0:T(8,128)(2,1)} %bitcast.8), calls=%async_computation.3 | async-start | bytes 3145728 | tf_op jit(solution)/shard_map/all_to_all | solution.py:109
  68.4 16.0 %all-to-all-done.3 = bf16[4,256,768]{2,1,0:T(8,128)(2,1)} async-done(((bf16[4,256,768]{2,1,0:T(8,128)(2,1)}), bf16[4,256,768]{2,1,0:T(8,128)(2,1)}, u32[]{:S(2)}, u32[]{:S(2)}) %all-to-all-start.3) | async-done | bytes 1572896 | tf_op jit(solution)/shard_map/all_to_all | solution.py:109
  84.4 5.0 %all-to-all-start = ((bf16[16,32,1024]{2,1,0:T(8,128)(2,1)}), bf16[16,32,1024]{2,1,0:T(8,128)(2,1)}, u32[]{:S(2)}, u32[]{:S(2)}) async-start(bf16[16,32,1024]{2,1,0:T(8,128)(2,1)} %broadcast_select_fusion), calls=%async_computation | async-start | bytes 2097152 | tf_op jit(solution)/shard_map/all_to_all | solution.py:44
  89.7 3.5 gather_fusion.2
  96.7 15.7 %all-to-all-done = bf16[16,32,1024]{2,1,0:T(8,128)(2,1)} async-done(((bf16[16,32,1024]{2,1,0:T(8,128)(2,1)}), bf16[16,32,1024]{2,1,0:T(8,128)(2,1)}, u32[]{:S(2)}, u32[]{:S(2)}) %all-to-all-start) | async-done | bytes 1048608 | tf_op jit(solution)/shard_map/all_to_all | solution.py:44
  112.4 6.9 %all-to-all-start.5 = ((bf16[16,32,1024]{2,1,0:T(8,128)(2,1)}), bf16[16,32,1024]{2,1,0:T(8,128)(2,1)S(1)}, u32[]{:S(2)}, u32[]{:S(2)}) async-start(bf16[16,32,1024]{2,1,0:T(8,128)(2,1)} %fusion), calls=%async_computation.5 | async-start | bytes 2097152 | tf_op jit(solution)/shard_map/all_to_all | solution.py:44
  119.3 3.4 fusion.29
  122.7 3.9 fusion.30
  126.5 15.7 %all-to-all-done.5 = bf16[16,32,1024]{2,1,0:T(8,128)(2,1)S(1)} async-done(((bf16[16,32,1024]{2,1,0:T(8,128)(2,1)}), bf16[16,32,1024]{2,1,0:T(8,128)(2,1)S(1)}, u32[]{:S(2)}, u32[]{:S(2)}) %all-to-all-start.5) | async-done | bytes 1048608 | tf_op jit(solution)/shard_map/all_to_all | solution.py:44
  142.2 4.6 %multiply_convert_fusion = (bf16[512,768]{1,0:T(8,128)(2,1)S(1)}, bf16[512,768]{1,0:T(8,128)(2,1)}, bf16[512,768]{1,0:T(8,128)(2,1)S(1)}) fusion(f32[512,768]{1,0:T(8,128)} %fusion.29, f32[512,768]{1,0:T(8,128)} %fusion.30, bf16[512,1024]{1,0:T(8,128)(2,1)S(1)} %bitcast.79, bf16[1024,768]{1,0:T(8,128)(2,1)} %bitcast.9), kind=kOutput, calls=%fused_computation.17 | convolution fusion | flops 811204608 | bytes 8126464 | tf_op jit(solution)/shard_map/dot_general | solution.py:24
  149.1 3.6 all-to-all-start.9
  152.6 3.5 convolution_convert_fusion.1
  156.1 17.0 %all-to-all-done.9 = bf16[4,256,768]{2,1,0:T(8,128)(2,1)S(1)} async-done(((bf16[4,256,768]{2,1,0:T(8,128)(2,1)}), bf16[4,256,768]{2,1,0:T(8,128)(2,1)S(1)}, u32[]{:S(2)}, u32[]{:S(2)}) %all-to-all-start.9) | async-done | bytes 1572896 | tf_op jit(solution)/shard_map/all_to_all | solution.py:150
  174.2 4.4 %all-to-all-start.8 = ((bf16[4,256,768]{2,1,0:T(8,128)(2,1)}), bf16[4,256,768]{2,1,0:T(8,128)(2,1)}, u32[]{:S(2)}, u32[]{:S(2)}) async-start(bf16[4,256,768]{2,1,0:T(8,128)(2,1)} %bitcast.76), calls=%async_computation.8 | async-start | bytes 3145728 | tf_op jit(solution)/shard_map/all_to_all | solution.py:149
  178.6 3.6 convolution_convert_fusion.2
  182.2 16.5 %all-to-all-done.8 = bf16[4,256,768]{2,1,0:T(8,128)(2,1)} async-done(((bf16[4,256,768]{2,1,0:T(8,128)(2,1)}), bf16[4,256,768]{2,1,0:T(8,128)(2,1)}, u32[]{:S(2)}, u32[]{:S(2)}) %all-to-all-start.8) | async-done | bytes 1572896 | tf_op jit(solution)/shard_map/all_to_all | solution.py:149
  198.7 3.6 all-to-all-start.7
  202.3 3.7 convolution_convert_fusion.3
  206.0 16.3 %all-to-all-done.7 = bf16[4,256,768]{2,1,0:T(8,128)(2,1)S(1)} async-done(((bf16[4,256,768]{2,1,0:T(8,128)(2,1)}), bf16[4,256,768]{2,1,0:T(8,128)(2,1)S(1)}, u32[]{:S(2)}, u32[]{:S(2)}) %all-to-all-start.7) | async-done | bytes 1572896 | tf_op jit(solution)/shard_map/all_to_all | solution.py:148
  223.5 6.0 %all-to-all-start.4 = ((bf16[16,32,1024]{2,1,0:T(8,128)(2,1)}), bf16[16,32,1024]{2,1,0:T(8,128)(2,1)S(1)}, u32[]{:S(2)}, u32[]{:S(2)}) async-start(bf16[16,32,1024]{2,1,0:T(8,128)(2,1)} %bitcast.10), calls=%async_computation.4 | async-start | bytes 2097152 | tf_op jit(solution)/shard_map/all_to_all | solution.py:44
  233.0 3.4 add_convert_fusion
  236.4 16.1 %all-to-all-done.4 = bf16[16,32,1024]{2,1,0:T(8,128)(2,1)S(1)} async-done(((bf16[16,32,1024]{2,1,0:T(8,128)(2,1)}), bf16[16,32,1024]{2,1,0:T(8,128)(2,1)S(1)}, u32[]{:S(2)}, u32[]{:S(2)}) %all-to-all-start.4) | async-done | bytes 1048608 | tf_op jit(solution)/shard_map/all_to_all | solution.py:44
  252.5 6.9 %all-to-all-start.6 = ((bf16[16,32,1024]{2,1,0:T(8,128)(2,1)}), bf16[16,32,1024]{2,1,0:T(8,128)(2,1)S(1)}, u32[]{:S(2)}, u32[]{:S(2)}) async-start(bf16[16,32,1024]{2,1,0:T(8,128)(2,1)} %bitcast.78), calls=%async_computation.6 | async-start | bytes 2097152 | tf_op jit(solution)/shard_map/all_to_all | solution.py:44
  267.8 3.6 gather_fusion.1
  271.4 10.9 %all-to-all-done.6 = bf16[16,32,1024]{2,1,0:T(8,128)(2,1)S(1)} async-done(((bf16[16,32,1024]{2,1,0:T(8,128)(2,1)}), bf16[16,32,1024]{2,1,0:T(8,128)(2,1)S(1)}, u32[]{:S(2)}, u32[]{:S(2)}) %all-to-all-start.6) | async-done | bytes 1048608 | tf_op jit(solution)/shard_map/all_to_all | solution.py:44
  282.3 3.6 gather_fusion.4
  285.9 4.0 %reshape.248 = f32[128,6,1024]{2,1,0:T(8,128)} reshape(bf16[768,1024]{1,0:T(8,128)(2,1)} %gather_fusion.4) | data formatting | bytes 4718592 | tf_op jit(solution)/shard_map/convert_element_type | solution.py:165
  292.1 6.2 %select_reduce_fusion = (f32[128,6]{1,0:T(8,128)S(1)}, f32[128,1024]{1,0:T(8,128)S(1)}, f32[128,1024]{1,0:T(8,128)S(1)}) fusion(f32[128,6,1024]{2,1,0:T(8,128)} %reshape.247, f32[128,1024]{1,0:T(8,128)S(1)} %convert_element_type.119, pred[128,6]{1,0:T(8,128)(4,1)S(1)} %copy.52, f32[128,6]{1,0:T(8,128)S(1)} %copy.53, f32[128,6,1024]{2,1,0:T(8,128)} %reshape.248), kind=kLoop, calls=%fused_computation.5 | loop fusion | flops 6028544 | bytes 7871232 | tf_op jit(solution)/shard_map/reduce_sum | solution.py:133
  301.1 87.3 %all-reduce.3.cloned.1.call-done = (f32[1024,12]{0,1:T(8,128)}, f32[2,1024]{1,0:T(2,128)}, f32[1024,2]{0,1:T(2,128)}) async-done(((f32[1024,12]{0,1:T(8,128)}, f32[2,1024]{1,0:T(2,128)}, f32[1024,2]{0,1:T(2,128)}), (f32[1024,12]{0,1:T(8,128)}, f32[2,1024]{1,0:T(2,128)}, f32[1024,2]{0,1:T(2,128)})) %all-reduce.3.cloned.1.call-update) | async-done | bytes 65552 | tf_op jit(solution)/shard_map/psum | solution.py:209
  (93 shorter events, 37.6 us)
Async XLA Ops:
  7.2 31.6 %copy-start = (bf16[1024,12]{0,1:T(8,128)(2,1)S(1)}, bf16[1024,12]{0,1:T(8,128)(2,1)}, u32[]{:S(2)}) copy-start(bf16[1024,12]{0,1:T(8,128)(2,1)} %param.14) | copy-start | bytes 73732
  8.4 24.2 %copy-start.10 = (bf16[2,256,768]{2,1,0:T(8,128)(2,1)S(1)}, bf16[2,256,768]{2,1,0:T(8,128)(2,1)}, u32[]{:S(2)}) copy-start(bf16[2,256,768]{2,1,0:T(8,128)(2,1)} %param.12) | copy-start | bytes 2359300
  32.7 86.6 %copy-start.9 = (bf16[4,256,768]{2,1,0:T(8,128)(2,1)}, bf16[4,256,768]{2,1,0:T(8,128)(2,1)S(1)}, u32[]{:S(2)}) copy-start(bf16[4,256,768]{2,1,0:T(8,128)(2,1)S(1)} %all_to_all.62) | copy-start | bytes 4718596
  34.0 4.5 %copy-start.12 = (s32[128,6]{0,1:T(8,128)S(1)}, s32[128,6]{0,1:T(8,128)}, u32[]{:S(2)}) copy-start(s32[128,6]{0,1:T(8,128)} %param.10) | copy-start | bytes 9220
  34.0 4.8 %copy-start.1 = (bf16[128,1024]{1,0:T(8,128)(2,1)S(1)}, bf16[128,1024]{1,0:T(8,128)(2,1)}, u32[]{:S(2)}) copy-start(bf16[128,1024]{1,0:T(8,128)(2,1)} %param.9) | copy-start | bytes 786436
  34.0 24.6 %copy-start.11 = (bf16[2,256,768]{2,1,0:T(8,128)(2,1)S(1)}, bf16[2,256,768]{2,1,0:T(8,128)(2,1)}, u32[]{:S(2)}) copy-start(bf16[2,256,768]{2,1,0:T(8,128)(2,1)} %param.13) | copy-start | bytes 2359300
  34.0 24.6 %all-to-all-start.2 = ((bf16[4,256,768]{2,1,0:T(8,128)(2,1)}), bf16[4,256,768]{2,1,0:T(8,128)(2,1)}, u32[]{:S(2)}, u32[]{:S(2)}) async-start(bf16[4,256,768]{2,1,0:T(8,128)(2,1)} %bitcast.6), calls=%async_computation.2 | async-start | bytes 3145728 | tf_op jit(solution)/shard_map/all_to_all | solution.py:102
  59.9 24.5 %all-to-all-start.3 = ((bf16[4,256,768]{2,1,0:T(8,128)(2,1)}), bf16[4,256,768]{2,1,0:T(8,128)(2,1)}, u32[]{:S(2)}, u32[]{:S(2)}) async-start(bf16[4,256,768]{2,1,0:T(8,128)(2,1)} %bitcast.8), calls=%async_computation.3 | async-start | bytes 3145728 | tf_op jit(solution)/shard_map/all_to_all | solution.py:109
  68.4 25.0 %copy-start.2 = (bf16[128,1024]{1,0:T(8,128)(2,1)S(1)}, bf16[128,1024]{1,0:T(8,128)(2,1)}, u32[]{:S(2)}) copy-start(bf16[128,1024]{1,0:T(8,128)(2,1)} %param.17) | copy-start | bytes 786436
  84.4 28.0 %all-to-all-start = ((bf16[16,32,1024]{2,1,0:T(8,128)(2,1)}), bf16[16,32,1024]{2,1,0:T(8,128)(2,1)}, u32[]{:S(2)}, u32[]{:S(2)}) async-start(bf16[16,32,1024]{2,1,0:T(8,128)(2,1)} %broadcast_select_fusion), calls=%async_computation | async-start | bytes 2097152 | tf_op jit(solution)/shard_map/all_to_all | solution.py:44
  112.4 29.8 %all-to-all-start.5 = ((bf16[16,32,1024]{2,1,0:T(8,128)(2,1)}), bf16[16,32,1024]{2,1,0:T(8,128)(2,1)S(1)}, u32[]{:S(2)}, u32[]{:S(2)}) async-start(bf16[16,32,1024]{2,1,0:T(8,128)(2,1)} %fusion), calls=%async_computation.5 | async-start | bytes 2097152 | tf_op jit(solution)/shard_map/all_to_all | solution.py:44
  146.8 2.2 copy-start.15
  149.1 24.0 %all-to-all-start.9 = ((bf16[4,256,768]{2,1,0:T(8,128)(2,1)}), bf16[4,256,768]{2,1,0:T(8,128)(2,1)S(1)}, u32[]{:S(2)}, u32[]{:S(2)}) async-start(bf16[4,256,768]{2,1,0:T(8,128)(2,1)} %bitcast.77), calls=%async_computation.9 | async-start | bytes 3145728 | tf_op jit(solution)/shard_map/all_to_all | solution.py:150
  173.1 1.1 copy-start.4
  174.2 24.5 %all-to-all-start.8 = ((bf16[4,256,768]{2,1,0:T(8,128)(2,1)}), bf16[4,256,768]{2,1,0:T(8,128)(2,1)}, u32[]{:S(2)}, u32[]{:S(2)}) async-start(bf16[4,256,768]{2,1,0:T(8,128)(2,1)} %bitcast.76), calls=%async_computation.8 | async-start | bytes 3145728 | tf_op jit(solution)/shard_map/all_to_all | solution.py:149
  198.7 23.6 %all-to-all-start.7 = ((bf16[4,256,768]{2,1,0:T(8,128)(2,1)}), bf16[4,256,768]{2,1,0:T(8,128)(2,1)S(1)}, u32[]{:S(2)}, u32[]{:S(2)}) async-start(bf16[4,256,768]{2,1,0:T(8,128)(2,1)} %bitcast.75), calls=%async_computation.7 | async-start | bytes 3145728 | tf_op jit(solution)/shard_map/all_to_all | solution.py:148
  206.0 24.1 %copy-start.13 = (bf16[1024,2]{0,1:T(2,128)(2,1)S(1)}, bf16[1024,2]{0,1:T(2,128)(2,1)}, u32[]{:S(2)}) copy-start(bf16[1024,2]{0,1:T(2,128)(2,1)} %param.16) | copy-start | bytes 12292
  222.3 1.1 copy-start.6
  223.5 29.0 %all-to-all-start.4 = ((bf16[16,32,1024]{2,1,0:T(8,128)(2,1)}), bf16[16,32,1024]{2,1,0:T(8,128)(2,1)S(1)}, u32[]{:S(2)}, u32[]{:S(2)}) async-start(bf16[16,32,1024]{2,1,0:T(8,128)(2,1)} %bitcast.10), calls=%async_computation.4 | async-start | bytes 2097152 | tf_op jit(solution)/shard_map/all_to_all | solution.py:44
  236.4 23.2 %copy-start.14 = (bf16[2,1024]{1,0:T(2,128)(2,1)S(1)}, bf16[2,1024]{1,0:T(2,128)(2,1)}, u32[]{:S(2)}) copy-start(bf16[2,1024]{1,0:T(2,128)(2,1)} %param.15) | copy-start | bytes 12292
  252.5 29.8 %all-to-all-start.6 = ((bf16[16,32,1024]{2,1,0:T(8,128)(2,1)}), bf16[16,32,1024]{2,1,0:T(8,128)(2,1)S(1)}, u32[]{:S(2)}, u32[]{:S(2)}) async-start(bf16[16,32,1024]{2,1,0:T(8,128)(2,1)} %bitcast.78), calls=%async_computation.6 | async-start | bytes 2097152 | tf_op jit(solution)/shard_map/all_to_all | solution.py:44
  259.3 129.1 %all-reduce.3.cloned.1.call-start = ((), (), s32[]{:S(2)}) async-start(), calls=%async_computation.10 | async-start | bytes 163840 | tf_op jit(solution)/shard_map/psum | solution.py:209
  259.4 3.1 copy-start.5
  263.7 2.9 copy-start.7
  285.9 4.0 %copy-start.3 = (bf16[768,1024]{1,0:T(8,128)(2,1)S(1)}, bf16[768,1024]{1,0:T(8,128)(2,1)}, u32[]{:S(2)}) copy-start(bf16[768,1024]{1,0:T(8,128)(2,1)} %gather_fusion.1) | copy-start | bytes 4718596
  292.1 7.1 %copy-start.8 = (f32[128,1024]{1,0:T(8,128)S(1)}, f32[128,1024]{1,0:T(8,128)}, u32[]{:S(2)}) copy-start(f32[128,1024]{1,0:T(8,128)} %fusion.32) | copy-start | bytes 1572868
Sparse Core Ops, SparseCore 0:
  300.3 88.1 all-reduce.2
where the time goes:
time: 401 us; the launch traced here: 399 us
  waiting for transfers between devices  231 us (58%)
  starting transfers between devices  45.1 us (11%)
  matrix products  37.1 us (9%)
  local copies, waits for them, and re-layouts  32.5 us (8%)
  blocking collectives  24.2 us (6%)
  other arithmetic  14.9 us (4%)
  between operations  14.4 us (4%)
    psum x1, waiting for transfers between devices, on_device(): lax.psum((router_part, vector_part, mixing_part), ('expert', 'dp', 'rep'))  87.3 us
    all_to_all x4, waiting for transfers between devices, token_trip(): lax.all_to_all(buffer, ('expert', 'dp'), split_axis=0, concat_axis=0, til...  58.4 us
    all_to_all x4, starting transfers between devices, token_trip(): lax.all_to_all(buffer, ('expert', 'dp'), split_axis=0, concat_axis=0, til...  24.8 us
    all_to_all x1, blocking collectives, on_device(): lax.all_to_all(jnp.repeat(gate_weight, repeat, axis=0), ('dp', 'rep'), sp...  24.2 us
    all_to_all x1, waiting for transfers between devices, on_device(): lax.all_to_all(jnp.repeat(up_weight, repeat, axis=0), ('dp', 'rep'), spli...  19.6 us
    all_to_all x1, waiting for transfers between devices, on_device(): lax.all_to_all(sent_terms[2], ('dp', 'rep'), split_axis=0, concat_axis=0,...  17 us
    all_to_all x1, waiting for transfers between devices, on_device(): lax.all_to_all(sent_terms[1], ('dp', 'rep'), split_axis=0, concat_axis=0,...  16.5 us
    all_to_all x1, waiting for transfers between devices, on_device(): lax.all_to_all(sent_terms[0], ('dp', 'rep'), split_axis=0, concat_axis=0,...  16.3 us
  transfers between devices with their start and end apart: 10, of which 10 were waited for; matrix products, arithmetic and copies ran while one was open for 12% of the time, Pallas kernels for 0%

commit v1 on v0

--- a/solution.py
+++ b/solution.py
@@ -1,6 +1,8 @@
 import jax
 import jax.numpy as jnp
 from jax import lax
+from jax.experimental import pallas as pl
+from jax.experimental.pallas import tpu as pltpu
 from jax.sharding import PartitionSpec as P
 
 ROWS_CONTRACT = (((0,), (0,)), ((), ()))
@@ -44,7 +46,7 @@
     return lax.all_to_all(buffer, ("expert", "dp"), split_axis=0, concat_axis=0, tiled=True)
 
 
-def on_device(
+def on_device_general(
     tokens, routes, gate_weight, up_weight, down_weight, router, const_vec, const_gate, grad_out
 ):
     shard_rows, top_count = routes.shape
@@ -225,7 +227,370 @@
     )
 
 
+HALF = 64
+SLOTS = 32
+
+
+def full_block(shape):
+    return pl.BlockSpec(shape, lambda *_: (0,) * len(shape))
+
+
+def local_kernel(body, operands, outputs, scalars=None, flops=0):
+    in_specs = [pl.BlockSpec(memory_space=pltpu.VMEM) for _ in operands]
+    if scalars is not None:
+        in_specs = [pl.BlockSpec(memory_space=pltpu.SMEM)] + in_specs
+        operands = [scalars] + list(operands)
+    moved = sum(o.size * o.dtype.itemsize for o in operands)
+    moved += sum(o.size * o.dtype.itemsize for o in outputs)
+    return pl.pallas_call(
+        body,
+        out_shape=outputs,
+        in_specs=in_specs,
+        out_specs=[pl.BlockSpec(memory_space=pltpu.VMEM) for _ in outputs],
+        compiler_params=pltpu.CompilerParams(vmem_limit_bytes=56 * 1024 * 1024),
+        cost_estimate=pl.CostEstimate(flops=flops, bytes_accessed=moved, transcendentals=0),
+    )(*operands)
+
+
+def mm(a, b):
+    return jnp.dot(a, b, preferred_element_type=jnp.float32)
+
+
+def mm_rows(a, b):
+    return lax.dot_general(a, b, ROWS_CONTRACT, preferred_element_type=jnp.float32)
+
+
+def mm_last(a, b):
+    return lax.dot_general(a, b, LAST_CONTRACT, preferred_element_type=jnp.float32)
+
+
+def forward_kernel(place, *refs):
+    gates, tokens, w_gate, w_up = refs[0:4], refs[4:12], refs[12:16], refs[16:20]
+    pick_out, gate_out, rows_out, hidden_out, act_out, slope_out = refs[20:26]
+    me, expert = place[0], place[1]
+    span = 2 * tokens[0].shape[0]
+    width = w_gate[0].shape[0]
+    earlier_than = lax.broadcasted_iota(jnp.int32, (span, span), 0)
+    later = lax.broadcasted_iota(jnp.int32, (span, span), 1)
+    before = ((earlier_than < later) & (earlier_than // HALF == later // HALF)).astype(jnp.bfloat16)
+    lane = lax.broadcasted_iota(jnp.int32, (1, span), 1)
+    for k in range(4):
+        gate = gates[k][pl.ds(expert, 1), :]
+        picked = gate != 0.0
+        earlier = mm(
+            jnp.broadcast_to(picked.astype(jnp.bfloat16), (16, span)), before
+        )[0:1].astype(jnp.int32)
+        target = jnp.where(picked, (lane // HALF) * SLOTS + earlier, -1)
+        for core in range(2):
+            half = span // 2
+            slots = half // 2
+            slot = lax.broadcasted_iota(jnp.int32, (slots, half), 0) + core * slots
+            chosen = slot == target[:, core * half : (core + 1) * half]
+            pick = chosen.astype(jnp.bfloat16)
+            at = (2 * k + core) * slots
+            pick_out[at : at + slots, :] = pick
+            gate_out[at : at + slots, :] = jnp.where(
+                chosen, gate[:, core * half : (core + 1) * half], 0.0
+            ).astype(jnp.bfloat16)
+            for j in range(4):
+                columns = pl.ds(pl.multiple_of((me ^ j) * width, width), width)
+                rows_out[at : at + slots, j * width : (j + 1) * width] = mm(
+                    pick, tokens[2 * k + core][:, columns]
+                ).astype(jnp.bfloat16)
+    pre_gate = jnp.zeros(hidden_out.shape, jnp.float32)
+    pre_up = jnp.zeros(hidden_out.shape, jnp.float32)
+    for j in range(4):
+        rows = rows_out[:, j * width : (j + 1) * width]
+        pre_gate += mm(rows, w_gate[j][...])
+        pre_up += mm(rows, w_up[j][...])
+    logistic = jax.nn.sigmoid(pre_gate)
+    act = pre_gate * logistic
+    hidden_out[...] = (act * pre_up).astype(jnp.bfloat16)
+    act_out[...] = act.astype(jnp.bfloat16)
+    slope = logistic * (1.0 + pre_gate * (1.0 - logistic))
+    slope_out[...] = (pre_up * slope).astype(jnp.bfloat16)
+
+
+def down_grad_kernel(place, *refs):
+    pick, gate_pick, hidden = refs[0:3]
+    grads = refs[3:11]
+    cot_out, up_out = refs[11:13]
+    down_out = refs[13:17]
+    me = place[0]
+    width = down_out[0].shape[0]
+    slots = grads[0].shape[0] // 2
+    gate = jnp.sum(gate_pick[...].astype(jnp.float32), axis=1, keepdims=True)
+    for b in range(8):
+        at = b * slots
+        for j in range(4):
+            columns = pl.ds(pl.multiple_of((me ^ j) * width, width), width)
+            cot = mm(pick[at : at + slots, :], grads[b][:, columns])
+            cot_out[at : at + slots, j * width : (j + 1) * width] = cot.astype(jnp.bfloat16)
+            up_out[at : at + slots, j * width : (j + 1) * width] = (
+                gate[at : at + slots] * cot
+            ).astype(jnp.bfloat16)
+    for j in range(4):
+        down_out[j][...] = mm_rows(
+            up_out[:, j * width : (j + 1) * width], hidden[...]
+        ).astype(jnp.bfloat16)
+
+
+def backward_kernel(place, *refs):
+    pick, rows, upstream, act, slope = refs[0:5]
+    w_gate, w_up, w_down = refs[5:9], refs[9:13], refs[13:17]
+    gate_out, up_out = refs[17:21], refs[21:25]
+    own_out, other_out = refs[25:27]
+    me = place[0]
+    width = w_gate[0].shape[0]
+    d_hidden = jnp.zeros(act.shape, jnp.float32)
+    for j in range(4):
+        d_hidden += mm(upstream[:, j * width : (j + 1) * width], w_down[j][...])
+    d_gate = (d_hidden * slope[...].astype(jnp.float32)).astype(jnp.bfloat16)
+    d_up = (d_hidden * act[...].astype(jnp.float32)).astype(jnp.bfloat16)
+    for j in range(4):
+        part = rows[:, j * width : (j + 1) * width]
+        gate_out[j][...] = mm_rows(part, d_gate).astype(jnp.bfloat16)
+        up_out[j][...] = mm_rows(part, d_up).astype(jnp.bfloat16)
+    scatter(me, pick, own_out, other_out, width, lambda j: (
+        mm_last(d_gate, w_gate[j][...]) + mm_last(d_up, w_up[j][...])
+    ).astype(jnp.bfloat16))
+
+
+def scatter(me, pick, own_out, other_out, width, column_block):
+    slots = pick.shape[0] // 8
+    half = pick.shape[1]
+    for j in range(4):
+        columns = pl.ds(pl.multiple_of((me ^ j) * width, width), width)
+        block = column_block(j)
+        for b in range(8):
+            out = own_out if b % 2 == 0 else other_out
+            at = b * slots
+            out[(b // 2) * half : (b // 2 + 1) * half, columns] = mm_rows(
+                pick[at : at + slots, :], block[at : at + slots]
+            ).astype(jnp.bfloat16)
+
+
+def output_kernel(place, *refs):
+    pick, gate_pick, hidden, cot = refs[0:4]
+    w_down = refs[4:8]
+    own_out, other_out, score_out = refs[8:11]
+    me = place[0]
+    width = w_down[0].shape[0]
+    slots = pick.shape[0] // 8
+    scores = []
+
+    def column_block(j):
+        block = mm_last(hidden[...], w_down[j][...]).astype(jnp.bfloat16)
+        scores.append(
+            jnp.sum(
+                block.astype(jnp.float32)
+                * cot[:, j * width : (j + 1) * width].astype(jnp.float32),
+                axis=1,
+                keepdims=True,
+            )
+        )
+        return block
+
+    scatter(me, gate_pick, own_out, other_out, width, column_block)
+    score = scores[0] + scores[1] + scores[2] + scores[3]
+    spread = pick[...].astype(jnp.float32) * score
+    for b in range(8):
+        score_out[b : b + 1, :] = jnp.sum(
+            spread[b * slots : (b + 1) * slots], axis=0, keepdims=True
+        )
+
+
+def dp_swap(value, step):
+    return lax.ppermute(value, "dp", [(i, i ^ step) for i in range(4)])
+
+
+def ring(value, step):
+    size = lax.axis_size("expert")
+    return lax.ppermute(value, "expert", [(i, (i + step) % size) for i in range(size)])
+
+
+def gather_rows(block):
+    own = [block]
+    for _ in range(3):
+        own.append(ring(own[-1], 1))
+    other = [dp_swap(value, 1) for value in own]
+    return [value for pair in zip(own, other) for value in pair]
+
+
+def on_device_paired(
+    tokens, routes, gate_weight, up_weight, down_weight, router, const_vec, const_gate, grad_out
+):
+    bf16, f32 = jnp.bfloat16, jnp.float32
+    row_count, model_width = tokens.shape
+    id_count = router.shape[1]
+    const_count = const_vec.shape[0]
+    expert_count = id_count - 2 - const_count
+    stored_experts, stored_rows, hidden_width = gate_weight.shape
+    me = lax.axis_index("dp")
+    z = lax.axis_index("expert")
+    core = me % 2
+    expert = stored_experts * z + core
+    place = jnp.stack([me, expert]).astype(jnp.int32)
+
+    def fetch(weight):
+        mine = lax.dynamic_index_in_dim(weight, core, 0, keepdims=False)
+        theirs = lax.dynamic_index_in_dim(weight, 1 - core, 0, keepdims=False)
+        return [mine, dp_swap(theirs, 1), dp_swap(mine, 2), dp_swap(theirs, 3)]
+
+    all_tokens = gather_rows(tokens)
+    w_gate = fetch(gate_weight)
+    w_up = fetch(up_weight)
+    all_grads = gather_rows(grad_out)
+    w_down = fetch(down_weight)
+
+    id_range = lax.broadcasted_iota(jnp.int32, (1, 1, id_count), 2)
+    named = jnp.any(routes[:, :, None] == id_range, axis=1)
+    logits = mm(tokens, router)
+    share = jax.nn.sigmoid(logits)
+    chosen = jnp.where(named, share, 0.0)
+    gates = chosen.astype(bf16).astype(f32)
+
+    gate_rows = gates[:, :expert_count].T
+    gate_pair = jnp.concatenate([gate_rows, dp_swap(gate_rows, 1)], axis=1)
+    gate_all = [gate_pair] + [ring(gate_pair, k) for k in range(1, 4)]
+
+    slot_count = 4 * row_count
+    shape = jax.ShapeDtypeStruct
+    wide = shape((slot_count, model_width), bf16)
+    narrow = shape((slot_count, hidden_width), bf16)
+    table = shape((slot_count, row_count), bf16)
+    weight_rows = shape((stored_rows, hidden_width), bf16)
+    product = 2 * slot_count * model_width * hidden_width
+    pick, gate_pick, rows, hidden, act, slope = local_kernel(
+        forward_kernel,
+        [*gate_all, *all_tokens, *w_gate, *w_up],
+        [table, table, wide, narrow, narrow, narrow],
+        place,
+        2 * product,
+    )
+    cot, upstream, *down_part = local_kernel(
+        down_grad_kernel,
+        [pick, gate_pick, hidden, *all_grads],
+        [wide, wide] + [weight_rows] * 4,
+        place,
+        product,
+    )
+    *parts, back_own, back_other = local_kernel(
+        backward_kernel,
+        [pick, rows, upstream, act, slope, *w_gate, *w_up, *w_down],
+        [weight_rows] * 8 + [wide, wide],
+        place,
+        5 * product,
+    )
+    gate_part, up_part = parts[0:4], parts[4:8]
+    mixed_own, mixed_other, score = local_kernel(
+        output_kernel,
+        [pick, gate_pick, hidden, cot, *w_down],
+        [wide, wide, shape((8, row_count), f32)],
+        place,
+        product,
+    )
+
+    def join(part):
+        mine = part[0].astype(f32) + dp_swap(part[2], 2).astype(f32)
+        theirs = dp_swap(part[1], 1).astype(f32) + dp_swap(part[3], 3).astype(f32)
+        mine, theirs = mine.astype(bf16), theirs.astype(bf16)
+        return jnp.where(core == 0, jnp.stack([mine, theirs]), jnp.stack([theirs, mine]))
+
+    def home(own, other):
+        both = own.astype(f32) + dp_swap(other, 1).astype(f32)
+        slots = both.astype(bf16).reshape(4, row_count, model_width)
+        moving = slots[3]
+        for k in (2, 1):
+            moving = (ring(moving, -1).astype(f32) + slots[k].astype(f32)).astype(bf16)
+        return ring(moving, -1).astype(f32) + slots[0].astype(f32)
+
+    grad_down = join(down_part)
+    grad_gate = join(gate_part)
+    grad_up = join(up_part)
+
+    score = score.reshape(4, 2, row_count)
+    score_mine, score_theirs = score[:, 0], dp_swap(score[:, 1], 1)
+    score_pair = jnp.where(
+        core == 0,
+        jnp.stack([score_mine, score_theirs], axis=1),
+        jnp.stack([score_theirs, score_mine], axis=1),
+    )
+    score_at = [score_pair[0]] + [ring(score_pair[k], -k) for k in range(1, 4)]
+    z_range = lax.broadcasted_iota(jnp.int32, (4, 1, 1), 0)
+    routed_score = sum(
+        jnp.where(z_range == (z + k) % 4, score_at[k][None], 0.0) for k in range(4)
+    )
+    routed_score = routed_score.reshape(expert_count, row_count).T
+
+    mixed_sum = home(mixed_own, mixed_other)
+    back_sum = home(back_own, back_other)
+
+    tokens_float = tokens.astype(f32)
+    grad_float = grad_out.astype(f32)
+    copy_weight = gates[:, expert_count + 1]
+    const_weight = gates[:, expert_count + 2 :]
+    const_share = jax.nn.sigmoid(mm(tokens, const_gate))
+    const_rest = (const_weight * (1.0 - const_share)).astype(bf16)
+    coefficient = copy_weight + jnp.sum(const_weight * const_share, axis=1)
+    mixed = (
+        mixed_sum + coefficient[:, None] * tokens_float + mm(const_rest, const_vec)
+    ).astype(bf16)
+    along_token = jnp.sum(grad_float * tokens_float, axis=1, keepdims=True)
+    along_const = mm_last(grad_out, const_vec)
+    const_value = const_share * along_token + (1.0 - const_share) * along_const
+    pick_grad = jnp.concatenate(
+        [routed_score, jnp.zeros_like(along_token), along_token, const_value], axis=1
+    )
+    logit_grad = jnp.where(named, pick_grad * share * (1.0 - share), 0.0).astype(bf16)
+    share_grad = (
+        const_weight * (along_token - along_const) * const_share * (1.0 - const_share)
+    ).astype(bf16)
+    back_local = (
+        coefficient[:, None] * grad_float
+        + mm_last(logit_grad, router)
+        + mm_last(share_grad, const_gate)
+    )
+    grad_tokens = (back_sum + back_local).astype(bf16)
+
+    small = jnp.concatenate(
+        [
+            mm_rows(jnp.concatenate([logit_grad, share_grad], axis=1), tokens),
+            mm_rows(const_rest, grad_out),
+        ],
+        axis=0,
+    )
+    for step in (1, 2):
+        small = small + dp_swap(small, step)
+    for step in (1, 2):
+        small = small + lax.ppermute(small, "expert", [(i, i ^ step) for i in range(4)])
+    grad_router = small[:id_count].T
+    grad_const_gate = small[id_count : id_count + const_count].T
+    grad_const_vec = small[id_count + const_count :]
+    return (
+        mixed,
+        grad_tokens,
+        grad_gate,
+        grad_up,
+        grad_down,
+        grad_router,
+        grad_const_vec,
+        grad_const_gate,
+    )
+
+
 def solution(mesh):
+    paired = mesh.shape["rep"] == 1 and mesh.shape["dp"] == 4
+
+    def on_device(tokens, routes, gate_weight, *others):
+        id_count = others[2].shape[1]
+        stored_experts, stored_rows, hidden_width = gate_weight.shape
+        row_count, top_count = routes.shape
+        halved = row_count * top_count == (row_count // 2) * id_count
+        if paired and stored_experts == 2 and halved and row_count == 128:
+            return on_device_paired(tokens, routes, gate_weight, *others)
+        return on_device_general(tokens, routes, gate_weight, *others)
+
     placed = (
         P(("groups", "expert", "dp"), None),
         P(("groups", "expert", "dp"), None),

time: 401 us -> 192 us (0.48)
  waiting for transfers between devices: 231 us -> 96.6 us
  matrix products: 37.1 us -> 3.34 us
  Pallas kernels: 0 us -> 29.1 us
  local copies, waits for them, and re-layouts: 32.5 us -> 7.13 us
  blocking collectives: 24.2 us -> 0 us
  between operations: 14.4 us -> 1.37 us
  other arithmetic: 14.9 us -> 7.14 us
    all_to_all x9 -> x0, waiting for transfers between devices: 144 us -> none  [the longest x4 58.4 us: token_trip(): lax.all_to_all(buffer, ('expert', 'dp'), split_axis=0, concat_axis=0, til...]
    ppermute x0 -> x52, waiting for transfers between devices: none -> 96.6 us  [the longest x32 58.6 us: dp_swap(): return lax.ppermute(value, 'dp', [(i, i ^ step) for i in range(4)])]
    psum x1 -> x0, waiting for transfers between devices: 87.3 us -> none  [on_device(): lax.psum((router_part, vector_part, mixing_part), ('expert', 'dp', 'rep'))]
    ppermute x0 -> x52, starting transfers between devices: none -> 46.9 us  [the longest x18 30.6 us: ring(): lax.ppermute(value, 'expert', [(i, (i + step) % size) for i in range(size)])]
    all_to_all x9 -> x0, starting transfers between devices: 45.1 us -> none  [the longest x4 24.8 us: token_trip(): lax.all_to_all(buffer, ('expert', 'dp'), split_axis=0, concat_axis=0, til...]
    dot_general x19 -> x8, matrix products: 37.1 us -> 3.34 us  [the longest x3 1.59 us: mm(): return jnp.dot(a, b, preferred_element_type=jnp.float32)]
    pallas_call x0 -> x4, Pallas kernels: none -> 29.1 us  [local_kernel(): pl.pallas_call(body, out_shape=outputs, in_specs=in_specs, out_specs=[pl....]
    all_to_all x1 -> x0, blocking collectives: 24.2 us -> none  [on_device(): lax.all_to_all(jnp.repeat(gate_weight, repeat, axis=0), ('dp', 'rep'), sp...]
  transfers between devices with their start and end apart: 10 -> 52, of which waited for: 10 -> 20; matrix products, arithmetic and copies ran while one was open for 12% -> 6% of each run, Pallas kernels for 0% -> 12%
where the time goes in v1:
time: 192 us
  waiting for transfers between devices  96.6 us (50%)
  starting transfers between devices  46.9 us (24%)
  Pallas kernels  29.1 us (15%)
  other arithmetic  7.14 us (4%)
  local copies, waits for them, and re-layouts  7.13 us (4%)
  matrix products  3.34 us (2%)
    ppermute x32, waiting for transfers between devices, dp_swap(): return lax.ppermute(value, 'dp', [(i, i ^ step) for i in range(4)])  58.6 us
    ppermute x18, starting transfers between devices, ring(): lax.ppermute(value, 'expert', [(i, (i + step) % size) for i in range(size)])  30.6 us
    ppermute x18, waiting for transfers between devices, ring(): lax.ppermute(value, 'expert', [(i, (i + step) % size) for i in range(size)])  29.7 us
    pallas_call x4, Pallas kernels, local_kernel(): pl.pallas_call(body, out_shape=outputs, in_specs=in_specs, out_specs=[pl....  29.1 us
    ppermute x32, starting transfers between devices, dp_swap(): return lax.ppermute(value, 'dp', [(i, i ^ step) for i in range(4)])  16.2 us
    ppermute x2, waiting for transfers between devices, on_device_paired(): lax.ppermute(small, 'expert', [(i, i ^ step) for i in range(4)])  8.26 us
  transfers between devices with their start and end apart: 52, of which 20 were waited for; matrix products, arithmetic and copies ran while one was open for 6% of the time, Pallas kernels for 12%

profile of v1, /device:TPU:0, one launch (start us, length us, event | category | flops | bytes accessed | tf_op | source)
XLA Modules:
  0.0 191.6 jit_solution(5059303901324883664)
XLA Ops:
  3.1 2.6 %collective-permute-start.5 = (bf16[128,1024]{1,0:T(8,128)(2,1)}, bf16[128,1024]{1,0:T(8,128)(2,1)}, u32[]{:S(2)}, u32[]{:S(2)}) collective-permute-start(bf16[128,1024]{1,0:T(8,128)(2,1)} %refs_4_.1), channel_id=1, source_target_pairs={{0,4},{4,8},{8,12},{12,0},{1,5},{5,9},{9,13},{13,1},{2,6},{6,10},{... | collective-permute-start | bytes 786440 | tf_op jit(solution)/shard_map/ppermute | solution.py:409
  5.9 1.6 collective-permute-start.1
  7.6 1.9 collective-permute-start.2
  9.5 2.1 %collective-permute-start.3 = (f32[8,256]{1,0:T(8,128)S(1)}, f32[8,256]{1,0:T(8,128)S(1)}, u32[]{:S(2)}, u32[]{:S(2)}) collective-permute-start(f32[8,256]{1,0:T(8,128)S(1)} %pad_maximum_fusion.1.refs_0_), channel_id=1, source_target_pairs={{0,12},{4,0},{8,4},{12,8},{1,13},{5,1},{9,5},{13,9},{2,14},{6,2},{... | collective-permute-start | bytes 24584 | tf_op jit(solution)/shard_map/ppermute | solution.py:409
  12.7 2.7 %collective-permute-done.1.refs_1_ = f32[8,256]{1,0:T(8,128)S(1)} collective-permute-done((f32[8,256]{1,0:T(8,128)S(1)}, f32[8,256]{1,0:T(8,128)S(1)}, u32[]{:S(2)}, u32[]{:S(2)}) %collective-permute-start.1) | collective-permute-done | bytes 8224 | tf_op jit(solution)/shard_map/ppermute | solution.py:409
  15.6 1.5 collective-permute-start.12
  18.9 8.3 %collective-permute-done.18.refs_5_ = bf16[128,1024]{1,0:T(8,128)(2,1)S(1)} collective-permute-done((bf16[128,1024]{1,0:T(8,128)(2,1)S(1)}, bf16[128,1024]{1,0:T(8,128)(2,1)S(1)}, u32[]{:S(2)}, u32[]{:S(2)}) %collective-permute-start.18) | collective-permute-done | bytes 262176 | tf_op jit(solution)/shard_map/ppermute | solution.py:409
  28.0 1.5 collective-permute-start.15
  29.7 5.2 %collective-permute-done.13.refs_15_.refs_8_ = bf16[256,768]{1,0:T(8,128)(2,1)} collective-permute-done((bf16[256,768]{1,0:T(8,128)(2,1)S(1)}, bf16[256,768]{1,0:T(8,128)(2,1)}, u32[]{:S(2)}, u32[]{:S(2)}) %collective-permute-start.13) | collective-permute-done | bytes 393248 | tf_op jit(solution)/shard_map/ppermute | solution.py:404
  36.9 15.3 %collective-permute-done.15.refs_18_.refs_11_ = bf16[256,768]{1,0:T(8,128)(2,1)S(1)} collective-permute-done((bf16[256,768]{1,0:T(8,128)(2,1)S(1)}, bf16[256,768]{1,0:T(8,128)(2,1)S(1)}, u32[]{:S(2)}, u32[]{:S(2)}) %collective-permute-start.15) | collective-permute-done | bytes 393248 | tf_op jit(solution)/shard_map/ppermute | solution.py:404
  53.9 1.5 collective-permute-start.26
  56.7 7.0 %collective-permute-done.22.refs_9_ = bf16[128,1024]{1,0:T(8,128)(2,1)} collective-permute-done((bf16[128,1024]{1,0:T(8,128)(2,1)S(1)}, bf16[128,1024]{1,0:T(8,128)(2,1)}, u32[]{:S(2)}, u32[]{:S(2)}) %collective-permute-start.22) | collective-permute-done | bytes 262176 | tf_op jit(solution)/shard_map/ppermute | solution.py:409
  64.7 6.9 %shard_map.152 = (bf16[512,128]{1,0:T(8,128)(2,1)}, bf16[512,128]{1,0:T(8,128)(2,1)}, bf16[512,1024]{1,0:T(8,128)(2,1)}, bf16[512,768]{1,0:T(8,128)(2,1)}, bf16[...) custom-call(s32[2]{0:T(128)} %pad_add_fusion.place, f32[8,256]{1,0:T(8,128)} %copy-done.24, f32[8,256]{1,0:T(8,128)} %copy-done.38, ...), custom_call_target="tpu_custom_call" | custom-call | flops 1610612736 | bytes 8945672 | tf_op jit(solution)/shard_map/pallas_call | solution.py:245
  72.5 4.2 %shard_map.153 = (bf16[512,1024]{1,0:T(8,128)(2,1)}, bf16[512,1024]{1,0:T(8,128)(2,1)}, bf16[256,768]{1,0:T(8,128)(2,1)}, bf16[256,768]{1,0:T(8,128)(2,1)}, bf16...) custom-call(s32[2]{0:T(128)} %pad_add_fusion.place, bf16[512,128]{1,0:T(8,128)(2,1)} %get-tuple-element.33.refs_0_, ...), custom_call_target="tpu_custom_call" | custom-call | flops 805306368 | bytes 6815752 | tf_op jit(solution)/shard_map/pallas_call | solution.py:245
  77.8 6.1 %shard_map.154 = (bf16[512,1024]{1,0:T(8,128)(2,1)}, bf16[512,1024]{1,0:T(8,128)(2,1)}, f32[8,128]{1,0:T(8,128)}) custom-call(s32[2]{0:T(128)} %pad_add_fusion.place, bf16[512,128]{1,0:T(8,128)(2,1)} %get-tuple-element.33.refs_0_, bf16[512,128]{1,0:T(8,128)(2,1)} %get-tuple-element.34.refs_1_, bf16[512,768]{1,0:T(8,128)(2,1)} %get-tuple-element.35.refs_2_, ...), custom_call_target="tpu_custom_call" | custom-call | flops 805306368 | bytes 5771272 | tf_op jit(solution)/shard_map/pallas_call | solution.py:245
  89.2 11.8 %shard_map.155 = (bf16[256,768]{1,0:T(8,128)(2,1)}, bf16[256,768]{1,0:T(8,128)(2,1)}, bf16[256,768]{1,0:T(8,128)(2,1)}, bf16[256,768]{1,0:T(8,128)(2,1)}, bf16[2...) custom-call(s32[2]{0:T(128)} %pad_add_fusion.place, ...), custom_call_target="tpu_custom_call" | custom-call | flops 4026531840 | bytes 13762568 | tf_op jit(solution)/shard_map/pallas_call | solution.py:245
  101.8 1.5 collective-permute-start.42
  104.2 9.0 %collective-permute-done.45 = bf16[256,768]{1,0:T(8,128)(2,1)S(1)} collective-permute-done((bf16[256,768]{1,0:T(8,128)(2,1)S(1)}, bf16[256,768]{1,0:T(8,128)(2,1)S(1)}, u32[]{:S(2)}, u32[]{:S(2)}) %collective-permute-start.45) | collective-permute-done | bytes 393248 | tf_op jit(solution)/shard_map/ppermute | solution.py:404
  113.8 7.8 %collective-permute-done.42 = bf16[256,768]{1,0:T(8,128)(2,1)S(1)} collective-permute-done((bf16[256,768]{1,0:T(8,128)(2,1)}, bf16[256,768]{1,0:T(8,128)(2,1)S(1)}, u32[]{:S(2)}, u32[]{:S(2)}) %collective-permute-start.42) | collective-permute-done | bytes 393248 | tf_op jit(solution)/shard_map/ppermute | solution.py:404
  122.5 6.6 %collective-permute-done.44 = bf16[256,768]{1,0:T(8,128)(2,1)S(1)} collective-permute-done((bf16[256,768]{1,0:T(8,128)(2,1)}, bf16[256,768]{1,0:T(8,128)(2,1)S(1)}, u32[]{:S(2)}, u32[]{:S(2)}) %collective-permute-start.44) | collective-permute-done | bytes 393248 | tf_op jit(solution)/shard_map/ppermute | solution.py:404
  130.0 8.5 %collective-permute-done.39 = bf16[256,768]{1,0:T(8,128)(2,1)S(1)} collective-permute-done((bf16[256,768]{1,0:T(8,128)(2,1)S(1)}, bf16[256,768]{1,0:T(8,128)(2,1)S(1)}, u32[]{:S(2)}, u32[]{:S(2)}) %collective-permute-start.39) | collective-permute-done | bytes 393248 | tf_op jit(solution)/shard_map/ppermute | solution.py:404
  139.1 2.5 %collective-permute-start.28 = (bf16[128,1024]{1,0:T(8,128)(2,1)S(1)}, bf16[128,1024]{1,0:T(8,128)(2,1)S(1)}, u32[]{:S(2)}, u32[]{:S(2)}) collective-permute-start(bf16[128,1024]{1,0:T(8,128)(2,1)S(1)} %slice.89), channel_id=1, source_target_pairs={{0,12},{4,0},{8,4},{12,8},{1,13},{5,1},{9,5},{13,9},{2,14},{6,2},{... | collective-permute-start | bytes 786440 | tf_op jit(solution)/shard_map/ppermute | solution.py:409
  142.6 3.4 %collective-permute-done.41 = bf16[256,768]{1,0:T(8,128)(2,1)S(1)} collective-permute-done((bf16[256,768]{1,0:T(8,128)(2,1)S(1)}, bf16[256,768]{1,0:T(8,128)(2,1)S(1)}, u32[]{:S(2)}, u32[]{:S(2)}) %collective-permute-start.41) | collective-permute-done | bytes 393248 | tf_op jit(solution)/shard_map/ppermute | solution.py:404
  147.0 3.9 %collective-permute-start.29 = (bf16[128,1024]{1,0:T(8,128)(2,1)S(1)}, bf16[128,1024]{1,0:T(8,128)(2,1)S(1)}, u32[]{:S(2)}, u32[]{:S(2)}) collective-permute-start(bf16[128,1024]{1,0:T(8,128)(2,1)S(1)} %add_convert_fusion.12), channel_id=1, source_target_pairs={{0,12},{4,0},{8,4},{12,8},{1,13},{5,1},{9,5},{13,9},{2,14},{6,2},{... | collective-permute-start | bytes 786440 | tf_op jit(solution)/shard_map/ppermute | solution.py:409
  151.5 6.2 %collective-permute-done.29 = bf16[128,1024]{1,0:T(8,128)(2,1)S(1)} collective-permute-done((bf16[128,1024]{1,0:T(8,128)(2,1)S(1)}, bf16[128,1024]{1,0:T(8,128)(2,1)S(1)}, u32[]{:S(2)}, u32[]{:S(2)}) %collective-permute-start.29) | collective-permute-done | bytes 262176 | tf_op jit(solution)/shard_map/ppermute | solution.py:409
  157.8 4.3 %collective-permute-start.30 = (bf16[128,1024]{1,0:T(8,128)(2,1)S(1)}, bf16[128,1024]{1,0:T(8,128)(2,1)S(1)}, u32[]{:S(2)}, u32[]{:S(2)}) collective-permute-start(bf16[128,1024]{1,0:T(8,128)(2,1)S(1)} %add_convert_fusion.11), channel_id=1, source_target_pairs={{0,12},{4,0},{8,4},{12,8},{1,13},{5,1},{9,5},{13,9},{2,14},{6,2},{... | collective-permute-start | bytes 786440 | tf_op jit(solution)/shard_map/ppermute | solution.py:409
  163.4 4.3 %collective-permute-start.33 = (bf16[128,1024]{1,0:T(8,128)(2,1)S(1)}, bf16[128,1024]{1,0:T(8,128)(2,1)S(1)}, u32[]{:S(2)}, u32[]{:S(2)}) collective-permute-start(bf16[128,1024]{1,0:T(8,128)(2,1)S(1)} %add_convert_fusion.10), channel_id=1, source_target_pairs={{0,12},{4,0},{8,4},{12,8},{1,13},{5,1},{9,5},{13,9},{2,14},{6,2},{... | collective-permute-start | bytes 786440 | tf_op jit(solution)/shard_map/ppermute | solution.py:409
  170.4 1.9 %collective-permute-done.33 = bf16[128,1024]{1,0:T(8,128)(2,1)S(1)} collective-permute-done((bf16[128,1024]{1,0:T(8,128)(2,1)S(1)}, bf16[128,1024]{1,0:T(8,128)(2,1)S(1)}, u32[]{:S(2)}, u32[]{:S(2)}) %collective-permute-start.33) | collective-permute-done | bytes 262176 | tf_op jit(solution)/shard_map/ppermute | solution.py:409
  172.4 3.9 %collective-permute-start.34 = (bf16[128,1024]{1,0:T(8,128)(2,1)S(1)}, bf16[128,1024]{1,0:T(8,128)(2,1)S(1)}, u32[]{:S(2)}, u32[]{:S(2)}) collective-permute-start(bf16[128,1024]{1,0:T(8,128)(2,1)S(1)} %add_convert_fusion.9), channel_id=1, source_target_pairs={{0,12},{4,0},{8,4},{12,8},{1,13},{5,1},{9,5},{13,9},{2,14},{6,2},{... | collective-permute-start | bytes 786440 | tf_op jit(solution)/shard_map/ppermute | solution.py:409
  177.9 2.7 %collective-permute-done.49 = f32[16,1024]{1,0:T(8,128)S(1)} collective-permute-done((f32[16,1024]{1,0:T(8,128)S(1)}, f32[16,1024]{1,0:T(8,128)S(1)}, u32[]{:S(2)}, u32[]{:S(2)}) %collective-permute-start.49) | collective-permute-done | bytes 65568 | tf_op jit(solution)/shard_map/ppermute | solution.py:404
  181.0 4.0 %collective-permute-done.50 = f32[16,1024]{1,0:T(8,128)S(1)} collective-permute-done((f32[16,1024]{1,0:T(8,128)S(1)}, f32[16,1024]{1,0:T(8,128)S(1)}, u32[]{:S(2)}, u32[]{:S(2)}) %collective-permute-start.50) | collective-permute-done | bytes 65568 | tf_op jit(solution)/shard_map/ppermute | solution.py:566
  186.1 4.3 %collective-permute-done.51 = f32[16,1024]{1,0:T(8,128)S(1)} collective-permute-done((f32[16,1024]{1,0:T(8,128)S(1)}, f32[16,1024]{1,0:T(8,128)S(1)}, u32[]{:S(2)}, u32[]{:S(2)}) %collective-permute-start.51) | collective-permute-done | bytes 65568 | tf_op jit(solution)/shard_map/ppermute | solution.py:566
  (221 shorter events, 35.0 us)
Async XLA Ops:
  3.1 14.6 %collective-permute-start.5 = (bf16[128,1024]{1,0:T(8,128)(2,1)}, bf16[128,1024]{1,0:T(8,128)(2,1)}, u32[]{:S(2)}, u32[]{:S(2)}) collective-permute-start(bf16[128,1024]{1,0:T(8,128)(2,1)} %refs_4_.1), channel_id=1, source_target_pairs={{0,4},{4,8},{8,12},{12,0},{1,5},{5,9},{9,13},{13,1},{2,6},{6,10},{... | collective-permute-start | bytes 786440 | tf_op jit(solution)/shard_map/ppermute | solution.py:409
  5.8 12.1 %collective-permute-start.4 = (bf16[128,1024]{1,0:T(8,128)(2,1)}, bf16[128,1024]{1,0:T(8,128)(2,1)S(1)}, u32[]{:S(2)}, u32[]{:S(2)}) collective-permute-start(bf16[128,1024]{1,0:T(8,128)(2,1)} %refs_4_.1), channel_id=1, source_target_pairs={{0,1},{1,0},{2,3},{3,2},{4,5},{5,4},{6,7},{7,6},{8,9},{9,8},{10,11... | collective-permute-start | bytes 786440 | tf_op jit(solution)/shard_map/ppermute | solution.py:404
  15.4 12.0 %collective-permute-start.11 = (bf16[256,768]{1,0:T(8,128)(2,1)S(1)}, bf16[256,768]{1,0:T(8,128)(2,1)}, u32[]{:S(2)}, u32[]{:S(2)}) collective-permute-start(bf16[256,768]{1,0:T(8,128)(2,1)S(1)} %get-tuple-element.62), channel_id=1, source_target_pairs={{0,1},{1,0},{2,3},{3,2},{4,5},{5,4},{6,7},{7,6},{8,9},{9,8},{10,11... | collective-permute-start | bytes 1179656 | tf_op jit(solution)/shard_map/ppermute | solution.py:404
  15.6 12.5 %collective-permute-start.12 = (bf16[256,768]{1,0:T(8,128)(2,1)S(1)}, bf16[256,768]{1,0:T(8,128)(2,1)}, u32[]{:S(2)}, u32[]{:S(2)}) collective-permute-start(bf16[256,768]{1,0:T(8,128)(2,1)S(1)} %get-tuple-element.63.refs_12_.refs_5_), channel_id=1, source_target_pairs={{0,2},{1,3},{2,0},{3,1},{4,6},{5,7},{6,4},{7,5},{8,10},{9,11},{10,... | collective-permute-start | bytes 1179656 | tf_op jit(solution)/shard_map/ppermute | solution.py:404
  17.8 17.2 %collective-permute-start.13 = (bf16[256,768]{1,0:T(8,128)(2,1)S(1)}, bf16[256,768]{1,0:T(8,128)(2,1)}, u32[]{:S(2)}, u32[]{:S(2)}) collective-permute-start(bf16[256,768]{1,0:T(8,128)(2,1)S(1)} %get-tuple-element.62), channel_id=1, source_target_pairs={{0,3},{1,2},{2,1},{3,0},{4,7},{5,6},{6,5},{7,4},{8,11},{9,10},{10,... | collective-permute-start | bytes 1179656 | tf_op jit(solution)/shard_map/ppermute | solution.py:404
  27.4 24.8 %collective-permute-start.16 = (bf16[256,768]{1,0:T(8,128)(2,1)S(1)}, bf16[256,768]{1,0:T(8,128)(2,1)S(1)}, u32[]{:S(2)}, u32[]{:S(2)}) collective-permute-start(bf16[256,768]{1,0:T(8,128)(2,1)S(1)} %get-tuple-element.60), channel_id=1, source_target_pairs={{0,3},{1,2},{2,1},{3,0},{4,7},{5,6},{6,5},{7,4},{8,11},{9,10},{10,... | collective-permute-start | bytes 1179656 | tf_op jit(solution)/shard_map/ppermute | solution.py:404
  28.0 24.2 %collective-permute-start.15 = (bf16[256,768]{1,0:T(8,128)(2,1)S(1)}, bf16[256,768]{1,0:T(8,128)(2,1)S(1)}, u32[]{:S(2)}, u32[]{:S(2)}) collective-permute-start(bf16[256,768]{1,0:T(8,128)(2,1)S(1)} %get-tuple-element.61.refs_16_.refs_9_), channel_id=1, source_target_pairs={{0,2},{1,3},{2,0},{3,1},{4,6},{5,7},{6,4},{7,5},{8,10},{9,11},{10,... | collective-permute-start | bytes 1179656 | tf_op jit(solution)/shard_map/ppermute | solution.py:404
  34.9 18.2 %collective-permute-start.20 = (bf16[128,1024]{1,0:T(8,128)(2,1)S(1)}, bf16[128,1024]{1,0:T(8,128)(2,1)S(1)}, u32[]{:S(2)}, u32[]{:S(2)}) collective-permute-start(bf16[128,1024]{1,0:T(8,128)(2,1)S(1)} %collective-permute-done.18.refs_5_), channel_id=1, source_target_pairs={{0,4},{4,8},{8,12},{12,0},{1,5},{5,9},{9,13},{13,1},{2,6},{6,10},{... | collective-permute-start | bytes 786440 | tf_op jit(solution)/shard_map/ppermute | solution.py:409
  36.7 16.4 %collective-permute-start.9 = (bf16[128,1024]{1,0:T(8,128)(2,1)}, bf16[128,1024]{1,0:T(8,128)(2,1)}, u32[]{:S(2)}, u32[]{:S(2)}) collective-permute-start(bf16[128,1024]{1,0:T(8,128)(2,1)} %collective-permute-done.7.refs_8_), channel_id=1, source_target_pairs={{0,4},{4,8},{8,12},{12,0},{1,5},{5,9},{9,13},{13,1},{2,6},{6,10},{... | collective-permute-start | bytes 786440 | tf_op jit(solution)/shard_map/ppermute | solution.py:409
  36.7 17.0 %collective-permute-start.6 = (bf16[128,1024]{1,0:T(8,128)(2,1)}, bf16[128,1024]{1,0:T(8,128)(2,1)}, u32[]{:S(2)}, u32[]{:S(2)}) collective-permute-start(bf16[128,1024]{1,0:T(8,128)(2,1)} %collective-permute-done.5.refs_6_), channel_id=1, source_target_pairs={{0,1},{1,0},{2,3},{3,2},{4,5},{5,4},{6,7},{7,6},{8,9},{9,8},{10,11... | collective-permute-start | bytes 786440 | tf_op jit(solution)/shard_map/ppermute | solution.py:404
  53.1 10.6 %collective-permute-start.22 = (bf16[128,1024]{1,0:T(8,128)(2,1)S(1)}, bf16[128,1024]{1,0:T(8,128)(2,1)}, u32[]{:S(2)}, u32[]{:S(2)}) collective-permute-start(bf16[128,1024]{1,0:T(8,128)(2,1)S(1)} %collective-permute-done.20.refs_7_), channel_id=1, source_target_pairs={{0,4},{4,8},{8,12},{12,0},{1,5},{5,9},{9,13},{13,1},{2,6},{6,10},{... | collective-permute-start | bytes 786440 | tf_op jit(solution)/shard_map/ppermute | solution.py:409
  53.7 23.0 %collective-permute-start.24 = (bf16[256,768]{1,0:T(8,128)(2,1)S(1)}, bf16[256,768]{1,0:T(8,128)(2,1)S(1)}, u32[]{:S(2)}, u32[]{:S(2)}) collective-permute-start(bf16[256,768]{1,0:T(8,128)(2,1)S(1)} %get-tuple-element.58), channel_id=1, source_target_pairs={{0,1},{1,0},{2,3},{3,2},{4,5},{5,4},{6,7},{7,6},{8,9},{9,8},{10,11... | collective-permute-start | bytes 1179656 | tf_op jit(solution)/shard_map/ppermute | solution.py:404
  53.9 22.8 %collective-permute-start.26 = (bf16[256,768]{1,0:T(8,128)(2,1)S(1)}, bf16[256,768]{1,0:T(8,128)(2,1)S(1)}, u32[]{:S(2)}, u32[]{:S(2)}) collective-permute-start(bf16[256,768]{1,0:T(8,128)(2,1)S(1)} %get-tuple-element.58), channel_id=1, source_target_pairs={{0,3},{1,2},{2,1},{3,0},{4,7},{5,6},{6,5},{7,4},{8,11},{9,10},{10,... | collective-permute-start | bytes 1179656 | tf_op jit(solution)/shard_map/ppermute | solution.py:404
  56.1 20.6 %collective-permute-start.25 = (bf16[256,768]{1,0:T(8,128)(2,1)S(1)}, bf16[256,768]{1,0:T(8,128)(2,1)S(1)}, u32[]{:S(2)}, u32[]{:S(2)}) collective-permute-start(bf16[256,768]{1,0:T(8,128)(2,1)S(1)} %get-tuple-element.59.refs_4_.refs_13_), channel_id=1, source_target_pairs={{0,2},{1,3},{2,0},{3,1},{4,6},{5,7},{6,4},{7,5},{8,10},{9,11},{10,... | collective-permute-start | bytes 1179656 | tf_op jit(solution)/shard_map/ppermute | solution.py:404
  85.4 18.0 %collective-permute-start.46 = (bf16[256,768]{1,0:T(8,128)(2,1)S(1)}, bf16[256,768]{1,0:T(8,128)(2,1)S(1)}, u32[]{:S(2)}, u32[]{:S(2)}) collective-permute-start(bf16[256,768]{1,0:T(8,128)(2,1)S(1)} %copy-done.32), channel_id=1, source_target_pairs={{0,1},{1,0},{2,3},{3,2},{4,5},{5,4},{6,7},{7,6},{8,9},{9,8},{10,11... | collective-permute-start | bytes 1179656 | tf_op jit(solution)/shard_map/ppermute | solution.py:404
  86.0 17.5 %collective-permute-start.47 = (bf16[256,768]{1,0:T(8,128)(2,1)S(1)}, bf16[256,768]{1,0:T(8,128)(2,1)S(1)}, u32[]{:S(2)}, u32[]{:S(2)}) collective-permute-start(bf16[256,768]{1,0:T(8,128)(2,1)S(1)} %copy-done.31), channel_id=1, source_target_pairs={{0,3},{1,2},{2,1},{3,0},{4,7},{5,6},{6,5},{7,4},{8,11},{9,10},{10,... | collective-permute-start | bytes 1179656 | tf_op jit(solution)/shard_map/ppermute | solution.py:404
  87.2 14.0 %collective-permute-start.36 = (f32[2,128]{1,0:T(2,128)S(1)}, f32[2,128]{1,0:T(2,128)S(1)}, u32[]{:S(2)}, u32[]{:S(2)}) collective-permute-start(f32[2,128]{1,0:T(2,128)S(1)} %bitcast.79), channel_id=1, source_target_pairs={{0,12},{4,0},{8,4},{12,8},{1,13},{5,1},{9,5},{13,9},{2,14},{6,2},{... | collective-permute-start | bytes 3080 | tf_op jit(solution)/shard_map/ppermute | solution.py:409
  87.9 13.3 %collective-permute-start.37 = (f32[2,128]{1,0:T(2,128)S(1)}, f32[2,128]{1,0:T(2,128)S(1)}, u32[]{:S(2)}, u32[]{:S(2)}) collective-permute-start(f32[2,128]{1,0:T(2,128)S(1)} %bitcast.78), channel_id=1, source_target_pairs={{0,8},{4,12},{8,0},{12,4},{1,9},{5,13},{9,1},{13,5},{2,10},{6,14},... | collective-permute-start | bytes 3080 | tf_op jit(solution)/shard_map/ppermute | solution.py:409
  87.9 13.9 %collective-permute-start.38 = (f32[2,128]{1,0:T(2,128)S(1)}, f32[2,128]{1,0:T(2,128)S(1)}, u32[]{:S(2)}, u32[]{:S(2)}) collective-permute-start(f32[2,128]{1,0:T(2,128)S(1)} %bitcast.77), channel_id=1, source_target_pairs={{0,4},{4,8},{8,12},{12,0},{1,5},{5,9},{9,13},{13,1},{2,6},{6,10},{... | collective-permute-start | bytes 3080 | tf_op jit(solution)/shard_map/ppermute | solution.py:409
  101.1 37.5 %collective-permute-start.27 = (bf16[512,1024]{1,0:T(8,128)(2,1)S(1)}, bf16[512,1024]{1,0:T(8,128)(2,1)S(1)}, u32[]{:S(2)}, u32[]{:S(2)}) collective-permute-start(bf16[512,1024]{1,0:T(8,128)(2,1)S(1)} %copy-done.25), channel_id=1, source_target_pairs={{0,1},{1,0},{2,3},{3,2},{4,5},{5,4},{6,7},{7,6},{8,9},{9,8},{10,11... | collective-permute-start | bytes 3145736 | tf_op jit(solution)/shard_map/ppermute | solution.py:404
  101.2 12.0 %collective-permute-start.45 = (bf16[256,768]{1,0:T(8,128)(2,1)S(1)}, bf16[256,768]{1,0:T(8,128)(2,1)S(1)}, u32[]{:S(2)}, u32[]{:S(2)}) collective-permute-start(bf16[256,768]{1,0:T(8,128)(2,1)S(1)} %copy-done.30), channel_id=1, source_target_pairs={{0,2},{1,3},{2,0},{3,1},{4,6},{5,7},{6,4},{7,5},{8,10},{9,11},{10,... | collective-permute-start | bytes 1179656 | tf_op jit(solution)/shard_map/ppermute | solution.py:404
  101.8 19.8 %collective-permute-start.42 = (bf16[256,768]{1,0:T(8,128)(2,1)}, bf16[256,768]{1,0:T(8,128)(2,1)S(1)}, u32[]{:S(2)}, u32[]{:S(2)}) collective-permute-start(bf16[256,768]{1,0:T(8,128)(2,1)} %get-tuple-element.51), channel_id=1, source_target_pairs={{0,2},{1,3},{2,0},{3,1},{4,6},{5,7},{6,4},{7,5},{8,10},{9,11},{10,... | collective-permute-start | bytes 1179656 | tf_op jit(solution)/shard_map/ppermute | solution.py:404
  103.4 18.4 %collective-permute-start.43 = (bf16[256,768]{1,0:T(8,128)(2,1)}, bf16[256,768]{1,0:T(8,128)(2,1)S(1)}, u32[]{:S(2)}, u32[]{:S(2)}) collective-permute-start(bf16[256,768]{1,0:T(8,128)(2,1)} %get-tuple-element.52), channel_id=1, source_target_pairs={{0,1},{1,0},{2,3},{3,2},{4,5},{5,4},{6,7},{7,6},{8,9},{9,8},{10,11... | collective-permute-start | bytes 1179656 | tf_op jit(solution)/shard_map/ppermute | solution.py:404
  103.5 25.6 %collective-permute-start.44 = (bf16[256,768]{1,0:T(8,128)(2,1)}, bf16[256,768]{1,0:T(8,128)(2,1)S(1)}, u32[]{:S(2)}, u32[]{:S(2)}) collective-permute-start(bf16[256,768]{1,0:T(8,128)(2,1)} %get-tuple-element.53), channel_id=1, source_target_pairs={{0,3},{1,2},{2,1},{3,0},{4,7},{5,6},{6,5},{7,4},{8,11},{9,10},{10,... | collective-permute-start | bytes 1179656 | tf_op jit(solution)/shard_map/ppermute | solution.py:404
  113.2 25.3 %collective-permute-start.39 = (bf16[256,768]{1,0:T(8,128)(2,1)S(1)}, bf16[256,768]{1,0:T(8,128)(2,1)S(1)}, u32[]{:S(2)}, u32[]{:S(2)}) collective-permute-start(bf16[256,768]{1,0:T(8,128)(2,1)S(1)} %copy-done.35), channel_id=1, source_target_pairs={{0,2},{1,3},{2,0},{3,1},{4,6},{5,7},{6,4},{7,5},{8,10},{9,11},{10,... | collective-permute-start | bytes 1179656 | tf_op jit(solution)/shard_map/ppermute | solution.py:404
  121.6 21.0 %collective-permute-start.40 = (bf16[256,768]{1,0:T(8,128)(2,1)S(1)}, bf16[256,768]{1,0:T(8,128)(2,1)S(1)}, u32[]{:S(2)}, u32[]{:S(2)}) collective-permute-start(bf16[256,768]{1,0:T(8,128)(2,1)S(1)} %copy-done.34), channel_id=1, source_target_pairs={{0,1},{1,0},{2,3},{3,2},{4,5},{5,4},{6,7},{7,6},{8,9},{9,8},{10,11... | collective-permute-start | bytes 1179656 | tf_op jit(solution)/shard_map/ppermute | solution.py:404
  121.8 24.2 %collective-permute-start.41 = (bf16[256,768]{1,0:T(8,128)(2,1)S(1)}, bf16[256,768]{1,0:T(8,128)(2,1)S(1)}, u32[]{:S(2)}, u32[]{:S(2)}) collective-permute-start(bf16[256,768]{1,0:T(8,128)(2,1)S(1)} %copy-done.33), channel_id=1, source_target_pairs={{0,3},{1,2},{2,1},{3,0},{4,7},{5,6},{6,5},{7,4},{8,11},{9,10},{10,... | collective-permute-start | bytes 1179656 | tf_op jit(solution)/shard_map/ppermute | solution.py:404
  129.1 21.8 %collective-permute-start.31 = (bf16[512,1024]{1,0:T(8,128)(2,1)S(1)}, bf16[512,1024]{1,0:T(8,128)(2,1)S(1)}, u32[]{:S(2)}, u32[]{:S(2)}) collective-permute-start(bf16[512,1024]{1,0:T(8,128)(2,1)S(1)} %copy-done.26), channel_id=1, source_target_pairs={{0,1},{1,0},{2,3},{3,2},{4,5},{5,4},{6,7},{7,6},{8,9},{9,8},{10,11... | collective-permute-start | bytes 3145736 | tf_op jit(solution)/shard_map/ppermute | solution.py:404
  147.0 10.7 %collective-permute-start.29 = (bf16[128,1024]{1,0:T(8,128)(2,1)S(1)}, bf16[128,1024]{1,0:T(8,128)(2,1)S(1)}, u32[]{:S(2)}, u32[]{:S(2)}) collective-permute-start(bf16[128,1024]{1,0:T(8,128)(2,1)S(1)} %add_convert_fusion.12), channel_id=1, source_target_pairs={{0,12},{4,0},{8,4},{12,8},{1,13},{5,1},{9,5},{13,9},{2,14},{6,2},{... | collective-permute-start | bytes 786440 | tf_op jit(solution)/shard_map/ppermute | solution.py:409
  151.3 11.9 %collective-permute-start.32 = (bf16[128,1024]{1,0:T(8,128)(2,1)S(1)}, bf16[128,1024]{1,0:T(8,128)(2,1)S(1)}, u32[]{:S(2)}, u32[]{:S(2)}) collective-permute-start(bf16[128,1024]{1,0:T(8,128)(2,1)S(1)} %slice.95), channel_id=1, source_target_pairs={{0,12},{4,0},{8,4},{12,8},{1,13},{5,1},{9,5},{13,9},{2,14},{6,2},{... | collective-permute-start | bytes 786440 | tf_op jit(solution)/shard_map/ppermute | solution.py:409
  157.8 11.1 %collective-permute-start.30 = (bf16[128,1024]{1,0:T(8,128)(2,1)S(1)}, bf16[128,1024]{1,0:T(8,128)(2,1)S(1)}, u32[]{:S(2)}, u32[]{:S(2)}) collective-permute-start(bf16[128,1024]{1,0:T(8,128)(2,1)S(1)} %add_convert_fusion.11), channel_id=1, source_target_pairs={{0,12},{4,0},{8,4},{12,8},{1,13},{5,1},{9,5},{13,9},{2,14},{6,2},{... | collective-permute-start | bytes 786440 | tf_op jit(solution)/shard_map/ppermute | solution.py:409
  172.4 12.7 %collective-permute-start.34 = (bf16[128,1024]{1,0:T(8,128)(2,1)S(1)}, bf16[128,1024]{1,0:T(8,128)(2,1)S(1)}, u32[]{:S(2)}, u32[]{:S(2)}) collective-permute-start(bf16[128,1024]{1,0:T(8,128)(2,1)S(1)} %add_convert_fusion.9), channel_id=1, source_target_pairs={{0,12},{4,0},{8,4},{12,8},{1,13},{5,1},{9,5},{13,9},{2,14},{6,2},{... | collective-permute-start | bytes 786440 | tf_op jit(solution)/shard_map/ppermute | solution.py:409
  (61 other events, 740.5 us)

commit v2 on v0

--- a/solution.py
+++ b/solution.py
@@ -1,6 +1,8 @@
 import jax
 import jax.numpy as jnp
 from jax import lax
+from jax.experimental import pallas as pl
+from jax.experimental.pallas import tpu as pltpu
 from jax.sharding import PartitionSpec as P
 
 ROWS_CONTRACT = (((0,), (0,)), ((), ()))
@@ -44,7 +46,7 @@
     return lax.all_to_all(buffer, ("expert", "dp"), split_axis=0, concat_axis=0, tiled=True)
 
 
-def on_device(
+def on_device_general(
     tokens, routes, gate_weight, up_weight, down_weight, router, const_vec, const_gate, grad_out
 ):
     shard_rows, top_count = routes.shape
@@ -225,7 +227,459 @@
     )
 
 
+HALF = 64
+SLOTS = 32
+SCRATCH_BYTES = 56 * 1024 * 1024
+
+
+def local_kernel(body, scalars, operands, outputs, scratch, flops):
+    moved = sum(o.size * o.dtype.itemsize for o in [*operands, *outputs])
+    return pl.pallas_call(
+        body,
+        out_shape=outputs,
+        in_specs=[pl.BlockSpec(memory_space=pltpu.SMEM)]
+        + [pl.BlockSpec(memory_space=pl.ANY) for _ in operands],
+        out_specs=[pl.BlockSpec(memory_space=pltpu.VMEM) for _ in outputs],
+        scratch_shapes=scratch,
+        compiler_params=pltpu.CompilerParams(vmem_limit_bytes=SCRATCH_BYTES),
+        cost_estimate=pl.CostEstimate(flops=0, bytes_accessed=0, transcendentals=0),
+    )(scalars, *operands)
+
+
+def bring(pairs, sems):
+    copies = [
+        pltpu.make_async_copy(source, target, sems.at[i])
+        for i, (source, target) in enumerate(pairs)
+    ]
+    for copy in copies:
+        copy.start()
+    return copies
+
+
+def mm(a, b):
+    return jnp.dot(a, b, preferred_element_type=jnp.float32)
+
+
+def mm_rows(a, b):
+    return lax.dot_general(a, b, ROWS_CONTRACT, preferred_element_type=jnp.float32)
+
+
+def mm_last(a, b):
+    return lax.dot_general(a, b, LAST_CONTRACT, preferred_element_type=jnp.float32)
+
+
+def weight_pairs(core, parts, target):
+    stored, *fetched = parts
+    width = target.shape[0] // 4
+    sources = [stored.at[core], *fetched]
+    return [(s, target.at[pl.ds(j * width, width)]) for j, s in enumerate(sources)]
+
+
+def payload_kernel(tokens, grads, routes, router, out):
+    count = tokens.shape[0]
+    ids = lax.broadcasted_iota(jnp.int32, (router.shape[0], count), 0)
+    named = routes[0:1, :] == ids
+    for k in range(1, routes.shape[0]):
+        named = named | (routes[k : k + 1, :] == ids)
+    gates = jnp.where(named, jax.nn.sigmoid(mm_last(router[...], tokens[...])), 0.0)
+    out[0:count, :] = tokens[...]
+    out[count : 2 * count, :] = grads[...]
+    for e in range(out.shape[1] // count):
+        out[2 * count :, e * count : (e + 1) * count] = jnp.broadcast_to(
+            gates[e : e + 1], (16, count)
+        ).astype(jnp.bfloat16)
+
+
+def forward_kernel(place, *refs):
+    payloads = refs[0:8]
+    gate_weight, up_weight, partner, cross, cross_partner = refs[8:13]
+    (pick_out, gate_out, rows_out, cot_out, hidden_out, act_out, slope_out, keep_out,
+     partner_out, cross_out) = refs[13:23]
+    blocks, w_gate, w_up, upstream, sems = refs[23:28]
+    me, expert = place[0], place[1]
+    core = me & 1
+    count = pick_out.shape[1]
+    slots = count // HALF * SLOTS
+    copies = bring(
+        [(payloads[b], blocks.at[b]) for b in range(8)]
+        + weight_pairs(core, (gate_weight, partner.at[0], cross.at[0], cross_partner.at[0]), w_gate)
+        + weight_pairs(core, (up_weight, partner.at[1], cross.at[1], cross_partner.at[1]), w_up),
+        sems,
+    )
+    width = w_gate.shape[0] // 4
+    row = lax.broadcasted_iota(jnp.int32, (count, count), 0)
+    column = lax.broadcasted_iota(jnp.int32, (count, count), 1)
+    before = ((row < column) & (row // HALF == column // HALF)).astype(jnp.bfloat16)
+    lane = lax.broadcasted_iota(jnp.int32, (1, count), 1)
+    slot = lax.broadcasted_iota(jnp.int32, (slots, count), 0)
+    mine = pl.ds(pl.multiple_of(expert * count, count), count)
+    for b in range(8):
+        copies[b].wait()
+    gates = jnp.concatenate(
+        [blocks[b, 2 * count :, mine].astype(jnp.float32)[0:1] for b in range(8)], axis=0
+    )
+    picked = gates != 0.0
+    earlier = mm(picked.astype(jnp.bfloat16), before).astype(jnp.int32)
+    target = jnp.where(picked, (lane // HALF) * SLOTS + earlier, -1)
+    for b in range(8):
+        chosen = slot == target[b : b + 1]
+        pick = chosen.astype(jnp.bfloat16)
+        gate_pick = jnp.where(chosen, gates[b : b + 1], 0.0)
+        gate = jnp.sum(gate_pick, axis=1, keepdims=True)
+        at = b * slots
+        pick_out[at : at + slots, :] = pick
+        gate_out[at : at + slots, :] = gate_pick.astype(jnp.bfloat16)
+        for j in range(4):
+            columns = pl.ds(pl.multiple_of((me ^ j) * width, width), width)
+            here = (slice(at, at + slots), slice(j * width, (j + 1) * width))
+            rows_out[here] = mm(pick, blocks[b, 0:count, columns]).astype(jnp.bfloat16)
+            cot = mm(pick, blocks[b, count : 2 * count, columns])
+            cot_out[here] = cot.astype(jnp.bfloat16)
+            upstream[here] = (gate * cot).astype(jnp.bfloat16)
+    for copy in copies[8:]:
+        copy.wait()
+    pre_gate = mm(rows_out[...], w_gate[...])
+    pre_up = mm(rows_out[...], w_up[...])
+    logistic = jax.nn.sigmoid(pre_gate)
+    act = pre_gate * logistic
+    hidden_out[...] = (act * pre_up).astype(jnp.bfloat16)
+    act_out[...] = act.astype(jnp.bfloat16)
+    slope = logistic * (1.0 + pre_gate * (1.0 - logistic))
+    slope_out[...] = (pre_up * slope).astype(jnp.bfloat16)
+    outs = (keep_out, partner_out.at[0], cross_out, partner_out.at[1])
+    for j in (2, 1, 3, 0):
+        outs[j][...] = mm_rows(
+            upstream[:, j * width : (j + 1) * width], hidden_out[...]
+        ).astype(jnp.bfloat16)
+
+
+def scatter(me, pick, own_out, other_out, column_block):
+    width = own_out.shape[1] // 4
+    slots = pick.shape[0] // 8
+    count = pick.shape[1]
+    for j in range(4):
+        columns = pl.ds(pl.multiple_of((me ^ j) * width, width), width)
+        block = column_block(j, columns).astype(jnp.bfloat16)
+        for b in range(8):
+            out = own_out if b % 2 == 0 else other_out
+            at = b * slots
+            out[(b // 2) * count : (b // 2 + 1) * count, columns] = mm_rows(
+                pick[at : at + slots, :], block[at : at + slots]
+            ).astype(jnp.bfloat16)
+
+
+def output_kernel(place, *refs):
+    gate_pick_in, hidden_in, down_weight, partner, cross, cross_partner = refs[0:6]
+    own_out, other_out = refs[6:8]
+    gate_pick, hidden, w_down, sems = refs[8:12]
+    me = place[0]
+    copies = bring(
+        weight_pairs(me & 1, (down_weight, partner, cross, cross_partner), w_down)
+        + [(gate_pick_in, gate_pick), (hidden_in, hidden)],
+        sems,
+    )
+    for copy in copies:
+        copy.wait()
+    width = w_down.shape[0] // 4
+    scatter(me, gate_pick, own_out, other_out, lambda j, _: (
+        mm_last(hidden[...], w_down[j * width : (j + 1) * width])
+    ))
+
+
+def backward_kernel(place, *refs):
+    (pick_in, gate_pick_in, rows_in, hidden_in, cot_in, act_in, slope_in, router_in,
+     down_weight, partner, cross, cross_partner) = refs[0:12]
+    d_gate_out, d_up_out, logit_out, router_out, keep_out, partner_out, cross_out = refs[12:19]
+    pick, gate_pick, rows, hidden, cot, act, slope, router, w_down, sems = refs[19:29]
+    me, expert = place[0], place[1]
+    copies = bring(
+        [(cot_in, cot)]
+        + weight_pairs(me & 1, (down_weight, partner, cross, cross_partner), w_down)
+        + [(gate_pick_in, gate_pick), (hidden_in, hidden), (rows_in, rows), (act_in, act),
+           (slope_in, slope), (router_in, router)],
+        sems,
+    )
+    for copy in copies:
+        copy.wait()
+    width = w_down.shape[0] // 4
+    along = mm(cot[...], w_down[...])
+    score = jnp.sum(hidden[...].astype(jnp.float32) * along, axis=1, keepdims=True)
+    gate = jnp.sum(gate_pick[...].astype(jnp.float32), axis=1, keepdims=True)
+    d_hidden = gate * along
+    d_gate_out[...] = (d_hidden * slope[...].astype(jnp.float32)).astype(jnp.bfloat16)
+    d_up_out[...] = (d_hidden * act[...].astype(jnp.float32)).astype(jnp.bfloat16)
+    outs = (keep_out, partner_out.at[0], cross_out, partner_out.at[1])
+    for j in range(4):
+        part = rows[:, j * width : (j + 1) * width]
+        outs[j][0] = mm_rows(part, d_gate_out[...]).astype(jnp.bfloat16)
+        outs[j][1] = mm_rows(part, d_up_out[...]).astype(jnp.bfloat16)
+    ids = router.shape[0]
+    logits = jnp.zeros((pick_in.shape[0], ids), jnp.float32)
+    for j in range(4):
+        columns = pl.ds(pl.multiple_of((me ^ j) * width, width), width)
+        logits += mm_last(
+            rows[:, j * width : (j + 1) * width], router[:, columns].astype(jnp.bfloat16)
+        )
+    named = lax.broadcasted_iota(jnp.int32, (1, ids), 1) == expert
+    share = jax.nn.sigmoid(jnp.sum(jnp.where(named, logits, 0.0), axis=1, keepdims=True))
+    slope_grad = jnp.where(gate != 0.0, score * share * (1.0 - share), 0.0)
+    logit_grad = jnp.broadcast_to(slope_grad, logit_out.shape).astype(jnp.bfloat16)
+    logit_out[...] = logit_grad
+    for j in range(4):
+        columns = pl.ds(pl.multiple_of((me ^ j) * width, width), width)
+        total = mm_rows(logit_grad, rows[:, j * width : (j + 1) * width])
+        router_out[:, columns] = total[0 : router_out.shape[0]]
+
+
+def back_kernel(place, *refs):
+    (pick_in, d_gate_in, d_up_in, logit_in, router_in, gate_weight, up_weight, partner,
+     cross, cross_partner) = refs[0:10]
+    own_out, other_out = refs[10:12]
+    pick, d_gate, d_up, logit_grad, router, w_gate, w_up, sems = refs[12:20]
+    me, expert = place[0], place[1]
+    core = me & 1
+    copies = bring(
+        [(pick_in, pick), (d_gate_in, d_gate), (d_up_in, d_up), (logit_in, logit_grad),
+         (router_in, router)]
+        + weight_pairs(core, (gate_weight, partner.at[0], cross.at[0], cross_partner.at[0]), w_gate)
+        + weight_pairs(core, (up_weight, partner.at[1], cross.at[1], cross_partner.at[1]), w_up),
+        sems,
+    )
+    for copy in copies:
+        copy.wait()
+    width = w_gate.shape[0] // 4
+    slope_grad = logit_grad[:, 0:1].astype(jnp.float32)
+
+    def column_block(j, columns):
+        here = slice(j * width, (j + 1) * width)
+        return (
+            mm_last(d_gate[...], w_gate[here])
+            + mm_last(d_up[...], w_up[here])
+            + slope_grad * router[pl.ds(expert, 1), columns]
+        )
+
+    scatter(me, pick, own_out, other_out, column_block)
+
+
+def dp_swap(value, step):
+    return lax.ppermute(value, "dp", [(i, i ^ step) for i in range(4)])
+
+
+def ring(value, step):
+    size = lax.axis_size("expert")
+    return lax.ppermute(value, "expert", [(i, (i + step) % size) for i in range(size)])
+
+
+def after(value, *earlier):
+    return lax.optimization_barrier((value, *earlier))[0]
+
+
+def on_device_paired(
+    tokens, routes, gate_weight, up_weight, down_weight, router, const_vec, const_gate, grad_out
+):
+    bf16, f32 = jnp.bfloat16, jnp.float32
+    row_count, model_width = tokens.shape
+    id_count = router.shape[1]
+    const_count = const_vec.shape[0]
+    expert_count = id_count - 2 - const_count
+    stored_experts, stored_rows, hidden_width = gate_weight.shape
+    me = lax.axis_index("dp")
+    z = lax.axis_index("expert")
+    core = me % 2
+    expert = stored_experts * z + core
+    place = jnp.stack([me, expert]).astype(jnp.int32)
+
+    def of_expert(weight, which):
+        return lax.dynamic_index_in_dim(weight, which, 0, keepdims=False)
+
+    shape = jax.ShapeDtypeStruct
+    vmem = pltpu.VMEM
+    slot_count = 4 * row_count
+    wide, narrow = (slot_count, model_width), (slot_count, hidden_width)
+    table = (slot_count, row_count)
+    weight_rows = (stored_rows, hidden_width)
+    whole_weight = vmem((model_width, hidden_width), bf16)
+    product = 2 * slot_count * model_width * hidden_width
+
+    payload = pl.pallas_call(
+        payload_kernel,
+        out_shape=shape((2 * row_count + 16, model_width), bf16),
+        cost_estimate=pl.CostEstimate(flops=0, bytes_accessed=2 << 20, transcendentals=0),
+    )(tokens, grad_out, routes.T, router.T)
+    near = ring(payload, 1)
+    far_side = ring(payload, -1)
+    mine_in = jnp.stack([of_expert(gate_weight, core), of_expert(up_weight, core)])
+    theirs_in = jnp.stack([of_expert(gate_weight, 1 - core), of_expert(up_weight, 1 - core)])
+    in_cross, in_cross_partner = dp_swap(mine_in, 2), dp_swap(theirs_in, 3)
+    mine_down, theirs_down = of_expert(down_weight, core), of_expert(down_weight, 1 - core)
+    in_partner = dp_swap(theirs_in, 1)
+    down_partner = dp_swap(after(theirs_down, in_partner), 1)
+    payload_partner = dp_swap(after(payload, down_partner), 1)
+    far = ring(near, 1)
+    near_partner = dp_swap(after(near, payload_partner), 1)
+    far_side_partner = dp_swap(after(far_side, near_partner), 1)
+    far_partner = dp_swap(far, 1)
+    mine_down, theirs_down = lax.optimization_barrier(
+        (mine_down, theirs_down, in_cross, in_cross_partner)
+    )[0:2]
+    down_cross, down_cross_partner = dp_swap(mine_down, 2), dp_swap(theirs_down, 3)
+    payloads = [payload, payload_partner, near, near_partner, far, far_partner, far_side,
+                far_side_partner]
+    in_weights = [gate_weight, up_weight, in_partner, in_cross, in_cross_partner]
+    router_rows = jnp.pad(router.T.astype(f32), ((0, 16 - id_count), (0, 0)))
+    pick, gate_pick, rows, cot, hidden, act, slope, down_keep, down_theirs, down_sent = local_kernel(
+        forward_kernel,
+        place,
+        [*payloads, *in_weights],
+        [shape(table, bf16)] * 2 + [shape(wide, bf16)] * 2 + [shape(narrow, bf16)] * 3
+        + [shape(weight_rows, bf16), shape((2, *weight_rows), bf16), shape(weight_rows, bf16)],
+        [vmem((8, *payload.shape), bf16), whole_weight, whole_weight, vmem(wide, bf16),
+         pltpu.SemaphoreType.DMA((16,))],
+        3 * product,
+    )
+    down_cross, down_cross_partner, hidden = lax.optimization_barrier(
+        (down_cross, down_cross_partner, hidden)
+    )
+    down_weights = [down_weight, down_partner, down_cross, down_cross_partner]
+    mixed_own, mixed_other = local_kernel(
+        output_kernel,
+        place,
+        [gate_pick, hidden, *down_weights],
+        [shape(wide, bf16)] * 2,
+        [vmem(table, bf16), vmem(narrow, bf16), whole_weight, pltpu.SemaphoreType.DMA((6,))],
+        product,
+    )
+    d_gate, d_up, logit_grad, router_row, in_keep, in_theirs, in_sent = local_kernel(
+        backward_kernel,
+        place,
+        [pick, gate_pick, rows, hidden, cot, act, slope, router_rows, *down_weights],
+        [shape(narrow, bf16)] * 2 + [shape(table, bf16), shape((8, model_width), f32)]
+        + [shape((2, *weight_rows), bf16), shape((2, 2, *weight_rows), bf16),
+           shape((2, *weight_rows), bf16)],
+        [vmem(table, bf16)] * 2 + [vmem(wide, bf16), vmem(narrow, bf16), vmem(wide, bf16),
+         vmem(narrow, bf16), vmem(narrow, bf16), vmem(router_rows.shape, f32), whole_weight,
+         pltpu.SemaphoreType.DMA((11,))],
+        3 * product,
+    )
+    down_came = dp_swap(down_sent, 2)
+    down_from = dp_swap(down_theirs, 1)
+    down_came_partner = dp_swap(down_from[1], 2)
+    in_came = dp_swap(in_sent, 2)
+    down_came, down_came_partner, in_theirs, d_gate = lax.optimization_barrier(
+        (down_came, down_came_partner, in_theirs, d_gate)
+    )
+    back_own, back_other = local_kernel(
+        back_kernel,
+        place,
+        [pick, d_gate, d_up, logit_grad, router_rows, *in_weights],
+        [shape(wide, bf16)] * 2,
+        [vmem(table, bf16), vmem(narrow, bf16), vmem(narrow, bf16), vmem(table, bf16),
+         vmem(router_rows.shape, f32), whole_weight, whole_weight,
+         pltpu.SemaphoreType.DMA((13,))],
+        2 * product,
+    )
+
+    def pair(mine, theirs):
+        return jnp.where(
+            core == 0, jnp.stack([mine, theirs], axis=-3), jnp.stack([theirs, mine], axis=-3)
+        )
+
+    def add(one, two):
+        return one.astype(f32) + two.astype(f32)
+
+    grad_down = pair(add(down_keep, down_came), add(down_from[0], down_came_partner)).astype(bf16)
+    in_from = dp_swap(in_theirs, 1)
+    in_came_partner = dp_swap(in_from[1], 2)
+
+    def home(own, other):
+        both = (own.astype(f32) + dp_swap(other, 1).astype(f32)).astype(bf16)
+        slots = both.reshape(4, row_count, model_width)
+        side = ring(slots[3], 1)
+        near = (ring(slots[2], -1).astype(f32) + slots[1].astype(f32)).astype(bf16)
+        return side, near, slots[0]
+
+    mixed_parts = home(mixed_own, mixed_other)
+    back_parts = home(back_own, back_other)
+    in_came, in_came_partner = lax.optimization_barrier(
+        (in_came, in_came_partner, back_parts[1])
+    )[0:2]
+    grad_in = pair(add(in_keep, in_came), add(in_from[0], in_came_partner)).astype(bf16)
+    grad_gate, grad_up = grad_in[0], grad_in[1]
+    mixed_sum = add(ring(mixed_parts[1], -1), mixed_parts[0]) + mixed_parts[2].astype(f32)
+    back_sum = add(ring(back_parts[1], -1), back_parts[0]) + back_parts[2].astype(f32)
+
+    id_range = lax.broadcasted_iota(jnp.int32, (1, 1, id_count), 2)
+    named = jnp.any(routes[:, :, None] == id_range, axis=1)[:, expert_count:]
+    share = jax.nn.sigmoid(mm(tokens, router[:, expert_count:]))
+    gates = jnp.where(named, share, 0.0).astype(bf16).astype(f32)
+    tokens_float = tokens.astype(f32)
+    grad_float = grad_out.astype(f32)
+    copy_weight = gates[:, 1]
+    const_weight = gates[:, 2:]
+    const_share = jax.nn.sigmoid(mm(tokens, const_gate))
+    const_rest = (const_weight * (1.0 - const_share)).astype(bf16)
+    coefficient = copy_weight + jnp.sum(const_weight * const_share, axis=1)
+    mixed = (
+        mixed_sum + coefficient[:, None] * tokens_float + mm(const_rest, const_vec)
+    ).astype(bf16)
+    along_token = jnp.sum(grad_float * tokens_float, axis=1, keepdims=True)
+    along_const = mm_last(grad_out, const_vec)
+    const_value = const_share * along_token + (1.0 - const_share) * along_const
+    pick_grad = jnp.concatenate(
+        [jnp.zeros_like(along_token), along_token, const_value], axis=1
+    )
+    null_grad = jnp.where(named, pick_grad * share * (1.0 - share), 0.0).astype(bf16)
+    share_grad = (
+        const_weight * (along_token - along_const) * const_share * (1.0 - const_share)
+    ).astype(bf16)
+    back_local = (
+        coefficient[:, None] * grad_float
+        + mm_last(null_grad, router[:, expert_count:])
+        + mm_last(share_grad, const_gate)
+    )
+    grad_tokens = (back_sum + back_local).astype(bf16)
+
+    small = jnp.concatenate(
+        [
+            mm_rows(jnp.concatenate([null_grad, share_grad], axis=1), tokens),
+            mm_rows(const_rest, grad_out),
+        ],
+        axis=0,
+    )
+    experts = lax.broadcasted_iota(jnp.int32, (expert_count, 1), 0)
+    routed = jnp.where(experts == expert, router_row[0:1], 0.0)
+    small = jnp.concatenate([routed, small], axis=0)
+    for step in (1, 2):
+        small = small + dp_swap(small, step)
+    for step in (1, 2):
+        small = small + lax.ppermute(small, "expert", [(i, i ^ step) for i in range(4)])
+    grad_router = small[:id_count].T
+    grad_const_gate = small[id_count : id_count + const_count].T
+    grad_const_vec = small[id_count + const_count :]
+    return (
+        mixed,
+        grad_tokens,
+        grad_gate,
+        grad_up,
+        grad_down,
+        grad_router,
+        grad_const_vec,
+        grad_const_gate,
+    )
+
+
 def solution(mesh):
+    paired = mesh.shape["rep"] == 1 and mesh.shape["dp"] == 4
+
+    def on_device(tokens, routes, gate_weight, *others):
+        id_count = others[2].shape[1]
+        stored_experts, stored_rows, hidden_width = gate_weight.shape
+        row_count, top_count = routes.shape
+        halved = row_count * top_count == (row_count // 2) * id_count
+        if paired and stored_experts == 2 and halved and row_count == 128:
+            return on_device_paired(tokens, routes, gate_weight, *others)
+        return on_device_general(tokens, routes, gate_weight, *others)
+
     placed = (
         P(("groups", "expert", "dp"), None),
         P(("groups", "expert", "dp"), None),

time: 401 us -> 154 us (0.38)
  waiting for transfers between devices: 231 us -> 69.5 us
  matrix products: 37.1 us -> 3.65 us
  Pallas kernels: 0 us -> 33.4 us
  local copies, waits for them, and re-layouts: 32.5 us -> 7.33 us
  blocking collectives: 24.2 us -> 0 us
  starting transfers between devices: 45.1 us -> 28.3 us
  between operations: 14.4 us -> 1.13 us
  other arithmetic: 14.9 us -> 10.2 us
    all_to_all x9 -> x0, waiting for transfers between devices: 144 us -> none  [the longest x4 58.4 us: token_trip(): lax.all_to_all(buffer, ('expert', 'dp'), split_axis=0, concat_axis=0, til...]
    psum x1 -> x0, waiting for transfers between devices: 87.3 us -> none  [on_device(): lax.psum((router_part, vector_part, mixing_part), ('expert', 'dp', 'rep'))]
    ppermute x0 -> x31, waiting for transfers between devices: none -> 69.5 us  [the longest x9 48.8 us: ring(): lax.ppermute(value, 'expert', [(i, (i + step) % size) for i in range(size)])]
    all_to_all x9 -> x0, starting transfers between devices: 45.1 us -> none  [the longest x4 24.8 us: token_trip(): lax.all_to_all(buffer, ('expert', 'dp'), split_axis=0, concat_axis=0, til...]
    dot_general x19 -> x8, matrix products: 37.1 us -> 3.65 us  [the longest x3 1.85 us: mm(): return jnp.dot(a, b, preferred_element_type=jnp.float32)]
    pallas_call x0 -> x5, Pallas kernels: none -> 33.4 us  [the longest x4 31.4 us: local_kernel(): pl.pallas_call(body, out_shape=outputs, in_specs=[pl.BlockSpec(memory_spa...]
    ppermute x0 -> x31, starting transfers between devices: none -> 28.3 us  [the longest x9 15.1 us: ring(): lax.ppermute(value, 'expert', [(i, (i + step) % size) for i in range(size)])]
    all_to_all x1 -> x0, blocking collectives: 24.2 us -> none  [on_device(): lax.all_to_all(jnp.repeat(gate_weight, repeat, axis=0), ('dp', 'rep'), sp...]
  transfers between devices with their start and end apart: 10 -> 31, of which waited for: 10 -> 14; matrix products, arithmetic and copies ran while one was open for 12% -> 11% of each run, Pallas kernels for 0% -> 18%
where the time goes in v2:
time: 154 us
  waiting for transfers between devices  69.5 us (45%)
  Pallas kernels  33.4 us (22%)
  starting transfers between devices  28.3 us (18%)
  other arithmetic  10.2 us (7%)
  local copies, waits for them, and re-layouts  7.33 us (5%)
  matrix products  3.65 us (2%)
    ppermute x9, waiting for transfers between devices, ring(): lax.ppermute(value, 'expert', [(i, (i + step) % size) for i in range(size)])  48.8 us
    pallas_call x4, Pallas kernels, local_kernel(): pl.pallas_call(body, out_shape=outputs, in_specs=[pl.BlockSpec(memory_spa...  31.4 us
    ppermute x9, starting transfers between devices, ring(): lax.ppermute(value, 'expert', [(i, (i + step) % size) for i in range(size)])  15.1 us
    ppermute x20, starting transfers between devices, dp_swap(): return lax.ppermute(value, 'dp', [(i, i ^ step) for i in range(4)])  13.1 us
    ppermute x20, waiting for transfers between devices, dp_swap(): return lax.ppermute(value, 'dp', [(i, i ^ step) for i in range(4)])  12.4 us
    ppermute x2, waiting for transfers between devices, on_device_paired(): lax.ppermute(small, 'expert', [(i, i ^ step) for i in range(4)])  8.27 us
  transfers between devices with their start and end apart: 31, of which 14 were waited for; matrix products, arithmetic and copies ran while one was open for 11% of the time, Pallas kernels for 18%

profile of v2, /device:TPU:0, one launch (start us, length us, event | category | flops | bytes accessed | tf_op | source)
XLA Modules:
  0.0 153.6 jit_solution(7082343471254582243)
XLA Ops:
  0.7 1.5 constant_dynamic-slice_fusion
  5.1 2.0 %shard_map.152.refs_0_ = bf16[272,1024]{1,0:T(8,128)(2,1)} custom-call(bf16[128,1024]{1,0:T(8,128)(2,1)} %tokens.1, bf16[128,1024]{1,0:T(8,128)(2,1)} %grads.1, s32[6,128]{1,0:T(8,128)} %bitcast.62, bf16[12,1024]{1,0:T(8,128)(2,1)} %bitcast.60), custom_call_target="tpu_custom_call" | custom-call | bytes 2097152 | tf_op jit(solution)/shard_map/pallas_call | solution.py:504
  7.1 2.9 %collective-permute-start.3 = (bf16[272,1024]{1,0:T(8,128)(2,1)}, bf16[272,1024]{1,0:T(8,128)(2,1)S(1)}, u32[]{:S(2)}, u32[]{:S(2)}) collective-permute-start(bf16[272,1024]{1,0:T(8,128)(2,1)} %shard_map.152.refs_0_), channel_id=1, source_target_pairs={{0,4},{4,8},{8,12},{12,0},{1,5},{5,9},{9,13},{13,1},{2,6},{6,10},{... | collective-permute-start | bytes 1671176 | tf_op jit(solution)/shard_map/ppermute | solution.py:470
  10.1 1.6 %collective-permute-start.9 = (bf16[2,256,768]{2,1,0:T(8,128)(2,1)S(1)}, bf16[2,256,768]{2,1,0:T(8,128)(2,1)S(1)}, u32[]{:S(2)}, u32[]{:S(2)}) collective-permute-start(bf16[2,256,768]{2,1,0:T(8,128)(2,1)S(1)} %pad_maximum_fusion.1), channel_id=1, source_target_pairs={{0,2},{1,3},{2,0},{3,1},{4,6},{5,7},{6,4},{7,5},{8,10},{9,11},{10,... | collective-permute-start | bytes 2359304 | tf_op jit(solution)/shard_map/ppermute | solution.py:465
  12.0 2.6 %collective-permute-start.7 = (bf16[272,1024]{1,0:T(8,128)(2,1)S(1)}, bf16[272,1024]{1,0:T(8,128)(2,1)}, u32[]{:S(2)}, u32[]{:S(2)}) collective-permute-start(bf16[272,1024]{1,0:T(8,128)(2,1)S(1)} %copy-done.7), channel_id=1, source_target_pairs={{0,12},{4,0},{8,4},{12,8},{1,13},{5,1},{9,5},{13,9},{2,14},{6,2},{... | collective-permute-start | bytes 1671176 | tf_op jit(solution)/shard_map/ppermute | solution.py:470
  14.6 11.1 %collective-permute-done.3.refs_2_ = bf16[272,1024]{1,0:T(8,128)(2,1)S(1)} collective-permute-done((bf16[272,1024]{1,0:T(8,128)(2,1)}, bf16[272,1024]{1,0:T(8,128)(2,1)S(1)}, u32[]{:S(2)}, u32[]{:S(2)}) %collective-permute-start.3) | collective-permute-done | bytes 557088 | tf_op jit(solution)/shard_map/ppermute | solution.py:470
  25.8 23.5 %collective-permute-done.5.refs_4_ = bf16[272,1024]{1,0:T(8,128)(2,1)} collective-permute-done((bf16[272,1024]{1,0:T(8,128)(2,1)S(1)}, bf16[272,1024]{1,0:T(8,128)(2,1)}, u32[]{:S(2)}, u32[]{:S(2)}) %collective-permute-start.5) | collective-permute-done | bytes 557088 | tf_op jit(solution)/shard_map/ppermute | solution.py:470
  49.9 1.6 %collective-permute-start.11 = (bf16[256,768]{1,0:T(8,128)(2,1)}, bf16[256,768]{1,0:T(8,128)(2,1)S(1)}, u32[]{:S(2)}, u32[]{:S(2)}) collective-permute-start(bf16[256,768]{1,0:T(8,128)(2,1)} %get-tuple-element.49), channel_id=1, source_target_pairs={{0,2},{1,3},{2,0},{3,1},{4,6},{5,7},{6,4},{7,5},{8,10},{9,11},{10,... | collective-permute-start | bytes 1179656 | tf_op jit(solution)/shard_map/ppermute | solution.py:465
  52.4 7.8 %shard_map.153 = (bf16[512,128]{1,0:T(8,128)(2,1)}, bf16[512,128]{1,0:T(8,128)(2,1)}, bf16[512,1024]{1,0:T(8,128)(2,1)}, bf16[512,1024]{1,0:T(8,128)(2,1)}, bf16...) custom-call(s32[2]{0:T(128)} %pad_add_fusion.place, ...), custom_call_target="tpu_custom_call" | custom-call | tf_op jit(solution)/shard_map/pallas_call | solution.py:237
  60.3 1.9 %collective-permute-done.11.refs_4_.refs_10_ = bf16[256,768]{1,0:T(8,128)(2,1)S(1)} collective-permute-done((bf16[256,768]{1,0:T(8,128)(2,1)}, bf16[256,768]{1,0:T(8,128)(2,1)S(1)}, u32[]{:S(2)}, u32[]{:S(2)}) %collective-permute-start.11) | collective-permute-done | bytes 393248 | tf_op jit(solution)/shard_map/ppermute | solution.py:465
  62.2 6.7 %collective-permute-done.12.refs_5_.refs_11_ = bf16[256,768]{1,0:T(8,128)(2,1)} collective-permute-done((bf16[256,768]{1,0:T(8,128)(2,1)S(1)}, bf16[256,768]{1,0:T(8,128)(2,1)}, u32[]{:S(2)}, u32[]{:S(2)}) %collective-permute-start.12) | collective-permute-done | bytes 393248 | tf_op jit(solution)/shard_map/ppermute | solution.py:465
  68.9 6.5 %shard_map.154 = (bf16[512,1024]{1,0:T(8,128)(2,1)}, bf16[512,1024]{1,0:T(8,128)(2,1)}) custom-call(s32[2]{0:T(128)} %pad_add_fusion.place, bf16[512,128]{1,0:T(8,128)(2,1)} %get-tuple-element.48.refs_0_.refs_1_, bf16[512,768]{1,0:T(8,128)(2,1)} %get-tuple-element.52.refs_1_.refs_3_, bf16[2,256,768]{2,1,0:T(8,128)(2,1)} %refs_8_.3, ...), custom_call_target="tpu_custom_call" | custom-call | tf_op jit(solution)/shard_map/pallas_call | solution.py:237
  80.1 1.7 %collective-permute-start.14 = (bf16[128,1024]{1,0:T(8,128)(2,1)S(1)}, bf16[128,1024]{1,0:T(8,128)(2,1)S(1)}, u32[]{:S(2)}, u32[]{:S(2)}) collective-permute-start(bf16[128,1024]{1,0:T(8,128)(2,1)S(1)} %get-tuple-element.84), channel_id=1, source_target_pairs={{0,12},{4,0},{8,4},{12,8},{1,13},{5,1},{9,5},{13,9},{2,14},{6,2},{... | collective-permute-start | bytes 786440 | tf_op jit(solution)/shard_map/ppermute | solution.py:470
  82.4 1.5 collective-permute-start.17
  84.9 3.9 %collective-permute-done.14 = bf16[128,1024]{1,0:T(8,128)(2,1)S(1)} collective-permute-done((bf16[128,1024]{1,0:T(8,128)(2,1)S(1)}, bf16[128,1024]{1,0:T(8,128)(2,1)S(1)}, u32[]{:S(2)}, u32[]{:S(2)}) %collective-permute-start.14) | collective-permute-done | bytes 262176 | tf_op jit(solution)/shard_map/ppermute | solution.py:470
  88.9 4.1 %collective-permute-start.15 = (bf16[128,1024]{1,0:T(8,128)(2,1)S(1)}, bf16[128,1024]{1,0:T(8,128)(2,1)}, u32[]{:S(2)}, u32[]{:S(2)}) collective-permute-start(bf16[128,1024]{1,0:T(8,128)(2,1)S(1)} %add_convert_fusion.4), channel_id=1, source_target_pairs={{0,12},{4,0},{8,4},{12,8},{1,13},{5,1},{9,5},{13,9},{2,14},{6,2},{... | collective-permute-start | bytes 786440 | tf_op jit(solution)/shard_map/ppermute | solution.py:470
  93.5 8.3 %shard_map.155 = (bf16[512,768]{1,0:T(8,128)(2,1)}, bf16[512,768]{1,0:T(8,128)(2,1)}, bf16[512,128]{1,0:T(8,128)(2,1)}, f32[8,1024]{1,0:T(8,128)}, bf16[2,256,76...) custom-call(s32[2]{0:T(128)} %pad_add_fusion.place, ...), custom_call_target="tpu_custom_call" | custom-call | tf_op jit(solution)/shard_map/pallas_call | solution.py:237
  102.6 1.5 collective-permute-start.24
  104.2 8.8 %shard_map.156 = (bf16[512,1024]{1,0:T(8,128)(2,1)}, bf16[512,1024]{1,0:T(8,128)(2,1)}) custom-call(s32[2]{0:T(128)} %pad_add_fusion.place, bf16[512,128]{1,0:T(8,128)(2,1)} %get-tuple-element.57.refs_0_, bf16[512,768]{1,0:T(8,128)(2,1)} %get-tuple-element.66.refs_1_, bf16[512,768]{1,0:T(8,128)(2,1)} %get-tuple-element.67.refs_2_, ...), custom_call_target="tpu_custom_call" | custom-call | tf_op jit(solution)/shard_map/pallas_call | solution.py:237
  113.6 2.0 %fusion.14 = (f32[128]{0:T(128)S(1)}, bf16[128,1024]{1,0:T(8,128)(2,1)}) fusion(bf16[128,1024]{1,0:T(8,128)(2,1)S(1)} %copy-done.2, bf16[128,1024]{1,0:T(8,128)(2,1)S(1)} %copy-done.3, f32[128,1024]{1,0:T(8,128)S(1)} %fusion.30, f32[128]{0:T(128)S(1)} %copy-done.27, bf16[512,1024]{1,0:T(8,128)(2,1)S(1)} %add_convert_fusion.1, ...), kind=kLoop, calls=%fused_computation.34 | loop fusion | flops 1703808 | bytes 2098176 | tf_op jit(solution)/shard_map/reduce_sum | solution.py:625
  116.9 1.1 add_bitcast_fusion.1
  118.7 1.1 fusion.10
  119.9 2.8 %collective-permute-done.28 = f32[16,1024]{1,0:T(8,128)S(1)} collective-permute-done((f32[16,1024]{1,0:T(8,128)S(1)}, f32[16,1024]{1,0:T(8,128)S(1)}, u32[]{:S(2)}, u32[]{:S(2)}) %collective-permute-start.28) | collective-permute-done | bytes 65568 | tf_op jit(solution)/shard_map/ppermute | solution.py:465
  123.8 3.2 %collective-permute-done.29 = f32[16,1024]{1,0:T(8,128)S(1)} collective-permute-done((f32[16,1024]{1,0:T(8,128)S(1)}, f32[16,1024]{1,0:T(8,128)S(1)}, u32[]{:S(2)}, u32[]{:S(2)}) %collective-permute-start.29) | collective-permute-done | bytes 65568 | tf_op jit(solution)/shard_map/ppermute | solution.py:655
  127.4 5.0 %collective-permute-done.30 = f32[16,1024]{1,0:T(8,128)S(1)} collective-permute-done((f32[16,1024]{1,0:T(8,128)S(1)}, f32[16,1024]{1,0:T(8,128)S(1)}, u32[]{:S(2)}, u32[]{:S(2)}) %collective-permute-start.30) | collective-permute-done | bytes 65568 | tf_op jit(solution)/shard_map/ppermute | solution.py:655
  133.1 1.9 %collective-permute-start.23 = (bf16[128,1024]{1,0:T(8,128)(2,1)S(1)}, bf16[128,1024]{1,0:T(8,128)(2,1)S(1)}, u32[]{:S(2)}, u32[]{:S(2)}) collective-permute-start(bf16[128,1024]{1,0:T(8,128)(2,1)S(1)} %get-tuple-element.83), channel_id=1, source_target_pairs={{0,4},{4,8},{8,12},{12,0},{1,5},{5,9},{9,13},{13,1},{2,6},{6,10},{... | collective-permute-start | bytes 786440 | tf_op jit(solution)/shard_map/ppermute | solution.py:470
  135.1 2.0 %collective-permute-start.26 = (bf16[2,256,768]{2,1,0:T(8,128)(2,1)S(1)}, bf16[2,256,768]{2,1,0:T(8,128)(2,1)S(1)}, u32[]{:S(2)}, u32[]{:S(2)}) collective-permute-start(bf16[2,256,768]{2,1,0:T(8,128)(2,1)S(1)} %slice_bitcast_fusion.3), channel_id=1, source_target_pairs={{0,2},{1,3},{2,0},{3,1},{4,6},{5,7},{6,4},{7,5},{8,10},{9,11},{10,... | collective-permute-start | bytes 2359304 | tf_op jit(solution)/shard_map/ppermute | solution.py:465
  137.0 5.9 %collective-permute-done.21 = bf16[128,1024]{1,0:T(8,128)(2,1)S(1)} collective-permute-done((bf16[128,1024]{1,0:T(8,128)(2,1)S(1)}, bf16[128,1024]{1,0:T(8,128)(2,1)S(1)}, u32[]{:S(2)}, u32[]{:S(2)}) %collective-permute-start.21) | collective-permute-done | bytes 262176 | tf_op jit(solution)/shard_map/ppermute | solution.py:470
  143.0 1.4 collective-permute-start.22
  146.7 3.4 %collective-permute-done.22 = bf16[128,1024]{1,0:T(8,128)(2,1)S(1)} collective-permute-done((bf16[128,1024]{1,0:T(8,128)(2,1)S(1)}, bf16[128,1024]{1,0:T(8,128)(2,1)S(1)}, u32[]{:S(2)}, u32[]{:S(2)}) %collective-permute-start.22) | collective-permute-done | bytes 262176 | tf_op jit(solution)/shard_map/ppermute | solution.py:470
  150.1 1.1 add_convert_fusion.2
  152.3 1.2 slice_bitcast_fusion
  (139 shorter events, 20.9 us)
Async XLA Ops:
  0.6 76.4 %copy-start = (bf16[1024,2]{0,1:T(2,128)(2,1)S(1)}, bf16[1024,2]{0,1:T(2,128)(2,1)}, u32[]{:S(2)}) copy-start(bf16[1024,2]{0,1:T(2,128)(2,1)} %param.16) | copy-start | bytes 12292
  2.3 2.4 %collective-permute-start = (bf16[2,256,768]{2,1,0:T(8,128)(2,1)S(1)}, bf16[2,256,768]{2,1,0:T(8,128)(2,1)S(1)}, u32[]{:S(2)}, u32[]{:S(2)}) collective-permute-start(bf16[2,256,768]{2,1,0:T(8,128)(2,1)S(1)} %pad_maximum_fusion), channel_id=1, source_target_pairs={{0,1},{1,0},{2,3},{3,2},{4,5},{5,4},{6,7},{7,6},{8,9},{9,8},{10,11... | collective-permute-start | bytes 2359304 | tf_op jit(solution)/shard_map/ppermute | solution.py:465
  4.7 5.3 %collective-permute-start.1 = (bf16[256,768]{1,0:T(8,128)(2,1)S(1)}, bf16[256,768]{1,0:T(8,128)(2,1)S(1)}, u32[]{:S(2)}, u32[]{:S(2)}) collective-permute-start(bf16[256,768]{1,0:T(8,128)(2,1)S(1)} %get-tuple-element.50), channel_id=1, source_target_pairs={{0,1},{1,0},{2,3},{3,2},{4,5},{5,4},{6,7},{7,6},{8,9},{9,8},{10,11... | collective-permute-start | bytes 1179656 | tf_op jit(solution)/shard_map/ppermute | solution.py:465
  7.1 18.6 %collective-permute-start.3 = (bf16[272,1024]{1,0:T(8,128)(2,1)}, bf16[272,1024]{1,0:T(8,128)(2,1)S(1)}, u32[]{:S(2)}, u32[]{:S(2)}) collective-permute-start(bf16[272,1024]{1,0:T(8,128)(2,1)} %shard_map.152.refs_0_), channel_id=1, source_target_pairs={{0,4},{4,8},{8,12},{12,0},{1,5},{5,9},{9,13},{13,1},{2,6},{6,10},{... | collective-permute-start | bytes 1671176 | tf_op jit(solution)/shard_map/ppermute | solution.py:470
  10.0 15.7 %collective-permute-start.2 = (bf16[272,1024]{1,0:T(8,128)(2,1)}, bf16[272,1024]{1,0:T(8,128)(2,1)S(1)}, u32[]{:S(2)}, u32[]{:S(2)}) collective-permute-start(bf16[272,1024]{1,0:T(8,128)(2,1)} %shard_map.152.refs_0_), channel_id=1, source_target_pairs={{0,1},{1,0},{2,3},{3,2},{4,5},{5,4},{6,7},{7,6},{8,9},{9,8},{10,11... | collective-permute-start | bytes 1671176 | tf_op jit(solution)/shard_map/ppermute | solution.py:465
  10.1 39.8 %collective-permute-start.9 = (bf16[2,256,768]{2,1,0:T(8,128)(2,1)S(1)}, bf16[2,256,768]{2,1,0:T(8,128)(2,1)S(1)}, u32[]{:S(2)}, u32[]{:S(2)}) collective-permute-start(bf16[2,256,768]{2,1,0:T(8,128)(2,1)S(1)} %pad_maximum_fusion.1), channel_id=1, source_target_pairs={{0,2},{1,3},{2,0},{3,1},{4,6},{5,7},{6,4},{7,5},{8,10},{9,11},{10,... | collective-permute-start | bytes 2359304 | tf_op jit(solution)/shard_map/ppermute | solution.py:465
  11.7 38.2 %collective-permute-start.10 = (bf16[2,256,768]{2,1,0:T(8,128)(2,1)S(1)}, bf16[2,256,768]{2,1,0:T(8,128)(2,1)S(1)}, u32[]{:S(2)}, u32[]{:S(2)}) collective-permute-start(bf16[2,256,768]{2,1,0:T(8,128)(2,1)S(1)} %copy-done.13), channel_id=1, source_target_pairs={{0,3},{1,2},{2,1},{3,0},{4,7},{5,6},{6,5},{7,4},{8,11},{9,10},{10,... | collective-permute-start | bytes 2359304 | tf_op jit(solution)/shard_map/ppermute | solution.py:465
  12.0 37.3 %collective-permute-start.7 = (bf16[272,1024]{1,0:T(8,128)(2,1)S(1)}, bf16[272,1024]{1,0:T(8,128)(2,1)}, u32[]{:S(2)}, u32[]{:S(2)}) collective-permute-start(bf16[272,1024]{1,0:T(8,128)(2,1)S(1)} %copy-done.7), channel_id=1, source_target_pairs={{0,12},{4,0},{8,4},{12,8},{1,13},{5,1},{9,5},{13,9},{2,14},{6,2},{... | collective-permute-start | bytes 1671176 | tf_op jit(solution)/shard_map/ppermute | solution.py:470
  25.7 23.6 %collective-permute-start.5 = (bf16[272,1024]{1,0:T(8,128)(2,1)S(1)}, bf16[272,1024]{1,0:T(8,128)(2,1)}, u32[]{:S(2)}, u32[]{:S(2)}) collective-permute-start(bf16[272,1024]{1,0:T(8,128)(2,1)S(1)} %collective-permute-done.3.refs_2_), channel_id=1, source_target_pairs={{0,4},{4,8},{8,12},{12,0},{1,5},{5,9},{9,13},{13,1},{2,6},{6,10},{... | collective-permute-start | bytes 1671176 | tf_op jit(solution)/shard_map/ppermute | solution.py:470
  25.7 23.6 %collective-permute-start.4 = (bf16[272,1024]{1,0:T(8,128)(2,1)S(1)}, bf16[272,1024]{1,0:T(8,128)(2,1)S(1)}, u32[]{:S(2)}, u32[]{:S(2)}) collective-permute-start(bf16[272,1024]{1,0:T(8,128)(2,1)S(1)} %collective-permute-done.3.refs_2_), channel_id=1, source_target_pairs={{0,1},{1,0},{2,3},{3,2},{4,5},{5,4},{6,7},{7,6},{8,9},{9,8},{10,11... | collective-permute-start | bytes 1671176 | tf_op jit(solution)/shard_map/ppermute | solution.py:465
  49.3 3.1 %collective-permute-start.6 = (bf16[272,1024]{1,0:T(8,128)(2,1)}, bf16[272,1024]{1,0:T(8,128)(2,1)}, u32[]{:S(2)}, u32[]{:S(2)}) collective-permute-start(bf16[272,1024]{1,0:T(8,128)(2,1)} %collective-permute-done.5.refs_4_), channel_id=1, source_target_pairs={{0,1},{1,0},{2,3},{3,2},{4,5},{5,4},{6,7},{7,6},{8,9},{9,8},{10,11... | collective-permute-start | bytes 1671176 | tf_op jit(solution)/shard_map/ppermute | solution.py:465
  49.3 3.1 %collective-permute-start.8 = (bf16[272,1024]{1,0:T(8,128)(2,1)}, bf16[272,1024]{1,0:T(8,128)(2,1)}, u32[]{:S(2)}, u32[]{:S(2)}) collective-permute-start(bf16[272,1024]{1,0:T(8,128)(2,1)} %collective-permute-done.7.refs_6_), channel_id=1, source_target_pairs={{0,1},{1,0},{2,3},{3,2},{4,5},{5,4},{6,7},{7,6},{8,9},{9,8},{10,11... | collective-permute-start | bytes 1671176 | tf_op jit(solution)/shard_map/ppermute | solution.py:465
  49.9 12.3 %collective-permute-start.11 = (bf16[256,768]{1,0:T(8,128)(2,1)}, bf16[256,768]{1,0:T(8,128)(2,1)S(1)}, u32[]{:S(2)}, u32[]{:S(2)}) collective-permute-start(bf16[256,768]{1,0:T(8,128)(2,1)} %get-tuple-element.49), channel_id=1, source_target_pairs={{0,2},{1,3},{2,0},{3,1},{4,6},{5,7},{6,4},{7,5},{8,10},{9,11},{10,... | collective-permute-start | bytes 1179656 | tf_op jit(solution)/shard_map/ppermute | solution.py:465
  51.5 17.4 %collective-permute-start.12 = (bf16[256,768]{1,0:T(8,128)(2,1)S(1)}, bf16[256,768]{1,0:T(8,128)(2,1)}, u32[]{:S(2)}, u32[]{:S(2)}) collective-permute-start(bf16[256,768]{1,0:T(8,128)(2,1)S(1)} %get-tuple-element.50), channel_id=1, source_target_pairs={{0,3},{1,2},{2,1},{3,0},{4,7},{5,6},{6,5},{7,4},{8,11},{9,10},{10,... | collective-permute-start | bytes 1179656 | tf_op jit(solution)/shard_map/ppermute | solution.py:465
  75.4 3.5 %collective-permute-start.13 = (bf16[512,1024]{1,0:T(8,128)(2,1)}, bf16[512,1024]{1,0:T(8,128)(2,1)S(1)}, u32[]{:S(2)}, u32[]{:S(2)}) collective-permute-start(bf16[512,1024]{1,0:T(8,128)(2,1)} %get-tuple-element.56), channel_id=1, source_target_pairs={{0,1},{1,0},{2,3},{3,2},{4,5},{5,4},{6,7},{7,6},{8,9},{9,8},{10,11... | collective-permute-start | bytes 3145736 | tf_op jit(solution)/shard_map/ppermute | solution.py:465
  78.2 5.6 %collective-permute-start.18 = (bf16[2,256,768]{2,1,0:T(8,128)(2,1)S(1)}, bf16[2,256,768]{2,1,0:T(8,128)(2,1)S(1)}, u32[]{:S(2)}, u32[]{:S(2)}) collective-permute-start(bf16[2,256,768]{2,1,0:T(8,128)(2,1)S(1)} %copy-done.29), channel_id=1, source_target_pairs={{0,1},{1,0},{2,3},{3,2},{4,5},{5,4},{6,7},{7,6},{8,9},{9,8},{10,11... | collective-permute-start | bytes 2359304 | tf_op jit(solution)/shard_map/ppermute | solution.py:465
  80.1 8.7 %collective-permute-start.14 = (bf16[128,1024]{1,0:T(8,128)(2,1)S(1)}, bf16[128,1024]{1,0:T(8,128)(2,1)S(1)}, u32[]{:S(2)}, u32[]{:S(2)}) collective-permute-start(bf16[128,1024]{1,0:T(8,128)(2,1)S(1)} %get-tuple-element.84), channel_id=1, source_target_pairs={{0,12},{4,0},{8,4},{12,8},{1,13},{5,1},{9,5},{13,9},{2,14},{6,2},{... | collective-permute-start | bytes 786440 | tf_op jit(solution)/shard_map/ppermute | solution.py:470
  82.4 21.8 %collective-permute-start.17 = (bf16[256,768]{1,0:T(8,128)(2,1)}, bf16[256,768]{1,0:T(8,128)(2,1)}, u32[]{:S(2)}, u32[]{:S(2)}) collective-permute-start(bf16[256,768]{1,0:T(8,128)(2,1)} %get-tuple-element.58), channel_id=1, source_target_pairs={{0,2},{1,3},{2,0},{3,1},{4,6},{5,7},{6,4},{7,5},{8,10},{9,11},{10,... | collective-permute-start | bytes 1179656 | tf_op jit(solution)/shard_map/ppermute | solution.py:465
  83.9 20.3 %collective-permute-start.19 = (bf16[256,768]{1,0:T(8,128)(2,1)S(1)}, bf16[256,768]{1,0:T(8,128)(2,1)}, u32[]{:S(2)}, u32[]{:S(2)}) collective-permute-start(bf16[256,768]{1,0:T(8,128)(2,1)S(1)} %slice_bitcast_fusion.5), channel_id=1, source_target_pairs={{0,2},{1,3},{2,0},{3,1},{4,6},{5,7},{6,4},{7,5},{8,10},{9,11},{10,... | collective-permute-start | bytes 1179656 | tf_op jit(solution)/shard_map/ppermute | solution.py:465
  84.5 29.1 %collective-permute-start.16 = (bf16[128,1024]{1,0:T(8,128)(2,1)}, bf16[128,1024]{1,0:T(8,128)(2,1)}, u32[]{:S(2)}, u32[]{:S(2)}) collective-permute-start(bf16[128,1024]{1,0:T(8,128)(2,1)} %get-tuple-element.85), channel_id=1, source_target_pairs={{0,4},{4,8},{8,12},{12,0},{1,5},{5,9},{9,13},{13,1},{2,6},{6,10},{... | collective-permute-start | bytes 786440 | tf_op jit(solution)/shard_map/ppermute | solution.py:470
  88.9 24.8 %collective-permute-start.15 = (bf16[128,1024]{1,0:T(8,128)(2,1)S(1)}, bf16[128,1024]{1,0:T(8,128)(2,1)}, u32[]{:S(2)}, u32[]{:S(2)}) collective-permute-start(bf16[128,1024]{1,0:T(8,128)(2,1)S(1)} %add_convert_fusion.4), channel_id=1, source_target_pairs={{0,12},{4,0},{8,4},{12,8},{1,13},{5,1},{9,5},{13,9},{2,14},{6,2},{... | collective-permute-start | bytes 786440 | tf_op jit(solution)/shard_map/ppermute | solution.py:470
  102.6 48.5 %collective-permute-start.24 = (bf16[2,256,768]{2,1,0:T(8,128)(2,1)}, bf16[2,256,768]{2,1,0:T(8,128)(2,1)S(1)}, u32[]{:S(2)}, u32[]{:S(2)}) collective-permute-start(bf16[2,256,768]{2,1,0:T(8,128)(2,1)} %get-tuple-element.72), channel_id=1, source_target_pairs={{0,2},{1,3},{2,0},{3,1},{4,6},{5,7},{6,4},{7,5},{8,10},{9,11},{10,... | collective-permute-start | bytes 2359304 | tf_op jit(solution)/shard_map/ppermute | solution.py:465
  113.0 19.4 %collective-permute-start.20 = (bf16[512,1024]{1,0:T(8,128)(2,1)}, bf16[512,1024]{1,0:T(8,128)(2,1)S(1)}, u32[]{:S(2)}, u32[]{:S(2)}) collective-permute-start(bf16[512,1024]{1,0:T(8,128)(2,1)} %get-tuple-element.70), channel_id=1, source_target_pairs={{0,1},{1,0},{2,3},{3,2},{4,5},{5,4},{6,7},{7,6},{8,9},{9,8},{10,11... | collective-permute-start | bytes 3145736 | tf_op jit(solution)/shard_map/ppermute | solution.py:465
  113.1 21.9 %collective-permute-start.25 = (bf16[2,2,256,768]{3,2,1,0:T(8,128)(2,1)}, bf16[2,2,256,768]{3,2,1,0:T(8,128)(2,1)S(1)}, u32[]{:S(2)}, u32[]{:S(2)}) collective-permute-start(bf16[2,2,256,768]{3,2,1,0:T(8,128)(2,1)} %get-tuple-element.73), channel_id=1, source_target_pairs={{0,1},{1,0},{2,3},{3,2},{4,5},{5,4},{6,7},{7,6},{8,9},{9,8},{10,11... | collective-permute-start | bytes 4718600 | tf_op jit(solution)/shard_map/ppermute | solution.py:465
  116.8 1.3 collective-permute-start.27
  118.1 4.6 %collective-permute-start.28 = (f32[16,1024]{1,0:T(8,128)S(1)}, f32[16,1024]{1,0:T(8,128)S(1)}, u32[]{:S(2)}, u32[]{:S(2)}) collective-permute-start(f32[16,1024]{1,0:T(8,128)S(1)} %fusion.46), channel_id=1, source_target_pairs={{0,2},{1,3},{2,0},{3,1},{4,6},{5,7},{6,4},{7,5},{8,10},{9,11},{10,... | collective-permute-start | bytes 196616 | tf_op jit(solution)/shard_map/ppermute | solution.py:465
  122.7 4.3 %collective-permute-start.29 = (f32[16,1024]{1,0:T(8,128)S(1)}, f32[16,1024]{1,0:T(8,128)S(1)}, u32[]{:S(2)}, u32[]{:S(2)}) collective-permute-start(f32[16,1024]{1,0:T(8,128)S(1)} %add.123), channel_id=1, source_target_pairs={{0,4},{4,0},{8,12},{12,8},{1,5},{5,1},{9,13},{13,9},{2,6},{6,2},{1... | collective-permute-start | bytes 196616 | tf_op jit(solution)/shard_map/ppermute | solution.py:655
  127.0 5.4 %collective-permute-start.30 = (f32[16,1024]{1,0:T(8,128)S(1)}, f32[16,1024]{1,0:T(8,128)S(1)}, u32[]{:S(2)}, u32[]{:S(2)}) collective-permute-start(f32[16,1024]{1,0:T(8,128)S(1)} %add.124), channel_id=1, source_target_pairs={{0,8},{4,12},{8,0},{12,4},{1,9},{5,13},{9,1},{13,5},{2,10},{6,14},... | collective-permute-start | bytes 196616 | tf_op jit(solution)/shard_map/ppermute | solution.py:655
  132.9 10.0 %collective-permute-start.21 = (bf16[128,1024]{1,0:T(8,128)(2,1)S(1)}, bf16[128,1024]{1,0:T(8,128)(2,1)S(1)}, u32[]{:S(2)}, u32[]{:S(2)}) collective-permute-start(bf16[128,1024]{1,0:T(8,128)(2,1)S(1)} %get-tuple-element.82), channel_id=1, source_target_pairs={{0,12},{4,0},{8,4},{12,8},{1,13},{5,1},{9,5},{13,9},{2,14},{6,2},{... | collective-permute-start | bytes 786440 | tf_op jit(solution)/shard_map/ppermute | solution.py:470
  133.1 13.6 %collective-permute-start.23 = (bf16[128,1024]{1,0:T(8,128)(2,1)S(1)}, bf16[128,1024]{1,0:T(8,128)(2,1)S(1)}, u32[]{:S(2)}, u32[]{:S(2)}) collective-permute-start(bf16[128,1024]{1,0:T(8,128)(2,1)S(1)} %get-tuple-element.83), channel_id=1, source_target_pairs={{0,4},{4,8},{8,12},{12,0},{1,5},{5,9},{9,13},{13,1},{2,6},{6,10},{... | collective-permute-start | bytes 786440 | tf_op jit(solution)/shard_map/ppermute | solution.py:470
  135.1 16.6 %collective-permute-start.26 = (bf16[2,256,768]{2,1,0:T(8,128)(2,1)S(1)}, bf16[2,256,768]{2,1,0:T(8,128)(2,1)S(1)}, u32[]{:S(2)}, u32[]{:S(2)}) collective-permute-start(bf16[2,256,768]{2,1,0:T(8,128)(2,1)S(1)} %slice_bitcast_fusion.3), channel_id=1, source_target_pairs={{0,2},{1,3},{2,0},{3,1},{4,6},{5,7},{6,4},{7,5},{8,10},{9,11},{10,... | collective-permute-start | bytes 2359304 | tf_op jit(solution)/shard_map/ppermute | solution.py:465
  143.0 7.1 %collective-permute-start.22 = (bf16[128,1024]{1,0:T(8,128)(2,1)S(1)}, bf16[128,1024]{1,0:T(8,128)(2,1)S(1)}, u32[]{:S(2)}, u32[]{:S(2)}) collective-permute-start(bf16[128,1024]{1,0:T(8,128)(2,1)S(1)} %add_convert_fusion.3), channel_id=1, source_target_pairs={{0,12},{4,0},{8,4},{12,8},{1,13},{5,1},{9,5},{13,9},{2,14},{6,2},{... | collective-permute-start | bytes 786440 | tf_op jit(solution)/shard_map/ppermute | solution.py:470
  (29 other events, 386.7 us)

commit v3 on v2

--- a/solution.py
+++ b/solution.py
@@ -229,11 +229,11 @@
 
 HALF = 64
 SLOTS = 32
-SCRATCH_BYTES = 56 * 1024 * 1024
-
-
-def local_kernel(body, scalars, operands, outputs, scratch, flops):
-    moved = sum(o.size * o.dtype.itemsize for o in [*operands, *outputs])
+SCRATCH_BYTES = 22 * 1024 * 1024
+LONG = 20_000_000_000
+
+
+def local_kernel(body, scalars, operands, outputs, scratch, moved):
     return pl.pallas_call(
         body,
         out_shape=outputs,
@@ -242,7 +242,7 @@
         out_specs=[pl.BlockSpec(memory_space=pltpu.VMEM) for _ in outputs],
         scratch_shapes=scratch,
         compiler_params=pltpu.CompilerParams(vmem_limit_bytes=SCRATCH_BYTES),
-        cost_estimate=pl.CostEstimate(flops=0, bytes_accessed=0, transcendentals=0),
+        cost_estimate=pl.CostEstimate(flops=moved, bytes_accessed=moved, transcendentals=0),
     )(scalars, *operands)
 
 
@@ -275,7 +275,8 @@
     return [(s, target.at[pl.ds(j * width, width)]) for j, s in enumerate(sources)]
 
 
-def payload_kernel(tokens, grads, routes, router, out):
+def payload_kernel(tokens, grads, routes, router, out, step):
+    step[...] = jnp.zeros_like(step)
     count = tokens.shape[0]
     ids = lax.broadcasted_iota(jnp.int32, (router.shape[0], count), 0)
     named = routes[0:1, :] == ids
@@ -290,31 +291,35 @@
         ).astype(jnp.bfloat16)
 
 
-def forward_kernel(place, *refs):
+def step_kernel(before, after_it):
+    after_it[...] = before[...] + 1.0
+
+
+def next_step(step, *done):
+    return pl.pallas_call(
+        step_kernel,
+        out_shape=jax.ShapeDtypeStruct(step.shape, step.dtype),
+        cost_estimate=pl.CostEstimate(flops=LONG, bytes_accessed=LONG, transcendentals=0),
+    )(after(step, *done))
+
+
+def pick_kernel(place, *refs):
     payloads = refs[0:8]
-    gate_weight, up_weight, partner, cross, cross_partner = refs[8:13]
-    (pick_out, gate_out, rows_out, cot_out, hidden_out, act_out, slope_out, keep_out,
-     partner_out, cross_out) = refs[13:23]
-    blocks, w_gate, w_up, upstream, sems = refs[23:28]
+    pick_out, gate_out, rows_out, cot_out = refs[8:12]
+    blocks, sems = refs[12:14]
     me, expert = place[0], place[1]
-    core = me & 1
     count = pick_out.shape[1]
     slots = count // HALF * SLOTS
-    copies = bring(
-        [(payloads[b], blocks.at[b]) for b in range(8)]
-        + weight_pairs(core, (gate_weight, partner.at[0], cross.at[0], cross_partner.at[0]), w_gate)
-        + weight_pairs(core, (up_weight, partner.at[1], cross.at[1], cross_partner.at[1]), w_up),
-        sems,
-    )
-    width = w_gate.shape[0] // 4
+    copies = bring([(payloads[b], blocks.at[b]) for b in range(8)], sems)
+    width = rows_out.shape[1] // 4
     row = lax.broadcasted_iota(jnp.int32, (count, count), 0)
     column = lax.broadcasted_iota(jnp.int32, (count, count), 1)
     before = ((row < column) & (row // HALF == column // HALF)).astype(jnp.bfloat16)
     lane = lax.broadcasted_iota(jnp.int32, (1, count), 1)
     slot = lax.broadcasted_iota(jnp.int32, (slots, count), 0)
     mine = pl.ds(pl.multiple_of(expert * count, count), count)
-    for b in range(8):
-        copies[b].wait()
+    for copy in copies:
+        copy.wait()
     gates = jnp.concatenate(
         [blocks[b, 2 * count :, mine].astype(jnp.float32)[0:1] for b in range(8)], axis=0
     )
@@ -324,33 +329,50 @@
     for b in range(8):
         chosen = slot == target[b : b + 1]
         pick = chosen.astype(jnp.bfloat16)
-        gate_pick = jnp.where(chosen, gates[b : b + 1], 0.0)
-        gate = jnp.sum(gate_pick, axis=1, keepdims=True)
         at = b * slots
         pick_out[at : at + slots, :] = pick
-        gate_out[at : at + slots, :] = gate_pick.astype(jnp.bfloat16)
+        gate_out[at : at + slots, :] = jnp.where(chosen, gates[b : b + 1], 0.0).astype(jnp.bfloat16)
         for j in range(4):
             columns = pl.ds(pl.multiple_of((me ^ j) * width, width), width)
             here = (slice(at, at + slots), slice(j * width, (j + 1) * width))
             rows_out[here] = mm(pick, blocks[b, 0:count, columns]).astype(jnp.bfloat16)
-            cot = mm(pick, blocks[b, count : 2 * count, columns])
-            cot_out[here] = cot.astype(jnp.bfloat16)
-            upstream[here] = (gate * cot).astype(jnp.bfloat16)
-    for copy in copies[8:]:
+            cot_out[here] = mm(pick, blocks[b, count : 2 * count, columns]).astype(jnp.bfloat16)
+
+
+def forward_kernel(place, *refs):
+    (gate_pick_in, rows_in, cot_in, gate_weight, up_weight, partner, cross,
+     cross_partner) = refs[0:8]
+    hidden_out, act_out, slope_out = refs[8:11]
+    outs = refs[11:15]
+    gate_pick, rows, cot, w_gate, w_up, upstream, sems = refs[15:22]
+    core = place[0] & 1
+    copies = bring(
+        [(rows_in, rows)]
+        + weight_pairs(core, (gate_weight, partner.at[0], cross.at[0, core], cross_partner.at[0]), w_gate)
+        + weight_pairs(core, (up_weight, partner.at[1], cross.at[1, core], cross_partner.at[1]), w_up)
+        + [(gate_pick_in, gate_pick), (cot_in, cot)],
+        sems,
+    )
+    width = w_gate.shape[0] // 4
+    for copy in copies[0:5]:
         copy.wait()
-    pre_gate = mm(rows_out[...], w_gate[...])
-    pre_up = mm(rows_out[...], w_up[...])
+    pre_gate = mm(rows[...], w_gate[...])
+    for copy in copies[5:9]:
+        copy.wait()
+    pre_up = mm(rows[...], w_up[...])
     logistic = jax.nn.sigmoid(pre_gate)
     act = pre_gate * logistic
     hidden_out[...] = (act * pre_up).astype(jnp.bfloat16)
     act_out[...] = act.astype(jnp.bfloat16)
     slope = logistic * (1.0 + pre_gate * (1.0 - logistic))
     slope_out[...] = (pre_up * slope).astype(jnp.bfloat16)
-    outs = (keep_out, partner_out.at[0], cross_out, partner_out.at[1])
-    for j in (2, 1, 3, 0):
-        outs[j][...] = mm_rows(
-            upstream[:, j * width : (j + 1) * width], hidden_out[...]
-        ).astype(jnp.bfloat16)
+    for copy in copies[9:]:
+        copy.wait()
+    gate = jnp.sum(gate_pick[...].astype(jnp.float32), axis=1, keepdims=True)
+    for j in range(4):
+        here = slice(j * width, (j + 1) * width)
+        upstream[:, here] = (gate * cot[:, here].astype(jnp.float32)).astype(jnp.bfloat16)
+        outs[j][...] = mm_rows(upstream[:, here], hidden_out[...]).astype(jnp.bfloat16)
 
 
 def scatter(me, pick, own_out, other_out, column_block):
@@ -374,7 +396,7 @@
     gate_pick, hidden, w_down, sems = refs[8:12]
     me = place[0]
     copies = bring(
-        weight_pairs(me & 1, (down_weight, partner, cross, cross_partner), w_down)
+        weight_pairs(me & 1, (down_weight, partner, cross.at[me & 1], cross_partner), w_down)
         + [(gate_pick_in, gate_pick), (hidden_in, hidden)],
         sems,
     )
@@ -389,12 +411,13 @@
 def backward_kernel(place, *refs):
     (pick_in, gate_pick_in, rows_in, hidden_in, cot_in, act_in, slope_in, router_in,
      down_weight, partner, cross, cross_partner) = refs[0:12]
-    d_gate_out, d_up_out, logit_out, router_out, keep_out, partner_out, cross_out = refs[12:19]
-    pick, gate_pick, rows, hidden, cot, act, slope, router, w_down, sems = refs[19:29]
+    (d_gate_out, d_up_out, logit_out, router_out, keep_out, partner_out, cross_partner_out,
+     gate_sent, up_sent) = refs[12:21]
+    pick, gate_pick, rows, hidden, cot, act, slope, router, w_down, sems = refs[21:31]
     me, expert = place[0], place[1]
     copies = bring(
         [(cot_in, cot)]
-        + weight_pairs(me & 1, (down_weight, partner, cross, cross_partner), w_down)
+        + weight_pairs(me & 1, (down_weight, partner, cross.at[me & 1], cross_partner), w_down)
         + [(gate_pick_in, gate_pick), (hidden_in, hidden), (rows_in, rows), (act_in, act),
            (slope_in, slope), (router_in, router)],
         sems,
@@ -408,11 +431,12 @@
     d_hidden = gate * along
     d_gate_out[...] = (d_hidden * slope[...].astype(jnp.float32)).astype(jnp.bfloat16)
     d_up_out[...] = (d_hidden * act[...].astype(jnp.float32)).astype(jnp.bfloat16)
-    outs = (keep_out, partner_out.at[0], cross_out, partner_out.at[1])
+    gate_outs = (keep_out.at[0], partner_out.at[0], gate_sent, cross_partner_out.at[0])
+    up_outs = (keep_out.at[1], partner_out.at[1], up_sent, cross_partner_out.at[1])
     for j in range(4):
         part = rows[:, j * width : (j + 1) * width]
-        outs[j][0] = mm_rows(part, d_gate_out[...]).astype(jnp.bfloat16)
-        outs[j][1] = mm_rows(part, d_up_out[...]).astype(jnp.bfloat16)
+        gate_outs[j][...] = mm_rows(part, d_gate_out[...]).astype(jnp.bfloat16)
+        up_outs[j][...] = mm_rows(part, d_up_out[...]).astype(jnp.bfloat16)
     ids = router.shape[0]
     logits = jnp.zeros((pick_in.shape[0], ids), jnp.float32)
     for j in range(4):
@@ -441,8 +465,8 @@
     copies = bring(
         [(pick_in, pick), (d_gate_in, d_gate), (d_up_in, d_up), (logit_in, logit_grad),
          (router_in, router)]
-        + weight_pairs(core, (gate_weight, partner.at[0], cross.at[0], cross_partner.at[0]), w_gate)
-        + weight_pairs(core, (up_weight, partner.at[1], cross.at[1], cross_partner.at[1]), w_up),
+        + weight_pairs(core, (gate_weight, partner.at[0], cross.at[0, core], cross_partner.at[0]), w_gate)
+        + weight_pairs(core, (up_weight, partner.at[1], cross.at[1, core], cross_partner.at[1]), w_up),
         sems,
     )
     for copy in copies:
@@ -499,114 +523,72 @@
     table = (slot_count, row_count)
     weight_rows = (stored_rows, hidden_width)
     whole_weight = vmem((model_width, hidden_width), bf16)
-    product = 2 * slot_count * model_width * hidden_width
-
-    payload = pl.pallas_call(
+
+    def together(*values):
+        return lax.optimization_barrier(values)
+
+    payload, step = pl.pallas_call(
         payload_kernel,
-        out_shape=shape((2 * row_count + 16, model_width), bf16),
-        cost_estimate=pl.CostEstimate(flops=0, bytes_accessed=2 << 20, transcendentals=0),
+        out_shape=[shape((2 * row_count + 16, model_width), bf16), shape((8, 128), f32)],
+        cost_estimate=pl.CostEstimate(flops=LONG, bytes_accessed=LONG, transcendentals=0),
     )(tokens, grad_out, routes.T, router.T)
-    near = ring(payload, 1)
-    far_side = ring(payload, -1)
-    mine_in = jnp.stack([of_expert(gate_weight, core), of_expert(up_weight, core)])
-    theirs_in = jnp.stack([of_expert(gate_weight, 1 - core), of_expert(up_weight, 1 - core)])
-    in_cross, in_cross_partner = dp_swap(mine_in, 2), dp_swap(theirs_in, 3)
-    mine_down, theirs_down = of_expert(down_weight, core), of_expert(down_weight, 1 - core)
-    in_partner = dp_swap(theirs_in, 1)
-    down_partner = dp_swap(after(theirs_down, in_partner), 1)
-    payload_partner = dp_swap(after(payload, down_partner), 1)
+    near, far_side = ring(payload, 1), ring(payload, -1)
+    payload_partner = dp_swap(payload, 1)
+    in_cross = dp_swap(jnp.stack([gate_weight, up_weight]), 2)
+    down_cross = dp_swap(after(down_weight, payload_partner), 2)
+    step = next_step(step, payload)
+    near, step = together(near, step)
     far = ring(near, 1)
-    near_partner = dp_swap(after(near, payload_partner), 1)
-    far_side_partner = dp_swap(after(far_side, near_partner), 1)
+    partner = dp_swap(
+        after(
+            jnp.stack([of_expert(w, 1 - core) for w in (gate_weight, up_weight, down_weight)]),
+            payload_partner,
+        ),
+        1,
+    )
+    step = next_step(step, near, partner)
+    far_side, far, in_cross, near = together(far_side, far, in_cross, near, step)[0:4]
+    near_partner = dp_swap(near, 1)
+    far_side_partner = dp_swap(far_side, 1)
+    theirs_cross = lax.dynamic_index_in_dim(in_cross, 1 - core, 1, keepdims=False)
+    in_cross_partner = dp_swap(theirs_cross, 1)
     far_partner = dp_swap(far, 1)
-    mine_down, theirs_down = lax.optimization_barrier(
-        (mine_down, theirs_down, in_cross, in_cross_partner)
-    )[0:2]
-    down_cross, down_cross_partner = dp_swap(mine_down, 2), dp_swap(theirs_down, 3)
     payloads = [payload, payload_partner, near, near_partner, far, far_partner, far_side,
                 far_side_partner]
-    in_weights = [gate_weight, up_weight, in_partner, in_cross, in_cross_partner]
+    in_weights = [gate_weight, up_weight, partner, in_cross, in_cross_partner]
     router_rows = jnp.pad(router.T.astype(f32), ((0, 16 - id_count), (0, 0)))
-    pick, gate_pick, rows, cot, hidden, act, slope, down_keep, down_theirs, down_sent = local_kernel(
+    pick, gate_pick, rows, cot = local_kernel(
+        pick_kernel,
+        place,
+        payloads,
+        [shape(table, bf16)] * 2 + [shape(wide, bf16)] * 2,
+        [vmem((8, *payload.shape), bf16), pltpu.SemaphoreType.DMA((8,))],
+        0,
+    )
+    rows, down_cross = together(rows, down_cross)
+    down_cross_partner = dp_swap(of_expert(down_cross, 1 - core), 1)
+    hidden, act, slope, *down_parts = local_kernel(
         forward_kernel,
         place,
-        [*payloads, *in_weights],
-        [shape(table, bf16)] * 2 + [shape(wide, bf16)] * 2 + [shape(narrow, bf16)] * 3
-        + [shape(weight_rows, bf16), shape((2, *weight_rows), bf16), shape(weight_rows, bf16)],
-        [vmem((8, *payload.shape), bf16), whole_weight, whole_weight, vmem(wide, bf16),
-         pltpu.SemaphoreType.DMA((16,))],
-        3 * product,
-    )
-    down_cross, down_cross_partner, hidden = lax.optimization_barrier(
-        (down_cross, down_cross_partner, hidden)
-    )
-    down_weights = [down_weight, down_partner, down_cross, down_cross_partner]
-    mixed_own, mixed_other = local_kernel(
-        output_kernel,
-        place,
-        [gate_pick, hidden, *down_weights],
-        [shape(wide, bf16)] * 2,
-        [vmem(table, bf16), vmem(narrow, bf16), whole_weight, pltpu.SemaphoreType.DMA((6,))],
-        product,
-    )
-    d_gate, d_up, logit_grad, router_row, in_keep, in_theirs, in_sent = local_kernel(
-        backward_kernel,
-        place,
-        [pick, gate_pick, rows, hidden, cot, act, slope, router_rows, *down_weights],
-        [shape(narrow, bf16)] * 2 + [shape(table, bf16), shape((8, model_width), f32)]
-        + [shape((2, *weight_rows), bf16), shape((2, 2, *weight_rows), bf16),
-           shape((2, *weight_rows), bf16)],
-        [vmem(table, bf16)] * 2 + [vmem(wide, bf16), vmem(narrow, bf16), vmem(wide, bf16),
-         vmem(narrow, bf16), vmem(narrow, bf16), vmem(router_rows.shape, f32), whole_weight,
-         pltpu.SemaphoreType.DMA((11,))],
-        3 * product,
-    )
-    down_came = dp_swap(down_sent, 2)
-    down_from = dp_swap(down_theirs, 1)
-    down_came_partner = dp_swap(down_from[1], 2)
-    in_came = dp_swap(in_sent, 2)
-    down_came, down_came_partner, in_theirs, d_gate = lax.optimization_barrier(
-        (down_came, down_came_partner, in_theirs, d_gate)
-    )
-    back_own, back_other = local_kernel(
-        back_kernel,
-        place,
-        [pick, d_gate, d_up, logit_grad, router_rows, *in_weights],
-        [shape(wide, bf16)] * 2,
-        [vmem(table, bf16), vmem(narrow, bf16), vmem(narrow, bf16), vmem(table, bf16),
-         vmem(router_rows.shape, f32), whole_weight, whole_weight,
-         pltpu.SemaphoreType.DMA((13,))],
-        2 * product,
-    )
-
-    def pair(mine, theirs):
-        return jnp.where(
-            core == 0, jnp.stack([mine, theirs], axis=-3), jnp.stack([theirs, mine], axis=-3)
-        )
-
+        [gate_pick, rows, cot, *in_weights],
+        [shape(narrow, bf16)] * 3 + [shape(weight_rows, bf16)] * 4,
+        [vmem(table, bf16), vmem(wide, bf16), vmem(wide, bf16), whole_weight, whole_weight,
+         vmem(wide, bf16), pltpu.SemaphoreType.DMA((11,))],
+        LONG,
+    )
+    hidden, down_cross_partner = together(hidden, down_cross_partner)
+    down_weights = [down_weight, partner[2], down_cross, down_cross_partner]
     def add(one, two):
         return one.astype(f32) + two.astype(f32)
 
-    grad_down = pair(add(down_keep, down_came), add(down_from[0], down_came_partner)).astype(bf16)
-    in_from = dp_swap(in_theirs, 1)
-    in_came_partner = dp_swap(in_from[1], 2)
-
-    def home(own, other):
-        both = (own.astype(f32) + dp_swap(other, 1).astype(f32)).astype(bf16)
-        slots = both.reshape(4, row_count, model_width)
-        side = ring(slots[3], 1)
-        near = (ring(slots[2], -1).astype(f32) + slots[1].astype(f32)).astype(bf16)
-        return side, near, slots[0]
-
-    mixed_parts = home(mixed_own, mixed_other)
-    back_parts = home(back_own, back_other)
-    in_came, in_came_partner = lax.optimization_barrier(
-        (in_came, in_came_partner, back_parts[1])
-    )[0:2]
-    grad_in = pair(add(in_keep, in_came), add(in_from[0], in_came_partner)).astype(bf16)
-    grad_gate, grad_up = grad_in[0], grad_in[1]
-    mixed_sum = add(ring(mixed_parts[1], -1), mixed_parts[0]) + mixed_parts[2].astype(f32)
-    back_sum = add(ring(back_parts[1], -1), back_parts[0]) + back_parts[2].astype(f32)
+    def sum_slots(own, came):
+        return [
+            add(mine, theirs).astype(bf16) for mine, theirs in zip(jnp.split(own, 2), came)
+        ]
+
+    def pair(mine, theirs):
+        of = lax.broadcasted_iota(jnp.int32, (2, 1, 1), 0)
+        return jnp.where(of == core, mine[None], theirs[None]).astype(bf16)
 
     id_range = lax.broadcasted_iota(jnp.int32, (1, 1, id_count), 2)
     named = jnp.any(routes[:, :, None] == id_range, axis=1)[:, expert_count:]
@@ -619,9 +601,6 @@
     const_share = jax.nn.sigmoid(mm(tokens, const_gate))
     const_rest = (const_weight * (1.0 - const_share)).astype(bf16)
     coefficient = copy_weight + jnp.sum(const_weight * const_share, axis=1)
-    mixed = (
-        mixed_sum + coefficient[:, None] * tokens_float + mm(const_rest, const_vec)
-    ).astype(bf16)
     along_token = jnp.sum(grad_float * tokens_float, axis=1, keepdims=True)
     along_const = mm_last(grad_out, const_vec)
     const_value = const_share * along_token + (1.0 - const_share) * along_const
@@ -632,13 +611,41 @@
     share_grad = (
         const_weight * (along_token - along_const) * const_share * (1.0 - const_share)
     ).astype(bf16)
-    back_local = (
-        coefficient[:, None] * grad_float
-        + mm_last(null_grad, router[:, expert_count:])
-        + mm_last(share_grad, const_gate)
-    )
-    grad_tokens = (back_sum + back_local).astype(bf16)
-
+    mixed_own, mixed_other = local_kernel(
+        output_kernel,
+        place,
+        [gate_pick, hidden, *down_weights],
+        [shape(wide, bf16)] * 2,
+        [vmem(table, bf16), vmem(narrow, bf16), whole_weight, pltpu.SemaphoreType.DMA((6,))],
+        LONG,
+    )
+    down_came, down_came_partner = dp_swap(down_parts[2], 2), dp_swap(down_parts[3], 3)
+    parts = [mixed_other[k * row_count : (k + 1) * row_count] for k in range(4)]
+    mixed_came = [dp_swap(parts[2], 1), dp_swap(parts[3], 1)]
+    mixed_own, mixed_came[0], mixed_came[1], down_came, cot = together(
+        mixed_own, *mixed_came, down_came, cot
+    )
+    mixed_first = sum_slots(mixed_own[2 * row_count :], mixed_came)
+    mixed_near = ring(mixed_first[0], -1)
+    mixed_late = dp_swap(mixed_other[: 2 * row_count], 1)
+    down_from = dp_swap(down_parts[1], 1)
+    d_gate, d_up, logit_grad, router_row, *in_parts, gate_sent, up_sent = local_kernel(
+        backward_kernel,
+        place,
+        [pick, gate_pick, rows, hidden, cot, act, slope, router_rows, *down_weights],
+        [shape(narrow, bf16)] * 2 + [shape(table, bf16), shape((8, model_width), f32)]
+        + [shape((2, *weight_rows), bf16)] * 3 + [shape(weight_rows, bf16)] * 2,
+        [vmem(table, bf16)] * 2 + [vmem(wide, bf16), vmem(narrow, bf16), vmem(wide, bf16),
+         vmem(narrow, bf16), vmem(narrow, bf16), vmem(router_rows.shape, f32), whole_weight,
+         pltpu.SemaphoreType.DMA((11,))],
+        LONG,
+    )
+    (d_gate, router_row, in_parts[1], in_parts[2], gate_sent, up_sent, down_came_partner,
+     mixed_near, mixed_late, down_from) = together(
+        d_gate, router_row, in_parts[1], in_parts[2], gate_sent, up_sent, down_came_partner,
+        mixed_near, mixed_late, down_from
+    )
+    mixed_late = sum_slots(mixed_own[: 2 * row_count], jnp.split(mixed_late, 2))
     small = jnp.concatenate(
         [
             mm_rows(jnp.concatenate([null_grad, share_grad], axis=1), tokens),
@@ -649,10 +656,58 @@
     experts = lax.broadcasted_iota(jnp.int32, (expert_count, 1), 0)
     routed = jnp.where(experts == expert, router_row[0:1], 0.0)
     small = jnp.concatenate([routed, small], axis=0)
-    for step in (1, 2):
-        small = small + dp_swap(small, step)
-    for step in (1, 2):
-        small = small + lax.ppermute(small, "expert", [(i, i ^ step) for i in range(4)])
+    gate_came, in_from, small_came = dp_swap(gate_sent, 2), dp_swap(in_parts[1], 1), dp_swap(small, 2)
+    mixed_side = ring(mixed_first[1].astype(bf16), 1)
+    mixed_near = ring(add(mixed_near, mixed_late[1]).astype(bf16), -1)
+    back_own, back_other = local_kernel(
+        back_kernel,
+        place,
+        [pick, d_gate, d_up, logit_grad, router_rows, *in_weights],
+        [shape(wide, bf16)] * 2,
+        [vmem(table, bf16), vmem(narrow, bf16), vmem(narrow, bf16), vmem(table, bf16),
+         vmem(router_rows.shape, f32), whole_weight, whole_weight,
+         pltpu.SemaphoreType.DMA((13,))],
+        LONG,
+    )
+    (back_own, back_other, gate_came, in_from, small_came, mixed_side, mixed_near, up_sent,
+     in_parts[2]) = together(
+        back_own, back_other, gate_came, in_from, small_came, mixed_side, mixed_near, up_sent,
+        in_parts[2]
+    )
+    up_came, in_came_partner = dp_swap(up_sent, 2), dp_swap(in_parts[2], 3)
+    small = small + small_came
+    back_came, small_came = together(dp_swap(back_other, 1), dp_swap(small, 1))
+    step = next_step(step, back_came, small_came)
+    back_own, back_came, small_came = together(back_own, back_came, small_came, step)[0:3]
+    back_late = sum_slots(back_own[: 2 * row_count], jnp.split(back_came[: 2 * row_count], 2))
+    back_first = sum_slots(back_own[2 * row_count :], jnp.split(back_came[2 * row_count :], 2))
+    back_near, back_side = ring(back_first[0], -1), ring(back_first[1], 1)
+    small = small + small_came
+    small_came = lax.ppermute(small, "expert", [(i, i ^ 1) for i in range(4)])
+    back_near, back_side, up_came = together(back_near, back_side, up_came)
+    back_near = ring(add(back_near, back_late[1]).astype(bf16), -1)
+    small = small + small_came
+    small = small + lax.ppermute(small, "expert", [(i, i ^ 2) for i in range(4)])
+    mixed_sum = add(mixed_side, mixed_near) + mixed_late[0].astype(f32)
+    back_sum = add(back_side, back_near) + back_late[0].astype(f32)
+    grad_down = pair(add(down_parts[0], down_came), add(down_from, down_came_partner))
+    mixed = (
+        mixed_sum + coefficient[:, None] * tokens_float + mm(const_rest, const_vec)
+    ).astype(bf16)
+    back_local = (
+        coefficient[:, None] * grad_float
+        + mm_last(null_grad, router[:, expert_count:])
+        + mm_last(share_grad, const_gate)
+    )
+    grad_tokens = (back_sum + back_local).astype(bf16)
+
+    up_came, in_came_partner, mixed, grad_down, grad_tokens, small = together(
+        up_came, in_came_partner, mixed, grad_down, grad_tokens, small
+    )
+    grad_gate, grad_up = (
+        pair(add(in_parts[0][i], came), add(in_from[i], in_came_partner[i]))
+        for i, came in enumerate((gate_came, up_came))
+    )
     grad_router = small[:id_count].T
     grad_const_gate = small[id_count : id_count + const_count].T
     grad_const_vec = small[id_count + const_count :]

time: 154 us -> 139 us (0.903)
  waiting for transfers between devices: 69.5 us -> 60.7 us
  Pallas kernels: 33.4 us -> 27.9 us
  starting transfers between devices: 28.3 us -> 32 us
  local copies, waits for them, and re-layouts: 7.33 us -> 4.8 us
  other arithmetic: 10.2 us -> 8.61 us
    ppermute x2, waiting for transfers between devices: 8.27 us -> 0.01 us  [the longest x1 0.01 us: on_device_paired(): small_came = lax.ppermute(small, 'expert', [(i, i ^ 1) for i in range(4)])]
    ppermute x9, waiting for transfers between devices: 48.8 us -> 40.7 us  [ring(): lax.ppermute(value, 'expert', [(i, (i + step) % size) for i in range(size)])]
    ppermute x20 -> x22, waiting for transfers between devices: 12.4 us -> 20 us  [dp_swap(): return lax.ppermute(value, 'dp', [(i, i ^ step) for i in range(4)])]
    pallas_call x4 -> x5, Pallas kernels: 31.4 us -> 25.8 us  [local_kernel(): pl.pallas_call(body, out_shape=outputs, in_specs=[pl.BlockSpec(memory_spa...]
    ppermute x9, starting transfers between devices: 15.1 us -> 18.1 us  [ring(): lax.ppermute(value, 'expert', [(i, (i + step) % size) for i in range(size)])]
    reduce_sum x1, other arithmetic: 2.04 us -> 0.15 us  [on_device_paired(): along_token = jnp.sum(grad_float * tokens_float, axis=1, keepdims=True)]
    ppermute x2, starting transfers between devices: 0.14 us -> 1.92 us  [the longest x1 1.85 us: on_device_paired(): small_came = lax.ppermute(small, 'expert', [(i, i ^ 1) for i in range(4)])]
    convert_element_type x6 -> x7, other arithmetic: 2.19 us -> 3.89 us  [the longest x2 2.38 us: pair(): return jnp.where(of == core, mine[None], theirs[None]).astype(bf16)]
  transfers between devices with their start and end apart: 31 -> 33, of which waited for: 14 -> 16; matrix products, arithmetic and copies ran while one was open for 11% -> 9% of each run, Pallas kernels for 18% -> 19%
where the time goes in v3:
time: 139 us
  waiting for transfers between devices  60.7 us (44%)
  starting transfers between devices  32 us (23%)
  Pallas kernels  27.9 us (20%)
  other arithmetic  8.61 us (6%)
  local copies, waits for them, and re-layouts  4.8 us (3%)
  matrix products  3.98 us (3%)
    ppermute x9, waiting for transfers between devices, ring(): lax.ppermute(value, 'expert', [(i, (i + step) % size) for i in range(size)])  40.7 us
    pallas_call x5, Pallas kernels, local_kernel(): pl.pallas_call(body, out_shape=outputs, in_specs=[pl.BlockSpec(memory_spa...  25.8 us
    ppermute x22, waiting for transfers between devices, dp_swap(): return lax.ppermute(value, 'dp', [(i, i ^ step) for i in range(4)])  20 us
    ppermute x9, starting transfers between devices, ring(): lax.ppermute(value, 'expert', [(i, (i + step) % size) for i in range(size)])  18.1 us
    ppermute x22, starting transfers between devices, dp_swap(): return lax.ppermute(value, 'dp', [(i, i ^ step) for i in range(4)])  12.1 us
  transfers between devices with their start and end apart: 33, of which 16 were waited for; matrix products, arithmetic and copies ran while one was open for 9% of the time, Pallas kernels for 19%

profile of v3, /device:TPU:0, one launch (start us, length us, event | category | flops | bytes accessed | tf_op | source)
XLA Modules:
  0.0 139.1 jit_solution(6118448535197910746)
XLA Ops:
  0.7 2.2 %shard_map.152 = (bf16[272,1024]{1,0:T(8,128)(2,1)}, f32[8,128]{1,0:T(8,128)}) custom-call(bf16[128,1024]{1,0:T(8,128)(2,1)} %tokens.1, bf16[128,1024]{1,0:T(8,128)(2,1)} %grads.1, s32[6,128]{1,0:T(8,128)} %bitcast.54, bf16[12,1024]{1,0:T(8,128)(2,1)} %bitcast.50), custom_call_target="tpu_custom_call" | custom-call | flops 20000000000 | bytes 20000000000 | tf_op jit(solution)/shard_map/pallas_call | solution.py:530
  2.8 3.0 %collective-permute-start.2 = (bf16[272,1024]{1,0:T(8,128)(2,1)}, bf16[272,1024]{1,0:T(8,128)(2,1)S(1)}, u32[]{:S(2)}, u32[]{:S(2)}) collective-permute-start(bf16[272,1024]{1,0:T(8,128)(2,1)} %get-tuple-element.81.refs_0_), channel_id=1, source_target_pairs={{0,4},{4,8},{8,12},{12,0},{1,5},{5,9},{9,13},{13,1},{2,6},{6,10},{... | collective-permute-start | bytes 1671176 | tf_op jit(solution)/shard_map/ppermute | solution.py:494
  5.8 2.0 %collective-permute-start.1 = (bf16[272,1024]{1,0:T(8,128)(2,1)}, bf16[272,1024]{1,0:T(8,128)(2,1)S(1)}, u32[]{:S(2)}, u32[]{:S(2)}) collective-permute-start(bf16[272,1024]{1,0:T(8,128)(2,1)} %get-tuple-element.81.refs_0_), channel_id=1, source_target_pairs={{0,12},{4,0},{8,4},{12,8},{1,13},{5,1},{9,5},{13,9},{2,14},{6,2},{... | collective-permute-start | bytes 1671176 | tf_op jit(solution)/shard_map/ppermute | solution.py:494
  7.9 1.3 pad_maximum_fusion
  9.2 1.7 %collective-permute-start.4 = (bf16[2,2,256,768]{3,2,1,0:T(8,128)(2,1)}, bf16[2,2,256,768]{3,2,1,0:T(8,128)(2,1)}, u32[]{:S(2)}, u32[]{:S(2)}) collective-permute-start(bf16[2,2,256,768]{3,2,1,0:T(8,128)(2,1)} %pad_maximum_fusion), channel_id=1, source_target_pairs={{0,2},{1,3},{2,0},{3,1},{4,6},{5,7},{6,4},{7,5},{8,10},{9,11},{10,... | collective-permute-start | bytes 4718600 | tf_op jit(solution)/shard_map/ppermute | solution.py:489
  14.9 6.7 %collective-permute-done.2.refs_2_ = bf16[272,1024]{1,0:T(8,128)(2,1)S(1)} collective-permute-done((bf16[272,1024]{1,0:T(8,128)(2,1)}, bf16[272,1024]{1,0:T(8,128)(2,1)S(1)}, u32[]{:S(2)}, u32[]{:S(2)}) %collective-permute-start.2) | collective-permute-done | bytes 557088 | tf_op jit(solution)/shard_map/ppermute | solution.py:494
  24.0 1.7 %collective-permute-start.8 = (bf16[2,256,768]{2,1,0:T(8,128)(2,1)}, bf16[2,256,768]{2,1,0:T(8,128)(2,1)S(1)}, u32[]{:S(2)}, u32[]{:S(2)}) collective-permute-start(bf16[2,256,768]{2,1,0:T(8,128)(2,1)} %refs_8_.1), channel_id=1, source_target_pairs={{0,2},{1,3},{2,0},{3,1},{4,6},{5,7},{6,4},{7,5},{8,10},{9,11},{10,... | collective-permute-start | bytes 2359304 | tf_op jit(solution)/shard_map/ppermute | solution.py:489
  25.7 6.6 %collective-permute-done.1.refs_6_ = bf16[272,1024]{1,0:T(8,128)(2,1)S(1)} collective-permute-done((bf16[272,1024]{1,0:T(8,128)(2,1)}, bf16[272,1024]{1,0:T(8,128)(2,1)S(1)}, u32[]{:S(2)}, u32[]{:S(2)}) %collective-permute-start.1) | collective-permute-done | bytes 557088 | tf_op jit(solution)/shard_map/ppermute | solution.py:494
  32.3 12.4 %collective-permute-done.3.refs_4_ = bf16[272,1024]{1,0:T(8,128)(2,1)} collective-permute-done((bf16[272,1024]{1,0:T(8,128)(2,1)S(1)}, bf16[272,1024]{1,0:T(8,128)(2,1)}, u32[]{:S(2)}, u32[]{:S(2)}) %collective-permute-start.3) | collective-permute-done | bytes 557088 | tf_op jit(solution)/shard_map/ppermute | solution.py:494
  44.7 1.9 %collective-permute-done.4.refs_6_.refs_8_ = bf16[2,2,256,768]{3,2,1,0:T(8,128)(2,1)} collective-permute-done((bf16[2,2,256,768]{3,2,1,0:T(8,128)(2,1)}, bf16[2,2,256,768]{3,2,1,0:T(8,128)(2,1)}, u32[]{:S(2)}, u32[]{:S(2)}) %collective-permute-start.4) | collective-permute-done | bytes 1572896 | tf_op jit(solution)/shard_map/ppermute | solution.py:489
  46.7 1.2 dynamic-slice_bitcast_fusion
  50.3 1.5 %collective-permute-done.5.refs_3_ = bf16[272,1024]{1,0:T(8,128)(2,1)S(1)} collective-permute-done((bf16[272,1024]{1,0:T(8,128)(2,1)S(1)}, bf16[272,1024]{1,0:T(8,128)(2,1)S(1)}, u32[]{:S(2)}, u32[]{:S(2)}) %collective-permute-start.5) | collective-permute-done | bytes 557088 | tf_op jit(solution)/shard_map/ppermute | solution.py:489
  52.6 2.8 %shard_map.153 = (bf16[512,128]{1,0:T(8,128)(2,1)S(1)}, bf16[512,128]{1,0:T(8,128)(2,1)S(1)}, bf16[512,1024]{1,0:T(8,128)(2,1)S(1)}, bf16[512,1024]{1,0:T(8,128)(2,1)S(1)}) custom-call(s32[2]{0:T(128)S(1)} %pad_add_fusion.place, bf16[272,1024]{1,0:T(8,128)(2,1)S(1)} %copy-done.3, bf16[272,1024]{1,0:T(8,128)(2,1)S(1)} %collective-permute-done.refs_1_, ...), custom_call_target="tpu_custom_call" | custom-call | tf_op jit(solution)/shard_map/pallas_call | solution.py:237
  55.4 7.6 %collective-permute-done.8.refs_4_.refs_10_ = bf16[2,256,768]{2,1,0:T(8,128)(2,1)S(1)} collective-permute-done((bf16[2,256,768]{2,1,0:T(8,128)(2,1)}, bf16[2,256,768]{2,1,0:T(8,128)(2,1)S(1)}, u32[]{:S(2)}, u32[]{:S(2)}) %collective-permute-start.8) | collective-permute-done | bytes 786464 | tf_op jit(solution)/shard_map/ppermute | solution.py:489
  63.2 5.8 %shard_map.154 = (bf16[512,768]{1,0:T(8,128)(2,1)S(1)}, bf16[512,768]{1,0:T(8,128)(2,1)S(1)}, bf16[512,768]{1,0:T(8,128)(2,1)S(1)}, bf16[256,768]{1,0:T(8,128)(2...) custom-call(s32[2]{0:T(128)S(1)} %pad_add_fusion.place, ...), custom_call_target="tpu_custom_call" | custom-call | flops 20000000000 | bytes 20000000000 | tf_op jit(solution)/shard_map/pallas_call | solution.py:237
  68.9 1.8 %collective-permute-start.14 = (bf16[256,768]{1,0:T(8,128)(2,1)S(1)}, bf16[256,768]{1,0:T(8,128)(2,1)S(1)}, u32[]{:S(2)}, u32[]{:S(2)}) collective-permute-start(bf16[256,768]{1,0:T(8,128)(2,1)S(1)} %get-tuple-element.99), channel_id=1, source_target_pairs={{0,2},{1,3},{2,0},{3,1},{4,6},{5,7},{6,4},{7,5},{8,10},{9,11},{10,... | collective-permute-start | bytes 1179656 | tf_op jit(solution)/shard_map/ppermute | solution.py:489
  70.7 4.2 %shard_map.155 = (bf16[512,1024]{1,0:T(8,128)(2,1)S(1)}, bf16[512,1024]{1,0:T(8,128)(2,1)S(1)}) custom-call(s32[2]{0:T(128)S(1)} %pad_add_fusion.place, bf16[512,128]{1,0:T(8,128)(2,1)S(1)} %get-tuple-element.86.refs_0_.refs_1_, bf16[512,768]{1,0:T(8,128)(2,1)S(1)} %get-tuple-element.95.refs_1_.refs_3_, bf16[2,256,768]{2,1,0:T(8,128)(2,1)S(1)} %copy-done.5, ...), custom_call_target="tpu_custom_call" | custom-call | flops 20000000000 | bytes 20000000000 | tf_op jit(solution)/shard_map/pallas_call | solution.py:237
  76.4 4.5 %collective-permute-done.14 = bf16[256,768]{1,0:T(8,128)(2,1)S(1)} collective-permute-done((bf16[256,768]{1,0:T(8,128)(2,1)S(1)}, bf16[256,768]{1,0:T(8,128)(2,1)S(1)}, u32[]{:S(2)}, u32[]{:S(2)}) %collective-permute-start.14) | collective-permute-done | bytes 393248 | tf_op jit(solution)/shard_map/ppermute | solution.py:489
  81.0 2.3 %collective-permute-start.16 = (bf16[128,1024]{1,0:T(8,128)(2,1)S(1)}, bf16[128,1024]{1,0:T(8,128)(2,1)S(1)}, u32[]{:S(2)}, u32[]{:S(2)}) collective-permute-start(bf16[128,1024]{1,0:T(8,128)(2,1)S(1)} %add_convert_fusion.10), channel_id=1, source_target_pairs={{0,12},{4,0},{8,4},{12,8},{1,13},{5,1},{9,5},{13,9},{2,14},{6,2},{... | collective-permute-start | bytes 786440 | tf_op jit(solution)/shard_map/ppermute | solution.py:494
  83.3 5.7 %shard_map.156 = (bf16[512,768]{1,0:T(8,128)(2,1)S(1)}, bf16[512,768]{1,0:T(8,128)(2,1)S(1)}, bf16[512,128]{1,0:T(8,128)(2,1)S(1)}, f32[8,1024]{1,0:T(8,128)S(1)...) custom-call(s32[2]{0:T(128)S(1)} %pad_add_fusion.place, ...), custom_call_target="tpu_custom_call" | custom-call | flops 20000000000 | bytes 20000000000 | tf_op jit(solution)/shard_map/pallas_call | solution.py:237
  90.1 1.8 %collective-permute-start.21 = (f32[16,1024]{1,0:T(8,128)S(1)}, f32[16,1024]{1,0:T(8,128)S(1)}, u32[]{:S(2)}, u32[]{:S(2)}) collective-permute-start(f32[16,1024]{1,0:T(8,128)S(1)} %pad_maximum_fusion.2), channel_id=1, source_target_pairs={{0,2},{1,3},{2,0},{3,1},{4,6},{5,7},{6,4},{7,5},{8,10},{9,11},{10,... | collective-permute-start | bytes 196616 | tf_op jit(solution)/shard_map/ppermute | solution.py:489
  92.1 3.7 %collective-permute-start.23 = (bf16[128,1024]{1,0:T(8,128)(2,1)S(1)}, bf16[128,1024]{1,0:T(8,128)(2,1)S(1)}, u32[]{:S(2)}, u32[]{:S(2)}) collective-permute-start(bf16[128,1024]{1,0:T(8,128)(2,1)S(1)} %get-tuple-element.158), channel_id=1, source_target_pairs={{0,12},{4,0},{8,4},{12,8},{1,13},{5,1},{9,5},{13,9},{2,14},{6,2},{... | collective-permute-start | bytes 786440 | tf_op jit(solution)/shard_map/ppermute | solution.py:494
  96.3 7.2 %shard_map.157 = (bf16[512,1024]{1,0:T(8,128)(2,1)S(1)}, bf16[512,1024]{1,0:T(8,128)(2,1)S(1)}) custom-call(s32[2]{0:T(128)S(1)} %pad_add_fusion.place, bf16[512,128]{1,0:T(8,128)(2,1)S(1)} %get-tuple-element.85.refs_0_, bf16[512,768]{1,0:T(8,128)(2,1)S(1)} %get-tuple-element.113.refs_1_, bf16[512,768]{1,0:T(8,128)(2,1)S(1)} %get-tuple-element.114.refs_2_, ...), custom_call_target="tpu_custom_call" | custom-call | flops 20000000000 | bytes 20000000000 | tf_op jit(solution)/shard_map/pallas_call | solution.py:237
  103.5 3.8 %collective-permute-done.22 = bf16[128,1024]{1,0:T(8,128)(2,1)S(1)} collective-permute-done((bf16[128,1024]{1,0:T(8,128)(2,1)S(1)}, bf16[128,1024]{1,0:T(8,128)(2,1)S(1)}, u32[]{:S(2)}, u32[]{:S(2)}) %collective-permute-start.22) | collective-permute-done | bytes 262176 | tf_op jit(solution)/shard_map/ppermute | solution.py:494
  110.0 1.8 %collective-permute-start.31 = (f32[16,1024]{1,0:T(8,128)S(1)}, f32[16,1024]{1,0:T(8,128)S(1)}, u32[]{:S(2)}, u32[]{:S(2)}) collective-permute-start(f32[16,1024]{1,0:T(8,128)S(1)} %add.150), channel_id=1, source_target_pairs={{0,4},{4,0},{8,12},{12,8},{1,5},{5,1},{9,13},{13,9},{2,6},{6,2},{1... | collective-permute-start | bytes 196616 | tf_op jit(solution)/shard_map/ppermute | solution.py:686
  112.4 3.6 %collective-permute-start.26 = (bf16[128,1024]{1,0:T(8,128)(2,1)S(1)}, bf16[128,1024]{1,0:T(8,128)(2,1)S(1)}, u32[]{:S(2)}, u32[]{:S(2)}) collective-permute-start(bf16[128,1024]{1,0:T(8,128)(2,1)S(1)} %get-tuple-element.155), channel_id=1, source_target_pairs={{0,12},{4,0},{8,4},{12,8},{1,13},{5,1},{9,5},{13,9},{2,14},{6,2},{... | collective-permute-start | bytes 786440 | tf_op jit(solution)/shard_map/ppermute | solution.py:494
  117.1 3.3 %collective-permute-done.28 = bf16[256,768]{1,0:T(8,128)(2,1)S(1)} collective-permute-done((bf16[256,768]{1,0:T(8,128)(2,1)S(1)}, bf16[256,768]{1,0:T(8,128)(2,1)S(1)}, u32[]{:S(2)}, u32[]{:S(2)}) %collective-permute-start.28) | collective-permute-done | bytes 393248 | tf_op jit(solution)/shard_map/ppermute | solution.py:489
  120.4 2.7 %collective-permute-done.27 = bf16[128,1024]{1,0:T(8,128)(2,1)S(1)} collective-permute-done((bf16[128,1024]{1,0:T(8,128)(2,1)S(1)}, bf16[128,1024]{1,0:T(8,128)(2,1)S(1)}, u32[]{:S(2)}, u32[]{:S(2)}) %collective-permute-start.27) | collective-permute-done | bytes 262176 | tf_op jit(solution)/shard_map/ppermute | solution.py:494
  123.1 3.6 %collective-permute-done.26 = bf16[128,1024]{1,0:T(8,128)(2,1)S(1)} collective-permute-done((bf16[128,1024]{1,0:T(8,128)(2,1)S(1)}, bf16[128,1024]{1,0:T(8,128)(2,1)S(1)}, u32[]{:S(2)}, u32[]{:S(2)}) %collective-permute-start.26) | collective-permute-done | bytes 262176 | tf_op jit(solution)/shard_map/ppermute | solution.py:494
  126.8 3.2 %collective-permute-start.30 = (bf16[128,1024]{1,0:T(8,128)(2,1)S(1)}, bf16[128,1024]{1,0:T(8,128)(2,1)S(1)}, u32[]{:S(2)}, u32[]{:S(2)}) collective-permute-start(bf16[128,1024]{1,0:T(8,128)(2,1)S(1)} %add_convert_fusion.2), channel_id=1, source_target_pairs={{0,12},{4,0},{8,4},{12,8},{1,13},{5,1},{9,5},{13,9},{2,14},{6,2},{... | collective-permute-start | bytes 786440 | tf_op jit(solution)/shard_map/ppermute | solution.py:494
  131.1 4.0 %collective-permute-done.30 = bf16[128,1024]{1,0:T(8,128)(2,1)S(1)} collective-permute-done((bf16[128,1024]{1,0:T(8,128)(2,1)S(1)}, bf16[128,1024]{1,0:T(8,128)(2,1)S(1)}, u32[]{:S(2)}, u32[]{:S(2)}) %collective-permute-start.30) | collective-permute-done | bytes 262176 | tf_op jit(solution)/shard_map/ppermute | solution.py:494
  137.7 1.4 select_convert_fusion
  (118 shorter events, 21.0 us)
Async XLA Ops:
  2.8 18.8 %collective-permute-start.2 = (bf16[272,1024]{1,0:T(8,128)(2,1)}, bf16[272,1024]{1,0:T(8,128)(2,1)S(1)}, u32[]{:S(2)}, u32[]{:S(2)}) collective-permute-start(bf16[272,1024]{1,0:T(8,128)(2,1)} %get-tuple-element.81.refs_0_), channel_id=1, source_target_pairs={{0,4},{4,8},{8,12},{12,0},{1,5},{5,9},{9,13},{13,1},{2,6},{6,10},{... | collective-permute-start | bytes 1671176 | tf_op jit(solution)/shard_map/ppermute | solution.py:494
  5.8 26.5 %collective-permute-start.1 = (bf16[272,1024]{1,0:T(8,128)(2,1)}, bf16[272,1024]{1,0:T(8,128)(2,1)S(1)}, u32[]{:S(2)}, u32[]{:S(2)}) collective-permute-start(bf16[272,1024]{1,0:T(8,128)(2,1)} %get-tuple-element.81.refs_0_), channel_id=1, source_target_pairs={{0,12},{4,0},{8,4},{12,8},{1,13},{5,1},{9,5},{13,9},{2,14},{6,2},{... | collective-permute-start | bytes 1671176 | tf_op jit(solution)/shard_map/ppermute | solution.py:494
  7.9 5.8 %collective-permute-start = (bf16[272,1024]{1,0:T(8,128)(2,1)}, bf16[272,1024]{1,0:T(8,128)(2,1)S(1)}, u32[]{:S(2)}, u32[]{:S(2)}) collective-permute-start(bf16[272,1024]{1,0:T(8,128)(2,1)} %get-tuple-element.81.refs_0_), channel_id=1, source_target_pairs={{0,1},{1,0},{2,3},{3,2},{4,5},{5,4},{6,7},{7,6},{8,9},{9,8},{10,11... | collective-permute-start | bytes 1671176 | tf_op jit(solution)/shard_map/ppermute | solution.py:489
  9.2 37.5 %collective-permute-start.4 = (bf16[2,2,256,768]{3,2,1,0:T(8,128)(2,1)}, bf16[2,2,256,768]{3,2,1,0:T(8,128)(2,1)}, u32[]{:S(2)}, u32[]{:S(2)}) collective-permute-start(bf16[2,2,256,768]{3,2,1,0:T(8,128)(2,1)} %pad_maximum_fusion), channel_id=1, source_target_pairs={{0,2},{1,3},{2,0},{3,1},{4,6},{5,7},{6,4},{7,5},{8,10},{9,11},{10,... | collective-permute-start | bytes 4718600 | tf_op jit(solution)/shard_map/ppermute | solution.py:489
  13.7 34.9 %collective-permute-start.9 = (bf16[3,256,768]{2,1,0:T(8,128)(2,1)}, bf16[3,256,768]{2,1,0:T(8,128)(2,1)}, u32[]{:S(2)}, u32[]{:S(2)}) collective-permute-start(bf16[3,256,768]{2,1,0:T(8,128)(2,1)} %pad_maximum_fusion.1), channel_id=1, source_target_pairs={{0,1},{1,0},{2,3},{3,2},{4,5},{5,4},{6,7},{7,6},{8,9},{9,8},{10,11... | collective-permute-start | bytes 3538952 | tf_op jit(solution)/shard_map/ppermute | solution.py:489
  21.6 23.1 %collective-permute-start.3 = (bf16[272,1024]{1,0:T(8,128)(2,1)S(1)}, bf16[272,1024]{1,0:T(8,128)(2,1)}, u32[]{:S(2)}, u32[]{:S(2)}) collective-permute-start(bf16[272,1024]{1,0:T(8,128)(2,1)S(1)} %collective-permute-done.2.refs_2_), channel_id=1, source_target_pairs={{0,4},{4,8},{8,12},{12,0},{1,5},{5,9},{9,13},{13,1},{2,6},{6,10},{... | collective-permute-start | bytes 1671176 | tf_op jit(solution)/shard_map/ppermute | solution.py:494
  24.0 39.1 %collective-permute-start.8 = (bf16[2,256,768]{2,1,0:T(8,128)(2,1)}, bf16[2,256,768]{2,1,0:T(8,128)(2,1)S(1)}, u32[]{:S(2)}, u32[]{:S(2)}) collective-permute-start(bf16[2,256,768]{2,1,0:T(8,128)(2,1)} %refs_8_.1), channel_id=1, source_target_pairs={{0,2},{1,3},{2,0},{3,1},{4,6},{5,7},{6,4},{7,5},{8,10},{9,11},{10,... | collective-permute-start | bytes 2359304 | tf_op jit(solution)/shard_map/ppermute | solution.py:489
  47.9 15.3 %collective-permute-start.10 = (bf16[2,256,768]{2,1,0:T(8,128)(2,1)S(1)}, bf16[2,256,768]{2,1,0:T(8,128)(2,1)S(1)}, u32[]{:S(2)}, u32[]{:S(2)}) collective-permute-start(bf16[2,256,768]{2,1,0:T(8,128)(2,1)S(1)} %dynamic-slice_bitcast_fusion), channel_id=1, source_target_pairs={{0,1},{1,0},{2,3},{3,2},{4,5},{5,4},{6,7},{7,6},{8,9},{9,8},{10,11... | collective-permute-start | bytes 2359304 | tf_op jit(solution)/shard_map/ppermute | solution.py:489
  48.0 3.8 %collective-permute-start.5 = (bf16[272,1024]{1,0:T(8,128)(2,1)S(1)}, bf16[272,1024]{1,0:T(8,128)(2,1)S(1)}, u32[]{:S(2)}, u32[]{:S(2)}) collective-permute-start(bf16[272,1024]{1,0:T(8,128)(2,1)S(1)} %collective-permute-done.2.refs_2_), channel_id=1, source_target_pairs={{0,1},{1,0},{2,3},{3,2},{4,5},{5,4},{6,7},{7,6},{8,9},{9,8},{10,11... | collective-permute-start | bytes 1671176 | tf_op jit(solution)/shard_map/ppermute | solution.py:489
  48.5 3.5 %collective-permute-start.6 = (bf16[272,1024]{1,0:T(8,128)(2,1)}, bf16[272,1024]{1,0:T(8,128)(2,1)S(1)}, u32[]{:S(2)}, u32[]{:S(2)}) collective-permute-start(bf16[272,1024]{1,0:T(8,128)(2,1)} %collective-permute-done.3.refs_4_), channel_id=1, source_target_pairs={{0,1},{1,0},{2,3},{3,2},{4,5},{5,4},{6,7},{7,6},{8,9},{9,8},{10,11... | collective-permute-start | bytes 1671176 | tf_op jit(solution)/shard_map/ppermute | solution.py:489
  48.6 4.0 %collective-permute-start.7 = (bf16[272,1024]{1,0:T(8,128)(2,1)S(1)}, bf16[272,1024]{1,0:T(8,128)(2,1)S(1)}, u32[]{:S(2)}, u32[]{:S(2)}) collective-permute-start(bf16[272,1024]{1,0:T(8,128)(2,1)S(1)} %collective-permute-done.1.refs_6_), channel_id=1, source_target_pairs={{0,1},{1,0},{2,3},{3,2},{4,5},{5,4},{6,7},{7,6},{8,9},{9,8},{10,11... | collective-permute-start | bytes 1671176 | tf_op jit(solution)/shard_map/ppermute | solution.py:489
  63.1 7.7 %collective-permute-start.11 = (bf16[256,768]{1,0:T(8,128)(2,1)S(1)}, bf16[256,768]{1,0:T(8,128)(2,1)S(1)}, u32[]{:S(2)}, u32[]{:S(2)}) collective-permute-start(bf16[256,768]{1,0:T(8,128)(2,1)S(1)} %dynamic-slice_bitcast_fusion.1), channel_id=1, source_target_pairs={{0,1},{1,0},{2,3},{3,2},{4,5},{5,4},{6,7},{7,6},{8,9},{9,8},{10,11... | collective-permute-start | bytes 1179656 | tf_op jit(solution)/shard_map/ppermute | solution.py:489
  68.9 12.0 %collective-permute-start.14 = (bf16[256,768]{1,0:T(8,128)(2,1)S(1)}, bf16[256,768]{1,0:T(8,128)(2,1)S(1)}, u32[]{:S(2)}, u32[]{:S(2)}) collective-permute-start(bf16[256,768]{1,0:T(8,128)(2,1)S(1)} %get-tuple-element.99), channel_id=1, source_target_pairs={{0,2},{1,3},{2,0},{3,1},{4,6},{5,7},{6,4},{7,5},{8,10},{9,11},{10,... | collective-permute-start | bytes 1179656 | tf_op jit(solution)/shard_map/ppermute | solution.py:489
  75.0 5.9 %collective-permute-start.13 = (bf16[128,1024]{1,0:T(8,128)(2,1)S(1)}, bf16[128,1024]{1,0:T(8,128)(2,1)S(1)}, u32[]{:S(2)}, u32[]{:S(2)}) collective-permute-start(bf16[128,1024]{1,0:T(8,128)(2,1)S(1)} %get-tuple-element.160), channel_id=1, source_target_pairs={{0,1},{1,0},{2,3},{3,2},{4,5},{5,4},{6,7},{7,6},{8,9},{9,8},{10,11... | collective-permute-start | bytes 786440 | tf_op jit(solution)/shard_map/ppermute | solution.py:489
  75.3 5.7 %collective-permute-start.12 = (bf16[128,1024]{1,0:T(8,128)(2,1)S(1)}, bf16[128,1024]{1,0:T(8,128)(2,1)S(1)}, u32[]{:S(2)}, u32[]{:S(2)}) collective-permute-start(bf16[128,1024]{1,0:T(8,128)(2,1)S(1)} %get-tuple-element.161), channel_id=1, source_target_pairs={{0,1},{1,0},{2,3},{3,2},{4,5},{5,4},{6,7},{7,6},{8,9},{9,8},{10,11... | collective-permute-start | bytes 786440 | tf_op jit(solution)/shard_map/ppermute | solution.py:489
  75.9 13.2 %collective-permute-start.15 = (bf16[256,768]{1,0:T(8,128)(2,1)S(1)}, bf16[256,768]{1,0:T(8,128)(2,1)S(1)}, u32[]{:S(2)}, u32[]{:S(2)}) collective-permute-start(bf16[256,768]{1,0:T(8,128)(2,1)S(1)} %get-tuple-element.109), channel_id=1, source_target_pairs={{0,3},{1,2},{2,1},{3,0},{4,7},{5,6},{6,5},{7,4},{8,11},{9,10},{10,... | collective-permute-start | bytes 1179656 | tf_op jit(solution)/shard_map/ppermute | solution.py:489
  76.1 13.0 %collective-permute-start.18 = (bf16[256,768]{1,0:T(8,128)(2,1)S(1)}, bf16[256,768]{1,0:T(8,128)(2,1)S(1)}, u32[]{:S(2)}, u32[]{:S(2)}) collective-permute-start(bf16[256,768]{1,0:T(8,128)(2,1)S(1)} %get-tuple-element.112), channel_id=1, source_target_pairs={{0,1},{1,0},{2,3},{3,2},{4,5},{5,4},{6,7},{7,6},{8,9},{9,8},{10,11... | collective-permute-start | bytes 1179656 | tf_op jit(solution)/shard_map/ppermute | solution.py:489
  80.9 9.0 %collective-permute-start.17 = (bf16[256,1024]{1,0:T(8,128)(2,1)S(1)}, bf16[256,1024]{1,0:T(8,128)(2,1)S(1)}, u32[]{:S(2)}, u32[]{:S(2)}) collective-permute-start(bf16[256,1024]{1,0:T(8,128)(2,1)S(1)} %slice.76), channel_id=1, source_target_pairs={{0,1},{1,0},{2,3},{3,2},{4,5},{5,4},{6,7},{7,6},{8,9},{9,8},{10,11... | collective-permute-start | bytes 1572872 | tf_op jit(solution)/shard_map/ppermute | solution.py:489
  81.0 8.9 %collective-permute-start.16 = (bf16[128,1024]{1,0:T(8,128)(2,1)S(1)}, bf16[128,1024]{1,0:T(8,128)(2,1)S(1)}, u32[]{:S(2)}, u32[]{:S(2)}) collective-permute-start(bf16[128,1024]{1,0:T(8,128)(2,1)S(1)} %add_convert_fusion.10), channel_id=1, source_target_pairs={{0,12},{4,0},{8,4},{12,8},{1,13},{5,1},{9,5},{13,9},{2,14},{6,2},{... | collective-permute-start | bytes 786440 | tf_op jit(solution)/shard_map/ppermute | solution.py:494
  90.1 13.4 %collective-permute-start.21 = (f32[16,1024]{1,0:T(8,128)S(1)}, f32[16,1024]{1,0:T(8,128)S(1)}, u32[]{:S(2)}, u32[]{:S(2)}) collective-permute-start(f32[16,1024]{1,0:T(8,128)S(1)} %pad_maximum_fusion.2), channel_id=1, source_target_pairs={{0,2},{1,3},{2,0},{3,1},{4,6},{5,7},{6,4},{7,5},{8,10},{9,11},{10,... | collective-permute-start | bytes 196616 | tf_op jit(solution)/shard_map/ppermute | solution.py:489
  92.1 11.4 %collective-permute-start.23 = (bf16[128,1024]{1,0:T(8,128)(2,1)S(1)}, bf16[128,1024]{1,0:T(8,128)(2,1)S(1)}, u32[]{:S(2)}, u32[]{:S(2)}) collective-permute-start(bf16[128,1024]{1,0:T(8,128)(2,1)S(1)} %get-tuple-element.158), channel_id=1, source_target_pairs={{0,12},{4,0},{8,4},{12,8},{1,13},{5,1},{9,5},{13,9},{2,14},{6,2},{... | collective-permute-start | bytes 786440 | tf_op jit(solution)/shard_map/ppermute | solution.py:494
  95.7 11.5 %collective-permute-start.22 = (bf16[128,1024]{1,0:T(8,128)(2,1)S(1)}, bf16[128,1024]{1,0:T(8,128)(2,1)S(1)}, u32[]{:S(2)}, u32[]{:S(2)}) collective-permute-start(bf16[128,1024]{1,0:T(8,128)(2,1)S(1)} %get-tuple-element.159), channel_id=1, source_target_pairs={{0,4},{4,8},{8,12},{12,0},{1,5},{5,9},{9,13},{13,1},{2,6},{6,10},{... | collective-permute-start | bytes 786440 | tf_op jit(solution)/shard_map/ppermute | solution.py:494
  95.7 11.5 %collective-permute-start.19 = (bf16[256,768]{1,0:T(8,128)(2,1)S(1)}, bf16[256,768]{1,0:T(8,128)(2,1)S(1)}, u32[]{:S(2)}, u32[]{:S(2)}) collective-permute-start(bf16[256,768]{1,0:T(8,128)(2,1)S(1)} %get-tuple-element.118), channel_id=1, source_target_pairs={{0,2},{1,3},{2,0},{3,1},{4,6},{5,7},{6,4},{7,5},{8,10},{9,11},{10,... | collective-permute-start | bytes 1179656 | tf_op jit(solution)/shard_map/ppermute | solution.py:489
  96.3 11.0 %collective-permute-start.20 = (bf16[2,256,768]{2,1,0:T(8,128)(2,1)S(1)}, bf16[2,256,768]{2,1,0:T(8,128)(2,1)S(1)}, u32[]{:S(2)}, u32[]{:S(2)}) collective-permute-start(bf16[2,256,768]{2,1,0:T(8,128)(2,1)S(1)} %get-tuple-element.119), channel_id=1, source_target_pairs={{0,1},{1,0},{2,3},{3,2},{4,5},{5,4},{6,7},{7,6},{8,9},{9,8},{10,11... | collective-permute-start | bytes 2359304 | tf_op jit(solution)/shard_map/ppermute | solution.py:489
  107.3 2.8 %collective-permute-start.24 = (bf16[512,1024]{1,0:T(8,128)(2,1)S(1)}, bf16[512,1024]{1,0:T(8,128)(2,1)S(1)}, u32[]{:S(2)}, u32[]{:S(2)}) collective-permute-start(bf16[512,1024]{1,0:T(8,128)(2,1)S(1)} %get-tuple-element.127), channel_id=1, source_target_pairs={{0,1},{1,0},{2,3},{3,2},{4,5},{5,4},{6,7},{7,6},{8,9},{9,8},{10,11... | collective-permute-start | bytes 3145736 | tf_op jit(solution)/shard_map/ppermute | solution.py:489
  108.4 12.0 %collective-permute-start.28 = (bf16[256,768]{1,0:T(8,128)(2,1)S(1)}, bf16[256,768]{1,0:T(8,128)(2,1)S(1)}, u32[]{:S(2)}, u32[]{:S(2)}) collective-permute-start(bf16[256,768]{1,0:T(8,128)(2,1)S(1)} %get-tuple-element.133), channel_id=1, source_target_pairs={{0,2},{1,3},{2,0},{3,1},{4,6},{5,7},{6,4},{7,5},{8,10},{9,11},{10,... | collective-permute-start | bytes 1179656 | tf_op jit(solution)/shard_map/ppermute | solution.py:489
  109.0 27.1 %collective-permute-start.29 = (bf16[2,256,768]{2,1,0:T(8,128)(2,1)S(1)}, bf16[2,256,768]{2,1,0:T(8,128)(2,1)S(1)}, u32[]{:S(2)}, u32[]{:S(2)}) collective-permute-start(bf16[2,256,768]{2,1,0:T(8,128)(2,1)S(1)} %get-tuple-element.135), channel_id=1, source_target_pairs={{0,3},{1,2},{2,1},{3,0},{4,7},{5,6},{6,5},{7,4},{8,11},{9,10},{10,... | collective-permute-start | bytes 2359304 | tf_op jit(solution)/shard_map/ppermute | solution.py:489
  110.0 7.0 %collective-permute-start.31 = (f32[16,1024]{1,0:T(8,128)S(1)}, f32[16,1024]{1,0:T(8,128)S(1)}, u32[]{:S(2)}, u32[]{:S(2)}) collective-permute-start(f32[16,1024]{1,0:T(8,128)S(1)} %add.150), channel_id=1, source_target_pairs={{0,4},{4,0},{8,12},{12,8},{1,5},{5,1},{9,13},{13,9},{2,6},{6,2},{1... | collective-permute-start | bytes 196616 | tf_op jit(solution)/shard_map/ppermute | solution.py:686
  112.1 11.0 %collective-permute-start.27 = (bf16[128,1024]{1,0:T(8,128)(2,1)S(1)}, bf16[128,1024]{1,0:T(8,128)(2,1)S(1)}, u32[]{:S(2)}, u32[]{:S(2)}) collective-permute-start(bf16[128,1024]{1,0:T(8,128)(2,1)S(1)} %get-tuple-element.154), channel_id=1, source_target_pairs={{0,4},{4,8},{8,12},{12,0},{1,5},{5,9},{9,13},{13,1},{2,6},{6,10},{... | collective-permute-start | bytes 786440 | tf_op jit(solution)/shard_map/ppermute | solution.py:494
  112.4 14.3 %collective-permute-start.26 = (bf16[128,1024]{1,0:T(8,128)(2,1)S(1)}, bf16[128,1024]{1,0:T(8,128)(2,1)S(1)}, u32[]{:S(2)}, u32[]{:S(2)}) collective-permute-start(bf16[128,1024]{1,0:T(8,128)(2,1)S(1)} %get-tuple-element.155), channel_id=1, source_target_pairs={{0,12},{4,0},{8,4},{12,8},{1,13},{5,1},{9,5},{13,9},{2,14},{6,2},{... | collective-permute-start | bytes 786440 | tf_op jit(solution)/shard_map/ppermute | solution.py:494
  117.0 14.1 %collective-permute-start.32 = (f32[16,1024]{1,0:T(8,128)S(1)}, f32[16,1024]{1,0:T(8,128)S(1)}, u32[]{:S(2)}, u32[]{:S(2)}) collective-permute-start(f32[16,1024]{1,0:T(8,128)S(1)} %add.151), channel_id=1, source_target_pairs={{0,8},{4,12},{8,0},{12,4},{1,9},{5,13},{9,1},{13,5},{2,10},{6,14},... | collective-permute-start | bytes 196616 | tf_op jit(solution)/shard_map/ppermute | solution.py:690
  126.8 8.3 %collective-permute-start.30 = (bf16[128,1024]{1,0:T(8,128)(2,1)S(1)}, bf16[128,1024]{1,0:T(8,128)(2,1)S(1)}, u32[]{:S(2)}, u32[]{:S(2)}) collective-permute-start(bf16[128,1024]{1,0:T(8,128)(2,1)S(1)} %add_convert_fusion.2), channel_id=1, source_target_pairs={{0,12},{4,0},{8,4},{12,8},{1,13},{5,1},{9,5},{13,9},{2,14},{6,2},{... | collective-permute-start | bytes 786440 | tf_op jit(solution)/shard_map/ppermute | solution.py:494
  (17 other events, 139.0 us)

commit v4 on v3

--- a/solution.py
+++ b/solution.py
@@ -233,17 +233,22 @@
 LONG = 20_000_000_000
 
 
-def local_kernel(body, scalars, operands, outputs, scratch, moved):
+def local_kernel(body, scalars, operands, outputs, scratch, moved, mark=None):
+    marks = [] if mark is None else [mark]
+
+    def kernel(place, *refs):
+        body(place, *refs[len(marks) :])
+
     return pl.pallas_call(
-        body,
+        kernel,
         out_shape=outputs,
         in_specs=[pl.BlockSpec(memory_space=pltpu.SMEM)]
-        + [pl.BlockSpec(memory_space=pl.ANY) for _ in operands],
+        + [pl.BlockSpec(memory_space=pl.ANY) for _ in [*marks, *operands]],
         out_specs=[pl.BlockSpec(memory_space=pltpu.VMEM) for _ in outputs],
         scratch_shapes=scratch,
         compiler_params=pltpu.CompilerParams(vmem_limit_bytes=SCRATCH_BYTES),
         cost_estimate=pl.CostEstimate(flops=moved, bytes_accessed=moved, transcendentals=0),
-    )(scalars, *operands)
+    )(scalars, *marks, *operands)
 
 
 def bring(pairs, sems):
@@ -292,34 +297,42 @@
 
 
 def step_kernel(before, after_it):
-    after_it[...] = before[...] + 1.0
-
-
-def next_step(step, *done):
+    after_it[...] = before[...]
+
+
+def next_step(step):
     return pl.pallas_call(
         step_kernel,
         out_shape=jax.ShapeDtypeStruct(step.shape, step.dtype),
         cost_estimate=pl.CostEstimate(flops=LONG, bytes_accessed=LONG, transcendentals=0),
-    )(after(step, *done))
-
-
-def pick_kernel(place, *refs):
+    )(step)
+
+
+def forward_kernel(place, *refs):
     payloads = refs[0:8]
-    pick_out, gate_out, rows_out, cot_out = refs[8:12]
-    blocks, sems = refs[12:14]
+    gate_weight, up_weight, partner, cross, cross_partner = refs[8:13]
+    pick_out, gate_out, rows_out, cot_out, hidden_out, act_out, slope_out = refs[13:20]
+    outs = refs[20:24]
+    blocks, w_gate, w_up, upstream, sems = refs[24:29]
     me, expert = place[0], place[1]
+    core = me & 1
     count = pick_out.shape[1]
     slots = count // HALF * SLOTS
-    copies = bring([(payloads[b], blocks.at[b]) for b in range(8)], sems)
-    width = rows_out.shape[1] // 4
+    copies = bring(
+        [(payloads[b], blocks.at[b]) for b in range(8)]
+        + weight_pairs(core, (gate_weight, partner.at[0], cross.at[0], cross_partner.at[0]), w_gate)
+        + weight_pairs(core, (up_weight, partner.at[1], cross.at[1], cross_partner.at[1]), w_up),
+        sems,
+    )
+    width = w_gate.shape[0] // 4
     row = lax.broadcasted_iota(jnp.int32, (count, count), 0)
     column = lax.broadcasted_iota(jnp.int32, (count, count), 1)
     before = ((row < column) & (row // HALF == column // HALF)).astype(jnp.bfloat16)
     lane = lax.broadcasted_iota(jnp.int32, (1, count), 1)
     slot = lax.broadcasted_iota(jnp.int32, (slots, count), 0)
     mine = pl.ds(pl.multiple_of(expert * count, count), count)
-    for copy in copies:
-        copy.wait()
+    for b in range(8):
+        copies[b].wait()
     gates = jnp.concatenate(
         [blocks[b, 2 * count :, mine].astype(jnp.float32)[0:1] for b in range(8)], axis=0
     )
@@ -329,50 +342,32 @@
     for b in range(8):
         chosen = slot == target[b : b + 1]
         pick = chosen.astype(jnp.bfloat16)
+        gate_pick = jnp.where(chosen, gates[b : b + 1], 0.0)
+        gate = jnp.sum(gate_pick, axis=1, keepdims=True)
         at = b * slots
         pick_out[at : at + slots, :] = pick
-        gate_out[at : at + slots, :] = jnp.where(chosen, gates[b : b + 1], 0.0).astype(jnp.bfloat16)
+        gate_out[at : at + slots, :] = gate_pick.astype(jnp.bfloat16)
         for j in range(4):
             columns = pl.ds(pl.multiple_of((me ^ j) * width, width), width)
             here = (slice(at, at + slots), slice(j * width, (j + 1) * width))
             rows_out[here] = mm(pick, blocks[b, 0:count, columns]).astype(jnp.bfloat16)
-            cot_out[here] = mm(pick, blocks[b, count : 2 * count, columns]).astype(jnp.bfloat16)
-
-
-def forward_kernel(place, *refs):
-    (gate_pick_in, rows_in, cot_in, gate_weight, up_weight, partner, cross,
-     cross_partner) = refs[0:8]
-    hidden_out, act_out, slope_out = refs[8:11]
-    outs = refs[11:15]
-    gate_pick, rows, cot, w_gate, w_up, upstream, sems = refs[15:22]
-    core = place[0] & 1
-    copies = bring(
-        [(rows_in, rows)]
-        + weight_pairs(core, (gate_weight, partner.at[0], cross.at[0, core], cross_partner.at[0]), w_gate)
-        + weight_pairs(core, (up_weight, partner.at[1], cross.at[1, core], cross_partner.at[1]), w_up)
-        + [(gate_pick_in, gate_pick), (cot_in, cot)],
-        sems,
-    )
-    width = w_gate.shape[0] // 4
-    for copy in copies[0:5]:
+            cot = mm(pick, blocks[b, count : 2 * count, columns])
+            cot_out[here] = cot.astype(jnp.bfloat16)
+            upstream[here] = (gate * cot).astype(jnp.bfloat16)
+    for copy in copies[8:]:
         copy.wait()
-    pre_gate = mm(rows[...], w_gate[...])
-    for copy in copies[5:9]:
-        copy.wait()
-    pre_up = mm(rows[...], w_up[...])
+    pre_gate = mm(rows_out[...], w_gate[...])
+    pre_up = mm(rows_out[...], w_up[...])
     logistic = jax.nn.sigmoid(pre_gate)
     act = pre_gate * logistic
     hidden_out[...] = (act * pre_up).astype(jnp.bfloat16)
     act_out[...] = act.astype(jnp.bfloat16)
     slope = logistic * (1.0 + pre_gate * (1.0 - logistic))
     slope_out[...] = (pre_up * slope).astype(jnp.bfloat16)
-    for copy in copies[9:]:
-        copy.wait()
-    gate = jnp.sum(gate_pick[...].astype(jnp.float32), axis=1, keepdims=True)
-    for j in range(4):
-        here = slice(j * width, (j + 1) * width)
-        upstream[:, here] = (gate * cot[:, here].astype(jnp.float32)).astype(jnp.bfloat16)
-        outs[j][...] = mm_rows(upstream[:, here], hidden_out[...]).astype(jnp.bfloat16)
+    for j in (2, 1, 3, 0):
+        outs[j][...] = mm_rows(
+            upstream[:, j * width : (j + 1) * width], hidden_out[...]
+        ).astype(jnp.bfloat16)
 
 
 def scatter(me, pick, own_out, other_out, column_block):
@@ -396,7 +391,7 @@
     gate_pick, hidden, w_down, sems = refs[8:12]
     me = place[0]
     copies = bring(
-        weight_pairs(me & 1, (down_weight, partner, cross.at[me & 1], cross_partner), w_down)
+        weight_pairs(me & 1, (down_weight, partner.at[2], cross.at[me & 1], cross_partner), w_down)
         + [(gate_pick_in, gate_pick), (hidden_in, hidden)],
         sems,
     )
@@ -417,7 +412,7 @@
     me, expert = place[0], place[1]
     copies = bring(
         [(cot_in, cot)]
-        + weight_pairs(me & 1, (down_weight, partner, cross.at[me & 1], cross_partner), w_down)
+        + weight_pairs(me & 1, (down_weight, partner.at[2], cross.at[me & 1], cross_partner), w_down)
         + [(gate_pick_in, gate_pick), (hidden_in, hidden), (rows_in, rows), (act_in, act),
            (slope_in, slope), (router_in, router)],
         sems,
@@ -465,8 +460,8 @@
     copies = bring(
         [(pick_in, pick), (d_gate_in, d_gate), (d_up_in, d_up), (logit_in, logit_grad),
          (router_in, router)]
-        + weight_pairs(core, (gate_weight, partner.at[0], cross.at[0, core], cross_partner.at[0]), w_gate)
-        + weight_pairs(core, (up_weight, partner.at[1], cross.at[1, core], cross_partner.at[1]), w_up),
+        + weight_pairs(core, (gate_weight, partner.at[0], cross.at[0], cross_partner.at[0]), w_gate)
+        + weight_pairs(core, (up_weight, partner.at[1], cross.at[1], cross_partner.at[1]), w_up),
         sems,
     )
     for copy in copies:
@@ -529,55 +524,57 @@
 
     payload, step = pl.pallas_call(
         payload_kernel,
-        out_shape=[shape((2 * row_count + 16, model_width), bf16), shape((8, 128), f32)],
+        out_shape=[shape((2 * row_count + 16, model_width), bf16), shape((8, 128), jnp.int32)],
         cost_estimate=pl.CostEstimate(flops=LONG, bytes_accessed=LONG, transcendentals=0),
     )(tokens, grad_out, routes.T, router.T)
-    near, far_side = ring(payload, 1), ring(payload, -1)
-    payload_partner = dp_swap(payload, 1)
-    in_cross = dp_swap(jnp.stack([gate_weight, up_weight]), 2)
+    group = lax.axis_index("groups")
+    near, payload_partner = ring(payload, 1), dp_swap(payload, 1)
+    payload, payload_partner = together(payload, payload_partner)
+    far_side = ring(payload, -1)
+    in_sent = jnp.where(group == 0, gate_weight, up_weight)
+    cut = stored_rows // 8 * 3
+    in_came = [dp_swap(in_sent[:, :cut], 2), dp_swap(in_sent[:, cut:], 2)]
     down_cross = dp_swap(after(down_weight, payload_partner), 2)
-    step = next_step(step, payload)
-    near, step = together(near, step)
+    in_other = [lax.ppermute(in_came[0], "groups", [(0, 1), (1, 0)])]
+    near, in_came[0], step = together(near, in_came[0], step)
     far = ring(near, 1)
     partner = dp_swap(
-        after(
-            jnp.stack([of_expert(w, 1 - core) for w in (gate_weight, up_weight, down_weight)]),
-            payload_partner,
-        ),
-        1,
-    )
-    step = next_step(step, near, partner)
-    far_side, far, in_cross, near = together(far_side, far, in_cross, near, step)[0:4]
-    near_partner = dp_swap(near, 1)
-    far_side_partner = dp_swap(far_side, 1)
-    theirs_cross = lax.dynamic_index_in_dim(in_cross, 1 - core, 1, keepdims=False)
-    in_cross_partner = dp_swap(theirs_cross, 1)
-    far_partner = dp_swap(far, 1)
+        jnp.stack([of_expert(w, 1 - core) for w in (gate_weight, up_weight, down_weight)]), 1
+    )
+    step = next_step(step)
+    in_came[1], partner, step = together(in_came[1], partner, step)
+    in_other.append(lax.ppermute(in_came[1], "groups", [(0, 1), (1, 0)]))
+    step = next_step(step)
+    in_other[0], in_other[1], step = together(*in_other, step)
+    far_side, far, step = together(far_side, far, step)
+    down_cross, step_down = together(down_cross, step)
+    near_partner, far_side_partner, far_partner = dp_swap(near, 1), dp_swap(far_side, 1), dp_swap(far, 1)
+
+    def of_core(first, second, which):
+        came = jnp.concatenate([of_expert(part, which) for part in first])
+        other = jnp.concatenate([of_expert(part, which) for part in second])
+        return jnp.where(group == 0, jnp.stack([came, other]), jnp.stack([other, came]))
+
+    in_cross = of_core(in_came, in_other, core)
+    in_cross_partner = dp_swap(of_core(in_came, in_other, 1 - core), 1)
+    down_cross_partner = dp_swap(of_expert(down_cross, 1 - core), 1)
     payloads = [payload, payload_partner, near, near_partner, far, far_partner, far_side,
                 far_side_partner]
     in_weights = [gate_weight, up_weight, partner, in_cross, in_cross_partner]
     router_rows = jnp.pad(router.T.astype(f32), ((0, 16 - id_count), (0, 0)))
-    pick, gate_pick, rows, cot = local_kernel(
-        pick_kernel,
-        place,
-        payloads,
-        [shape(table, bf16)] * 2 + [shape(wide, bf16)] * 2,
-        [vmem((8, *payload.shape), bf16), pltpu.SemaphoreType.DMA((8,))],
-        0,
-    )
-    rows, down_cross = together(rows, down_cross)
-    down_cross_partner = dp_swap(of_expert(down_cross, 1 - core), 1)
-    hidden, act, slope, *down_parts = local_kernel(
+    pick, gate_pick, rows, cot, hidden, act, slope, *down_parts = local_kernel(
         forward_kernel,
         place,
-        [gate_pick, rows, cot, *in_weights],
-        [shape(narrow, bf16)] * 3 + [shape(weight_rows, bf16)] * 4,
-        [vmem(table, bf16), vmem(wide, bf16), vmem(wide, bf16), whole_weight, whole_weight,
-         vmem(wide, bf16), pltpu.SemaphoreType.DMA((11,))],
+        [*payloads, *in_weights],
+        [shape(table, bf16)] * 2 + [shape(wide, bf16)] * 2 + [shape(narrow, bf16)] * 3
+        + [shape(weight_rows, bf16)] * 4,
+        [vmem((8, *payload.shape), bf16), whole_weight, whole_weight, vmem(wide, bf16),
+         pltpu.SemaphoreType.DMA((16,))],
         LONG,
+        step,
     )
     hidden, down_cross_partner = together(hidden, down_cross_partner)
-    down_weights = [down_weight, partner[2], down_cross, down_cross_partner]
+    down_weights = [down_weight, partner, down_cross, down_cross_partner]
     def add(one, two):
         return one.astype(f32) + two.astype(f32)
 
@@ -618,6 +615,7 @@
         [shape(wide, bf16)] * 2,
         [vmem(table, bf16), vmem(narrow, bf16), whole_weight, pltpu.SemaphoreType.DMA((6,))],
         LONG,
+        step_down,
     )
     down_came, down_came_partner = dp_swap(down_parts[2], 2), dp_swap(down_parts[3], 3)
     parts = [mixed_other[k * row_count : (k + 1) * row_count] for k in range(4)]
@@ -677,8 +675,6 @@
     up_came, in_came_partner = dp_swap(up_sent, 2), dp_swap(in_parts[2], 3)
     small = small + small_came
     back_came, small_came = together(dp_swap(back_other, 1), dp_swap(small, 1))
-    step = next_step(step, back_came, small_came)
-    back_own, back_came, small_came = together(back_own, back_came, small_came, step)[0:3]
     back_late = sum_slots(back_own[: 2 * row_count], jnp.split(back_came[: 2 * row_count], 2))
     back_first = sum_slots(back_own[2 * row_count :], jnp.split(back_came[2 * row_count :], 2))
     back_near, back_side = ring(back_first[0], -1), ring(back_first[1], 1)

time: 139 us -> 124 us (0.89)
  waiting for transfers between devices: 60.7 us -> 38.8 us
  local copies, waits for them, and re-layouts: 4.8 us -> 8.82 us
  starting transfers between devices: 32 us -> 33.7 us
    ppermute x9, waiting for transfers between devices: 40.7 us -> 14.9 us  [ring(): lax.ppermute(value, 'expert', [(i, (i + step) % size) for i in range(size)])]
    ppermute x0 -> x2, waiting for transfers between devices: none -> 8.04 us  [the longest x1 8.03 us: on_device_paired(): in_other.append(lax.ppermute(in_came[1], 'groups', [(0, 1), (1, 0)]))]
    squeeze x1 -> x5, local copies, waits for them, and re-layouts: 0.03 us -> 4.94 us  [of_expert(): return lax.dynamic_index_in_dim(weight, which, 0, keepdims=False)]
    ppermute x22 -> x23, waiting for transfers between devices: 20 us -> 15.9 us  [dp_swap(): return lax.ppermute(value, 'dp', [(i, i ^ step) for i in range(4)])]
    ppermute x0 -> x2, starting transfers between devices: none -> 3.04 us  [the longest x1 1.52 us: on_device_paired(): in_other.append(lax.ppermute(in_came[1], 'groups', [(0, 1), (1, 0)]))]
    squeeze x2 -> x0, local copies, waits for them, and re-layouts: 2.21 us -> none  [the longest x1 1.18 us: on_device_paired(): lax.dynamic_index_in_dim(in_cross, 1 - core, 1, keepdims=False)]
    slice x0 -> x2, local copies, waits for them, and re-layouts: none -> 1.54 us  [on_device_paired(): in_came = [dp_swap(in_sent[:, :cut], 2), dp_swap(in_sent[:, cut:], 2)]]
    ppermute x22 -> x23, starting transfers between devices: 12.1 us -> 11.4 us  [dp_swap(): return lax.ppermute(value, 'dp', [(i, i ^ step) for i in range(4)])]
  transfers between devices with their start and end apart: 33 -> 36, of which waited for: 16 -> 15; matrix products, arithmetic and copies ran while one was open for 9% -> 14% of each run, Pallas kernels for 19% -> 21%
where the time goes in v4:
time: 124 us; the launch traced here: 123 us
  waiting for transfers between devices  38.8 us (31%)
  starting transfers between devices  33.7 us (27%)
  Pallas kernels  28.1 us (23%)
  local copies, waits for them, and re-layouts  8.82 us (7%)
  other arithmetic  8.14 us (7%)
  matrix products  4.28 us (3%)
    pallas_call x4, Pallas kernels, local_kernel(): pl.pallas_call(kernel, out_shape=outputs, in_specs=[pl.BlockSpec(memory_s...  23.4 us
    ppermute x9, starting transfers between devices, ring(): lax.ppermute(value, 'expert', [(i, (i + step) % size) for i in range(size)])  17.3 us
    ppermute x23, waiting for transfers between devices, dp_swap(): return lax.ppermute(value, 'dp', [(i, i ^ step) for i in range(4)])  15.9 us
    ppermute x9, waiting for transfers between devices, ring(): lax.ppermute(value, 'expert', [(i, (i + step) % size) for i in range(size)])  14.9 us
    ppermute x23, starting transfers between devices, dp_swap(): return lax.ppermute(value, 'dp', [(i, i ^ step) for i in range(4)])  11.4 us
    ppermute x1, waiting for transfers between devices, on_device_paired(): in_other.append(lax.ppermute(in_came[1], 'groups', [(0, 1), (1, 0)]))  8.03 us
    squeeze x5, local copies, waits for them, and re-layouts, of_expert(): return lax.dynamic_index_in_dim(weight, which, 0, keepdims=False)  4.94 us
    dot_general x3, matrix products, mm(): return jnp.dot(a, b, preferred_element_type=jnp.float32)  2.6 us
  transfers between devices with their start and end apart: 36, of which 15 were waited for; matrix products, arithmetic and copies ran while one was open for 14% of the time, Pallas kernels for 21%

profile of v4, /device:TPU:0, one launch (start us, length us, event | category | flops | bytes accessed | tf_op | source)
XLA Modules:
  0.0 123.1 jit_solution(11529162765238672005)
XLA Ops:
  0.7 2.2 %shard_map.152 = (bf16[272,1024]{1,0:T(8,128)(2,1)}, s32[8,128]{1,0:T(8,128)}) custom-call(bf16[128,1024]{1,0:T(8,128)(2,1)} %tokens.1, bf16[128,1024]{1,0:T(8,128)(2,1)} %grads.1, s32[6,128]{1,0:T(8,128)} %bitcast.70, bf16[12,1024]{1,0:T(8,128)(2,1)} %bitcast.66), custom_call_target="tpu_custom_call" | custom-call | flops 20000000000 | bytes 20000000000 | tf_op jit(solution)/shard_map/pallas_call | solution.py:525
  2.8 3.0 %collective-permute-start.2 = (bf16[272,1024]{1,0:T(8,128)(2,1)}, bf16[272,1024]{1,0:T(8,128)(2,1)}, u32[]{:S(2)}, u32[]{:S(2)}) collective-permute-start(bf16[272,1024]{1,0:T(8,128)(2,1)} %get-tuple-element.89.refs_1_), channel_id=1, source_target_pairs={{0,4},{4,8},{8,12},{12,0},{1,5},{5,9},{9,13},{13,1},{2,6},{6,10},{... | collective-permute-start | bytes 1671176 | tf_op jit(solution)/shard_map/ppermute | solution.py:489
  6.7 1.5 %collective-permute-start.3 = (bf16[2,96,768]{2,1,0:T(8,128)(2,1)}, bf16[2,96,768]{2,1,0:T(8,128)(2,1)}, u32[]{:S(2)}, u32[]{:S(2)}) collective-permute-start(bf16[2,96,768]{2,1,0:T(8,128)(2,1)} %slice.95), channel_id=1, source_target_pairs={{0,2},{1,3},{2,0},{3,1},{4,6},{5,7},{6,4},{7,5},{8,10},{9,11},{10,... | collective-permute-start | bytes 884744 | tf_op jit(solution)/shard_map/ppermute | solution.py:484
  11.4 1.4 %multiply_reduce_fusion = (f32[128]{0:T(128)}, bf16[128,2]{0,1:T(2,128)(2,1)}, bf16[128,2]{0,1:T(2,128)(2,1)S(1)}, f32[128,2]{0,1:T(2,128)S(1)}) fusion(f32[128,4]{0,1:T(4,128)S(1)} %get-tuple-element.194, f32[128,2]{0,1:T(2,128)S(1)} %fusion.24, f32[128]{0:T(128)S(1)} %fusion.8, bf16[128,1024]{1,0:T(8,128)(2,1)S(1)} %copy-done.7, ...), kind=kOutput, calls=%fused_computation.76 | convolution fusion | flops 528256 | bytes 271360 | tf_op jit(solution)/shard_map/dot_general | solution.py:265
  14.3 2.5 %collective-permute-done.3 = bf16[2,96,768]{2,1,0:T(8,128)(2,1)} collective-permute-done((bf16[2,96,768]{2,1,0:T(8,128)(2,1)}, bf16[2,96,768]{2,1,0:T(8,128)(2,1)}, u32[]{:S(2)}, u32[]{:S(2)}) %collective-permute-start.3) | collective-permute-done | bytes 294944 | tf_op jit(solution)/shard_map/ppermute | solution.py:484
  16.8 1.5 %collective-permute-start.5 = (bf16[2,96,768]{2,1,0:T(8,128)(2,1)}, bf16[2,96,768]{2,1,0:T(8,128)(2,1)}, u32[]{:S(2)}, u32[]{:S(2)}) collective-permute-start(bf16[2,96,768]{2,1,0:T(8,128)(2,1)} %collective-permute-done.3), channel_id=1, source_target_pairs={{0,16},{16,0},{1,17},{17,1},{2,18},{18,2},{3,19},{19,3},{4,20},{20... | collective-permute-start | bytes 884744 | tf_op jit(solution)/shard_map/ppermute | solution.py:538
  18.3 2.2 %collective-permute-start.1 = (bf16[272,1024]{1,0:T(8,128)(2,1)}, bf16[272,1024]{1,0:T(8,128)(2,1)}, u32[]{:S(2)}, u32[]{:S(2)}) collective-permute-start(bf16[272,1024]{1,0:T(8,128)(2,1)} %get-tuple-element.89.refs_1_), channel_id=1, source_target_pairs={{0,12},{4,0},{8,4},{12,8},{1,13},{5,1},{9,5},{13,9},{2,14},{6,2},{... | collective-permute-start | bytes 1671176 | tf_op jit(solution)/shard_map/ppermute | solution.py:489
  22.2 1.7 %dynamic-slice_bitcast_fusion.6 = (bf16[96,768]{1,0:T(8,128)(2,1)}, bf16[96,768]{1,0:T(8,128)(2,1)}) fusion(bf16[2,96,768]{2,1,0:T(8,128)(2,1)} %collective-permute-done.3, s32[]{:T(128)S(6)} %select_n.66, s32[]{:T(128)S(6)} %select_n.67), kind=kLoop, calls=%fused_computation.51 | loop fusion | bytes 589832 | tf_op jit(solution)/shard_map/jit(dynamic_index_in_dim)/squeeze | solution.py:512
  23.9 3.1 %collective-permute-done.6 = bf16[2,160,768]{2,1,0:T(8,128)(2,1)} collective-permute-done((bf16[2,160,768]{2,1,0:T(8,128)(2,1)}, bf16[2,160,768]{2,1,0:T(8,128)(2,1)}, u32[]{:S(2)}, u32[]{:S(2)}) %collective-permute-start.6) | collective-permute-done | bytes 491552 | tf_op jit(solution)/shard_map/ppermute | solution.py:484
  26.9 1.5 %collective-permute-start.13 = (bf16[2,256,768]{2,1,0:T(8,128)(2,1)S(1)}, bf16[2,256,768]{2,1,0:T(8,128)(2,1)S(1)}, u32[]{:S(2)}, u32[]{:S(2)}) collective-permute-start(bf16[2,256,768]{2,1,0:T(8,128)(2,1)S(1)} %copy-done.3), channel_id=1, source_target_pairs={{0,2},{1,3},{2,0},{3,1},{4,6},{5,7},{6,4},{7,5},{8,10},{9,11},{10,... | collective-permute-start | bytes 2359304 | tf_op jit(solution)/shard_map/ppermute | solution.py:484
  28.4 1.5 %collective-permute-start.8 = (bf16[2,160,768]{2,1,0:T(8,128)(2,1)}, bf16[2,160,768]{2,1,0:T(8,128)(2,1)}, u32[]{:S(2)}, u32[]{:S(2)}) collective-permute-start(bf16[2,160,768]{2,1,0:T(8,128)(2,1)} %collective-permute-done.6), channel_id=1, source_target_pairs={{0,16},{16,0},{1,17},{17,1},{2,18},{18,2},{3,19},{19,3},{4,20},{20... | collective-permute-start | bytes 1474568 | tf_op jit(solution)/shard_map/ppermute | solution.py:546
  33.3 8.0 %collective-permute-done.8 = bf16[2,160,768]{2,1,0:T(8,128)(2,1)} collective-permute-done((bf16[2,160,768]{2,1,0:T(8,128)(2,1)}, bf16[2,160,768]{2,1,0:T(8,128)(2,1)}, u32[]{:S(2)}, u32[]{:S(2)}) %collective-permute-start.8) | collective-permute-done | bytes 491552 | tf_op jit(solution)/shard_map/ppermute | solution.py:546
  48.4 1.4 %collective-permute-done.11.refs_8_ = bf16[272,1024]{1,0:T(8,128)(2,1)S(1)} collective-permute-done((bf16[272,1024]{1,0:T(8,128)(2,1)}, bf16[272,1024]{1,0:T(8,128)(2,1)S(1)}, u32[]{:S(2)}, u32[]{:S(2)}) %collective-permute-start.11) | collective-permute-done | bytes 557088 | tf_op jit(solution)/shard_map/ppermute | solution.py:484
  49.7 6.0 %shard_map.155 = (bf16[512,128]{1,0:T(8,128)(2,1)S(1)}, bf16[512,128]{1,0:T(8,128)(2,1)S(1)}, bf16[512,1024]{1,0:T(8,128)(2,1)S(1)}, bf16[512,1024]{1,0:T(8,128)...) custom-call(s32[2]{0:T(128)S(1)} %pad_add_fusion.place, ...), custom_call_target="tpu_custom_call" | custom-call | flops 20000000000 | bytes 20000000000 | tf_op jit(solution)/shard_map/pallas_call | solution.py:242
  55.8 1.6 %collective-permute-start.17 = (bf16[256,768]{1,0:T(8,128)(2,1)S(1)}, bf16[256,768]{1,0:T(8,128)(2,1)S(1)}, u32[]{:S(2)}, u32[]{:S(2)}) collective-permute-start(bf16[256,768]{1,0:T(8,128)(2,1)S(1)} %get-tuple-element.115), channel_id=1, source_target_pairs={{0,2},{1,3},{2,0},{3,1},{4,6},{5,7},{6,4},{7,5},{8,10},{9,11},{10,... | collective-permute-start | bytes 1179656 | tf_op jit(solution)/shard_map/ppermute | solution.py:484
  57.3 4.4 %shard_map.156 = (bf16[512,1024]{1,0:T(8,128)(2,1)S(1)}, bf16[512,1024]{1,0:T(8,128)(2,1)S(1)}) custom-call(s32[2]{0:T(128)S(1)} %pad_add_fusion.place, s32[8,128]{1,0:T(8,128)S(1)} %copy-done.6, bf16[512,128]{1,0:T(8,128)(2,1)S(1)} %get-tuple-element.105.refs_1_, bf16[512,768]{1,0:T(8,128)(2,1)S(1)} %get-tuple-element.110.refs_2_.refs_3_, ...), custom_call_target="tpu_custom_call" | custom-call | flops 20000000000 | bytes 20000000000 | tf_op jit(solution)/shard_map/pallas_call | solution.py:242
  63.8 4.0 %collective-permute-done.17 = bf16[256,768]{1,0:T(8,128)(2,1)S(1)} collective-permute-done((bf16[256,768]{1,0:T(8,128)(2,1)S(1)}, bf16[256,768]{1,0:T(8,128)(2,1)S(1)}, u32[]{:S(2)}, u32[]{:S(2)}) %collective-permute-start.17) | collective-permute-done | bytes 393248 | tf_op jit(solution)/shard_map/ppermute | solution.py:484
  67.9 2.3 %collective-permute-start.19 = (bf16[128,1024]{1,0:T(8,128)(2,1)S(1)}, bf16[128,1024]{1,0:T(8,128)(2,1)S(1)}, u32[]{:S(2)}, u32[]{:S(2)}) collective-permute-start(bf16[128,1024]{1,0:T(8,128)(2,1)S(1)} %add_convert_fusion.10), channel_id=1, source_target_pairs={{0,12},{4,0},{8,4},{12,8},{1,13},{5,1},{9,5},{13,9},{2,14},{6,2},{... | collective-permute-start | bytes 786440 | tf_op jit(solution)/shard_map/ppermute | solution.py:489
  70.1 5.7 %shard_map.157 = (bf16[512,768]{1,0:T(8,128)(2,1)S(1)}, bf16[512,768]{1,0:T(8,128)(2,1)S(1)}, bf16[512,128]{1,0:T(8,128)(2,1)S(1)}, f32[8,1024]{1,0:T(8,128)S(1)...) custom-call(s32[2]{0:T(128)S(1)} %pad_add_fusion.place, ...), custom_call_target="tpu_custom_call" | custom-call | flops 20000000000 | bytes 20000000000 | tf_op jit(solution)/shard_map/pallas_call | solution.py:242
  76.0 1.6 %collective-permute-start.24 = (f32[16,1024]{1,0:T(8,128)S(1)}, f32[16,1024]{1,0:T(8,128)S(1)}, u32[]{:S(2)}, u32[]{:S(2)}) collective-permute-start(f32[16,1024]{1,0:T(8,128)S(1)} %pad_maximum_fusion.1), channel_id=1, source_target_pairs={{0,2},{1,3},{2,0},{3,1},{4,6},{5,7},{6,4},{7,5},{8,10},{9,11},{10,... | collective-permute-start | bytes 196616 | tf_op jit(solution)/shard_map/ppermute | solution.py:484
  77.8 2.7 %collective-permute-start.26 = (bf16[128,1024]{1,0:T(8,128)(2,1)S(1)}, bf16[128,1024]{1,0:T(8,128)(2,1)S(1)}, u32[]{:S(2)}, u32[]{:S(2)}) collective-permute-start(bf16[128,1024]{1,0:T(8,128)(2,1)S(1)} %get-tuple-element.172), channel_id=1, source_target_pairs={{0,12},{4,0},{8,4},{12,8},{1,13},{5,1},{9,5},{13,9},{2,14},{6,2},{... | collective-permute-start | bytes 786440 | tf_op jit(solution)/shard_map/ppermute | solution.py:489
  81.1 7.2 %shard_map.158 = (bf16[512,1024]{1,0:T(8,128)(2,1)S(1)}, bf16[512,1024]{1,0:T(8,128)(2,1)S(1)}) custom-call(s32[2]{0:T(128)S(1)} %pad_add_fusion.place, bf16[512,128]{1,0:T(8,128)(2,1)S(1)} %get-tuple-element.104.refs_0_, bf16[512,768]{1,0:T(8,128)(2,1)S(1)} %get-tuple-element.130.refs_1_, bf16[512,768]{1,0:T(8,128)(2,1)S(1)} %get-tuple-element.131.refs_2_, ...), custom_call_target="tpu_custom_call" | custom-call | flops 20000000000 | bytes 20000000000 | tf_op jit(solution)/shard_map/pallas_call | solution.py:242
  88.4 2.9 %collective-permute-done.25 = bf16[128,1024]{1,0:T(8,128)(2,1)S(1)} collective-permute-done((bf16[128,1024]{1,0:T(8,128)(2,1)S(1)}, bf16[128,1024]{1,0:T(8,128)(2,1)S(1)}, u32[]{:S(2)}, u32[]{:S(2)}) %collective-permute-start.25) | collective-permute-done | bytes 262176 | tf_op jit(solution)/shard_map/ppermute | solution.py:489
  92.4 1.5 %collective-permute-start.31 = (bf16[256,768]{1,0:T(8,128)(2,1)S(1)}, bf16[256,768]{1,0:T(8,128)(2,1)S(1)}, u32[]{:S(2)}, u32[]{:S(2)}) collective-permute-start(bf16[256,768]{1,0:T(8,128)(2,1)S(1)} %get-tuple-element.147), channel_id=1, source_target_pairs={{0,2},{1,3},{2,0},{3,1},{4,6},{5,7},{6,4},{7,5},{8,10},{9,11},{10,... | collective-permute-start | bytes 1179656 | tf_op jit(solution)/shard_map/ppermute | solution.py:484
  94.1 1.9 %collective-permute-start.34 = (f32[16,1024]{1,0:T(8,128)S(1)}, f32[16,1024]{1,0:T(8,128)S(1)}, u32[]{:S(2)}, u32[]{:S(2)}) collective-permute-start(f32[16,1024]{1,0:T(8,128)S(1)} %add.161), channel_id=1, source_target_pairs={{0,4},{4,0},{8,12},{12,8},{1,5},{5,1},{9,13},{13,9},{2,6},{6,2},{1... | collective-permute-start | bytes 196616 | tf_op jit(solution)/shard_map/ppermute | solution.py:682
  96.4 3.6 %collective-permute-start.29 = (bf16[128,1024]{1,0:T(8,128)(2,1)S(1)}, bf16[128,1024]{1,0:T(8,128)(2,1)S(1)}, u32[]{:S(2)}, u32[]{:S(2)}) collective-permute-start(bf16[128,1024]{1,0:T(8,128)(2,1)S(1)} %get-tuple-element.169), channel_id=1, source_target_pairs={{0,12},{4,0},{8,4},{12,8},{1,13},{5,1},{9,5},{13,9},{2,14},{6,2},{... | collective-permute-start | bytes 786440 | tf_op jit(solution)/shard_map/ppermute | solution.py:489
  101.1 3.3 %collective-permute-done.31 = bf16[256,768]{1,0:T(8,128)(2,1)S(1)} collective-permute-done((bf16[256,768]{1,0:T(8,128)(2,1)S(1)}, bf16[256,768]{1,0:T(8,128)(2,1)S(1)}, u32[]{:S(2)}, u32[]{:S(2)}) %collective-permute-start.31) | collective-permute-done | bytes 393248 | tf_op jit(solution)/shard_map/ppermute | solution.py:484
  104.4 2.7 %collective-permute-done.30 = bf16[128,1024]{1,0:T(8,128)(2,1)S(1)} collective-permute-done((bf16[128,1024]{1,0:T(8,128)(2,1)S(1)}, bf16[128,1024]{1,0:T(8,128)(2,1)S(1)}, u32[]{:S(2)}, u32[]{:S(2)}) %collective-permute-start.30) | collective-permute-done | bytes 262176 | tf_op jit(solution)/shard_map/ppermute | solution.py:489
  107.2 3.6 %collective-permute-done.29 = bf16[128,1024]{1,0:T(8,128)(2,1)S(1)} collective-permute-done((bf16[128,1024]{1,0:T(8,128)(2,1)S(1)}, bf16[128,1024]{1,0:T(8,128)(2,1)S(1)}, u32[]{:S(2)}, u32[]{:S(2)}) %collective-permute-start.29) | collective-permute-done | bytes 262176 | tf_op jit(solution)/shard_map/ppermute | solution.py:489
  110.9 3.2 %collective-permute-start.33 = (bf16[128,1024]{1,0:T(8,128)(2,1)S(1)}, bf16[128,1024]{1,0:T(8,128)(2,1)S(1)}, u32[]{:S(2)}, u32[]{:S(2)}) collective-permute-start(bf16[128,1024]{1,0:T(8,128)(2,1)S(1)} %add_convert_fusion.2), channel_id=1, source_target_pairs={{0,12},{4,0},{8,4},{12,8},{1,13},{5,1},{9,5},{13,9},{2,14},{6,2},{... | collective-permute-start | bytes 786440 | tf_op jit(solution)/shard_map/ppermute | solution.py:489
  115.2 4.0 %collective-permute-done.33 = bf16[128,1024]{1,0:T(8,128)(2,1)S(1)} collective-permute-done((bf16[128,1024]{1,0:T(8,128)(2,1)S(1)}, bf16[128,1024]{1,0:T(8,128)(2,1)S(1)}, u32[]{:S(2)}, u32[]{:S(2)}) %collective-permute-start.33) | collective-permute-done | bytes 262176 | tf_op jit(solution)/shard_map/ppermute | solution.py:489
  121.7 1.4 %select_convert_fusion = (bf16[2,256,768]{2,1,0:T(8,128)(2,1)}, bf16[2,256,768]{2,1,0:T(8,128)(2,1)}) fusion(bf16[256,768]{1,0:T(8,128)(2,1)S(1)} %get-tuple-element.170, bf16[256,768]{1,0:T(8,128)(2,1)S(1)} %get-tuple-element.176, pred[2]{0:T(512)(128)(4,1)S(1)} %iota_compare_fusion.1, bf16[256,768]{1,0:T(8,128)(2,1)S(1)} %get-tuple-element.171, ...), kind=kLoop, calls=%fused_computation | loop fusion | flops 786432 | bytes 3145730 | tf_op jit(solution)/shard_map/convert_element_type | solution.py:588
  (143 shorter events, 26.8 us)
Async XLA Ops:
  2.8 18.0 %collective-permute-start.2 = (bf16[272,1024]{1,0:T(8,128)(2,1)}, bf16[272,1024]{1,0:T(8,128)(2,1)}, u32[]{:S(2)}, u32[]{:S(2)}) collective-permute-start(bf16[272,1024]{1,0:T(8,128)(2,1)} %get-tuple-element.89.refs_1_), channel_id=1, source_target_pairs={{0,4},{4,8},{8,12},{12,0},{1,5},{5,9},{9,13},{13,1},{2,6},{6,10},{... | collective-permute-start | bytes 1671176 | tf_op jit(solution)/shard_map/ppermute | solution.py:489
  5.8 12.5 %collective-permute-start = (bf16[272,1024]{1,0:T(8,128)(2,1)}, bf16[272,1024]{1,0:T(8,128)(2,1)S(1)}, u32[]{:S(2)}, u32[]{:S(2)}) collective-permute-start(bf16[272,1024]{1,0:T(8,128)(2,1)} %get-tuple-element.89.refs_1_), channel_id=1, source_target_pairs={{0,1},{1,0},{2,3},{3,2},{4,5},{5,4},{6,7},{7,6},{8,9},{9,8},{10,11... | collective-permute-start | bytes 1671176 | tf_op jit(solution)/shard_map/ppermute | solution.py:484
  6.7 10.1 %collective-permute-start.3 = (bf16[2,96,768]{2,1,0:T(8,128)(2,1)}, bf16[2,96,768]{2,1,0:T(8,128)(2,1)}, u32[]{:S(2)}, u32[]{:S(2)}) collective-permute-start(bf16[2,96,768]{2,1,0:T(8,128)(2,1)} %slice.95), channel_id=1, source_target_pairs={{0,2},{1,3},{2,0},{3,1},{4,6},{5,7},{6,4},{7,5},{8,10},{9,11},{10,... | collective-permute-start | bytes 884744 | tf_op jit(solution)/shard_map/ppermute | solution.py:484
  9.0 18.0 %collective-permute-start.6 = (bf16[2,160,768]{2,1,0:T(8,128)(2,1)}, bf16[2,160,768]{2,1,0:T(8,128)(2,1)}, u32[]{:S(2)}, u32[]{:S(2)}) collective-permute-start(bf16[2,160,768]{2,1,0:T(8,128)(2,1)} %slice.96), channel_id=1, source_target_pairs={{0,2},{1,3},{2,0},{3,1},{4,6},{5,7},{6,4},{7,5},{8,10},{9,11},{10,... | collective-permute-start | bytes 1474568 | tf_op jit(solution)/shard_map/ppermute | solution.py:484
  10.8 17.6 %collective-permute-start.7 = (bf16[3,256,768]{2,1,0:T(8,128)(2,1)}, bf16[3,256,768]{2,1,0:T(8,128)(2,1)}, u32[]{:S(2)}, u32[]{:S(2)}) collective-permute-start(bf16[3,256,768]{2,1,0:T(8,128)(2,1)} %pad_maximum_fusion), channel_id=1, source_target_pairs={{0,1},{1,0},{2,3},{3,2},{4,5},{5,4},{6,7},{7,6},{8,9},{9,8},{10,11... | collective-permute-start | bytes 3538952 | tf_op jit(solution)/shard_map/ppermute | solution.py:484
  16.8 16.5 %collective-permute-start.5 = (bf16[2,96,768]{2,1,0:T(8,128)(2,1)}, bf16[2,96,768]{2,1,0:T(8,128)(2,1)}, u32[]{:S(2)}, u32[]{:S(2)}) collective-permute-start(bf16[2,96,768]{2,1,0:T(8,128)(2,1)} %collective-permute-done.3), channel_id=1, source_target_pairs={{0,16},{16,0},{1,17},{17,1},{2,18},{18,2},{3,19},{19,3},{4,20},{20... | collective-permute-start | bytes 884744 | tf_op jit(solution)/shard_map/ppermute | solution.py:538
  18.3 26.6 %collective-permute-start.1 = (bf16[272,1024]{1,0:T(8,128)(2,1)}, bf16[272,1024]{1,0:T(8,128)(2,1)}, u32[]{:S(2)}, u32[]{:S(2)}) collective-permute-start(bf16[272,1024]{1,0:T(8,128)(2,1)} %get-tuple-element.89.refs_1_), channel_id=1, source_target_pairs={{0,12},{4,0},{8,4},{12,8},{1,13},{5,1},{9,5},{13,9},{2,14},{6,2},{... | collective-permute-start | bytes 1671176 | tf_op jit(solution)/shard_map/ppermute | solution.py:489
  22.1 24.0 %collective-permute-start.4 = (bf16[272,1024]{1,0:T(8,128)(2,1)}, bf16[272,1024]{1,0:T(8,128)(2,1)}, u32[]{:S(2)}, u32[]{:S(2)}) collective-permute-start(bf16[272,1024]{1,0:T(8,128)(2,1)} %collective-permute-done.2.refs_3_), channel_id=1, source_target_pairs={{0,4},{4,8},{8,12},{12,0},{1,5},{5,9},{9,13},{13,1},{2,6},{6,10},{... | collective-permute-start | bytes 1671176 | tf_op jit(solution)/shard_map/ppermute | solution.py:489
  26.9 19.9 %collective-permute-start.13 = (bf16[2,256,768]{2,1,0:T(8,128)(2,1)S(1)}, bf16[2,256,768]{2,1,0:T(8,128)(2,1)S(1)}, u32[]{:S(2)}, u32[]{:S(2)}) collective-permute-start(bf16[2,256,768]{2,1,0:T(8,128)(2,1)S(1)} %copy-done.3), channel_id=1, source_target_pairs={{0,2},{1,3},{2,0},{3,1},{4,6},{5,7},{6,4},{7,5},{8,10},{9,11},{10,... | collective-permute-start | bytes 2359304 | tf_op jit(solution)/shard_map/ppermute | solution.py:484
  28.4 12.9 %collective-permute-start.8 = (bf16[2,160,768]{2,1,0:T(8,128)(2,1)}, bf16[2,160,768]{2,1,0:T(8,128)(2,1)}, u32[]{:S(2)}, u32[]{:S(2)}) collective-permute-start(bf16[2,160,768]{2,1,0:T(8,128)(2,1)} %collective-permute-done.6), channel_id=1, source_target_pairs={{0,16},{16,0},{1,17},{17,1},{2,18},{18,2},{3,19},{19,3},{4,20},{20... | collective-permute-start | bytes 1474568 | tf_op jit(solution)/shard_map/ppermute | solution.py:546
  43.6 6.1 %collective-permute-start.12 = (bf16[2,256,768]{2,1,0:T(8,128)(2,1)S(1)}, bf16[2,256,768]{2,1,0:T(8,128)(2,1)S(1)}, u32[]{:S(2)}, u32[]{:S(2)}) collective-permute-start(bf16[2,256,768]{2,1,0:T(8,128)(2,1)S(1)} %maximum_select_fusion.1), channel_id=1, source_target_pairs={{0,1},{1,0},{2,3},{3,2},{4,5},{5,4},{6,7},{7,6},{8,9},{9,8},{10,11... | collective-permute-start | bytes 2359304 | tf_op jit(solution)/shard_map/ppermute | solution.py:484
  44.8 2.4 %collective-permute-start.9 = (bf16[272,1024]{1,0:T(8,128)(2,1)}, bf16[272,1024]{1,0:T(8,128)(2,1)S(1)}, u32[]{:S(2)}, u32[]{:S(2)}) collective-permute-start(bf16[272,1024]{1,0:T(8,128)(2,1)} %collective-permute-done.2.refs_3_), channel_id=1, source_target_pairs={{0,1},{1,0},{2,3},{3,2},{4,5},{5,4},{6,7},{7,6},{8,9},{9,8},{10,11... | collective-permute-start | bytes 1671176 | tf_op jit(solution)/shard_map/ppermute | solution.py:484
  46.2 3.5 %collective-permute-start.11 = (bf16[272,1024]{1,0:T(8,128)(2,1)}, bf16[272,1024]{1,0:T(8,128)(2,1)S(1)}, u32[]{:S(2)}, u32[]{:S(2)}) collective-permute-start(bf16[272,1024]{1,0:T(8,128)(2,1)} %collective-permute-done.1.refs_7_), channel_id=1, source_target_pairs={{0,1},{1,0},{2,3},{3,2},{4,5},{5,4},{6,7},{7,6},{8,9},{9,8},{10,11... | collective-permute-start | bytes 1671176 | tf_op jit(solution)/shard_map/ppermute | solution.py:484
  46.9 8.9 %collective-permute-start.14 = (bf16[256,768]{1,0:T(8,128)(2,1)S(1)}, bf16[256,768]{1,0:T(8,128)(2,1)S(1)}, u32[]{:S(2)}, u32[]{:S(2)}) collective-permute-start(bf16[256,768]{1,0:T(8,128)(2,1)S(1)} %dynamic-slice_bitcast_fusion), channel_id=1, source_target_pairs={{0,1},{1,0},{2,3},{3,2},{4,5},{5,4},{6,7},{7,6},{8,9},{9,8},{10,11... | collective-permute-start | bytes 1179656 | tf_op jit(solution)/shard_map/ppermute | solution.py:484
  55.8 12.0 %collective-permute-start.17 = (bf16[256,768]{1,0:T(8,128)(2,1)S(1)}, bf16[256,768]{1,0:T(8,128)(2,1)S(1)}, u32[]{:S(2)}, u32[]{:S(2)}) collective-permute-start(bf16[256,768]{1,0:T(8,128)(2,1)S(1)} %get-tuple-element.115), channel_id=1, source_target_pairs={{0,2},{1,3},{2,0},{3,1},{4,6},{5,7},{6,4},{7,5},{8,10},{9,11},{10,... | collective-permute-start | bytes 1179656 | tf_op jit(solution)/shard_map/ppermute | solution.py:484
  62.7 13.1 %collective-permute-start.18 = (bf16[256,768]{1,0:T(8,128)(2,1)S(1)}, bf16[256,768]{1,0:T(8,128)(2,1)S(1)}, u32[]{:S(2)}, u32[]{:S(2)}) collective-permute-start(bf16[256,768]{1,0:T(8,128)(2,1)S(1)} %get-tuple-element.126), channel_id=1, source_target_pairs={{0,3},{1,2},{2,1},{3,0},{4,7},{5,6},{6,5},{7,4},{8,11},{9,10},{10,... | collective-permute-start | bytes 1179656 | tf_op jit(solution)/shard_map/ppermute | solution.py:484
  63.0 12.9 %collective-permute-start.21 = (bf16[256,768]{1,0:T(8,128)(2,1)S(1)}, bf16[256,768]{1,0:T(8,128)(2,1)S(1)}, u32[]{:S(2)}, u32[]{:S(2)}) collective-permute-start(bf16[256,768]{1,0:T(8,128)(2,1)S(1)} %get-tuple-element.129), channel_id=1, source_target_pairs={{0,1},{1,0},{2,3},{3,2},{4,5},{5,4},{6,7},{7,6},{8,9},{9,8},{10,11... | collective-permute-start | bytes 1179656 | tf_op jit(solution)/shard_map/ppermute | solution.py:484
  63.4 12.4 %collective-permute-start.20 = (bf16[256,1024]{1,0:T(8,128)(2,1)S(1)}, bf16[256,1024]{1,0:T(8,128)(2,1)S(1)}, u32[]{:S(2)}, u32[]{:S(2)}) collective-permute-start(bf16[256,1024]{1,0:T(8,128)(2,1)S(1)} %slice.80), channel_id=1, source_target_pairs={{0,1},{1,0},{2,3},{3,2},{4,5},{5,4},{6,7},{7,6},{8,9},{9,8},{10,11... | collective-permute-start | bytes 1572872 | tf_op jit(solution)/shard_map/ppermute | solution.py:484
  67.9 8.0 %collective-permute-start.19 = (bf16[128,1024]{1,0:T(8,128)(2,1)S(1)}, bf16[128,1024]{1,0:T(8,128)(2,1)S(1)}, u32[]{:S(2)}, u32[]{:S(2)}) collective-permute-start(bf16[128,1024]{1,0:T(8,128)(2,1)S(1)} %add_convert_fusion.10), channel_id=1, source_target_pairs={{0,12},{4,0},{8,4},{12,8},{1,13},{5,1},{9,5},{13,9},{2,14},{6,2},{... | collective-permute-start | bytes 786440 | tf_op jit(solution)/shard_map/ppermute | solution.py:489
  76.0 12.4 %collective-permute-start.24 = (f32[16,1024]{1,0:T(8,128)S(1)}, f32[16,1024]{1,0:T(8,128)S(1)}, u32[]{:S(2)}, u32[]{:S(2)}) collective-permute-start(f32[16,1024]{1,0:T(8,128)S(1)} %pad_maximum_fusion.1), channel_id=1, source_target_pairs={{0,2},{1,3},{2,0},{3,1},{4,6},{5,7},{6,4},{7,5},{8,10},{9,11},{10,... | collective-permute-start | bytes 196616 | tf_op jit(solution)/shard_map/ppermute | solution.py:484
  77.8 10.6 %collective-permute-start.26 = (bf16[128,1024]{1,0:T(8,128)(2,1)S(1)}, bf16[128,1024]{1,0:T(8,128)(2,1)S(1)}, u32[]{:S(2)}, u32[]{:S(2)}) collective-permute-start(bf16[128,1024]{1,0:T(8,128)(2,1)S(1)} %get-tuple-element.172), channel_id=1, source_target_pairs={{0,12},{4,0},{8,4},{12,8},{1,13},{5,1},{9,5},{13,9},{2,14},{6,2},{... | collective-permute-start | bytes 786440 | tf_op jit(solution)/shard_map/ppermute | solution.py:489
  80.5 10.8 %collective-permute-start.25 = (bf16[128,1024]{1,0:T(8,128)(2,1)S(1)}, bf16[128,1024]{1,0:T(8,128)(2,1)S(1)}, u32[]{:S(2)}, u32[]{:S(2)}) collective-permute-start(bf16[128,1024]{1,0:T(8,128)(2,1)S(1)} %get-tuple-element.173), channel_id=1, source_target_pairs={{0,4},{4,8},{8,12},{12,0},{1,5},{5,9},{9,13},{13,1},{2,6},{6,10},{... | collective-permute-start | bytes 786440 | tf_op jit(solution)/shard_map/ppermute | solution.py:489
  80.5 10.8 %collective-permute-start.22 = (bf16[256,768]{1,0:T(8,128)(2,1)S(1)}, bf16[256,768]{1,0:T(8,128)(2,1)S(1)}, u32[]{:S(2)}, u32[]{:S(2)}) collective-permute-start(bf16[256,768]{1,0:T(8,128)(2,1)S(1)} %get-tuple-element.135), channel_id=1, source_target_pairs={{0,2},{1,3},{2,0},{3,1},{4,6},{5,7},{6,4},{7,5},{8,10},{9,11},{10,... | collective-permute-start | bytes 1179656 | tf_op jit(solution)/shard_map/ppermute | solution.py:484
  81.1 10.2 %collective-permute-start.23 = (bf16[2,256,768]{2,1,0:T(8,128)(2,1)S(1)}, bf16[2,256,768]{2,1,0:T(8,128)(2,1)S(1)}, u32[]{:S(2)}, u32[]{:S(2)}) collective-permute-start(bf16[2,256,768]{2,1,0:T(8,128)(2,1)S(1)} %get-tuple-element.136), channel_id=1, source_target_pairs={{0,1},{1,0},{2,3},{3,2},{4,5},{5,4},{6,7},{7,6},{8,9},{9,8},{10,11... | collective-permute-start | bytes 2359304 | tf_op jit(solution)/shard_map/ppermute | solution.py:484
  91.3 2.8 %collective-permute-start.27 = (bf16[512,1024]{1,0:T(8,128)(2,1)S(1)}, bf16[512,1024]{1,0:T(8,128)(2,1)S(1)}, u32[]{:S(2)}, u32[]{:S(2)}) collective-permute-start(bf16[512,1024]{1,0:T(8,128)(2,1)S(1)} %get-tuple-element.144), channel_id=1, source_target_pairs={{0,1},{1,0},{2,3},{3,2},{4,5},{5,4},{6,7},{7,6},{8,9},{9,8},{10,11... | collective-permute-start | bytes 3145736 | tf_op jit(solution)/shard_map/ppermute | solution.py:484
  92.4 12.0 %collective-permute-start.31 = (bf16[256,768]{1,0:T(8,128)(2,1)S(1)}, bf16[256,768]{1,0:T(8,128)(2,1)S(1)}, u32[]{:S(2)}, u32[]{:S(2)}) collective-permute-start(bf16[256,768]{1,0:T(8,128)(2,1)S(1)} %get-tuple-element.147), channel_id=1, source_target_pairs={{0,2},{1,3},{2,0},{3,1},{4,6},{5,7},{6,4},{7,5},{8,10},{9,11},{10,... | collective-permute-start | bytes 1179656 | tf_op jit(solution)/shard_map/ppermute | solution.py:484
  93.9 26.2 %collective-permute-start.32 = (bf16[2,256,768]{2,1,0:T(8,128)(2,1)S(1)}, bf16[2,256,768]{2,1,0:T(8,128)(2,1)S(1)}, u32[]{:S(2)}, u32[]{:S(2)}) collective-permute-start(bf16[2,256,768]{2,1,0:T(8,128)(2,1)S(1)} %get-tuple-element.149), channel_id=1, source_target_pairs={{0,3},{1,2},{2,1},{3,0},{4,7},{5,6},{6,5},{7,4},{8,11},{9,10},{10,... | collective-permute-start | bytes 2359304 | tf_op jit(solution)/shard_map/ppermute | solution.py:484
  94.1 7.0 %collective-permute-start.34 = (f32[16,1024]{1,0:T(8,128)S(1)}, f32[16,1024]{1,0:T(8,128)S(1)}, u32[]{:S(2)}, u32[]{:S(2)}) collective-permute-start(f32[16,1024]{1,0:T(8,128)S(1)} %add.161), channel_id=1, source_target_pairs={{0,4},{4,0},{8,12},{12,8},{1,5},{5,1},{9,13},{13,9},{2,6},{6,2},{1... | collective-permute-start | bytes 196616 | tf_op jit(solution)/shard_map/ppermute | solution.py:682
  96.1 11.0 %collective-permute-start.30 = (bf16[128,1024]{1,0:T(8,128)(2,1)S(1)}, bf16[128,1024]{1,0:T(8,128)(2,1)S(1)}, u32[]{:S(2)}, u32[]{:S(2)}) collective-permute-start(bf16[128,1024]{1,0:T(8,128)(2,1)S(1)} %get-tuple-element.168), channel_id=1, source_target_pairs={{0,4},{4,8},{8,12},{12,0},{1,5},{5,9},{9,13},{13,1},{2,6},{6,10},{... | collective-permute-start | bytes 786440 | tf_op jit(solution)/shard_map/ppermute | solution.py:489
  96.4 14.3 %collective-permute-start.29 = (bf16[128,1024]{1,0:T(8,128)(2,1)S(1)}, bf16[128,1024]{1,0:T(8,128)(2,1)S(1)}, u32[]{:S(2)}, u32[]{:S(2)}) collective-permute-start(bf16[128,1024]{1,0:T(8,128)(2,1)S(1)} %get-tuple-element.169), channel_id=1, source_target_pairs={{0,12},{4,0},{8,4},{12,8},{1,13},{5,1},{9,5},{13,9},{2,14},{6,2},{... | collective-permute-start | bytes 786440 | tf_op jit(solution)/shard_map/ppermute | solution.py:489
  101.1 14.1 %collective-permute-start.35 = (f32[16,1024]{1,0:T(8,128)S(1)}, f32[16,1024]{1,0:T(8,128)S(1)}, u32[]{:S(2)}, u32[]{:S(2)}) collective-permute-start(f32[16,1024]{1,0:T(8,128)S(1)} %add.162), channel_id=1, source_target_pairs={{0,8},{4,12},{8,0},{12,4},{1,9},{5,13},{9,1},{13,5},{2,10},{6,14},... | collective-permute-start | bytes 196616 | tf_op jit(solution)/shard_map/ppermute | solution.py:686
  110.9 8.3 %collective-permute-start.33 = (bf16[128,1024]{1,0:T(8,128)(2,1)S(1)}, bf16[128,1024]{1,0:T(8,128)(2,1)S(1)}, u32[]{:S(2)}, u32[]{:S(2)}) collective-permute-start(bf16[128,1024]{1,0:T(8,128)(2,1)S(1)} %add_convert_fusion.2), channel_id=1, source_target_pairs={{0,12},{4,0},{8,4},{12,8},{1,13},{5,1},{9,5},{13,9},{2,14},{6,2},{... | collective-permute-start | bytes 786440 | tf_op jit(solution)/shard_map/ppermute | solution.py:489
  (24 other events, 104.7 us)

commit v5 on v4

--- a/solution.py
+++ b/solution.py
@@ -233,7 +233,7 @@
 LONG = 20_000_000_000
 
 
-def local_kernel(body, scalars, operands, outputs, scratch, moved, mark=None):
+def local_kernel(body, scalars, held, operands, outputs, scratch, moved, mark=None):
     marks = [] if mark is None else [mark]
 
     def kernel(place, *refs):
@@ -243,12 +243,14 @@
         kernel,
         out_shape=outputs,
         in_specs=[pl.BlockSpec(memory_space=pltpu.SMEM)]
-        + [pl.BlockSpec(memory_space=pl.ANY) for _ in [*marks, *operands]],
+        + [pl.BlockSpec(memory_space=pl.ANY) for _ in marks]
+        + [pl.BlockSpec(memory_space=pltpu.VMEM) for _ in held]
+        + [pl.BlockSpec(memory_space=pl.ANY) for _ in operands],
         out_specs=[pl.BlockSpec(memory_space=pltpu.VMEM) for _ in outputs],
         scratch_shapes=scratch,
         compiler_params=pltpu.CompilerParams(vmem_limit_bytes=SCRATCH_BYTES),
         cost_estimate=pl.CostEstimate(flops=moved, bytes_accessed=moved, transcendentals=0),
-    )(scalars, *marks, *operands)
+    )(scalars, *marks, *held, *operands)
 
 
 def bring(pairs, sems):
@@ -311,9 +313,9 @@
 def forward_kernel(place, *refs):
     payloads = refs[0:8]
     gate_weight, up_weight, partner, cross, cross_partner = refs[8:13]
-    pick_out, gate_out, rows_out, cot_out, hidden_out, act_out, slope_out = refs[13:20]
-    outs = refs[20:24]
-    blocks, w_gate, w_up, upstream, sems = refs[24:29]
+    (pick_out, gate_out, rows_out, cot_out, hidden_out, act_out, slope_out, upstream,
+     cross_out) = refs[13:22]
+    blocks, w_gate, w_up, sems = refs[22:26]
     me, expert = place[0], place[1]
     core = me & 1
     count = pick_out.shape[1]
@@ -364,10 +366,7 @@
     act_out[...] = act.astype(jnp.bfloat16)
     slope = logistic * (1.0 + pre_gate * (1.0 - logistic))
     slope_out[...] = (pre_up * slope).astype(jnp.bfloat16)
-    for j in (2, 1, 3, 0):
-        outs[j][...] = mm_rows(
-            upstream[:, j * width : (j + 1) * width], hidden_out[...]
-        ).astype(jnp.bfloat16)
+    cross_out[...] = mm_rows(upstream[:, 2 * width : 3 * width], hidden_out[...]).astype(jnp.bfloat16)
 
 
 def scatter(me, pick, own_out, other_out, column_block):
@@ -386,35 +385,36 @@
 
 
 def output_kernel(place, *refs):
-    gate_pick_in, hidden_in, down_weight, partner, cross, cross_partner = refs[0:6]
-    own_out, other_out = refs[6:8]
-    gate_pick, hidden, w_down, sems = refs[8:12]
+    gate_pick, hidden, upstream, down_weight, partner, cross, cross_partner = refs[0:7]
+    own_out, other_out = refs[7:9]
+    outs = refs[9:12]
+    w_down, sems = refs[12:14]
     me = place[0]
     copies = bring(
-        weight_pairs(me & 1, (down_weight, partner.at[2], cross.at[me & 1], cross_partner), w_down)
-        + [(gate_pick_in, gate_pick), (hidden_in, hidden)],
+        weight_pairs(me & 1, (down_weight, partner.at[2], cross.at[me & 1], cross_partner), w_down),
         sems,
     )
+    width = w_down.shape[0] // 4
+    for j, out in zip((0, 1, 3), outs):
+        out[...] = mm_rows(
+            upstream[:, j * width : (j + 1) * width], hidden[...]
+        ).astype(jnp.bfloat16)
     for copy in copies:
         copy.wait()
-    width = w_down.shape[0] // 4
     scatter(me, gate_pick, own_out, other_out, lambda j, _: (
         mm_last(hidden[...], w_down[j * width : (j + 1) * width])
     ))
 
 
 def backward_kernel(place, *refs):
-    (pick_in, gate_pick_in, rows_in, hidden_in, cot_in, act_in, slope_in, router_in,
-     down_weight, partner, cross, cross_partner) = refs[0:12]
+    (gate_pick, rows, hidden, cot, act, slope, router,
+     down_weight, partner, cross, cross_partner) = refs[0:11]
     (d_gate_out, d_up_out, logit_out, router_out, keep_out, partner_out, cross_partner_out,
-     gate_sent, up_sent) = refs[12:21]
-    pick, gate_pick, rows, hidden, cot, act, slope, router, w_down, sems = refs[21:31]
+     gate_sent, up_sent) = refs[11:20]
+    w_down, sems = refs[20:22]
     me, expert = place[0], place[1]
     copies = bring(
-        [(cot_in, cot)]
-        + weight_pairs(me & 1, (down_weight, partner.at[2], cross.at[me & 1], cross_partner), w_down)
-        + [(gate_pick_in, gate_pick), (hidden_in, hidden), (rows_in, rows), (act_in, act),
-           (slope_in, slope), (router_in, router)],
+        weight_pairs(me & 1, (down_weight, partner.at[2], cross.at[me & 1], cross_partner), w_down),
         sems,
     )
     for copy in copies:
@@ -433,7 +433,7 @@
         gate_outs[j][...] = mm_rows(part, d_gate_out[...]).astype(jnp.bfloat16)
         up_outs[j][...] = mm_rows(part, d_up_out[...]).astype(jnp.bfloat16)
     ids = router.shape[0]
-    logits = jnp.zeros((pick_in.shape[0], ids), jnp.float32)
+    logits = jnp.zeros((gate_pick.shape[0], ids), jnp.float32)
     for j in range(4):
         columns = pl.ds(pl.multiple_of((me ^ j) * width, width), width)
         logits += mm_last(
@@ -451,16 +451,14 @@
 
 
 def back_kernel(place, *refs):
-    (pick_in, d_gate_in, d_up_in, logit_in, router_in, gate_weight, up_weight, partner,
+    (pick, d_gate, d_up, logit_grad, router, gate_weight, up_weight, partner,
      cross, cross_partner) = refs[0:10]
     own_out, other_out = refs[10:12]
-    pick, d_gate, d_up, logit_grad, router, w_gate, w_up, sems = refs[12:20]
+    w_gate, w_up, sems = refs[12:15]
     me, expert = place[0], place[1]
     core = me & 1
     copies = bring(
-        [(pick_in, pick), (d_gate_in, d_gate), (d_up_in, d_up), (logit_in, logit_grad),
-         (router_in, router)]
-        + weight_pairs(core, (gate_weight, partner.at[0], cross.at[0], cross_partner.at[0]), w_gate)
+        weight_pairs(core, (gate_weight, partner.at[0], cross.at[0], cross_partner.at[0]), w_gate)
         + weight_pairs(core, (up_weight, partner.at[1], cross.at[1], cross_partner.at[1]), w_up),
         sems,
     )
@@ -562,13 +560,14 @@
                 far_side_partner]
     in_weights = [gate_weight, up_weight, partner, in_cross, in_cross_partner]
     router_rows = jnp.pad(router.T.astype(f32), ((0, 16 - id_count), (0, 0)))
-    pick, gate_pick, rows, cot, hidden, act, slope, *down_parts = local_kernel(
+    pick, gate_pick, rows, cot, hidden, act, slope, upstream, down_cross_part = local_kernel(
         forward_kernel,
         place,
+        [],
         [*payloads, *in_weights],
         [shape(table, bf16)] * 2 + [shape(wide, bf16)] * 2 + [shape(narrow, bf16)] * 3
-        + [shape(weight_rows, bf16)] * 4,
-        [vmem((8, *payload.shape), bf16), whole_weight, whole_weight, vmem(wide, bf16),
+        + [shape(wide, bf16), shape(weight_rows, bf16)],
+        [vmem((8, *payload.shape), bf16), whole_weight, whole_weight,
          pltpu.SemaphoreType.DMA((16,))],
         LONG,
         step,
@@ -608,16 +607,17 @@
     share_grad = (
         const_weight * (along_token - along_const) * const_share * (1.0 - const_share)
     ).astype(bf16)
-    mixed_own, mixed_other = local_kernel(
+    mixed_own, mixed_other, *down_parts = local_kernel(
         output_kernel,
         place,
-        [gate_pick, hidden, *down_weights],
-        [shape(wide, bf16)] * 2,
-        [vmem(table, bf16), vmem(narrow, bf16), whole_weight, pltpu.SemaphoreType.DMA((6,))],
+        [gate_pick, hidden, upstream],
+        down_weights,
+        [shape(wide, bf16)] * 2 + [shape(weight_rows, bf16)] * 3,
+        [whole_weight, pltpu.SemaphoreType.DMA((4,))],
         LONG,
         step_down,
     )
-    down_came, down_came_partner = dp_swap(down_parts[2], 2), dp_swap(down_parts[3], 3)
+    down_came, down_came_partner = dp_swap(down_cross_part, 2), dp_swap(down_parts[2], 3)
     parts = [mixed_other[k * row_count : (k + 1) * row_count] for k in range(4)]
     mixed_came = [dp_swap(parts[2], 1), dp_swap(parts[3], 1)]
     mixed_own, mixed_came[0], mixed_came[1], down_came, cot = together(
@@ -630,12 +630,11 @@
     d_gate, d_up, logit_grad, router_row, *in_parts, gate_sent, up_sent = local_kernel(
         backward_kernel,
         place,
-        [pick, gate_pick, rows, hidden, cot, act, slope, router_rows, *down_weights],
+        [gate_pick, rows, hidden, cot, act, slope, router_rows],
+        down_weights,
         [shape(narrow, bf16)] * 2 + [shape(table, bf16), shape((8, model_width), f32)]
         + [shape((2, *weight_rows), bf16)] * 3 + [shape(weight_rows, bf16)] * 2,
-        [vmem(table, bf16)] * 2 + [vmem(wide, bf16), vmem(narrow, bf16), vmem(wide, bf16),
-         vmem(narrow, bf16), vmem(narrow, bf16), vmem(router_rows.shape, f32), whole_weight,
-         pltpu.SemaphoreType.DMA((11,))],
+        [whole_weight, pltpu.SemaphoreType.DMA((4,))],
         LONG,
     )
     (d_gate, router_row, in_parts[1], in_parts[2], gate_sent, up_sent, down_came_partner,
@@ -660,11 +659,10 @@
     back_own, back_other = local_kernel(
         back_kernel,
         place,
-        [pick, d_gate, d_up, logit_grad, router_rows, *in_weights],
+        [pick, d_gate, d_up, logit_grad, router_rows],
+        in_weights,
         [shape(wide, bf16)] * 2,
-        [vmem(table, bf16), vmem(narrow, bf16), vmem(narrow, bf16), vmem(table, bf16),
-         vmem(router_rows.shape, f32), whole_weight, whole_weight,
-         pltpu.SemaphoreType.DMA((13,))],
+        [whole_weight, whole_weight, pltpu.SemaphoreType.DMA((8,))],
         LONG,
     )
     (back_own, back_other, gate_came, in_from, small_came, mixed_side, mixed_near, up_sent,
@@ -680,11 +678,16 @@
     back_near, back_side = ring(back_first[0], -1), ring(back_first[1], 1)
     small = small + small_came
     small_came = lax.ppermute(small, "expert", [(i, i ^ 1) for i in range(4)])
-    back_near, back_side, up_came = together(back_near, back_side, up_came)
+    back_near, back_side, up_came, mixed_near, small_came = together(
+        back_near, back_side, up_came, mixed_near, small_came
+    )
     back_near = ring(add(back_near, back_late[1]).astype(bf16), -1)
     small = small + small_came
     small = small + lax.ppermute(small, "expert", [(i, i ^ 2) for i in range(4)])
     mixed_sum = add(mixed_side, mixed_near) + mixed_late[0].astype(f32)
+    grad_router = small[:id_count].T
+    grad_const_gate = small[id_count : id_count + const_count].T
+    grad_const_vec = small[id_count + const_count :]
     back_sum = add(back_side, back_near) + back_late[0].astype(f32)
     grad_down = pair(add(down_parts[0], down_came), add(down_from, down_came_partner))
     mixed = (
@@ -697,16 +700,15 @@
     )
     grad_tokens = (back_sum + back_local).astype(bf16)
 
-    up_came, in_came_partner, mixed, grad_down, grad_tokens, small = together(
-        up_came, in_came_partner, mixed, grad_down, grad_tokens, small
+    mine = [add(in_parts[0][i], came).astype(bf16) for i, came in enumerate((gate_came, up_came))]
+    (mine[0], mine[1], in_came_partner, mixed, grad_down, grad_tokens, grad_router,
+     grad_const_gate, grad_const_vec) = together(
+        *mine, in_came_partner, mixed, grad_down, grad_tokens, grad_router, grad_const_gate,
+        grad_const_vec
     )
     grad_gate, grad_up = (
-        pair(add(in_parts[0][i], came), add(in_from[i], in_came_partner[i]))
-        for i, came in enumerate((gate_came, up_came))
-    )
-    grad_router = small[:id_count].T
-    grad_const_gate = small[id_count : id_count + const_count].T
-    grad_const_vec = small[id_count + const_count :]
+        pair(mine[i], add(in_from[i], in_came_partner[i])) for i in range(2)
+    )
     return (
         mixed,
         grad_tokens,

time: 124 us -> 123 us (level)
  Pallas kernels: 28.1 us -> 26.7 us
    ppermute x1, starting transfers between devices: 0.07 us -> 2.41 us  [on_device_paired(): lax.ppermute(small, 'expert', [(i, i ^ 2) for i in range(4)])]
    ppermute x9, starting transfers between devices: 17.3 us -> 15.5 us  [ring(): lax.ppermute(value, 'expert', [(i, (i + step) % size) for i in range(size)])]
    pallas_call x4, Pallas kernels: 23.4 us -> 22 us  [local_kernel(): pl.pallas_call(kernel, out_shape=outputs, in_specs=[pl.BlockSpec(memory_s...]
  transfers between devices with their start and end apart: 36 -> 36, of which waited for: 15 -> 16; matrix products, arithmetic and copies ran while one was open for 14% -> 15% of each run, Pallas kernels for 21% -> 20%
where the time goes in v5:
time: 123 us; the launch traced here: 122 us
  waiting for transfers between devices  38.2 us (31%)
  starting transfers between devices  34.2 us (28%)
  Pallas kernels  26.7 us (22%)
  local copies, waits for them, and re-layouts  9.31 us (8%)
  other arithmetic  8.16 us (7%)
  matrix products  4.28 us (3%)
    pallas_call x4, Pallas kernels, local_kernel(): pl.pallas_call(kernel, out_shape=outputs, in_specs=[pl.BlockSpec(memory_s...  22 us
    ppermute x9, starting transfers between devices, ring(): lax.ppermute(value, 'expert', [(i, (i + step) % size) for i in range(size)])  15.5 us
    ppermute x23, waiting for transfers between devices, dp_swap(): return lax.ppermute(value, 'dp', [(i, i ^ step) for i in range(4)])  15.2 us
    ppermute x9, waiting for transfers between devices, ring(): lax.ppermute(value, 'expert', [(i, (i + step) % size) for i in range(size)])  14.7 us
    ppermute x23, starting transfers between devices, dp_swap(): return lax.ppermute(value, 'dp', [(i, i ^ step) for i in range(4)])  11.4 us
    ppermute x1, waiting for transfers between devices, on_device_paired(): in_other.append(lax.ppermute(in_came[1], 'groups', [(0, 1), (1, 0)]))  8.03 us
    squeeze x5, local copies, waits for them, and re-layouts, of_expert(): return lax.dynamic_index_in_dim(weight, which, 0, keepdims=False)  4.94 us
    dot_general x3, matrix products, mm(): return jnp.dot(a, b, preferred_element_type=jnp.float32)  2.6 us
  transfers between devices with their start and end apart: 36, of which 16 were waited for; matrix products, arithmetic and copies ran while one was open for 15% of the time, Pallas kernels for 20%

profile of v5, /device:TPU:0, one launch (start us, length us, event | category | flops | bytes accessed | tf_op | source)
XLA Modules:
  0.0 122.0 jit_solution(11909087719504662048)
XLA Ops:
  0.7 2.2 %shard_map.152 = (bf16[272,1024]{1,0:T(8,128)(2,1)}, s32[8,128]{1,0:T(8,128)}) custom-call(bf16[128,1024]{1,0:T(8,128)(2,1)} %tokens.1, bf16[128,1024]{1,0:T(8,128)(2,1)} %grads.1, s32[6,128]{1,0:T(8,128)} %bitcast.70, bf16[12,1024]{1,0:T(8,128)(2,1)} %bitcast.66), custom_call_target="tpu_custom_call" | custom-call | flops 20000000000 | bytes 20000000000 | tf_op jit(solution)/shard_map/pallas_call | solution.py:523
  2.8 3.0 %collective-permute-start.2 = (bf16[272,1024]{1,0:T(8,128)(2,1)}, bf16[272,1024]{1,0:T(8,128)(2,1)}, u32[]{:S(2)}, u32[]{:S(2)}) collective-permute-start(bf16[272,1024]{1,0:T(8,128)(2,1)} %get-tuple-element.95.refs_1_), channel_id=1, source_target_pairs={{0,4},{4,8},{8,12},{12,0},{1,5},{5,9},{9,13},{13,1},{2,6},{6,10},{... | collective-permute-start | bytes 1671176 | tf_op jit(solution)/shard_map/ppermute | solution.py:487
  6.7 1.5 %collective-permute-start.3 = (bf16[2,96,768]{2,1,0:T(8,128)(2,1)}, bf16[2,96,768]{2,1,0:T(8,128)(2,1)}, u32[]{:S(2)}, u32[]{:S(2)}) collective-permute-start(bf16[2,96,768]{2,1,0:T(8,128)(2,1)} %slice.95), channel_id=1, source_target_pairs={{0,2},{1,3},{2,0},{3,1},{4,6},{5,7},{6,4},{7,5},{8,10},{9,11},{10,... | collective-permute-start | bytes 884744 | tf_op jit(solution)/shard_map/ppermute | solution.py:482
  11.4 1.4 %multiply_reduce_fusion = (f32[128]{0:T(128)}, bf16[128,2]{0,1:T(2,128)(2,1)}, bf16[128,2]{0,1:T(2,128)(2,1)S(1)}, f32[128,2]{0,1:T(2,128)S(1)}) fusion(f32[128,4]{0,1:T(4,128)S(1)} %get-tuple-element.206, f32[128,2]{0,1:T(2,128)S(1)} %fusion.27, f32[128]{0:T(128)S(1)} %fusion.10, bf16[128,1024]{1,0:T(8,128)(2,1)S(1)} %copy-done.7, ...), kind=kOutput, calls=%fused_computation.78 | convolution fusion | flops 528256 | bytes 271360 | tf_op jit(solution)/shard_map/dot_general | solution.py:267
  14.3 2.5 %collective-permute-done.3 = bf16[2,96,768]{2,1,0:T(8,128)(2,1)} collective-permute-done((bf16[2,96,768]{2,1,0:T(8,128)(2,1)}, bf16[2,96,768]{2,1,0:T(8,128)(2,1)}, u32[]{:S(2)}, u32[]{:S(2)}) %collective-permute-start.3) | collective-permute-done | bytes 294944 | tf_op jit(solution)/shard_map/ppermute | solution.py:482
  16.8 1.5 %collective-permute-start.5 = (bf16[2,96,768]{2,1,0:T(8,128)(2,1)}, bf16[2,96,768]{2,1,0:T(8,128)(2,1)}, u32[]{:S(2)}, u32[]{:S(2)}) collective-permute-start(bf16[2,96,768]{2,1,0:T(8,128)(2,1)} %collective-permute-done.3), channel_id=1, source_target_pairs={{0,16},{16,0},{1,17},{17,1},{2,18},{18,2},{3,19},{19,3},{4,20},{20... | collective-permute-start | bytes 884744 | tf_op jit(solution)/shard_map/ppermute | solution.py:536
  18.3 2.2 %collective-permute-start.1 = (bf16[272,1024]{1,0:T(8,128)(2,1)}, bf16[272,1024]{1,0:T(8,128)(2,1)}, u32[]{:S(2)}, u32[]{:S(2)}) collective-permute-start(bf16[272,1024]{1,0:T(8,128)(2,1)} %get-tuple-element.95.refs_1_), channel_id=1, source_target_pairs={{0,12},{4,0},{8,4},{12,8},{1,13},{5,1},{9,5},{13,9},{2,14},{6,2},{... | collective-permute-start | bytes 1671176 | tf_op jit(solution)/shard_map/ppermute | solution.py:487
  22.2 1.7 %dynamic-slice_bitcast_fusion.6 = (bf16[96,768]{1,0:T(8,128)(2,1)}, bf16[96,768]{1,0:T(8,128)(2,1)}) fusion(bf16[2,96,768]{2,1,0:T(8,128)(2,1)} %collective-permute-done.3, s32[]{:T(128)S(6)} %select_n.67, s32[]{:T(128)S(6)} %select_n.68), kind=kLoop, calls=%fused_computation.53 | loop fusion | bytes 589832 | tf_op jit(solution)/shard_map/jit(dynamic_index_in_dim)/squeeze | solution.py:510
  23.9 3.1 %collective-permute-done.6 = bf16[2,160,768]{2,1,0:T(8,128)(2,1)} collective-permute-done((bf16[2,160,768]{2,1,0:T(8,128)(2,1)}, bf16[2,160,768]{2,1,0:T(8,128)(2,1)}, u32[]{:S(2)}, u32[]{:S(2)}) %collective-permute-start.6) | collective-permute-done | bytes 491552 | tf_op jit(solution)/shard_map/ppermute | solution.py:482
  26.9 1.5 %collective-permute-start.13 = (bf16[2,256,768]{2,1,0:T(8,128)(2,1)S(1)}, bf16[2,256,768]{2,1,0:T(8,128)(2,1)S(1)}, u32[]{:S(2)}, u32[]{:S(2)}) collective-permute-start(bf16[2,256,768]{2,1,0:T(8,128)(2,1)S(1)} %copy-done.3), channel_id=1, source_target_pairs={{0,2},{1,3},{2,0},{3,1},{4,6},{5,7},{6,4},{7,5},{8,10},{9,11},{10,... | collective-permute-start | bytes 2359304 | tf_op jit(solution)/shard_map/ppermute | solution.py:482
  28.4 1.5 %collective-permute-start.8 = (bf16[2,160,768]{2,1,0:T(8,128)(2,1)}, bf16[2,160,768]{2,1,0:T(8,128)(2,1)}, u32[]{:S(2)}, u32[]{:S(2)}) collective-permute-start(bf16[2,160,768]{2,1,0:T(8,128)(2,1)} %collective-permute-done.6), channel_id=1, source_target_pairs={{0,16},{16,0},{1,17},{17,1},{2,18},{18,2},{3,19},{19,3},{4,20},{20... | collective-permute-start | bytes 1474568 | tf_op jit(solution)/shard_map/ppermute | solution.py:544
  33.3 8.0 %collective-permute-done.8 = bf16[2,160,768]{2,1,0:T(8,128)(2,1)} collective-permute-done((bf16[2,160,768]{2,1,0:T(8,128)(2,1)}, bf16[2,160,768]{2,1,0:T(8,128)(2,1)}, u32[]{:S(2)}, u32[]{:S(2)}) %collective-permute-start.8) | collective-permute-done | bytes 491552 | tf_op jit(solution)/shard_map/ppermute | solution.py:544
  48.4 1.4 %collective-permute-done.11.refs_8_ = bf16[272,1024]{1,0:T(8,128)(2,1)S(1)} collective-permute-done((bf16[272,1024]{1,0:T(8,128)(2,1)}, bf16[272,1024]{1,0:T(8,128)(2,1)S(1)}, u32[]{:S(2)}, u32[]{:S(2)}) %collective-permute-start.11) | collective-permute-done | bytes 557088 | tf_op jit(solution)/shard_map/ppermute | solution.py:482
  49.7 5.3 %shard_map.155 = (bf16[512,128]{1,0:T(8,128)(2,1)S(1)}, bf16[512,128]{1,0:T(8,128)(2,1)S(1)}, bf16[512,1024]{1,0:T(8,128)(2,1)S(1)}, bf16[512,1024]{1,0:T(8,128)...) custom-call(s32[2]{0:T(128)S(1)} %pad_add_fusion.place, ...), custom_call_target="tpu_custom_call" | custom-call | flops 20000000000 | bytes 20000000000 | tf_op jit(solution)/shard_map/pallas_call | solution.py:242
  55.0 1.5 %collective-permute-start.17 = (bf16[256,768]{1,0:T(8,128)(2,1)S(1)}, bf16[256,768]{1,0:T(8,128)(2,1)S(1)}, u32[]{:S(2)}, u32[]{:S(2)}) collective-permute-start(bf16[256,768]{1,0:T(8,128)(2,1)S(1)} %get-tuple-element.121), channel_id=1, source_target_pairs={{0,2},{1,3},{2,0},{3,1},{4,6},{5,7},{6,4},{7,5},{8,10},{9,11},{10,... | collective-permute-start | bytes 1179656 | tf_op jit(solution)/shard_map/ppermute | solution.py:482
  56.6 4.4 %shard_map.156 = (bf16[512,1024]{1,0:T(8,128)(2,1)S(1)}, bf16[512,1024]{1,0:T(8,128)(2,1)S(1)}, bf16[256,768]{1,0:T(8,128)(2,1)S(1)}, bf16[256,768]{1,0:T(8,128)(2,1)S(1)}, bf16[256,768]{1,0:T(8,128)(2,1)S(1)}) custom-call(s32[2]{0:T(128)S(1)} %pad_add_fusion.place, s32[8,128]{1,0:T(8,128)S(1)} %copy-done.6, ...), custom_call_target="tpu_custom_call" | custom-call | flops 20000000000 | bytes 20000000000 | tf_op jit(solution)/shard_map/pallas_call | solution.py:242
  63.0 4.1 %collective-permute-done.17 = bf16[256,768]{1,0:T(8,128)(2,1)S(1)} collective-permute-done((bf16[256,768]{1,0:T(8,128)(2,1)S(1)}, bf16[256,768]{1,0:T(8,128)(2,1)S(1)}, u32[]{:S(2)}, u32[]{:S(2)}) %collective-permute-start.17) | collective-permute-done | bytes 393248 | tf_op jit(solution)/shard_map/ppermute | solution.py:482
  67.1 2.2 %collective-permute-start.19 = (bf16[128,1024]{1,0:T(8,128)(2,1)S(1)}, bf16[128,1024]{1,0:T(8,128)(2,1)S(1)}, u32[]{:S(2)}, u32[]{:S(2)}) collective-permute-start(bf16[128,1024]{1,0:T(8,128)(2,1)S(1)} %add_convert_fusion.10), channel_id=1, source_target_pairs={{0,12},{4,0},{8,4},{12,8},{1,13},{5,1},{9,5},{13,9},{2,14},{6,2},{... | collective-permute-start | bytes 786440 | tf_op jit(solution)/shard_map/ppermute | solution.py:487
  69.4 5.6 %shard_map.157 = (bf16[512,768]{1,0:T(8,128)(2,1)S(1)}, bf16[512,768]{1,0:T(8,128)(2,1)S(1)}, bf16[512,128]{1,0:T(8,128)(2,1)S(1)}, f32[8,1024]{1,0:T(8,128)S(1)...) custom-call(s32[2]{0:T(128)S(1)} %pad_add_fusion.place, ...), custom_call_target="tpu_custom_call" | custom-call | flops 20000000000 | bytes 20000000000 | tf_op jit(solution)/shard_map/pallas_call | solution.py:242
  75.2 1.6 %collective-permute-start.24 = (f32[16,1024]{1,0:T(8,128)S(1)}, f32[16,1024]{1,0:T(8,128)S(1)}, u32[]{:S(2)}, u32[]{:S(2)}) collective-permute-start(f32[16,1024]{1,0:T(8,128)S(1)} %pad_maximum_fusion.1), channel_id=1, source_target_pairs={{0,2},{1,3},{2,0},{3,1},{4,6},{5,7},{6,4},{7,5},{8,10},{9,11},{10,... | collective-permute-start | bytes 196616 | tf_op jit(solution)/shard_map/ppermute | solution.py:482
  77.0 2.9 %collective-permute-start.26 = (bf16[128,1024]{1,0:T(8,128)(2,1)S(1)}, bf16[128,1024]{1,0:T(8,128)(2,1)S(1)}, u32[]{:S(2)}, u32[]{:S(2)}) collective-permute-start(bf16[128,1024]{1,0:T(8,128)(2,1)S(1)} %get-tuple-element.184), channel_id=1, source_target_pairs={{0,12},{4,0},{8,4},{12,8},{1,13},{5,1},{9,5},{13,9},{2,14},{6,2},{... | collective-permute-start | bytes 786440 | tf_op jit(solution)/shard_map/ppermute | solution.py:487
  80.4 6.7 %shard_map.158 = (bf16[512,1024]{1,0:T(8,128)(2,1)S(1)}, bf16[512,1024]{1,0:T(8,128)(2,1)S(1)}) custom-call(s32[2]{0:T(128)S(1)} %pad_add_fusion.place, bf16[512,128]{1,0:T(8,128)(2,1)S(1)} %get-tuple-element.127.refs_0_, bf16[512,768]{1,0:T(8,128)(2,1)S(1)} %get-tuple-element.138.refs_1_, bf16[512,768]{1,0:T(8,128)(2,1)S(1)} %get-tuple-element.139.refs_2_, ...), custom_call_target="tpu_custom_call" | custom-call | flops 20000000000 | bytes 20000000000 | tf_op jit(solution)/shard_map/pallas_call | solution.py:242
  87.1 3.5 %collective-permute-done.25 = bf16[128,1024]{1,0:T(8,128)(2,1)S(1)} collective-permute-done((bf16[128,1024]{1,0:T(8,128)(2,1)S(1)}, bf16[128,1024]{1,0:T(8,128)(2,1)S(1)}, u32[]{:S(2)}, u32[]{:S(2)}) %collective-permute-start.25) | collective-permute-done | bytes 262176 | tf_op jit(solution)/shard_map/ppermute | solution.py:487
  91.7 1.5 %collective-permute-start.31 = (bf16[256,768]{1,0:T(8,128)(2,1)S(1)}, bf16[256,768]{1,0:T(8,128)(2,1)S(1)}, u32[]{:S(2)}, u32[]{:S(2)}) collective-permute-start(bf16[256,768]{1,0:T(8,128)(2,1)S(1)} %get-tuple-element.156), channel_id=1, source_target_pairs={{0,2},{1,3},{2,0},{3,1},{4,6},{5,7},{6,4},{7,5},{8,10},{9,11},{10,... | collective-permute-start | bytes 1179656 | tf_op jit(solution)/shard_map/ppermute | solution.py:482
  93.4 1.8 %collective-permute-start.32 = (f32[16,1024]{1,0:T(8,128)S(1)}, f32[16,1024]{1,0:T(8,128)S(1)}, u32[]{:S(2)}, u32[]{:S(2)}) collective-permute-start(f32[16,1024]{1,0:T(8,128)S(1)} %add.146), channel_id=1, source_target_pairs={{0,4},{4,0},{8,12},{12,8},{1,5},{5,1},{9,13},{13,9},{2,6},{6,2},{1... | collective-permute-start | bytes 196616 | tf_op jit(solution)/shard_map/ppermute | solution.py:680
  95.7 3.6 %collective-permute-start.29 = (bf16[128,1024]{1,0:T(8,128)(2,1)S(1)}, bf16[128,1024]{1,0:T(8,128)(2,1)S(1)}, u32[]{:S(2)}, u32[]{:S(2)}) collective-permute-start(bf16[128,1024]{1,0:T(8,128)(2,1)S(1)} %get-tuple-element.181), channel_id=1, source_target_pairs={{0,12},{4,0},{8,4},{12,8},{1,13},{5,1},{9,5},{13,9},{2,14},{6,2},{... | collective-permute-start | bytes 786440 | tf_op jit(solution)/shard_map/ppermute | solution.py:487
  100.3 2.5 %collective-permute-done.31 = bf16[256,768]{1,0:T(8,128)(2,1)S(1)} collective-permute-done((bf16[256,768]{1,0:T(8,128)(2,1)S(1)}, bf16[256,768]{1,0:T(8,128)(2,1)S(1)}, u32[]{:S(2)}, u32[]{:S(2)}) %collective-permute-start.31) | collective-permute-done | bytes 393248 | tf_op jit(solution)/shard_map/ppermute | solution.py:482
  102.8 3.7 %collective-permute-done.30 = bf16[128,1024]{1,0:T(8,128)(2,1)S(1)} collective-permute-done((bf16[128,1024]{1,0:T(8,128)(2,1)S(1)}, bf16[128,1024]{1,0:T(8,128)(2,1)S(1)}, u32[]{:S(2)}, u32[]{:S(2)}) %collective-permute-start.30) | collective-permute-done | bytes 262176 | tf_op jit(solution)/shard_map/ppermute | solution.py:487
  106.5 2.8 %collective-permute-done.29 = bf16[128,1024]{1,0:T(8,128)(2,1)S(1)} collective-permute-done((bf16[128,1024]{1,0:T(8,128)(2,1)S(1)}, bf16[128,1024]{1,0:T(8,128)(2,1)S(1)}, u32[]{:S(2)}, u32[]{:S(2)}) %collective-permute-start.29) | collective-permute-done | bytes 262176 | tf_op jit(solution)/shard_map/ppermute | solution.py:487
  109.2 2.4 %collective-permute-start.35 = (f32[16,1024]{1,0:T(8,128)S(1)}, f32[16,1024]{1,0:T(8,128)S(1)}, u32[]{:S(2)}, u32[]{:S(2)}) collective-permute-start(f32[16,1024]{1,0:T(8,128)S(1)} %add.164), channel_id=1, source_target_pairs={{0,8},{4,12},{8,0},{12,4},{1,9},{5,13},{9,1},{13,5},{2,10},{6,14},... | collective-permute-start | bytes 196616 | tf_op jit(solution)/shard_map/ppermute | solution.py:686
  116.3 3.2 %collective-permute-done.34 = bf16[128,1024]{1,0:T(8,128)(2,1)S(1)} collective-permute-done((bf16[128,1024]{1,0:T(8,128)(2,1)S(1)}, bf16[128,1024]{1,0:T(8,128)(2,1)S(1)}, u32[]{:S(2)}, u32[]{:S(2)}) %collective-permute-start.34) | collective-permute-done | bytes 262176 | tf_op jit(solution)/shard_map/ppermute | solution.py:487
  120.6 1.4 %select_convert_fusion = (bf16[2,256,768]{2,1,0:T(8,128)(2,1)}, bf16[2,256,768]{2,1,0:T(8,128)(2,1)}) fusion(bf16[256,768]{1,0:T(8,128)(2,1)S(1)} %get-tuple-element.182, bf16[256,768]{1,0:T(8,128)(2,1)S(1)} %get-tuple-element.175, pred[2]{0:T(512)(128)(4,1)S(1)} %iota_compare_fusion.1, bf16[256,768]{1,0:T(8,128)(2,1)S(1)} %get-tuple-element.183, ...), kind=kLoop, calls=%fused_computation | loop fusion | flops 786432 | bytes 3145730 | tf_op jit(solution)/shard_map/convert_element_type | solution.py:587
  (143 shorter events, 28.7 us)
Async XLA Ops:
  2.8 18.0 %collective-permute-start.2 = (bf16[272,1024]{1,0:T(8,128)(2,1)}, bf16[272,1024]{1,0:T(8,128)(2,1)}, u32[]{:S(2)}, u32[]{:S(2)}) collective-permute-start(bf16[272,1024]{1,0:T(8,128)(2,1)} %get-tuple-element.95.refs_1_), channel_id=1, source_target_pairs={{0,4},{4,8},{8,12},{12,0},{1,5},{5,9},{9,13},{13,1},{2,6},{6,10},{... | collective-permute-start | bytes 1671176 | tf_op jit(solution)/shard_map/ppermute | solution.py:487
  5.8 12.5 %collective-permute-start = (bf16[272,1024]{1,0:T(8,128)(2,1)}, bf16[272,1024]{1,0:T(8,128)(2,1)S(1)}, u32[]{:S(2)}, u32[]{:S(2)}) collective-permute-start(bf16[272,1024]{1,0:T(8,128)(2,1)} %get-tuple-element.95.refs_1_), channel_id=1, source_target_pairs={{0,1},{1,0},{2,3},{3,2},{4,5},{5,4},{6,7},{7,6},{8,9},{9,8},{10,11... | collective-permute-start | bytes 1671176 | tf_op jit(solution)/shard_map/ppermute | solution.py:482
  6.7 10.1 %collective-permute-start.3 = (bf16[2,96,768]{2,1,0:T(8,128)(2,1)}, bf16[2,96,768]{2,1,0:T(8,128)(2,1)}, u32[]{:S(2)}, u32[]{:S(2)}) collective-permute-start(bf16[2,96,768]{2,1,0:T(8,128)(2,1)} %slice.95), channel_id=1, source_target_pairs={{0,2},{1,3},{2,0},{3,1},{4,6},{5,7},{6,4},{7,5},{8,10},{9,11},{10,... | collective-permute-start | bytes 884744 | tf_op jit(solution)/shard_map/ppermute | solution.py:482
  9.0 18.0 %collective-permute-start.6 = (bf16[2,160,768]{2,1,0:T(8,128)(2,1)}, bf16[2,160,768]{2,1,0:T(8,128)(2,1)}, u32[]{:S(2)}, u32[]{:S(2)}) collective-permute-start(bf16[2,160,768]{2,1,0:T(8,128)(2,1)} %slice.96), channel_id=1, source_target_pairs={{0,2},{1,3},{2,0},{3,1},{4,6},{5,7},{6,4},{7,5},{8,10},{9,11},{10,... | collective-permute-start | bytes 1474568 | tf_op jit(solution)/shard_map/ppermute | solution.py:482
  10.8 17.6 %collective-permute-start.7 = (bf16[3,256,768]{2,1,0:T(8,128)(2,1)}, bf16[3,256,768]{2,1,0:T(8,128)(2,1)}, u32[]{:S(2)}, u32[]{:S(2)}) collective-permute-start(bf16[3,256,768]{2,1,0:T(8,128)(2,1)} %pad_maximum_fusion), channel_id=1, source_target_pairs={{0,1},{1,0},{2,3},{3,2},{4,5},{5,4},{6,7},{7,6},{8,9},{9,8},{10,11... | collective-permute-start | bytes 3538952 | tf_op jit(solution)/shard_map/ppermute | solution.py:482
  16.8 16.5 %collective-permute-start.5 = (bf16[2,96,768]{2,1,0:T(8,128)(2,1)}, bf16[2,96,768]{2,1,0:T(8,128)(2,1)}, u32[]{:S(2)}, u32[]{:S(2)}) collective-permute-start(bf16[2,96,768]{2,1,0:T(8,128)(2,1)} %collective-permute-done.3), channel_id=1, source_target_pairs={{0,16},{16,0},{1,17},{17,1},{2,18},{18,2},{3,19},{19,3},{4,20},{20... | collective-permute-start | bytes 884744 | tf_op jit(solution)/shard_map/ppermute | solution.py:536
  18.3 26.6 %collective-permute-start.1 = (bf16[272,1024]{1,0:T(8,128)(2,1)}, bf16[272,1024]{1,0:T(8,128)(2,1)}, u32[]{:S(2)}, u32[]{:S(2)}) collective-permute-start(bf16[272,1024]{1,0:T(8,128)(2,1)} %get-tuple-element.95.refs_1_), channel_id=1, source_target_pairs={{0,12},{4,0},{8,4},{12,8},{1,13},{5,1},{9,5},{13,9},{2,14},{6,2},{... | collective-permute-start | bytes 1671176 | tf_op jit(solution)/shard_map/ppermute | solution.py:487
  22.1 24.0 %collective-permute-start.4 = (bf16[272,1024]{1,0:T(8,128)(2,1)}, bf16[272,1024]{1,0:T(8,128)(2,1)}, u32[]{:S(2)}, u32[]{:S(2)}) collective-permute-start(bf16[272,1024]{1,0:T(8,128)(2,1)} %collective-permute-done.2.refs_3_), channel_id=1, source_target_pairs={{0,4},{4,8},{8,12},{12,0},{1,5},{5,9},{9,13},{13,1},{2,6},{6,10},{... | collective-permute-start | bytes 1671176 | tf_op jit(solution)/shard_map/ppermute | solution.py:487
  26.9 19.9 %collective-permute-start.13 = (bf16[2,256,768]{2,1,0:T(8,128)(2,1)S(1)}, bf16[2,256,768]{2,1,0:T(8,128)(2,1)S(1)}, u32[]{:S(2)}, u32[]{:S(2)}) collective-permute-start(bf16[2,256,768]{2,1,0:T(8,128)(2,1)S(1)} %copy-done.3), channel_id=1, source_target_pairs={{0,2},{1,3},{2,0},{3,1},{4,6},{5,7},{6,4},{7,5},{8,10},{9,11},{10,... | collective-permute-start | bytes 2359304 | tf_op jit(solution)/shard_map/ppermute | solution.py:482
  28.4 12.9 %collective-permute-start.8 = (bf16[2,160,768]{2,1,0:T(8,128)(2,1)}, bf16[2,160,768]{2,1,0:T(8,128)(2,1)}, u32[]{:S(2)}, u32[]{:S(2)}) collective-permute-start(bf16[2,160,768]{2,1,0:T(8,128)(2,1)} %collective-permute-done.6), channel_id=1, source_target_pairs={{0,16},{16,0},{1,17},{17,1},{2,18},{18,2},{3,19},{19,3},{4,20},{20... | collective-permute-start | bytes 1474568 | tf_op jit(solution)/shard_map/ppermute | solution.py:544
  43.6 6.1 %collective-permute-start.12 = (bf16[2,256,768]{2,1,0:T(8,128)(2,1)S(1)}, bf16[2,256,768]{2,1,0:T(8,128)(2,1)S(1)}, u32[]{:S(2)}, u32[]{:S(2)}) collective-permute-start(bf16[2,256,768]{2,1,0:T(8,128)(2,1)S(1)} %maximum_select_fusion.1), channel_id=1, source_target_pairs={{0,1},{1,0},{2,3},{3,2},{4,5},{5,4},{6,7},{7,6},{8,9},{9,8},{10,11... | collective-permute-start | bytes 2359304 | tf_op jit(solution)/shard_map/ppermute | solution.py:482
  44.8 2.4 %collective-permute-start.9 = (bf16[272,1024]{1,0:T(8,128)(2,1)}, bf16[272,1024]{1,0:T(8,128)(2,1)S(1)}, u32[]{:S(2)}, u32[]{:S(2)}) collective-permute-start(bf16[272,1024]{1,0:T(8,128)(2,1)} %collective-permute-done.2.refs_3_), channel_id=1, source_target_pairs={{0,1},{1,0},{2,3},{3,2},{4,5},{5,4},{6,7},{7,6},{8,9},{9,8},{10,11... | collective-permute-start | bytes 1671176 | tf_op jit(solution)/shard_map/ppermute | solution.py:482
  46.2 3.5 %collective-permute-start.11 = (bf16[272,1024]{1,0:T(8,128)(2,1)}, bf16[272,1024]{1,0:T(8,128)(2,1)S(1)}, u32[]{:S(2)}, u32[]{:S(2)}) collective-permute-start(bf16[272,1024]{1,0:T(8,128)(2,1)} %collective-permute-done.1.refs_7_), channel_id=1, source_target_pairs={{0,1},{1,0},{2,3},{3,2},{4,5},{5,4},{6,7},{7,6},{8,9},{9,8},{10,11... | collective-permute-start | bytes 1671176 | tf_op jit(solution)/shard_map/ppermute | solution.py:482
  46.9 8.2 %collective-permute-start.14 = (bf16[256,768]{1,0:T(8,128)(2,1)S(1)}, bf16[256,768]{1,0:T(8,128)(2,1)S(1)}, u32[]{:S(2)}, u32[]{:S(2)}) collective-permute-start(bf16[256,768]{1,0:T(8,128)(2,1)S(1)} %dynamic-slice_bitcast_fusion), channel_id=1, source_target_pairs={{0,1},{1,0},{2,3},{3,2},{4,5},{5,4},{6,7},{7,6},{8,9},{9,8},{10,11... | collective-permute-start | bytes 1179656 | tf_op jit(solution)/shard_map/ppermute | solution.py:482
  55.0 12.0 %collective-permute-start.17 = (bf16[256,768]{1,0:T(8,128)(2,1)S(1)}, bf16[256,768]{1,0:T(8,128)(2,1)S(1)}, u32[]{:S(2)}, u32[]{:S(2)}) collective-permute-start(bf16[256,768]{1,0:T(8,128)(2,1)S(1)} %get-tuple-element.121), channel_id=1, source_target_pairs={{0,2},{1,3},{2,0},{3,1},{4,6},{5,7},{6,4},{7,5},{8,10},{9,11},{10,... | collective-permute-start | bytes 1179656 | tf_op jit(solution)/shard_map/ppermute | solution.py:482
  61.9 13.1 %collective-permute-start.18 = (bf16[256,768]{1,0:T(8,128)(2,1)S(1)}, bf16[256,768]{1,0:T(8,128)(2,1)S(1)}, u32[]{:S(2)}, u32[]{:S(2)}) collective-permute-start(bf16[256,768]{1,0:T(8,128)(2,1)S(1)} %get-tuple-element.134), channel_id=1, source_target_pairs={{0,3},{1,2},{2,1},{3,0},{4,7},{5,6},{6,5},{7,4},{8,11},{9,10},{10,... | collective-permute-start | bytes 1179656 | tf_op jit(solution)/shard_map/ppermute | solution.py:482
  62.2 12.8 %collective-permute-start.21 = (bf16[256,768]{1,0:T(8,128)(2,1)S(1)}, bf16[256,768]{1,0:T(8,128)(2,1)S(1)}, u32[]{:S(2)}, u32[]{:S(2)}) collective-permute-start(bf16[256,768]{1,0:T(8,128)(2,1)S(1)} %get-tuple-element.137), channel_id=1, source_target_pairs={{0,1},{1,0},{2,3},{3,2},{4,5},{5,4},{6,7},{7,6},{8,9},{9,8},{10,11... | collective-permute-start | bytes 1179656 | tf_op jit(solution)/shard_map/ppermute | solution.py:482
  62.7 12.4 %collective-permute-start.20 = (bf16[256,1024]{1,0:T(8,128)(2,1)S(1)}, bf16[256,1024]{1,0:T(8,128)(2,1)S(1)}, u32[]{:S(2)}, u32[]{:S(2)}) collective-permute-start(bf16[256,1024]{1,0:T(8,128)(2,1)S(1)} %slice.81), channel_id=1, source_target_pairs={{0,1},{1,0},{2,3},{3,2},{4,5},{5,4},{6,7},{7,6},{8,9},{9,8},{10,11... | collective-permute-start | bytes 1572872 | tf_op jit(solution)/shard_map/ppermute | solution.py:482
  67.1 7.9 %collective-permute-start.19 = (bf16[128,1024]{1,0:T(8,128)(2,1)S(1)}, bf16[128,1024]{1,0:T(8,128)(2,1)S(1)}, u32[]{:S(2)}, u32[]{:S(2)}) collective-permute-start(bf16[128,1024]{1,0:T(8,128)(2,1)S(1)} %add_convert_fusion.10), channel_id=1, source_target_pairs={{0,12},{4,0},{8,4},{12,8},{1,13},{5,1},{9,5},{13,9},{2,14},{6,2},{... | collective-permute-start | bytes 786440 | tf_op jit(solution)/shard_map/ppermute | solution.py:487
  75.2 11.9 %collective-permute-start.24 = (f32[16,1024]{1,0:T(8,128)S(1)}, f32[16,1024]{1,0:T(8,128)S(1)}, u32[]{:S(2)}, u32[]{:S(2)}) collective-permute-start(f32[16,1024]{1,0:T(8,128)S(1)} %pad_maximum_fusion.1), channel_id=1, source_target_pairs={{0,2},{1,3},{2,0},{3,1},{4,6},{5,7},{6,4},{7,5},{8,10},{9,11},{10,... | collective-permute-start | bytes 196616 | tf_op jit(solution)/shard_map/ppermute | solution.py:482
  77.0 10.1 %collective-permute-start.26 = (bf16[128,1024]{1,0:T(8,128)(2,1)S(1)}, bf16[128,1024]{1,0:T(8,128)(2,1)S(1)}, u32[]{:S(2)}, u32[]{:S(2)}) collective-permute-start(bf16[128,1024]{1,0:T(8,128)(2,1)S(1)} %get-tuple-element.184), channel_id=1, source_target_pairs={{0,12},{4,0},{8,4},{12,8},{1,13},{5,1},{9,5},{13,9},{2,14},{6,2},{... | collective-permute-start | bytes 786440 | tf_op jit(solution)/shard_map/ppermute | solution.py:487
  79.8 10.7 %collective-permute-start.25 = (bf16[128,1024]{1,0:T(8,128)(2,1)S(1)}, bf16[128,1024]{1,0:T(8,128)(2,1)S(1)}, u32[]{:S(2)}, u32[]{:S(2)}) collective-permute-start(bf16[128,1024]{1,0:T(8,128)(2,1)S(1)} %get-tuple-element.185), channel_id=1, source_target_pairs={{0,4},{4,8},{8,12},{12,0},{1,5},{5,9},{9,13},{13,1},{2,6},{6,10},{... | collective-permute-start | bytes 786440 | tf_op jit(solution)/shard_map/ppermute | solution.py:487
  79.9 10.7 %collective-permute-start.22 = (bf16[256,768]{1,0:T(8,128)(2,1)S(1)}, bf16[256,768]{1,0:T(8,128)(2,1)S(1)}, u32[]{:S(2)}, u32[]{:S(2)}) collective-permute-start(bf16[256,768]{1,0:T(8,128)(2,1)S(1)} %get-tuple-element.143), channel_id=1, source_target_pairs={{0,2},{1,3},{2,0},{3,1},{4,6},{5,7},{6,4},{7,5},{8,10},{9,11},{10,... | collective-permute-start | bytes 1179656 | tf_op jit(solution)/shard_map/ppermute | solution.py:482
  80.4 10.2 %collective-permute-start.23 = (bf16[2,256,768]{2,1,0:T(8,128)(2,1)S(1)}, bf16[2,256,768]{2,1,0:T(8,128)(2,1)S(1)}, u32[]{:S(2)}, u32[]{:S(2)}) collective-permute-start(bf16[2,256,768]{2,1,0:T(8,128)(2,1)S(1)} %get-tuple-element.144), channel_id=1, source_target_pairs={{0,1},{1,0},{2,3},{3,2},{4,5},{5,4},{6,7},{7,6},{8,9},{9,8},{10,11... | collective-permute-start | bytes 2359304 | tf_op jit(solution)/shard_map/ppermute | solution.py:482
  90.6 2.8 %collective-permute-start.27 = (bf16[512,1024]{1,0:T(8,128)(2,1)S(1)}, bf16[512,1024]{1,0:T(8,128)(2,1)S(1)}, u32[]{:S(2)}, u32[]{:S(2)}) collective-permute-start(bf16[512,1024]{1,0:T(8,128)(2,1)S(1)} %get-tuple-element.153), channel_id=1, source_target_pairs={{0,1},{1,0},{2,3},{3,2},{4,5},{5,4},{6,7},{7,6},{8,9},{9,8},{10,11... | collective-permute-start | bytes 3145736 | tf_op jit(solution)/shard_map/ppermute | solution.py:482
  91.7 11.1 %collective-permute-start.31 = (bf16[256,768]{1,0:T(8,128)(2,1)S(1)}, bf16[256,768]{1,0:T(8,128)(2,1)S(1)}, u32[]{:S(2)}, u32[]{:S(2)}) collective-permute-start(bf16[256,768]{1,0:T(8,128)(2,1)S(1)} %get-tuple-element.156), channel_id=1, source_target_pairs={{0,2},{1,3},{2,0},{3,1},{4,6},{5,7},{6,4},{7,5},{8,10},{9,11},{10,... | collective-permute-start | bytes 1179656 | tf_op jit(solution)/shard_map/ppermute | solution.py:482
  93.4 9.4 %collective-permute-start.32 = (f32[16,1024]{1,0:T(8,128)S(1)}, f32[16,1024]{1,0:T(8,128)S(1)}, u32[]{:S(2)}, u32[]{:S(2)}) collective-permute-start(f32[16,1024]{1,0:T(8,128)S(1)} %add.146), channel_id=1, source_target_pairs={{0,4},{4,0},{8,12},{12,8},{1,5},{5,1},{9,13},{13,9},{2,6},{6,2},{1... | collective-permute-start | bytes 196616 | tf_op jit(solution)/shard_map/ppermute | solution.py:680
  95.4 11.0 %collective-permute-start.30 = (bf16[128,1024]{1,0:T(8,128)(2,1)S(1)}, bf16[128,1024]{1,0:T(8,128)(2,1)S(1)}, u32[]{:S(2)}, u32[]{:S(2)}) collective-permute-start(bf16[128,1024]{1,0:T(8,128)(2,1)S(1)} %get-tuple-element.180), channel_id=1, source_target_pairs={{0,4},{4,8},{8,12},{12,0},{1,5},{5,9},{9,13},{13,1},{2,6},{6,10},{... | collective-permute-start | bytes 786440 | tf_op jit(solution)/shard_map/ppermute | solution.py:487
  95.7 13.5 %collective-permute-start.29 = (bf16[128,1024]{1,0:T(8,128)(2,1)S(1)}, bf16[128,1024]{1,0:T(8,128)(2,1)S(1)}, u32[]{:S(2)}, u32[]{:S(2)}) collective-permute-start(bf16[128,1024]{1,0:T(8,128)(2,1)S(1)} %get-tuple-element.181), channel_id=1, source_target_pairs={{0,12},{4,0},{8,4},{12,8},{1,13},{5,1},{9,5},{13,9},{2,14},{6,2},{... | collective-permute-start | bytes 786440 | tf_op jit(solution)/shard_map/ppermute | solution.py:487
  100.3 20.1 %collective-permute-start.33 = (bf16[2,256,768]{2,1,0:T(8,128)(2,1)S(1)}, bf16[2,256,768]{2,1,0:T(8,128)(2,1)S(1)}, u32[]{:S(2)}, u32[]{:S(2)}) collective-permute-start(bf16[2,256,768]{2,1,0:T(8,128)(2,1)S(1)} %get-tuple-element.160), channel_id=1, source_target_pairs={{0,3},{1,2},{2,1},{3,0},{4,7},{5,6},{6,5},{7,4},{8,11},{9,10},{10,... | collective-permute-start | bytes 2359304 | tf_op jit(solution)/shard_map/ppermute | solution.py:482
  109.2 5.8 %collective-permute-start.35 = (f32[16,1024]{1,0:T(8,128)S(1)}, f32[16,1024]{1,0:T(8,128)S(1)}, u32[]{:S(2)}, u32[]{:S(2)}) collective-permute-start(f32[16,1024]{1,0:T(8,128)S(1)} %add.164), channel_id=1, source_target_pairs={{0,8},{4,12},{8,0},{12,4},{1,9},{5,13},{9,1},{13,5},{2,10},{6,14},... | collective-permute-start | bytes 196616 | tf_op jit(solution)/shard_map/ppermute | solution.py:686
  111.8 7.7 %collective-permute-start.34 = (bf16[128,1024]{1,0:T(8,128)(2,1)S(1)}, bf16[128,1024]{1,0:T(8,128)(2,1)S(1)}, u32[]{:S(2)}, u32[]{:S(2)}) collective-permute-start(bf16[128,1024]{1,0:T(8,128)(2,1)S(1)} %add_convert_fusion.2), channel_id=1, source_target_pairs={{0,12},{4,0},{8,4},{12,8},{1,13},{5,1},{9,5},{13,9},{2,14},{6,2},{... | collective-permute-start | bytes 786440 | tf_op jit(solution)/shard_map/ppermute | solution.py:487
  (24 other events, 70.7 us)

commit v6 on v5

--- a/solution.py
+++ b/solution.py
@@ -299,13 +299,16 @@
 
 
 def step_kernel(before, after_it):
-    after_it[...] = before[...]
+    del before, after_it
 
 
 def next_step(step):
     return pl.pallas_call(
         step_kernel,
         out_shape=jax.ShapeDtypeStruct(step.shape, step.dtype),
+        in_specs=[pl.BlockSpec(memory_space=pl.ANY)],
+        out_specs=pl.BlockSpec(memory_space=pl.ANY),
+        input_output_aliases={0: 0},
         cost_estimate=pl.CostEstimate(flops=LONG, bytes_accessed=LONG, transcendentals=0),
     )(step)
 

time: 123 us -> 123 us (level)
  waiting for transfers between devices: 38.2 us -> 40.9 us
  Pallas kernels: 26.7 us -> 24.2 us
    pallas_call x2, Pallas kernels: 2.56 us -> 0.01 us  [next_step(): pl.pallas_call(step_kernel, out_shape=jax.ShapeDtypeStruct(step.shape, st...]
    ppermute x23, waiting for transfers between devices: 15.2 us -> 16.6 us  [dp_swap(): return lax.ppermute(value, 'dp', [(i, i ^ step) for i in range(4)])]
    ppermute x1, waiting for transfers between devices: 8.03 us -> 9.31 us  [on_device_paired(): in_other.append(lax.ppermute(in_came[1], 'groups', [(0, 1), (1, 0)]))]
  transfers between devices with their start and end apart: 36 -> 36, of which waited for: 16 -> 16; matrix products, arithmetic and copies ran while one was open for 15% -> 15% of each run, Pallas kernels for 20% -> 18%
where the time goes in v6:
time: 123 us; the launch traced here: 122 us
  waiting for transfers between devices  40.9 us (33%)
  starting transfers between devices  34.2 us (28%)
  Pallas kernels  24.2 us (20%)
  local copies, waits for them, and re-layouts  9.3 us (8%)
  other arithmetic  8.16 us (7%)
  matrix products  4.13 us (3%)
    pallas_call x4, Pallas kernels, local_kernel(): pl.pallas_call(kernel, out_shape=outputs, in_specs=[pl.BlockSpec(memory_s...  22 us
    ppermute x23, waiting for transfers between devices, dp_swap(): return lax.ppermute(value, 'dp', [(i, i ^ step) for i in range(4)])  16.6 us
    ppermute x9, starting transfers between devices, ring(): lax.ppermute(value, 'expert', [(i, (i + step) % size) for i in range(size)])  15.6 us
    ppermute x9, waiting for transfers between devices, ring(): lax.ppermute(value, 'expert', [(i, (i + step) % size) for i in range(size)])  14.7 us
    ppermute x23, starting transfers between devices, dp_swap(): return lax.ppermute(value, 'dp', [(i, i ^ step) for i in range(4)])  11.3 us
    ppermute x1, waiting for transfers between devices, on_device_paired(): in_other.append(lax.ppermute(in_came[1], 'groups', [(0, 1), (1, 0)]))  9.31 us
    squeeze x5, local copies, waits for them, and re-layouts, of_expert(): return lax.dynamic_index_in_dim(weight, which, 0, keepdims=False)  4.94 us
    dot_general x3, matrix products, mm(): return jnp.dot(a, b, preferred_element_type=jnp.float32)  2.5 us
  transfers between devices with their start and end apart: 36, of which 16 were waited for; matrix products, arithmetic and copies ran while one was open for 15% of the time, Pallas kernels for 18%

profile of v6, /device:TPU:0, one launch (start us, length us, event | category | flops | bytes accessed | tf_op | source)
XLA Modules:
  0.0 122.0 jit_solution(14996980462243043638)
XLA Ops:
  0.7 2.2 %shard_map.152 = (bf16[272,1024]{1,0:T(8,128)(2,1)}, s32[8,128]{1,0:T(8,128)}) custom-call(bf16[128,1024]{1,0:T(8,128)(2,1)} %tokens.1, bf16[128,1024]{1,0:T(8,128)(2,1)} %grads.1, s32[6,128]{1,0:T(8,128)} %bitcast.70, bf16[12,1024]{1,0:T(8,128)(2,1)} %bitcast.66), custom_call_target="tpu_custom_call" | custom-call | flops 20000000000 | bytes 20000000000 | tf_op jit(solution)/shard_map/pallas_call | solution.py:526
  2.8 3.0 %collective-permute-start.2 = (bf16[272,1024]{1,0:T(8,128)(2,1)}, bf16[272,1024]{1,0:T(8,128)(2,1)}, u32[]{:S(2)}, u32[]{:S(2)}) collective-permute-start(bf16[272,1024]{1,0:T(8,128)(2,1)} %get-tuple-element.95.refs_1_), channel_id=1, source_target_pairs={{0,4},{4,8},{8,12},{12,0},{1,5},{5,9},{9,13},{13,1},{2,6},{6,10},{... | collective-permute-start | bytes 1671176 | tf_op jit(solution)/shard_map/ppermute | solution.py:490
  6.7 1.5 %collective-permute-start.3 = (bf16[2,96,768]{2,1,0:T(8,128)(2,1)}, bf16[2,96,768]{2,1,0:T(8,128)(2,1)}, u32[]{:S(2)}, u32[]{:S(2)}) collective-permute-start(bf16[2,96,768]{2,1,0:T(8,128)(2,1)} %slice.95), channel_id=1, source_target_pairs={{0,2},{1,3},{2,0},{3,1},{4,6},{5,7},{6,4},{7,5},{8,10},{9,11},{10,... | collective-permute-start | bytes 884744 | tf_op jit(solution)/shard_map/ppermute | solution.py:485
  14.1 2.7 %collective-permute-done.3 = bf16[2,96,768]{2,1,0:T(8,128)(2,1)} collective-permute-done((bf16[2,96,768]{2,1,0:T(8,128)(2,1)}, bf16[2,96,768]{2,1,0:T(8,128)(2,1)}, u32[]{:S(2)}, u32[]{:S(2)}) %collective-permute-start.3) | collective-permute-done | bytes 294944 | tf_op jit(solution)/shard_map/ppermute | solution.py:485
  16.8 1.5 %collective-permute-start.5 = (bf16[2,96,768]{2,1,0:T(8,128)(2,1)}, bf16[2,96,768]{2,1,0:T(8,128)(2,1)}, u32[]{:S(2)}, u32[]{:S(2)}) collective-permute-start(bf16[2,96,768]{2,1,0:T(8,128)(2,1)} %collective-permute-done.3), channel_id=1, source_target_pairs={{0,16},{16,0},{1,17},{17,1},{2,18},{18,2},{3,19},{19,3},{4,20},{20... | collective-permute-start | bytes 884744 | tf_op jit(solution)/shard_map/ppermute | solution.py:539
  18.3 2.2 %collective-permute-start.1 = (bf16[272,1024]{1,0:T(8,128)(2,1)}, bf16[272,1024]{1,0:T(8,128)(2,1)}, u32[]{:S(2)}, u32[]{:S(2)}) collective-permute-start(bf16[272,1024]{1,0:T(8,128)(2,1)} %get-tuple-element.95.refs_1_), channel_id=1, source_target_pairs={{0,12},{4,0},{8,4},{12,8},{1,13},{5,1},{9,5},{13,9},{2,14},{6,2},{... | collective-permute-start | bytes 1671176 | tf_op jit(solution)/shard_map/ppermute | solution.py:490
  20.9 1.7 %dynamic-slice_bitcast_fusion.6 = (bf16[96,768]{1,0:T(8,128)(2,1)}, bf16[96,768]{1,0:T(8,128)(2,1)}) fusion(bf16[2,96,768]{2,1,0:T(8,128)(2,1)} %collective-permute-done.3, s32[]{:T(128)S(6)} %select_n.67, s32[]{:T(128)S(6)} %select_n.68), kind=kLoop, calls=%fused_computation.53 | loop fusion | bytes 589832 | tf_op jit(solution)/shard_map/jit(dynamic_index_in_dim)/squeeze | solution.py:513
  22.6 4.4 %collective-permute-done.6 = bf16[2,160,768]{2,1,0:T(8,128)(2,1)} collective-permute-done((bf16[2,160,768]{2,1,0:T(8,128)(2,1)}, bf16[2,160,768]{2,1,0:T(8,128)(2,1)}, u32[]{:S(2)}, u32[]{:S(2)}) %collective-permute-start.6) | collective-permute-done | bytes 491552 | tf_op jit(solution)/shard_map/ppermute | solution.py:485
  26.9 1.5 %collective-permute-start.13 = (bf16[2,256,768]{2,1,0:T(8,128)(2,1)S(1)}, bf16[2,256,768]{2,1,0:T(8,128)(2,1)S(1)}, u32[]{:S(2)}, u32[]{:S(2)}) collective-permute-start(bf16[2,256,768]{2,1,0:T(8,128)(2,1)S(1)} %copy-done.3), channel_id=1, source_target_pairs={{0,2},{1,3},{2,0},{3,1},{4,6},{5,7},{6,4},{7,5},{8,10},{9,11},{10,... | collective-permute-start | bytes 2359304 | tf_op jit(solution)/shard_map/ppermute | solution.py:485
  28.4 1.5 %collective-permute-start.8 = (bf16[2,160,768]{2,1,0:T(8,128)(2,1)}, bf16[2,160,768]{2,1,0:T(8,128)(2,1)}, u32[]{:S(2)}, u32[]{:S(2)}) collective-permute-start(bf16[2,160,768]{2,1,0:T(8,128)(2,1)} %collective-permute-done.6), channel_id=1, source_target_pairs={{0,16},{16,0},{1,17},{17,1},{2,18},{18,2},{3,19},{19,3},{4,20},{20... | collective-permute-start | bytes 1474568 | tf_op jit(solution)/shard_map/ppermute | solution.py:547
  32.0 9.3 %collective-permute-done.8 = bf16[2,160,768]{2,1,0:T(8,128)(2,1)} collective-permute-done((bf16[2,160,768]{2,1,0:T(8,128)(2,1)}, bf16[2,160,768]{2,1,0:T(8,128)(2,1)}, u32[]{:S(2)}, u32[]{:S(2)}) %collective-permute-start.8) | collective-permute-done | bytes 491552 | tf_op jit(solution)/shard_map/ppermute | solution.py:547
  44.9 1.3 %collective-permute-done.4.refs_5_ = bf16[272,1024]{1,0:T(8,128)(2,1)} collective-permute-done((bf16[272,1024]{1,0:T(8,128)(2,1)}, bf16[272,1024]{1,0:T(8,128)(2,1)}, u32[]{:S(2)}, u32[]{:S(2)}) %collective-permute-start.4) | collective-permute-done | bytes 557088 | tf_op jit(solution)/shard_map/ppermute | solution.py:490
  48.4 1.4 %collective-permute-done.11.refs_8_ = bf16[272,1024]{1,0:T(8,128)(2,1)S(1)} collective-permute-done((bf16[272,1024]{1,0:T(8,128)(2,1)}, bf16[272,1024]{1,0:T(8,128)(2,1)S(1)}, u32[]{:S(2)}, u32[]{:S(2)}) %collective-permute-start.11) | collective-permute-done | bytes 557088 | tf_op jit(solution)/shard_map/ppermute | solution.py:485
  49.7 5.3 %shard_map.155 = (bf16[512,128]{1,0:T(8,128)(2,1)S(1)}, bf16[512,128]{1,0:T(8,128)(2,1)S(1)}, bf16[512,1024]{1,0:T(8,128)(2,1)S(1)}, bf16[512,1024]{1,0:T(8,128)...) custom-call(s32[2]{0:T(128)S(1)} %pad_add_fusion.place, ...), custom_call_target="tpu_custom_call" | custom-call | flops 20000000000 | bytes 20000000000 | tf_op jit(solution)/shard_map/pallas_call | solution.py:242
  55.0 1.5 %collective-permute-start.17 = (bf16[256,768]{1,0:T(8,128)(2,1)S(1)}, bf16[256,768]{1,0:T(8,128)(2,1)S(1)}, u32[]{:S(2)}, u32[]{:S(2)}) collective-permute-start(bf16[256,768]{1,0:T(8,128)(2,1)S(1)} %get-tuple-element.121), channel_id=1, source_target_pairs={{0,2},{1,3},{2,0},{3,1},{4,6},{5,7},{6,4},{7,5},{8,10},{9,11},{10,... | collective-permute-start | bytes 1179656 | tf_op jit(solution)/shard_map/ppermute | solution.py:485
  56.6 4.4 %shard_map.156 = (bf16[512,1024]{1,0:T(8,128)(2,1)S(1)}, bf16[512,1024]{1,0:T(8,128)(2,1)S(1)}, bf16[256,768]{1,0:T(8,128)(2,1)S(1)}, bf16[256,768]{1,0:T(8,128)(2,1)S(1)}, bf16[256,768]{1,0:T(8,128)(2,1)S(1)}) custom-call(s32[2]{0:T(128)S(1)} %pad_add_fusion.place, s32[8,128]{1,0:T(8,128)S(1)} %copy-done.6, ...), custom_call_target="tpu_custom_call" | custom-call | flops 20000000000 | bytes 20000000000 | tf_op jit(solution)/shard_map/pallas_call | solution.py:242
  63.0 4.1 %collective-permute-done.17 = bf16[256,768]{1,0:T(8,128)(2,1)S(1)} collective-permute-done((bf16[256,768]{1,0:T(8,128)(2,1)S(1)}, bf16[256,768]{1,0:T(8,128)(2,1)S(1)}, u32[]{:S(2)}, u32[]{:S(2)}) %collective-permute-start.17) | collective-permute-done | bytes 393248 | tf_op jit(solution)/shard_map/ppermute | solution.py:485
  67.1 2.2 %collective-permute-start.19 = (bf16[128,1024]{1,0:T(8,128)(2,1)S(1)}, bf16[128,1024]{1,0:T(8,128)(2,1)S(1)}, u32[]{:S(2)}, u32[]{:S(2)}) collective-permute-start(bf16[128,1024]{1,0:T(8,128)(2,1)S(1)} %add_convert_fusion.10), channel_id=1, source_target_pairs={{0,12},{4,0},{8,4},{12,8},{1,13},{5,1},{9,5},{13,9},{2,14},{6,2},{... | collective-permute-start | bytes 786440 | tf_op jit(solution)/shard_map/ppermute | solution.py:490
  69.4 5.6 %shard_map.157 = (bf16[512,768]{1,0:T(8,128)(2,1)S(1)}, bf16[512,768]{1,0:T(8,128)(2,1)S(1)}, bf16[512,128]{1,0:T(8,128)(2,1)S(1)}, f32[8,1024]{1,0:T(8,128)S(1)...) custom-call(s32[2]{0:T(128)S(1)} %pad_add_fusion.place, ...), custom_call_target="tpu_custom_call" | custom-call | flops 20000000000 | bytes 20000000000 | tf_op jit(solution)/shard_map/pallas_call | solution.py:242
  75.2 1.5 %collective-permute-start.24 = (f32[16,1024]{1,0:T(8,128)S(1)}, f32[16,1024]{1,0:T(8,128)S(1)}, u32[]{:S(2)}, u32[]{:S(2)}) collective-permute-start(f32[16,1024]{1,0:T(8,128)S(1)} %pad_maximum_fusion.1), channel_id=1, source_target_pairs={{0,2},{1,3},{2,0},{3,1},{4,6},{5,7},{6,4},{7,5},{8,10},{9,11},{10,... | collective-permute-start | bytes 196616 | tf_op jit(solution)/shard_map/ppermute | solution.py:485
  77.0 2.9 %collective-permute-start.26 = (bf16[128,1024]{1,0:T(8,128)(2,1)S(1)}, bf16[128,1024]{1,0:T(8,128)(2,1)S(1)}, u32[]{:S(2)}, u32[]{:S(2)}) collective-permute-start(bf16[128,1024]{1,0:T(8,128)(2,1)S(1)} %get-tuple-element.184), channel_id=1, source_target_pairs={{0,12},{4,0},{8,4},{12,8},{1,13},{5,1},{9,5},{13,9},{2,14},{6,2},{... | collective-permute-start | bytes 786440 | tf_op jit(solution)/shard_map/ppermute | solution.py:490
  80.4 6.7 %shard_map.158 = (bf16[512,1024]{1,0:T(8,128)(2,1)S(1)}, bf16[512,1024]{1,0:T(8,128)(2,1)S(1)}) custom-call(s32[2]{0:T(128)S(1)} %pad_add_fusion.place, bf16[512,128]{1,0:T(8,128)(2,1)S(1)} %get-tuple-element.127.refs_0_, bf16[512,768]{1,0:T(8,128)(2,1)S(1)} %get-tuple-element.138.refs_1_, bf16[512,768]{1,0:T(8,128)(2,1)S(1)} %get-tuple-element.139.refs_2_, ...), custom_call_target="tpu_custom_call" | custom-call | flops 20000000000 | bytes 20000000000 | tf_op jit(solution)/shard_map/pallas_call | solution.py:242
  87.1 3.5 %collective-permute-done.25 = bf16[128,1024]{1,0:T(8,128)(2,1)S(1)} collective-permute-done((bf16[128,1024]{1,0:T(8,128)(2,1)S(1)}, bf16[128,1024]{1,0:T(8,128)(2,1)S(1)}, u32[]{:S(2)}, u32[]{:S(2)}) %collective-permute-start.25) | collective-permute-done | bytes 262176 | tf_op jit(solution)/shard_map/ppermute | solution.py:490
  91.7 1.5 %collective-permute-start.31 = (bf16[256,768]{1,0:T(8,128)(2,1)S(1)}, bf16[256,768]{1,0:T(8,128)(2,1)S(1)}, u32[]{:S(2)}, u32[]{:S(2)}) collective-permute-start(bf16[256,768]{1,0:T(8,128)(2,1)S(1)} %get-tuple-element.156), channel_id=1, source_target_pairs={{0,2},{1,3},{2,0},{3,1},{4,6},{5,7},{6,4},{7,5},{8,10},{9,11},{10,... | collective-permute-start | bytes 1179656 | tf_op jit(solution)/shard_map/ppermute | solution.py:485
  93.4 1.8 %collective-permute-start.32 = (f32[16,1024]{1,0:T(8,128)S(1)}, f32[16,1024]{1,0:T(8,128)S(1)}, u32[]{:S(2)}, u32[]{:S(2)}) collective-permute-start(f32[16,1024]{1,0:T(8,128)S(1)} %add.146), channel_id=1, source_target_pairs={{0,4},{4,0},{8,12},{12,8},{1,5},{5,1},{9,13},{13,9},{2,6},{6,2},{1... | collective-permute-start | bytes 196616 | tf_op jit(solution)/shard_map/ppermute | solution.py:683
  95.7 3.6 %collective-permute-start.29 = (bf16[128,1024]{1,0:T(8,128)(2,1)S(1)}, bf16[128,1024]{1,0:T(8,128)(2,1)S(1)}, u32[]{:S(2)}, u32[]{:S(2)}) collective-permute-start(bf16[128,1024]{1,0:T(8,128)(2,1)S(1)} %get-tuple-element.181), channel_id=1, source_target_pairs={{0,12},{4,0},{8,4},{12,8},{1,13},{5,1},{9,5},{13,9},{2,14},{6,2},{... | collective-permute-start | bytes 786440 | tf_op jit(solution)/shard_map/ppermute | solution.py:490
  100.3 2.5 %collective-permute-done.31 = bf16[256,768]{1,0:T(8,128)(2,1)S(1)} collective-permute-done((bf16[256,768]{1,0:T(8,128)(2,1)S(1)}, bf16[256,768]{1,0:T(8,128)(2,1)S(1)}, u32[]{:S(2)}, u32[]{:S(2)}) %collective-permute-start.31) | collective-permute-done | bytes 393248 | tf_op jit(solution)/shard_map/ppermute | solution.py:485
  102.8 3.7 %collective-permute-done.30 = bf16[128,1024]{1,0:T(8,128)(2,1)S(1)} collective-permute-done((bf16[128,1024]{1,0:T(8,128)(2,1)S(1)}, bf16[128,1024]{1,0:T(8,128)(2,1)S(1)}, u32[]{:S(2)}, u32[]{:S(2)}) %collective-permute-start.30) | collective-permute-done | bytes 262176 | tf_op jit(solution)/shard_map/ppermute | solution.py:490
  106.5 2.8 %collective-permute-done.29 = bf16[128,1024]{1,0:T(8,128)(2,1)S(1)} collective-permute-done((bf16[128,1024]{1,0:T(8,128)(2,1)S(1)}, bf16[128,1024]{1,0:T(8,128)(2,1)S(1)}, u32[]{:S(2)}, u32[]{:S(2)}) %collective-permute-start.29) | collective-permute-done | bytes 262176 | tf_op jit(solution)/shard_map/ppermute | solution.py:490
  109.2 2.4 %collective-permute-start.35 = (f32[16,1024]{1,0:T(8,128)S(1)}, f32[16,1024]{1,0:T(8,128)S(1)}, u32[]{:S(2)}, u32[]{:S(2)}) collective-permute-start(f32[16,1024]{1,0:T(8,128)S(1)} %add.164), channel_id=1, source_target_pairs={{0,8},{4,12},{8,0},{12,4},{1,9},{5,13},{9,1},{13,5},{2,10},{6,14},... | collective-permute-start | bytes 196616 | tf_op jit(solution)/shard_map/ppermute | solution.py:689
  116.3 3.2 %collective-permute-done.34 = bf16[128,1024]{1,0:T(8,128)(2,1)S(1)} collective-permute-done((bf16[128,1024]{1,0:T(8,128)(2,1)S(1)}, bf16[128,1024]{1,0:T(8,128)(2,1)S(1)}, u32[]{:S(2)}, u32[]{:S(2)}) %collective-permute-start.34) | collective-permute-done | bytes 262176 | tf_op jit(solution)/shard_map/ppermute | solution.py:490
  120.6 1.4 %select_convert_fusion = (bf16[2,256,768]{2,1,0:T(8,128)(2,1)}, bf16[2,256,768]{2,1,0:T(8,128)(2,1)}) fusion(bf16[256,768]{1,0:T(8,128)(2,1)S(1)} %get-tuple-element.182, bf16[256,768]{1,0:T(8,128)(2,1)S(1)} %get-tuple-element.175, pred[2]{0:T(512)(128)(4,1)S(1)} %iota_compare_fusion.1, bf16[256,768]{1,0:T(8,128)(2,1)S(1)} %get-tuple-element.183, ...), kind=kLoop, calls=%fused_computation | loop fusion | flops 786432 | bytes 3145730 | tf_op jit(solution)/shard_map/convert_element_type | solution.py:590
  (143 shorter events, 26.1 us)
Async XLA Ops:
  2.8 18.0 %collective-permute-start.2 = (bf16[272,1024]{1,0:T(8,128)(2,1)}, bf16[272,1024]{1,0:T(8,128)(2,1)}, u32[]{:S(2)}, u32[]{:S(2)}) collective-permute-start(bf16[272,1024]{1,0:T(8,128)(2,1)} %get-tuple-element.95.refs_1_), channel_id=1, source_target_pairs={{0,4},{4,8},{8,12},{12,0},{1,5},{5,9},{9,13},{13,1},{2,6},{6,10},{... | collective-permute-start | bytes 1671176 | tf_op jit(solution)/shard_map/ppermute | solution.py:490
  5.8 12.5 %collective-permute-start = (bf16[272,1024]{1,0:T(8,128)(2,1)}, bf16[272,1024]{1,0:T(8,128)(2,1)S(1)}, u32[]{:S(2)}, u32[]{:S(2)}) collective-permute-start(bf16[272,1024]{1,0:T(8,128)(2,1)} %get-tuple-element.95.refs_1_), channel_id=1, source_target_pairs={{0,1},{1,0},{2,3},{3,2},{4,5},{5,4},{6,7},{7,6},{8,9},{9,8},{10,11... | collective-permute-start | bytes 1671176 | tf_op jit(solution)/shard_map/ppermute | solution.py:485
  6.7 10.1 %collective-permute-start.3 = (bf16[2,96,768]{2,1,0:T(8,128)(2,1)}, bf16[2,96,768]{2,1,0:T(8,128)(2,1)}, u32[]{:S(2)}, u32[]{:S(2)}) collective-permute-start(bf16[2,96,768]{2,1,0:T(8,128)(2,1)} %slice.95), channel_id=1, source_target_pairs={{0,2},{1,3},{2,0},{3,1},{4,6},{5,7},{6,4},{7,5},{8,10},{9,11},{10,... | collective-permute-start | bytes 884744 | tf_op jit(solution)/shard_map/ppermute | solution.py:485
  9.0 18.0 %collective-permute-start.6 = (bf16[2,160,768]{2,1,0:T(8,128)(2,1)}, bf16[2,160,768]{2,1,0:T(8,128)(2,1)}, u32[]{:S(2)}, u32[]{:S(2)}) collective-permute-start(bf16[2,160,768]{2,1,0:T(8,128)(2,1)} %slice.96), channel_id=1, source_target_pairs={{0,2},{1,3},{2,0},{3,1},{4,6},{5,7},{6,4},{7,5},{8,10},{9,11},{10,... | collective-permute-start | bytes 1474568 | tf_op jit(solution)/shard_map/ppermute | solution.py:485
  10.8 17.6 %collective-permute-start.7 = (bf16[3,256,768]{2,1,0:T(8,128)(2,1)}, bf16[3,256,768]{2,1,0:T(8,128)(2,1)}, u32[]{:S(2)}, u32[]{:S(2)}) collective-permute-start(bf16[3,256,768]{2,1,0:T(8,128)(2,1)} %pad_maximum_fusion), channel_id=1, source_target_pairs={{0,1},{1,0},{2,3},{3,2},{4,5},{5,4},{6,7},{7,6},{8,9},{9,8},{10,11... | collective-permute-start | bytes 3538952 | tf_op jit(solution)/shard_map/ppermute | solution.py:485
  16.8 15.2 %collective-permute-start.5 = (bf16[2,96,768]{2,1,0:T(8,128)(2,1)}, bf16[2,96,768]{2,1,0:T(8,128)(2,1)}, u32[]{:S(2)}, u32[]{:S(2)}) collective-permute-start(bf16[2,96,768]{2,1,0:T(8,128)(2,1)} %collective-permute-done.3), channel_id=1, source_target_pairs={{0,16},{16,0},{1,17},{17,1},{2,18},{18,2},{3,19},{19,3},{4,20},{20... | collective-permute-start | bytes 884744 | tf_op jit(solution)/shard_map/ppermute | solution.py:539
  18.3 26.6 %collective-permute-start.1 = (bf16[272,1024]{1,0:T(8,128)(2,1)}, bf16[272,1024]{1,0:T(8,128)(2,1)}, u32[]{:S(2)}, u32[]{:S(2)}) collective-permute-start(bf16[272,1024]{1,0:T(8,128)(2,1)} %get-tuple-element.95.refs_1_), channel_id=1, source_target_pairs={{0,12},{4,0},{8,4},{12,8},{1,13},{5,1},{9,5},{13,9},{2,14},{6,2},{... | collective-permute-start | bytes 1671176 | tf_op jit(solution)/shard_map/ppermute | solution.py:490
  20.9 25.3 %collective-permute-start.4 = (bf16[272,1024]{1,0:T(8,128)(2,1)}, bf16[272,1024]{1,0:T(8,128)(2,1)}, u32[]{:S(2)}, u32[]{:S(2)}) collective-permute-start(bf16[272,1024]{1,0:T(8,128)(2,1)} %collective-permute-done.2.refs_3_), channel_id=1, source_target_pairs={{0,4},{4,8},{8,12},{12,0},{1,5},{5,9},{9,13},{13,1},{2,6},{6,10},{... | collective-permute-start | bytes 1671176 | tf_op jit(solution)/shard_map/ppermute | solution.py:490
  26.9 19.9 %collective-permute-start.13 = (bf16[2,256,768]{2,1,0:T(8,128)(2,1)S(1)}, bf16[2,256,768]{2,1,0:T(8,128)(2,1)S(1)}, u32[]{:S(2)}, u32[]{:S(2)}) collective-permute-start(bf16[2,256,768]{2,1,0:T(8,128)(2,1)S(1)} %copy-done.3), channel_id=1, source_target_pairs={{0,2},{1,3},{2,0},{3,1},{4,6},{5,7},{6,4},{7,5},{8,10},{9,11},{10,... | collective-permute-start | bytes 2359304 | tf_op jit(solution)/shard_map/ppermute | solution.py:485
  28.4 12.9 %collective-permute-start.8 = (bf16[2,160,768]{2,1,0:T(8,128)(2,1)}, bf16[2,160,768]{2,1,0:T(8,128)(2,1)}, u32[]{:S(2)}, u32[]{:S(2)}) collective-permute-start(bf16[2,160,768]{2,1,0:T(8,128)(2,1)} %collective-permute-done.6), channel_id=1, source_target_pairs={{0,16},{16,0},{1,17},{17,1},{2,18},{18,2},{3,19},{19,3},{4,20},{20... | collective-permute-start | bytes 1474568 | tf_op jit(solution)/shard_map/ppermute | solution.py:547
  43.6 6.1 %collective-permute-start.12 = (bf16[2,256,768]{2,1,0:T(8,128)(2,1)S(1)}, bf16[2,256,768]{2,1,0:T(8,128)(2,1)S(1)}, u32[]{:S(2)}, u32[]{:S(2)}) collective-permute-start(bf16[2,256,768]{2,1,0:T(8,128)(2,1)S(1)} %maximum_select_fusion.1), channel_id=1, source_target_pairs={{0,1},{1,0},{2,3},{3,2},{4,5},{5,4},{6,7},{7,6},{8,9},{9,8},{10,11... | collective-permute-start | bytes 2359304 | tf_op jit(solution)/shard_map/ppermute | solution.py:485
  44.8 2.4 %collective-permute-start.9 = (bf16[272,1024]{1,0:T(8,128)(2,1)}, bf16[272,1024]{1,0:T(8,128)(2,1)S(1)}, u32[]{:S(2)}, u32[]{:S(2)}) collective-permute-start(bf16[272,1024]{1,0:T(8,128)(2,1)} %collective-permute-done.2.refs_3_), channel_id=1, source_target_pairs={{0,1},{1,0},{2,3},{3,2},{4,5},{5,4},{6,7},{7,6},{8,9},{9,8},{10,11... | collective-permute-start | bytes 1671176 | tf_op jit(solution)/shard_map/ppermute | solution.py:485
  46.2 3.5 %collective-permute-start.11 = (bf16[272,1024]{1,0:T(8,128)(2,1)}, bf16[272,1024]{1,0:T(8,128)(2,1)S(1)}, u32[]{:S(2)}, u32[]{:S(2)}) collective-permute-start(bf16[272,1024]{1,0:T(8,128)(2,1)} %collective-permute-done.1.refs_7_), channel_id=1, source_target_pairs={{0,1},{1,0},{2,3},{3,2},{4,5},{5,4},{6,7},{7,6},{8,9},{9,8},{10,11... | collective-permute-start | bytes 1671176 | tf_op jit(solution)/shard_map/ppermute | solution.py:485
  46.9 8.2 %collective-permute-start.14 = (bf16[256,768]{1,0:T(8,128)(2,1)S(1)}, bf16[256,768]{1,0:T(8,128)(2,1)S(1)}, u32[]{:S(2)}, u32[]{:S(2)}) collective-permute-start(bf16[256,768]{1,0:T(8,128)(2,1)S(1)} %dynamic-slice_bitcast_fusion), channel_id=1, source_target_pairs={{0,1},{1,0},{2,3},{3,2},{4,5},{5,4},{6,7},{7,6},{8,9},{9,8},{10,11... | collective-permute-start | bytes 1179656 | tf_op jit(solution)/shard_map/ppermute | solution.py:485
  55.0 12.0 %collective-permute-start.17 = (bf16[256,768]{1,0:T(8,128)(2,1)S(1)}, bf16[256,768]{1,0:T(8,128)(2,1)S(1)}, u32[]{:S(2)}, u32[]{:S(2)}) collective-permute-start(bf16[256,768]{1,0:T(8,128)(2,1)S(1)} %get-tuple-element.121), channel_id=1, source_target_pairs={{0,2},{1,3},{2,0},{3,1},{4,6},{5,7},{6,4},{7,5},{8,10},{9,11},{10,... | collective-permute-start | bytes 1179656 | tf_op jit(solution)/shard_map/ppermute | solution.py:485
  61.9 13.1 %collective-permute-start.18 = (bf16[256,768]{1,0:T(8,128)(2,1)S(1)}, bf16[256,768]{1,0:T(8,128)(2,1)S(1)}, u32[]{:S(2)}, u32[]{:S(2)}) collective-permute-start(bf16[256,768]{1,0:T(8,128)(2,1)S(1)} %get-tuple-element.134), channel_id=1, source_target_pairs={{0,3},{1,2},{2,1},{3,0},{4,7},{5,6},{6,5},{7,4},{8,11},{9,10},{10,... | collective-permute-start | bytes 1179656 | tf_op jit(solution)/shard_map/ppermute | solution.py:485
  62.2 12.8 %collective-permute-start.21 = (bf16[256,768]{1,0:T(8,128)(2,1)S(1)}, bf16[256,768]{1,0:T(8,128)(2,1)S(1)}, u32[]{:S(2)}, u32[]{:S(2)}) collective-permute-start(bf16[256,768]{1,0:T(8,128)(2,1)S(1)} %get-tuple-element.137), channel_id=1, source_target_pairs={{0,1},{1,0},{2,3},{3,2},{4,5},{5,4},{6,7},{7,6},{8,9},{9,8},{10,11... | collective-permute-start | bytes 1179656 | tf_op jit(solution)/shard_map/ppermute | solution.py:485
  62.7 12.4 %collective-permute-start.20 = (bf16[256,1024]{1,0:T(8,128)(2,1)S(1)}, bf16[256,1024]{1,0:T(8,128)(2,1)S(1)}, u32[]{:S(2)}, u32[]{:S(2)}) collective-permute-start(bf16[256,1024]{1,0:T(8,128)(2,1)S(1)} %slice.81), channel_id=1, source_target_pairs={{0,1},{1,0},{2,3},{3,2},{4,5},{5,4},{6,7},{7,6},{8,9},{9,8},{10,11... | collective-permute-start | bytes 1572872 | tf_op jit(solution)/shard_map/ppermute | solution.py:485
  67.1 7.9 %collective-permute-start.19 = (bf16[128,1024]{1,0:T(8,128)(2,1)S(1)}, bf16[128,1024]{1,0:T(8,128)(2,1)S(1)}, u32[]{:S(2)}, u32[]{:S(2)}) collective-permute-start(bf16[128,1024]{1,0:T(8,128)(2,1)S(1)} %add_convert_fusion.10), channel_id=1, source_target_pairs={{0,12},{4,0},{8,4},{12,8},{1,13},{5,1},{9,5},{13,9},{2,14},{6,2},{... | collective-permute-start | bytes 786440 | tf_op jit(solution)/shard_map/ppermute | solution.py:490
  75.2 11.9 %collective-permute-start.24 = (f32[16,1024]{1,0:T(8,128)S(1)}, f32[16,1024]{1,0:T(8,128)S(1)}, u32[]{:S(2)}, u32[]{:S(2)}) collective-permute-start(f32[16,1024]{1,0:T(8,128)S(1)} %pad_maximum_fusion.1), channel_id=1, source_target_pairs={{0,2},{1,3},{2,0},{3,1},{4,6},{5,7},{6,4},{7,5},{8,10},{9,11},{10,... | collective-permute-start | bytes 196616 | tf_op jit(solution)/shard_map/ppermute | solution.py:485
  77.0 10.1 %collective-permute-start.26 = (bf16[128,1024]{1,0:T(8,128)(2,1)S(1)}, bf16[128,1024]{1,0:T(8,128)(2,1)S(1)}, u32[]{:S(2)}, u32[]{:S(2)}) collective-permute-start(bf16[128,1024]{1,0:T(8,128)(2,1)S(1)} %get-tuple-element.184), channel_id=1, source_target_pairs={{0,12},{4,0},{8,4},{12,8},{1,13},{5,1},{9,5},{13,9},{2,14},{6,2},{... | collective-permute-start | bytes 786440 | tf_op jit(solution)/shard_map/ppermute | solution.py:490
  79.9 10.7 %collective-permute-start.25 = (bf16[128,1024]{1,0:T(8,128)(2,1)S(1)}, bf16[128,1024]{1,0:T(8,128)(2,1)S(1)}, u32[]{:S(2)}, u32[]{:S(2)}) collective-permute-start(bf16[128,1024]{1,0:T(8,128)(2,1)S(1)} %get-tuple-element.185), channel_id=1, source_target_pairs={{0,4},{4,8},{8,12},{12,0},{1,5},{5,9},{9,13},{13,1},{2,6},{6,10},{... | collective-permute-start | bytes 786440 | tf_op jit(solution)/shard_map/ppermute | solution.py:490
  79.9 10.7 %collective-permute-start.22 = (bf16[256,768]{1,0:T(8,128)(2,1)S(1)}, bf16[256,768]{1,0:T(8,128)(2,1)S(1)}, u32[]{:S(2)}, u32[]{:S(2)}) collective-permute-start(bf16[256,768]{1,0:T(8,128)(2,1)S(1)} %get-tuple-element.143), channel_id=1, source_target_pairs={{0,2},{1,3},{2,0},{3,1},{4,6},{5,7},{6,4},{7,5},{8,10},{9,11},{10,... | collective-permute-start | bytes 1179656 | tf_op jit(solution)/shard_map/ppermute | solution.py:485
  80.4 10.2 %collective-permute-start.23 = (bf16[2,256,768]{2,1,0:T(8,128)(2,1)S(1)}, bf16[2,256,768]{2,1,0:T(8,128)(2,1)S(1)}, u32[]{:S(2)}, u32[]{:S(2)}) collective-permute-start(bf16[2,256,768]{2,1,0:T(8,128)(2,1)S(1)} %get-tuple-element.144), channel_id=1, source_target_pairs={{0,1},{1,0},{2,3},{3,2},{4,5},{5,4},{6,7},{7,6},{8,9},{9,8},{10,11... | collective-permute-start | bytes 2359304 | tf_op jit(solution)/shard_map/ppermute | solution.py:485
  90.6 2.8 %collective-permute-start.27 = (bf16[512,1024]{1,0:T(8,128)(2,1)S(1)}, bf16[512,1024]{1,0:T(8,128)(2,1)S(1)}, u32[]{:S(2)}, u32[]{:S(2)}) collective-permute-start(bf16[512,1024]{1,0:T(8,128)(2,1)S(1)} %get-tuple-element.153), channel_id=1, source_target_pairs={{0,1},{1,0},{2,3},{3,2},{4,5},{5,4},{6,7},{7,6},{8,9},{9,8},{10,11... | collective-permute-start | bytes 3145736 | tf_op jit(solution)/shard_map/ppermute | solution.py:485
  91.7 11.1 %collective-permute-start.31 = (bf16[256,768]{1,0:T(8,128)(2,1)S(1)}, bf16[256,768]{1,0:T(8,128)(2,1)S(1)}, u32[]{:S(2)}, u32[]{:S(2)}) collective-permute-start(bf16[256,768]{1,0:T(8,128)(2,1)S(1)} %get-tuple-element.156), channel_id=1, source_target_pairs={{0,2},{1,3},{2,0},{3,1},{4,6},{5,7},{6,4},{7,5},{8,10},{9,11},{10,... | collective-permute-start | bytes 1179656 | tf_op jit(solution)/shard_map/ppermute | solution.py:485
  93.4 9.4 %collective-permute-start.32 = (f32[16,1024]{1,0:T(8,128)S(1)}, f32[16,1024]{1,0:T(8,128)S(1)}, u32[]{:S(2)}, u32[]{:S(2)}) collective-permute-start(f32[16,1024]{1,0:T(8,128)S(1)} %add.146), channel_id=1, source_target_pairs={{0,4},{4,0},{8,12},{12,8},{1,5},{5,1},{9,13},{13,9},{2,6},{6,2},{1... | collective-permute-start | bytes 196616 | tf_op jit(solution)/shard_map/ppermute | solution.py:683
  95.4 11.0 %collective-permute-start.30 = (bf16[128,1024]{1,0:T(8,128)(2,1)S(1)}, bf16[128,1024]{1,0:T(8,128)(2,1)S(1)}, u32[]{:S(2)}, u32[]{:S(2)}) collective-permute-start(bf16[128,1024]{1,0:T(8,128)(2,1)S(1)} %get-tuple-element.180), channel_id=1, source_target_pairs={{0,4},{4,8},{8,12},{12,0},{1,5},{5,9},{9,13},{13,1},{2,6},{6,10},{... | collective-permute-start | bytes 786440 | tf_op jit(solution)/shard_map/ppermute | solution.py:490
  95.7 13.5 %collective-permute-start.29 = (bf16[128,1024]{1,0:T(8,128)(2,1)S(1)}, bf16[128,1024]{1,0:T(8,128)(2,1)S(1)}, u32[]{:S(2)}, u32[]{:S(2)}) collective-permute-start(bf16[128,1024]{1,0:T(8,128)(2,1)S(1)} %get-tuple-element.181), channel_id=1, source_target_pairs={{0,12},{4,0},{8,4},{12,8},{1,13},{5,1},{9,5},{13,9},{2,14},{6,2},{... | collective-permute-start | bytes 786440 | tf_op jit(solution)/shard_map/ppermute | solution.py:490
  100.3 20.1 %collective-permute-start.33 = (bf16[2,256,768]{2,1,0:T(8,128)(2,1)S(1)}, bf16[2,256,768]{2,1,0:T(8,128)(2,1)S(1)}, u32[]{:S(2)}, u32[]{:S(2)}) collective-permute-start(bf16[2,256,768]{2,1,0:T(8,128)(2,1)S(1)} %get-tuple-element.160), channel_id=1, source_target_pairs={{0,3},{1,2},{2,1},{3,0},{4,7},{5,6},{6,5},{7,4},{8,11},{9,10},{10,... | collective-permute-start | bytes 2359304 | tf_op jit(solution)/shard_map/ppermute | solution.py:485
  109.2 5.8 %collective-permute-start.35 = (f32[16,1024]{1,0:T(8,128)S(1)}, f32[16,1024]{1,0:T(8,128)S(1)}, u32[]{:S(2)}, u32[]{:S(2)}) collective-permute-start(f32[16,1024]{1,0:T(8,128)S(1)} %add.164), channel_id=1, source_target_pairs={{0,8},{4,12},{8,0},{12,4},{1,9},{5,13},{9,1},{13,5},{2,10},{6,14},... | collective-permute-start | bytes 196616 | tf_op jit(solution)/shard_map/ppermute | solution.py:689
  111.8 7.7 %collective-permute-start.34 = (bf16[128,1024]{1,0:T(8,128)(2,1)S(1)}, bf16[128,1024]{1,0:T(8,128)(2,1)S(1)}, u32[]{:S(2)}, u32[]{:S(2)}) collective-permute-start(bf16[128,1024]{1,0:T(8,128)(2,1)S(1)} %add_convert_fusion.2), channel_id=1, source_target_pairs={{0,12},{4,0},{8,4},{12,8},{1,13},{5,1},{9,5},{13,9},{2,14},{6,2},{... | collective-permute-start | bytes 786440 | tf_op jit(solution)/shard_map/ppermute | solution.py:490
  (24 other events, 69.3 us)

commit v7 on v6

--- a/solution.py
+++ b/solution.py
@@ -678,15 +678,17 @@
     back_came, small_came = together(dp_swap(back_other, 1), dp_swap(small, 1))
     back_late = sum_slots(back_own[: 2 * row_count], jnp.split(back_came[: 2 * row_count], 2))
     back_first = sum_slots(back_own[2 * row_count :], jnp.split(back_came[2 * row_count :], 2))
+    back_first[0], back_first[1], step = together(*back_first, step_down)
     back_near, back_side = ring(back_first[0], -1), ring(back_first[1], 1)
+    step = next_step(step)
     small = small + small_came
+    small, step = together(small, step)
     small_came = lax.ppermute(small, "expert", [(i, i ^ 1) for i in range(4)])
-    back_near, back_side, up_came, mixed_near, small_came = together(
-        back_near, back_side, up_came, mixed_near, small_came
-    )
+    back_near, up_came, mixed_near, small_came = together(back_near, up_came, mixed_near, small_came)
     back_near = ring(add(back_near, back_late[1]).astype(bf16), -1)
     small = small + small_came
     small = small + lax.ppermute(small, "expert", [(i, i ^ 2) for i in range(4)])
+    small = small + step[0:1, 0:1].astype(f32)
     mixed_sum = add(mixed_side, mixed_near) + mixed_late[0].astype(f32)
     grad_router = small[:id_count].T
     grad_const_gate = small[id_count : id_count + const_count].T

time: 123 us -> 122 us (level)
  waiting for transfers between devices: 40.9 us -> 37.6 us
  starting transfers between devices: 34.2 us -> 32.3 us
  local copies, waits for them, and re-layouts: 9.3 us -> 10.9 us
  other arithmetic: 8.16 us -> 9.7 us
    ppermute x9, waiting for transfers between devices: 14.7 us -> 8.83 us  [ring(): lax.ppermute(value, 'expert', [(i, (i + step) % size) for i in range(size)])]
    ppermute x1, waiting for transfers between devices: 0.22 us -> 2.01 us  [on_device_paired(): lax.ppermute(small, 'expert', [(i, i ^ 2) for i in range(4)])]
    ppermute x1, starting transfers between devices: 2.41 us -> 0.82 us  [on_device_paired(): lax.ppermute(small, 'expert', [(i, i ^ 2) for i in range(4)])]
    unnamed x40 -> x84, local copies, waits for them, and re-layouts: 1.4 us -> 2.56 us
  transfers between devices with their start and end apart: 36 -> 36, of which waited for: 16 -> 14; matrix products, arithmetic and copies ran while one was open for 15% -> 18% of each run, Pallas kernels for 18% -> 18%
where the time goes in v7:
time: 122 us
  waiting for transfers between devices  37.6 us (31%)
  starting transfers between devices  32.3 us (26%)
  Pallas kernels  24.2 us (20%)
  local copies, waits for them, and re-layouts  10.9 us (9%)
  other arithmetic  9.7 us (8%)
  matrix products  5.09 us (4%)
  between operations  1.98 us (2%)
    pallas_call x4, Pallas kernels, local_kernel(): pl.pallas_call(kernel, out_shape=outputs, in_specs=[pl.BlockSpec(memory_s...  22 us
    ppermute x23, waiting for transfers between devices, dp_swap(): return lax.ppermute(value, 'dp', [(i, i ^ step) for i in range(4)])  16.6 us
    ppermute x9, starting transfers between devices, ring(): lax.ppermute(value, 'expert', [(i, (i + step) % size) for i in range(size)])  15.5 us
    ppermute x23, starting transfers between devices, dp_swap(): return lax.ppermute(value, 'dp', [(i, i ^ step) for i in range(4)])  11.5 us
    ppermute x1, waiting for transfers between devices, on_device_paired(): in_other.append(lax.ppermute(in_came[1], 'groups', [(0, 1), (1, 0)]))  10.2 us
    ppermute x9, waiting for transfers between devices, ring(): lax.ppermute(value, 'expert', [(i, (i + step) % size) for i in range(size)])  8.83 us
    squeeze x5, local copies, waits for them, and re-layouts, of_expert(): return lax.dynamic_index_in_dim(weight, which, 0, keepdims=False)  4.24 us
    dot_general x3, matrix products, mm(): return jnp.dot(a, b, preferred_element_type=jnp.float32)  3.42 us
  transfers between devices with their start and end apart: 36, of which 14 were waited for; matrix products, arithmetic and copies ran while one was open for 18% of the time, Pallas kernels for 18%

profile of v7, /device:TPU:0, one launch (start us, length us, event | category | flops | bytes accessed | tf_op | source)
XLA Modules:
  0.0 121.8 jit_solution(17968851301851688069)
XLA Ops:
  0.7 2.2 %shard_map.152 = (bf16[272,1024]{1,0:T(8,128)(2,1)}, s32[8,128]{1,0:T(8,128)}) custom-call(bf16[128,1024]{1,0:T(8,128)(2,1)} %tokens.1, bf16[128,1024]{1,0:T(8,128)(2,1)} %grads.1, s32[6,128]{1,0:T(8,128)} %bitcast.71, bf16[12,1024]{1,0:T(8,128)(2,1)} %bitcast.67), custom_call_target="tpu_custom_call" | custom-call | flops 20000000000 | bytes 20000000000 | tf_op jit(solution)/shard_map/pallas_call | solution.py:526
  2.8 3.0 %collective-permute-start.2 = (bf16[272,1024]{1,0:T(8,128)(2,1)}, bf16[272,1024]{1,0:T(8,128)(2,1)}, u32[]{:S(2)}, u32[]{:S(2)}) collective-permute-start(bf16[272,1024]{1,0:T(8,128)(2,1)} %get-tuple-element.99.refs_1_), channel_id=1, source_target_pairs={{0,4},{4,8},{8,12},{12,0},{1,5},{5,9},{9,13},{13,1},{2,6},{6,10},{... | collective-permute-start | bytes 1671176 | tf_op jit(solution)/shard_map/ppermute | solution.py:490
  6.7 1.5 %collective-permute-start.3 = (bf16[2,96,768]{2,1,0:T(8,128)(2,1)}, bf16[2,96,768]{2,1,0:T(8,128)(2,1)}, u32[]{:S(2)}, u32[]{:S(2)}) collective-permute-start(bf16[2,96,768]{2,1,0:T(8,128)(2,1)} %slice.99), channel_id=1, source_target_pairs={{0,2},{1,3},{2,0},{3,1},{4,6},{5,7},{6,4},{7,5},{8,10},{9,11},{10,... | collective-permute-start | bytes 884744 | tf_op jit(solution)/shard_map/ppermute | solution.py:485
  11.4 1.2 %multiply_reduce_fusion = (f32[128]{0:T(128)}, bf16[128,2]{0,1:T(2,128)(2,1)}, bf16[128,2]{0,1:T(2,128)(2,1)S(1)}, f32[128,2]{0,1:T(2,128)S(1)}) fusion(f32[128,4]{0,1:T(4,128)S(1)} %get-tuple-element.214, f32[128,2]{0,1:T(2,128)S(1)} %fusion.27, f32[128]{0:T(128)S(1)} %fusion.10, bf16[128,1024]{1,0:T(8,128)(2,1)S(1)} %copy-done.13, ...), kind=kOutput, calls=%fused_computation.79 | convolution fusion | flops 528256 | bytes 271360 | tf_op jit(solution)/shard_map/dot_general | solution.py:267
  14.1 2.7 %collective-permute-done.3 = bf16[2,96,768]{2,1,0:T(8,128)(2,1)} collective-permute-done((bf16[2,96,768]{2,1,0:T(8,128)(2,1)}, bf16[2,96,768]{2,1,0:T(8,128)(2,1)}, u32[]{:S(2)}, u32[]{:S(2)}) %collective-permute-start.3) | collective-permute-done | bytes 294944 | tf_op jit(solution)/shard_map/ppermute | solution.py:485
  16.8 1.5 %collective-permute-start.5 = (bf16[2,96,768]{2,1,0:T(8,128)(2,1)}, bf16[2,96,768]{2,1,0:T(8,128)(2,1)}, u32[]{:S(2)}, u32[]{:S(2)}) collective-permute-start(bf16[2,96,768]{2,1,0:T(8,128)(2,1)} %collective-permute-done.3), channel_id=1, source_target_pairs={{0,16},{16,0},{1,17},{17,1},{2,18},{18,2},{3,19},{19,3},{4,20},{20... | collective-permute-start | bytes 884744 | tf_op jit(solution)/shard_map/ppermute | solution.py:539
  18.3 2.2 %collective-permute-start.1 = (bf16[272,1024]{1,0:T(8,128)(2,1)}, bf16[272,1024]{1,0:T(8,128)(2,1)}, u32[]{:S(2)}, u32[]{:S(2)}) collective-permute-start(bf16[272,1024]{1,0:T(8,128)(2,1)} %get-tuple-element.99.refs_1_), channel_id=1, source_target_pairs={{0,12},{4,0},{8,4},{12,8},{1,13},{5,1},{9,5},{13,9},{2,14},{6,2},{... | collective-permute-start | bytes 1671176 | tf_op jit(solution)/shard_map/ppermute | solution.py:490
  21.9 5.1 %collective-permute-done.6 = bf16[2,160,768]{2,1,0:T(8,128)(2,1)} collective-permute-done((bf16[2,160,768]{2,1,0:T(8,128)(2,1)}, bf16[2,160,768]{2,1,0:T(8,128)(2,1)}, u32[]{:S(2)}, u32[]{:S(2)}) %collective-permute-start.6) | collective-permute-done | bytes 491552 | tf_op jit(solution)/shard_map/ppermute | solution.py:485
  26.9 1.5 %collective-permute-start.13 = (bf16[2,256,768]{2,1,0:T(8,128)(2,1)S(1)}, bf16[2,256,768]{2,1,0:T(8,128)(2,1)S(1)}, u32[]{:S(2)}, u32[]{:S(2)}) collective-permute-start(bf16[2,256,768]{2,1,0:T(8,128)(2,1)S(1)} %copy-done.4), channel_id=1, source_target_pairs={{0,2},{1,3},{2,0},{3,1},{4,6},{5,7},{6,4},{7,5},{8,10},{9,11},{10,... | collective-permute-start | bytes 2359304 | tf_op jit(solution)/shard_map/ppermute | solution.py:485
  28.4 1.5 %collective-permute-start.8 = (bf16[2,160,768]{2,1,0:T(8,128)(2,1)}, bf16[2,160,768]{2,1,0:T(8,128)(2,1)}, u32[]{:S(2)}, u32[]{:S(2)}) collective-permute-start(bf16[2,160,768]{2,1,0:T(8,128)(2,1)} %collective-permute-done.6), channel_id=1, source_target_pairs={{0,16},{16,0},{1,17},{17,1},{2,18},{18,2},{3,19},{19,3},{4,20},{20... | collective-permute-start | bytes 1474568 | tf_op jit(solution)/shard_map/ppermute | solution.py:547
  31.1 10.2 %collective-permute-done.8 = bf16[2,160,768]{2,1,0:T(8,128)(2,1)} collective-permute-done((bf16[2,160,768]{2,1,0:T(8,128)(2,1)}, bf16[2,160,768]{2,1,0:T(8,128)(2,1)}, u32[]{:S(2)}, u32[]{:S(2)}) %collective-permute-start.8) | collective-permute-done | bytes 491552 | tf_op jit(solution)/shard_map/ppermute | solution.py:547
  44.9 1.3 %collective-permute-done.4.refs_5_ = bf16[272,1024]{1,0:T(8,128)(2,1)} collective-permute-done((bf16[272,1024]{1,0:T(8,128)(2,1)}, bf16[272,1024]{1,0:T(8,128)(2,1)}, u32[]{:S(2)}, u32[]{:S(2)}) %collective-permute-start.4) | collective-permute-done | bytes 557088 | tf_op jit(solution)/shard_map/ppermute | solution.py:490
  48.4 1.4 %collective-permute-done.11.refs_8_ = bf16[272,1024]{1,0:T(8,128)(2,1)S(1)} collective-permute-done((bf16[272,1024]{1,0:T(8,128)(2,1)}, bf16[272,1024]{1,0:T(8,128)(2,1)S(1)}, u32[]{:S(2)}, u32[]{:S(2)}) %collective-permute-start.11) | collective-permute-done | bytes 557088 | tf_op jit(solution)/shard_map/ppermute | solution.py:485
  49.7 5.3 %shard_map.155 = (bf16[512,128]{1,0:T(8,128)(2,1)S(1)}, bf16[512,128]{1,0:T(8,128)(2,1)S(1)}, bf16[512,1024]{1,0:T(8,128)(2,1)S(1)}, bf16[512,1024]{1,0:T(8,128)...) custom-call(s32[2]{0:T(128)S(1)} %pad_add_fusion.place, ...), custom_call_target="tpu_custom_call" | custom-call | flops 20000000000 | bytes 20000000000 | tf_op jit(solution)/shard_map/pallas_call | solution.py:242
  55.0 1.5 %collective-permute-start.17 = (bf16[256,768]{1,0:T(8,128)(2,1)S(1)}, bf16[256,768]{1,0:T(8,128)(2,1)S(1)}, u32[]{:S(2)}, u32[]{:S(2)}) collective-permute-start(bf16[256,768]{1,0:T(8,128)(2,1)S(1)} %get-tuple-element.125), channel_id=1, source_target_pairs={{0,2},{1,3},{2,0},{3,1},{4,6},{5,7},{6,4},{7,5},{8,10},{9,11},{10,... | collective-permute-start | bytes 1179656 | tf_op jit(solution)/shard_map/ppermute | solution.py:485
  56.6 4.4 %shard_map.156 = (bf16[512,1024]{1,0:T(8,128)(2,1)S(1)}, bf16[512,1024]{1,0:T(8,128)(2,1)S(1)}, bf16[256,768]{1,0:T(8,128)(2,1)S(1)}, bf16[256,768]{1,0:T(8,128)(2,1)S(1)}, bf16[256,768]{1,0:T(8,128)(2,1)S(1)}) custom-call(s32[2]{0:T(128)S(1)} %pad_add_fusion.place, s32[8,128]{1,0:T(8,128)S(1)} %copy-done.12, ...), custom_call_target="tpu_custom_call" | custom-call | flops 20000000000 | bytes 20000000000 | tf_op jit(solution)/shard_map/pallas_call | solution.py:242
  63.0 4.1 %collective-permute-done.17 = bf16[256,768]{1,0:T(8,128)(2,1)S(1)} collective-permute-done((bf16[256,768]{1,0:T(8,128)(2,1)S(1)}, bf16[256,768]{1,0:T(8,128)(2,1)S(1)}, u32[]{:S(2)}, u32[]{:S(2)}) %collective-permute-start.17) | collective-permute-done | bytes 393248 | tf_op jit(solution)/shard_map/ppermute | solution.py:485
  67.1 2.2 %collective-permute-start.19 = (bf16[128,1024]{1,0:T(8,128)(2,1)S(1)}, bf16[128,1024]{1,0:T(8,128)(2,1)S(1)}, u32[]{:S(2)}, u32[]{:S(2)}) collective-permute-start(bf16[128,1024]{1,0:T(8,128)(2,1)S(1)} %add_convert_fusion.10), channel_id=1, source_target_pairs={{0,12},{4,0},{8,4},{12,8},{1,13},{5,1},{9,5},{13,9},{2,14},{6,2},{... | collective-permute-start | bytes 786440 | tf_op jit(solution)/shard_map/ppermute | solution.py:490
  69.4 5.6 %shard_map.157 = (bf16[512,768]{1,0:T(8,128)(2,1)S(1)}, bf16[512,768]{1,0:T(8,128)(2,1)S(1)}, bf16[512,128]{1,0:T(8,128)(2,1)S(1)}, f32[8,1024]{1,0:T(8,128)S(1)...) custom-call(s32[2]{0:T(128)S(1)} %pad_add_fusion.place, ...), custom_call_target="tpu_custom_call" | custom-call | flops 20000000000 | bytes 20000000000 | tf_op jit(solution)/shard_map/pallas_call | solution.py:242
  75.2 1.5 %collective-permute-start.24 = (f32[16,1024]{1,0:T(8,128)S(1)}, f32[16,1024]{1,0:T(8,128)S(1)}, u32[]{:S(2)}, u32[]{:S(2)}) collective-permute-start(f32[16,1024]{1,0:T(8,128)S(1)} %pad_maximum_fusion.1), channel_id=1, source_target_pairs={{0,2},{1,3},{2,0},{3,1},{4,6},{5,7},{6,4},{7,5},{8,10},{9,11},{10,... | collective-permute-start | bytes 196616 | tf_op jit(solution)/shard_map/ppermute | solution.py:485
  77.0 2.9 %collective-permute-start.26 = (bf16[128,1024]{1,0:T(8,128)(2,1)S(1)}, bf16[128,1024]{1,0:T(8,128)(2,1)S(1)}, u32[]{:S(2)}, u32[]{:S(2)}) collective-permute-start(bf16[128,1024]{1,0:T(8,128)(2,1)S(1)} %get-tuple-element.192), channel_id=1, source_target_pairs={{0,12},{4,0},{8,4},{12,8},{1,13},{5,1},{9,5},{13,9},{2,14},{6,2},{... | collective-permute-start | bytes 786440 | tf_op jit(solution)/shard_map/ppermute | solution.py:490
  80.4 6.7 %shard_map.158 = (bf16[512,1024]{1,0:T(8,128)(2,1)S(1)}, bf16[512,1024]{1,0:T(8,128)(2,1)S(1)}) custom-call(s32[2]{0:T(128)S(1)} %pad_add_fusion.place, bf16[512,128]{1,0:T(8,128)(2,1)S(1)} %get-tuple-element.131.refs_0_, bf16[512,768]{1,0:T(8,128)(2,1)S(1)} %get-tuple-element.142.refs_1_, bf16[512,768]{1,0:T(8,128)(2,1)S(1)} %get-tuple-element.143.refs_2_, ...), custom_call_target="tpu_custom_call" | custom-call | flops 20000000000 | bytes 20000000000 | tf_op jit(solution)/shard_map/pallas_call | solution.py:242
  87.1 3.5 %collective-permute-done.25 = bf16[128,1024]{1,0:T(8,128)(2,1)S(1)} collective-permute-done((bf16[128,1024]{1,0:T(8,128)(2,1)S(1)}, bf16[128,1024]{1,0:T(8,128)(2,1)S(1)}, u32[]{:S(2)}, u32[]{:S(2)}) %collective-permute-start.25) | collective-permute-done | bytes 262176 | tf_op jit(solution)/shard_map/ppermute | solution.py:490
  92.3 1.5 %collective-permute-start.30 = (bf16[256,768]{1,0:T(8,128)(2,1)}, bf16[256,768]{1,0:T(8,128)(2,1)}, u32[]{:S(2)}, u32[]{:S(2)}) collective-permute-start(bf16[256,768]{1,0:T(8,128)(2,1)} %get-tuple-element.161), channel_id=1, source_target_pairs={{0,2},{1,3},{2,0},{3,1},{4,6},{5,7},{6,4},{7,5},{8,10},{9,11},{10,... | collective-permute-start | bytes 1179656 | tf_op jit(solution)/shard_map/ppermute | solution.py:485
  95.7 1.5 %collective-permute-start.31 = (f32[16,1024]{1,0:T(8,128)S(1)}, f32[16,1024]{1,0:T(8,128)S(1)}, u32[]{:S(2)}, u32[]{:S(2)}) collective-permute-start(f32[16,1024]{1,0:T(8,128)S(1)} %add.156), channel_id=1, source_target_pairs={{0,4},{4,0},{8,12},{12,8},{1,5},{5,1},{9,13},{13,9},{2,6},{6,2},{1... | collective-permute-start | bytes 196616 | tf_op jit(solution)/shard_map/ppermute | solution.py:686
  102.2 2.5 %collective-permute-done.30 = bf16[256,768]{1,0:T(8,128)(2,1)} collective-permute-done((bf16[256,768]{1,0:T(8,128)(2,1)}, bf16[256,768]{1,0:T(8,128)(2,1)}, u32[]{:S(2)}, u32[]{:S(2)}) %collective-permute-start.30) | collective-permute-done | bytes 393248 | tf_op jit(solution)/shard_map/ppermute | solution.py:485
  106.7 3.2 %collective-permute-start.34 = (bf16[128,1024]{1,0:T(8,128)(2,1)S(1)}, bf16[128,1024]{1,0:T(8,128)(2,1)S(1)}, u32[]{:S(2)}, u32[]{:S(2)}) collective-permute-start(bf16[128,1024]{1,0:T(8,128)(2,1)S(1)} %add_convert_fusion.2), channel_id=1, source_target_pairs={{0,12},{4,0},{8,4},{12,8},{1,13},{5,1},{9,5},{13,9},{2,14},{6,2},{... | collective-permute-start | bytes 786440 | tf_op jit(solution)/shard_map/ppermute | solution.py:490
  109.9 1.3 %fusion.8 = (bf16[256,768]{1,0:T(8,128)(2,1)S(1)}, bf16[256,768]{1,0:T(8,128)(2,1)S(1)}) fusion(bf16[256,768]{1,0:T(8,128)(2,1)} %collective-permute-done.30, bf16[2,256,768]{2,1,0:T(8,128)(2,1)S(1)} %get-tuple-element.130, bf16[256,768]{1,0:T(8,128)(2,1)S(1)} %copy-done.22), kind=kLoop, calls=%fused_computation.19 | loop fusion | flops 1572864 | bytes 2359296 | tf_op jit(solution)/shard_map/convert_element_type | solution.py:708
  111.3 2.0 %fusion.1 = bf16[128,1024]{1,0:T(8,128)(2,1)} fusion(bf16[128,2]{0,1:T(2,128)(2,1)S(1)} %copy-done.33, bf16[2,1024]{1,0:T(2,128)(2,1)S(1)} %copy-done.30, bf16[128,1024]{1,0:T(8,128)(2,1)S(1)} %copy-done.14, bf16[128,1024]{1,0:T(8,128)(2,1)S(1)} %copy-done.39, bf16[128,1024]{1,0:T(8,128)(2,1)S(1)} %copy-done.41, f32[128]{0:T(128)S(1)} %copy-done.36, ...), kind=kOutput, calls=%fused_computation.6 | convolution fusion | flops 2359296 | bytes 1577984 | tf_op jit(solution)/shard_map/dot_general | solution.py:267
  113.3 2.0 %collective-permute-done.35 = f32[16,1024]{1,0:T(8,128)S(1)} collective-permute-done((f32[16,1024]{1,0:T(8,128)S(1)}, f32[16,1024]{1,0:T(8,128)S(1)}, u32[]{:S(2)}, u32[]{:S(2)}) %collective-permute-start.35) | collective-permute-done | bytes 65568 | tf_op jit(solution)/shard_map/ppermute | solution.py:690
  116.6 2.8 %collective-permute-done.34 = bf16[128,1024]{1,0:T(8,128)(2,1)S(1)} collective-permute-done((bf16[128,1024]{1,0:T(8,128)(2,1)S(1)}, bf16[128,1024]{1,0:T(8,128)(2,1)S(1)}, u32[]{:S(2)}, u32[]{:S(2)}) %collective-permute-start.34) | collective-permute-done | bytes 262176 | tf_op jit(solution)/shard_map/ppermute | solution.py:490
  120.5 1.4 %select_convert_fusion = (bf16[2,256,768]{2,1,0:T(8,128)(2,1)}, bf16[2,256,768]{2,1,0:T(8,128)(2,1)}) fusion(bf16[256,768]{1,0:T(8,128)(2,1)S(1)} %get-tuple-element.190, bf16[256,768]{1,0:T(8,128)(2,1)S(1)} %get-tuple-element.183, pred[2]{0:T(512)(128)(4,1)S(1)} %copy-done.34, bf16[256,768]{1,0:T(8,128)(2,1)S(1)} %get-tuple-element.191, ...), kind=kLoop, calls=%fused_computation | loop fusion | flops 786432 | bytes 3145730 | tf_op jit(solution)/shard_map/convert_element_type | solution.py:590
  (189 shorter events, 28.7 us)
Async XLA Ops:
  2.8 18.0 %collective-permute-start.2 = (bf16[272,1024]{1,0:T(8,128)(2,1)}, bf16[272,1024]{1,0:T(8,128)(2,1)}, u32[]{:S(2)}, u32[]{:S(2)}) collective-permute-start(bf16[272,1024]{1,0:T(8,128)(2,1)} %get-tuple-element.99.refs_1_), channel_id=1, source_target_pairs={{0,4},{4,8},{8,12},{12,0},{1,5},{5,9},{9,13},{13,1},{2,6},{6,10},{... | collective-permute-start | bytes 1671176 | tf_op jit(solution)/shard_map/ppermute | solution.py:490
  5.8 12.5 %collective-permute-start = (bf16[272,1024]{1,0:T(8,128)(2,1)}, bf16[272,1024]{1,0:T(8,128)(2,1)S(1)}, u32[]{:S(2)}, u32[]{:S(2)}) collective-permute-start(bf16[272,1024]{1,0:T(8,128)(2,1)} %get-tuple-element.99.refs_1_), channel_id=1, source_target_pairs={{0,1},{1,0},{2,3},{3,2},{4,5},{5,4},{6,7},{7,6},{8,9},{9,8},{10,11... | collective-permute-start | bytes 1671176 | tf_op jit(solution)/shard_map/ppermute | solution.py:485
  6.7 10.1 %collective-permute-start.3 = (bf16[2,96,768]{2,1,0:T(8,128)(2,1)}, bf16[2,96,768]{2,1,0:T(8,128)(2,1)}, u32[]{:S(2)}, u32[]{:S(2)}) collective-permute-start(bf16[2,96,768]{2,1,0:T(8,128)(2,1)} %slice.99), channel_id=1, source_target_pairs={{0,2},{1,3},{2,0},{3,1},{4,6},{5,7},{6,4},{7,5},{8,10},{9,11},{10,... | collective-permute-start | bytes 884744 | tf_op jit(solution)/shard_map/ppermute | solution.py:485
  9.0 18.0 %collective-permute-start.6 = (bf16[2,160,768]{2,1,0:T(8,128)(2,1)}, bf16[2,160,768]{2,1,0:T(8,128)(2,1)}, u32[]{:S(2)}, u32[]{:S(2)}) collective-permute-start(bf16[2,160,768]{2,1,0:T(8,128)(2,1)} %slice.100), channel_id=1, source_target_pairs={{0,2},{1,3},{2,0},{3,1},{4,6},{5,7},{6,4},{7,5},{8,10},{9,11},{10,... | collective-permute-start | bytes 1474568 | tf_op jit(solution)/shard_map/ppermute | solution.py:485
  10.8 17.6 %collective-permute-start.7 = (bf16[3,256,768]{2,1,0:T(8,128)(2,1)}, bf16[3,256,768]{2,1,0:T(8,128)(2,1)}, u32[]{:S(2)}, u32[]{:S(2)}) collective-permute-start(bf16[3,256,768]{2,1,0:T(8,128)(2,1)} %pad_maximum_fusion), channel_id=1, source_target_pairs={{0,1},{1,0},{2,3},{3,2},{4,5},{5,4},{6,7},{7,6},{8,9},{9,8},{10,11... | collective-permute-start | bytes 3538952 | tf_op jit(solution)/shard_map/ppermute | solution.py:485
  16.8 14.3 %collective-permute-start.5 = (bf16[2,96,768]{2,1,0:T(8,128)(2,1)}, bf16[2,96,768]{2,1,0:T(8,128)(2,1)}, u32[]{:S(2)}, u32[]{:S(2)}) collective-permute-start(bf16[2,96,768]{2,1,0:T(8,128)(2,1)} %collective-permute-done.3), channel_id=1, source_target_pairs={{0,16},{16,0},{1,17},{17,1},{2,18},{18,2},{3,19},{19,3},{4,20},{20... | collective-permute-start | bytes 884744 | tf_op jit(solution)/shard_map/ppermute | solution.py:539
  18.3 26.6 %collective-permute-start.1 = (bf16[272,1024]{1,0:T(8,128)(2,1)}, bf16[272,1024]{1,0:T(8,128)(2,1)}, u32[]{:S(2)}, u32[]{:S(2)}) collective-permute-start(bf16[272,1024]{1,0:T(8,128)(2,1)} %get-tuple-element.99.refs_1_), channel_id=1, source_target_pairs={{0,12},{4,0},{8,4},{12,8},{1,13},{5,1},{9,5},{13,9},{2,14},{6,2},{... | collective-permute-start | bytes 1671176 | tf_op jit(solution)/shard_map/ppermute | solution.py:490
  20.9 25.3 %collective-permute-start.4 = (bf16[272,1024]{1,0:T(8,128)(2,1)}, bf16[272,1024]{1,0:T(8,128)(2,1)}, u32[]{:S(2)}, u32[]{:S(2)}) collective-permute-start(bf16[272,1024]{1,0:T(8,128)(2,1)} %collective-permute-done.2.refs_3_), channel_id=1, source_target_pairs={{0,4},{4,8},{8,12},{12,0},{1,5},{5,9},{9,13},{13,1},{2,6},{6,10},{... | collective-permute-start | bytes 1671176 | tf_op jit(solution)/shard_map/ppermute | solution.py:490
  26.9 19.9 %collective-permute-start.13 = (bf16[2,256,768]{2,1,0:T(8,128)(2,1)S(1)}, bf16[2,256,768]{2,1,0:T(8,128)(2,1)S(1)}, u32[]{:S(2)}, u32[]{:S(2)}) collective-permute-start(bf16[2,256,768]{2,1,0:T(8,128)(2,1)S(1)} %copy-done.4), channel_id=1, source_target_pairs={{0,2},{1,3},{2,0},{3,1},{4,6},{5,7},{6,4},{7,5},{8,10},{9,11},{10,... | collective-permute-start | bytes 2359304 | tf_op jit(solution)/shard_map/ppermute | solution.py:485
  28.4 12.9 %collective-permute-start.8 = (bf16[2,160,768]{2,1,0:T(8,128)(2,1)}, bf16[2,160,768]{2,1,0:T(8,128)(2,1)}, u32[]{:S(2)}, u32[]{:S(2)}) collective-permute-start(bf16[2,160,768]{2,1,0:T(8,128)(2,1)} %collective-permute-done.6), channel_id=1, source_target_pairs={{0,16},{16,0},{1,17},{17,1},{2,18},{18,2},{3,19},{19,3},{4,20},{20... | collective-permute-start | bytes 1474568 | tf_op jit(solution)/shard_map/ppermute | solution.py:547
  43.6 6.1 %collective-permute-start.12 = (bf16[2,256,768]{2,1,0:T(8,128)(2,1)S(1)}, bf16[2,256,768]{2,1,0:T(8,128)(2,1)S(1)}, u32[]{:S(2)}, u32[]{:S(2)}) collective-permute-start(bf16[2,256,768]{2,1,0:T(8,128)(2,1)S(1)} %maximum_select_fusion.1), channel_id=1, source_target_pairs={{0,1},{1,0},{2,3},{3,2},{4,5},{5,4},{6,7},{7,6},{8,9},{9,8},{10,11... | collective-permute-start | bytes 2359304 | tf_op jit(solution)/shard_map/ppermute | solution.py:485
  44.8 2.9 %collective-permute-start.9 = (bf16[272,1024]{1,0:T(8,128)(2,1)}, bf16[272,1024]{1,0:T(8,128)(2,1)S(1)}, u32[]{:S(2)}, u32[]{:S(2)}) collective-permute-start(bf16[272,1024]{1,0:T(8,128)(2,1)} %collective-permute-done.2.refs_3_), channel_id=1, source_target_pairs={{0,1},{1,0},{2,3},{3,2},{4,5},{5,4},{6,7},{7,6},{8,9},{9,8},{10,11... | collective-permute-start | bytes 1671176 | tf_op jit(solution)/shard_map/ppermute | solution.py:485
  46.2 3.5 %collective-permute-start.11 = (bf16[272,1024]{1,0:T(8,128)(2,1)}, bf16[272,1024]{1,0:T(8,128)(2,1)S(1)}, u32[]{:S(2)}, u32[]{:S(2)}) collective-permute-start(bf16[272,1024]{1,0:T(8,128)(2,1)} %collective-permute-done.1.refs_7_), channel_id=1, source_target_pairs={{0,1},{1,0},{2,3},{3,2},{4,5},{5,4},{6,7},{7,6},{8,9},{9,8},{10,11... | collective-permute-start | bytes 1671176 | tf_op jit(solution)/shard_map/ppermute | solution.py:485
  46.9 8.2 %collective-permute-start.14 = (bf16[256,768]{1,0:T(8,128)(2,1)S(1)}, bf16[256,768]{1,0:T(8,128)(2,1)S(1)}, u32[]{:S(2)}, u32[]{:S(2)}) collective-permute-start(bf16[256,768]{1,0:T(8,128)(2,1)S(1)} %dynamic-slice_bitcast_fusion), channel_id=1, source_target_pairs={{0,1},{1,0},{2,3},{3,2},{4,5},{5,4},{6,7},{7,6},{8,9},{9,8},{10,11... | collective-permute-start | bytes 1179656 | tf_op jit(solution)/shard_map/ppermute | solution.py:485
  55.0 12.0 %collective-permute-start.17 = (bf16[256,768]{1,0:T(8,128)(2,1)S(1)}, bf16[256,768]{1,0:T(8,128)(2,1)S(1)}, u32[]{:S(2)}, u32[]{:S(2)}) collective-permute-start(bf16[256,768]{1,0:T(8,128)(2,1)S(1)} %get-tuple-element.125), channel_id=1, source_target_pairs={{0,2},{1,3},{2,0},{3,1},{4,6},{5,7},{6,4},{7,5},{8,10},{9,11},{10,... | collective-permute-start | bytes 1179656 | tf_op jit(solution)/shard_map/ppermute | solution.py:485
  61.9 13.1 %collective-permute-start.18 = (bf16[256,768]{1,0:T(8,128)(2,1)S(1)}, bf16[256,768]{1,0:T(8,128)(2,1)S(1)}, u32[]{:S(2)}, u32[]{:S(2)}) collective-permute-start(bf16[256,768]{1,0:T(8,128)(2,1)S(1)} %get-tuple-element.138), channel_id=1, source_target_pairs={{0,3},{1,2},{2,1},{3,0},{4,7},{5,6},{6,5},{7,4},{8,11},{9,10},{10,... | collective-permute-start | bytes 1179656 | tf_op jit(solution)/shard_map/ppermute | solution.py:485
  62.2 12.8 %collective-permute-start.21 = (bf16[256,768]{1,0:T(8,128)(2,1)S(1)}, bf16[256,768]{1,0:T(8,128)(2,1)S(1)}, u32[]{:S(2)}, u32[]{:S(2)}) collective-permute-start(bf16[256,768]{1,0:T(8,128)(2,1)S(1)} %get-tuple-element.141), channel_id=1, source_target_pairs={{0,1},{1,0},{2,3},{3,2},{4,5},{5,4},{6,7},{7,6},{8,9},{9,8},{10,11... | collective-permute-start | bytes 1179656 | tf_op jit(solution)/shard_map/ppermute | solution.py:485
  62.7 12.4 %collective-permute-start.20 = (bf16[256,1024]{1,0:T(8,128)(2,1)S(1)}, bf16[256,1024]{1,0:T(8,128)(2,1)S(1)}, u32[]{:S(2)}, u32[]{:S(2)}) collective-permute-start(bf16[256,1024]{1,0:T(8,128)(2,1)S(1)} %slice.84), channel_id=1, source_target_pairs={{0,1},{1,0},{2,3},{3,2},{4,5},{5,4},{6,7},{7,6},{8,9},{9,8},{10,11... | collective-permute-start | bytes 1572872 | tf_op jit(solution)/shard_map/ppermute | solution.py:485
  67.1 8.0 %collective-permute-start.19 = (bf16[128,1024]{1,0:T(8,128)(2,1)S(1)}, bf16[128,1024]{1,0:T(8,128)(2,1)S(1)}, u32[]{:S(2)}, u32[]{:S(2)}) collective-permute-start(bf16[128,1024]{1,0:T(8,128)(2,1)S(1)} %add_convert_fusion.10), channel_id=1, source_target_pairs={{0,12},{4,0},{8,4},{12,8},{1,13},{5,1},{9,5},{13,9},{2,14},{6,2},{... | collective-permute-start | bytes 786440 | tf_op jit(solution)/shard_map/ppermute | solution.py:490
  75.2 11.9 %collective-permute-start.24 = (f32[16,1024]{1,0:T(8,128)S(1)}, f32[16,1024]{1,0:T(8,128)S(1)}, u32[]{:S(2)}, u32[]{:S(2)}) collective-permute-start(f32[16,1024]{1,0:T(8,128)S(1)} %pad_maximum_fusion.1), channel_id=1, source_target_pairs={{0,2},{1,3},{2,0},{3,1},{4,6},{5,7},{6,4},{7,5},{8,10},{9,11},{10,... | collective-permute-start | bytes 196616 | tf_op jit(solution)/shard_map/ppermute | solution.py:485
  77.0 10.1 %collective-permute-start.26 = (bf16[128,1024]{1,0:T(8,128)(2,1)S(1)}, bf16[128,1024]{1,0:T(8,128)(2,1)S(1)}, u32[]{:S(2)}, u32[]{:S(2)}) collective-permute-start(bf16[128,1024]{1,0:T(8,128)(2,1)S(1)} %get-tuple-element.192), channel_id=1, source_target_pairs={{0,12},{4,0},{8,4},{12,8},{1,13},{5,1},{9,5},{13,9},{2,14},{6,2},{... | collective-permute-start | bytes 786440 | tf_op jit(solution)/shard_map/ppermute | solution.py:490
  79.9 10.7 %collective-permute-start.25 = (bf16[128,1024]{1,0:T(8,128)(2,1)S(1)}, bf16[128,1024]{1,0:T(8,128)(2,1)S(1)}, u32[]{:S(2)}, u32[]{:S(2)}) collective-permute-start(bf16[128,1024]{1,0:T(8,128)(2,1)S(1)} %get-tuple-element.193), channel_id=1, source_target_pairs={{0,4},{4,8},{8,12},{12,0},{1,5},{5,9},{9,13},{13,1},{2,6},{6,10},{... | collective-permute-start | bytes 786440 | tf_op jit(solution)/shard_map/ppermute | solution.py:490
  79.9 10.7 %collective-permute-start.22 = (bf16[256,768]{1,0:T(8,128)(2,1)S(1)}, bf16[256,768]{1,0:T(8,128)(2,1)S(1)}, u32[]{:S(2)}, u32[]{:S(2)}) collective-permute-start(bf16[256,768]{1,0:T(8,128)(2,1)S(1)} %get-tuple-element.147), channel_id=1, source_target_pairs={{0,2},{1,3},{2,0},{3,1},{4,6},{5,7},{6,4},{7,5},{8,10},{9,11},{10,... | collective-permute-start | bytes 1179656 | tf_op jit(solution)/shard_map/ppermute | solution.py:485
  80.4 10.2 %collective-permute-start.23 = (bf16[2,256,768]{2,1,0:T(8,128)(2,1)S(1)}, bf16[2,256,768]{2,1,0:T(8,128)(2,1)S(1)}, u32[]{:S(2)}, u32[]{:S(2)}) collective-permute-start(bf16[2,256,768]{2,1,0:T(8,128)(2,1)S(1)} %get-tuple-element.148), channel_id=1, source_target_pairs={{0,1},{1,0},{2,3},{3,2},{4,5},{5,4},{6,7},{7,6},{8,9},{9,8},{10,11... | collective-permute-start | bytes 2359304 | tf_op jit(solution)/shard_map/ppermute | solution.py:485
  90.6 3.2 %collective-permute-start.27 = (bf16[512,1024]{1,0:T(8,128)(2,1)S(1)}, bf16[512,1024]{1,0:T(8,128)(2,1)S(1)}, u32[]{:S(2)}, u32[]{:S(2)}) collective-permute-start(bf16[512,1024]{1,0:T(8,128)(2,1)S(1)} %get-tuple-element.157), channel_id=1, source_target_pairs={{0,1},{1,0},{2,3},{3,2},{4,5},{5,4},{6,7},{7,6},{8,9},{9,8},{10,11... | collective-permute-start | bytes 3145736 | tf_op jit(solution)/shard_map/ppermute | solution.py:485
  92.3 12.3 %collective-permute-start.30 = (bf16[256,768]{1,0:T(8,128)(2,1)}, bf16[256,768]{1,0:T(8,128)(2,1)}, u32[]{:S(2)}, u32[]{:S(2)}) collective-permute-start(bf16[256,768]{1,0:T(8,128)(2,1)} %get-tuple-element.161), channel_id=1, source_target_pairs={{0,2},{1,3},{2,0},{3,1},{4,6},{5,7},{6,4},{7,5},{8,10},{9,11},{10,... | collective-permute-start | bytes 1179656 | tf_op jit(solution)/shard_map/ppermute | solution.py:485
  95.7 9.0 %collective-permute-start.31 = (f32[16,1024]{1,0:T(8,128)S(1)}, f32[16,1024]{1,0:T(8,128)S(1)}, u32[]{:S(2)}, u32[]{:S(2)}) collective-permute-start(f32[16,1024]{1,0:T(8,128)S(1)} %add.156), channel_id=1, source_target_pairs={{0,4},{4,0},{8,12},{12,8},{1,5},{5,1},{9,13},{13,9},{2,6},{6,2},{1... | collective-permute-start | bytes 196616 | tf_op jit(solution)/shard_map/ppermute | solution.py:686
  97.2 8.5 %collective-permute-start.29 = (bf16[128,1024]{1,0:T(8,128)(2,1)S(1)}, bf16[128,1024]{1,0:T(8,128)(2,1)S(1)}, u32[]{:S(2)}, u32[]{:S(2)}) collective-permute-start(bf16[128,1024]{1,0:T(8,128)(2,1)S(1)} %get-tuple-element.160), channel_id=1, source_target_pairs={{0,12},{4,0},{8,4},{12,8},{1,13},{5,1},{9,5},{13,9},{2,14},{6,2},{... | collective-permute-start | bytes 786440 | tf_op jit(solution)/shard_map/ppermute | solution.py:490
  99.1 21.2 %collective-permute-start.32 = (bf16[2,256,768]{2,1,0:T(8,128)(2,1)S(1)}, bf16[2,256,768]{2,1,0:T(8,128)(2,1)S(1)}, u32[]{:S(2)}, u32[]{:S(2)}) collective-permute-start(bf16[2,256,768]{2,1,0:T(8,128)(2,1)S(1)} %copy-done.9), channel_id=1, source_target_pairs={{0,3},{1,2},{2,1},{3,0},{4,7},{5,6},{6,5},{7,4},{8,11},{9,10},{10,... | collective-permute-start | bytes 2359304 | tf_op jit(solution)/shard_map/ppermute | solution.py:485
  101.1 15.5 %collective-permute-start.33 = (bf16[128,1024]{1,0:T(8,128)(2,1)}, bf16[128,1024]{1,0:T(8,128)(2,1)S(1)}, u32[]{:S(2)}, u32[]{:S(2)}) collective-permute-start(bf16[128,1024]{1,0:T(8,128)(2,1)} %get-tuple-element.174), channel_id=1, source_target_pairs={{0,4},{4,8},{8,12},{12,0},{1,5},{5,9},{9,13},{13,1},{2,6},{6,10},{... | collective-permute-start | bytes 786440 | tf_op jit(solution)/shard_map/ppermute | solution.py:490
  105.7 9.6 %collective-permute-start.35 = (f32[16,1024]{1,0:T(8,128)S(1)}, f32[16,1024]{1,0:T(8,128)S(1)}, u32[]{:S(2)}, u32[]{:S(2)}) collective-permute-start(f32[16,1024]{1,0:T(8,128)S(1)} %add.174), channel_id=1, source_target_pairs={{0,8},{4,12},{8,0},{12,4},{1,9},{5,13},{9,1},{13,5},{2,10},{6,14},... | collective-permute-start | bytes 196616 | tf_op jit(solution)/shard_map/ppermute | solution.py:690
  106.7 12.7 %collective-permute-start.34 = (bf16[128,1024]{1,0:T(8,128)(2,1)S(1)}, bf16[128,1024]{1,0:T(8,128)(2,1)S(1)}, u32[]{:S(2)}, u32[]{:S(2)}) collective-permute-start(bf16[128,1024]{1,0:T(8,128)(2,1)S(1)} %add_convert_fusion.2), channel_id=1, source_target_pairs={{0,12},{4,0},{8,4},{12,8},{1,13},{5,1},{9,5},{13,9},{2,14},{6,2},{... | collective-permute-start | bytes 786440 | tf_op jit(solution)/shard_map/ppermute | solution.py:490
  (46 other events, 236.2 us)
